TPU v7x, 32 devices: a whole 2x2x4 slice. The times are simulated.
32 devices in a mesh: dp: 8 (over z, x), mp: 4 (over y, core).
Axes of the slice: x: 2, y: 2, z: 4, core: 2. Of those that a mesh axis runs over, the one named last changes fastest.
Arguments:
- patch_rows: bfloat16 [4096, 768], P('dp'), may hold values from -6 to 6
- patches: int32 [64], replicated, may hold values from 100 to 256, as said below
- visible: int32 [64, 64], replicated, may hold values from -1 to 255, as said below
- owner: int32 [64], replicated, may hold values from 0 to 7, as said below
- qkv_weight: bfloat16 [768, 2304], P(None, 'mp'), may hold values from -0.21875 to 0.21875
- query_bias: bfloat16 [768], P('mp'), may hold values from -3 to 3
- value_bias: bfloat16 [768], P('mp'), may hold values from -3 to 3
- out_weight: bfloat16 [768, 768], P('mp'), may hold values from -1.25 to 1.25
- out_bias: bfloat16 [768], replicated, may hold values from -2 to 2
- first_gain: bfloat16 [768], replicated, may hold values from 0.5 to 1.5
- first_shift: bfloat16 [768], replicated, may hold values from -2 to 2
- second_gain: bfloat16 [768], replicated, may hold values from 0.5 to 1.5
- second_shift: bfloat16 [768], replicated, may hold values from -2 to 2
- up_weight: bfloat16 [768, 3072], P(None, 'mp'), may hold values from -0.21875 to 0.21875
- up_bias: bfloat16 [3072], P('mp'), may hold values from -2 to 2
- down_weight: bfloat16 [3072, 768], P('mp'), may hold values from -0.109375 to 0.109375
- down_bias: bfloat16 [768], replicated, may hold values from -2 to 2
- proj_weight: bfloat16 [768, 512], P(None, 'mp'), may hold values from -0.21875 to 0.21875
- proj_bias: bfloat16 [512], P('mp'), may hold values from -2 to 2
- mask_token: bfloat16 [512], P('mp'), may hold values from -3 to 3
- decoder_pos: bfloat16 [256, 512], P(None, 'mp'), may hold values from -3 to 3
- grid_cotangent: bfloat16 [64, 256, 512], P('dp', None, 'mp'), may hold values from -6 to 6
Outputs:
- grids: bfloat16 [64, 256, 512], P('dp', None, 'mp')
- input_grad: bfloat16 [4096, 768], P(('dp', 'mp'))
- qkv_weight_grad: float32 [768, 2304], P('dp', 'mp')
- query_bias_grad: float32 [768], P('mp')
- value_bias_grad: float32 [768], P('mp')
- out_weight_grad: float32 [768, 768], P('mp', 'dp')
- out_bias_grad: float32 [768], replicated
- first_gain_grad: float32 [768], replicated
- first_shift_grad: float32 [768], replicated
- second_gain_grad: float32 [768], replicated
- second_shift_grad: float32 [768], replicated
- up_weight_grad: float32 [768, 3072], P('dp', 'mp')
- up_bias_grad: float32 [3072], P('mp')
- down_weight_grad: float32 [3072, 768], P('mp', 'dp')
- down_bias_grad: float32 [768], replicated
- proj_weight_grad: float32 [768, 512], P('dp', 'mp')
- proj_bias_grad: float32 [512], P('mp')
- mask_token_grad: float32 [512], P('mp')
- decoder_pos_grad: float32 [256, 512], P('dp', 'mp')
Inputs may be any that keep to these rules, and one draw needn't show every extreme that they name: Every entry is 100, 196 or 256 (grids of 10, 14 or 16 patches a side); the first image has 100 and the second 256. `visible`: row g holds patches_g / 4 distinct positions below patches_g in its first entries and -1 in the rest. `owner`: the 8 images of each index of dp name every index of dp exactly once.
All inputs are finite; a program needn't handle non-finite values.
Results may differ from a plain program's by a relative error of at most 0.024.
Values may be sent and summed in bfloat16 or wider, within the bound.
No kernel may reach another device: no remote copies, remote signals or barrier semaphores. Data moves between devices by JAX's collectives and lax.ppermute only.
A program may use at most 192 MiB of HBM per device.

v0:
```python
from functools import partial
import math

import jax
import jax.numpy as jnp
from jax import lax
from jax.sharding import PartitionSpec as P

HEAD_DIM = 64
GRID = 256
VIS = 64


epsilon = 1e-06
highest = lax.Precision.HIGHEST
grid_sides = (10, 14, 16)


def layer_norm(inputs, norm_gain, norm_shift):
    center = inputs - jnp.mean(inputs, axis=-1, keepdims=True)
    spread = jnp.mean(center * center, axis=-1, keepdims=True)
    return center * lax.rsqrt(spread + epsilon) * norm_gain + norm_shift


def interp_table(side_cells, grid_edge):
    places = jnp.arange(grid_edge)
    numerator = (2 * places + 1) * grid_edge - side_cells
    lower_cell = numerator // (2 * side_cells)
    upper_share = numerator.astype(jnp.float32) / (2 * side_cells) - lower_cell.astype(jnp.float32)
    first_cell = jnp.clip(lower_cell, 0, grid_edge - 1)
    second_cell = jnp.clip(lower_cell + 1, 0, grid_edge - 1)
    columns = jnp.arange(grid_edge)
    lerp_rows = (1.0 - upper_share)[:, None] * (
        columns[None, :] == first_cell[:, None]
    ) + upper_share[:, None] * (columns[None, :] == second_cell[:, None])
    return lerp_rows[:side_cells]


def spread_table(table_pos, side_cells):
    grid_edge = math.isqrt(GRID)
    lerp_rows = interp_table(side_cells, grid_edge)
    pos_cube = table_pos.reshape(grid_edge, grid_edge, -1)
    full_grid = jnp.einsum("ia,jb,abc->ijc", lerp_rows, lerp_rows, pos_cube, precision=highest)
    flat_rows = full_grid.reshape(side_cells * side_cells, -1)
    return jnp.pad(flat_rows, ((0, GRID - side_cells * side_cells), (0, 0)))


def spread_back(grad_rows, side_cells):
    grid_edge = math.isqrt(GRID)
    lerp_rows = interp_table(side_cells, grid_edge)
    grad_cube = grad_rows[: side_cells * side_cells].reshape(side_cells, side_cells, -1)
    return jnp.einsum("ia,jb,ijc->abc", lerp_rows, lerp_rows, grad_cube, precision=highest).reshape(
        GRID, -1
    )


def matmul(left_op, right_op, pattern):
    return jnp.einsum(pattern, left_op, right_op, preferred_element_type=jnp.float32)


def local(
    patch_rows,
    patches,
    visible,
    owner,
    qkv_weight,
    query_bias,
    value_bias,
    out_weight,
    out_bias,
    first_gain,
    first_shift,
    second_gain,
    second_shift,
    up_weight,
    up_bias,
    down_weight,
    down_bias,
    proj_weight,
    proj_bias,
    mask_token,
    decoder_pos,
    grid_cotangent,
):
    low_type = jnp.bfloat16
    wide_type = jnp.float32
    data_ranks = lax.axis_size("dp")
    model_parts = lax.axis_size("mp")
    data_index = lax.axis_index("dp")
    model_index = lax.axis_index("mp")
    row_count = patch_rows.shape[0]
    image_count = row_count // VIS
    local_heads = qkv_weight.shape[1] // (3 * HEAD_DIM)
    share_rows = row_count // model_parts

    def combine(partial_sum):
        return lax.psum(partial_sum.astype(jnp.bfloat16), "mp").astype(jnp.float32)

    residual_in = patch_rows.astype(wide_type)
    normed_one, norm_one_back = jax.vjp(
        layer_norm, residual_in, first_gain.astype(wide_type), first_shift.astype(wide_type)
    )
    act_one = normed_one.astype(low_type)
    mixed_cols = matmul(act_one, qkv_weight, "rd,dc->rc").reshape(
        image_count, VIS, local_heads, 3, HEAD_DIM
    )
    queries = (
        mixed_cols[:, :, :, 0] + query_bias.astype(wide_type).reshape(local_heads, HEAD_DIM)
    ).astype(low_type)
    key_rows = mixed_cols[:, :, :, 1].astype(low_type)
    value_rows = (
        mixed_cols[:, :, :, 2] + value_bias.astype(wide_type).reshape(local_heads, HEAD_DIM)
    ).astype(low_type)
    own_patches = lax.dynamic_slice_in_dim(patches, data_index * image_count, image_count, 0)
    live_keys = (jnp.arange(VIS)[None, :] < (own_patches // 4)[:, None])[:, None, None, :]
    scale_factor = HEAD_DIM ** (-0.5)

    def score_block():
        raw_scores = matmul(queries, key_rows, "sqhd,skhd->shqk") * scale_factor
        return jnp.where(live_keys, raw_scores, -1e30)

    scores = score_block()
    row_top = jnp.max(scores, axis=-1, keepdims=True)
    raised = jnp.exp(scores - row_top)
    row_total = jnp.sum(raised, axis=-1, keepdims=True)
    log_total = row_top + jnp.log(row_total)
    prob_low = (raised / row_total).astype(low_type)
    attended = (
        matmul(prob_low, value_rows, "shqk,skhd->sqhd")
        .reshape(row_count, local_heads * HEAD_DIM)
        .astype(low_type)
    )
    hidden = (
        residual_in
        + combine(matmul(attended, out_weight, "rh,hd->rd"))
        + out_bias.astype(wide_type)
    )
    normed_two, norm_two_back = jax.vjp(
        layer_norm, hidden, second_gain.astype(wide_type), second_shift.astype(wide_type)
    )
    act_two = normed_two.astype(low_type)
    up_pre = matmul(act_two, up_weight, "rd,df->rf") + up_bias.astype(wide_type)
    activated, gelu_back = jax.vjp(partial(jax.nn.gelu, approximate=False), up_pre)
    acted_low = activated.astype(low_type)
    encoder_out = (
        hidden + combine(matmul(acted_low, down_weight, "rf,fd->rd")) + down_bias.astype(wide_type)
    )
    out_low = encoder_out.astype(low_type)
    encoded = (
        (matmul(out_low, proj_weight, "rd,dc->rc") + proj_bias.astype(wide_type))
        .astype(low_type)
        .reshape(image_count, VIS, -1)
    )
    own_owner = lax.dynamic_slice_in_dim(owner, data_index * image_count, image_count, 0)
    image_slots = jnp.arange(image_count)
    peer_match = own_owner[None, :] == jnp.arange(data_ranks)[:, None]
    sender_order = jnp.sum(jnp.where(peer_match, image_slots[None, :], 0), axis=1)
    arrived = lax.all_to_all(encoded[sender_order], "dp", split_axis=0, concat_axis=0, tiled=True)
    owner_table = owner.reshape(data_ranks, image_count)
    source_match = owner_table == data_index
    source_image = jnp.arange(data_ranks) * image_count + jnp.sum(
        jnp.where(source_match, image_slots[None, :], 0), axis=1
    )
    slot_visible = visible[source_image]
    slot_patches = patches[source_image]
    places = jnp.arange(GRID)
    onehot = (slot_visible[:, None, :] == places[None, :, None]).astype(low_type)
    seen_mask = jnp.sum(onehot.astype(wide_type), axis=2)
    valid_mask = (places[None, :] < slot_patches[:, None]).astype(wide_type)
    fill_mask = valid_mask - seen_mask
    table_pos = decoder_pos.astype(wide_type)
    layouts = [spread_table(table_pos, side_cells) for side_cells in grid_sides]
    position = jnp.where(
        (slot_patches == 100)[:, None, None],
        layouts[0],
        jnp.where((slot_patches == 196)[:, None, None], layouts[1], layouts[2]),
    )
    placed = matmul(onehot, arrived, "spk,skc->spc")
    grid_out = (placed + fill_mask[:, :, None] * mask_token.astype(wide_type) + position).astype(
        low_type
    )
    mask_grad = matmul(fill_mask.astype(low_type), grid_cotangent, "sp,spc->c")
    pos_grad = jnp.zeros(decoder_pos.shape, wide_type)
    for side_cells in grid_sides:
        chosen = (slot_patches == side_cells * side_cells).astype(low_type)
        pos_grad = pos_grad + spread_back(matmul(chosen, grid_cotangent, "s,spc->pc"), side_cells)
    back_rows = matmul(onehot, grid_cotangent, "spk,spc->skc").astype(low_type)
    returned = lax.all_to_all(back_rows, "dp", split_axis=0, concat_axis=0, tiled=True)
    enc_grad = returned[own_owner].reshape(row_count, -1)
    proj_bias_grad = jnp.sum(enc_grad, axis=0, dtype=wide_type)
    proj_weight_grad = matmul(out_low, enc_grad, "rd,rc->dc")
    out_grad = combine(matmul(enc_grad, proj_weight, "rc,dc->rd"))
    down_bias_grad = jnp.sum(out_grad, axis=0)
    down_low = out_grad.astype(low_type)
    down_weight_grad = matmul(acted_low, down_low, "rf,rd->fd")
    (up_grad,) = gelu_back(matmul(down_low, down_weight, "rd,fd->rf"))
    up_low = up_grad.astype(low_type)
    up_bias_grad = jnp.sum(up_low, axis=0, dtype=wide_type)
    up_weight_grad = matmul(act_two, up_low, "rd,rf->df")
    norm_two_grad = combine(matmul(up_low, up_weight, "rf,df->rd"))
    hidden_part, second_gain_grad, second_shift_grad = norm_two_back(norm_two_grad)
    hidden_grad = out_grad + hidden_part
    out_bias_grad = jnp.sum(hidden_grad, axis=0)
    attn_low = hidden_grad.astype(low_type)
    out_weight_grad = matmul(attended, attn_low, "rh,rd->hd")
    attended_grad = (
        matmul(attn_low, out_weight, "rd,hd->rh")
        .astype(low_type)
        .reshape(image_count, VIS, local_heads, HEAD_DIM)
    )
    value_low = matmul(prob_low, attended_grad, "shqk,sqhd->skhd").astype(low_type)
    recomputed = jnp.exp(score_block() - log_total)
    prob_grad = matmul(attended_grad, value_rows, "sqhd,skhd->shqk")
    score_low = (
        recomputed * (prob_grad - jnp.sum(recomputed * prob_grad, axis=-1, keepdims=True))
    ).astype(low_type)
    query_low = (matmul(score_low, key_rows, "shqk,skhd->sqhd") * scale_factor).astype(low_type)
    key_low = (matmul(score_low, queries, "shqk,sqhd->skhd") * scale_factor).astype(low_type)
    query_bias_grad = jnp.sum(query_low, axis=(0, 1), dtype=wide_type).reshape(-1)
    value_bias_grad = jnp.sum(value_low, axis=(0, 1), dtype=wide_type).reshape(-1)
    qkv_grad = jnp.stack((query_low, key_low, value_low), axis=3).reshape(row_count, -1)
    qkv_weight_grad = matmul(act_one, qkv_grad, "rd,rc->dc")
    norm_one_grad = combine(matmul(qkv_grad, qkv_weight, "rc,dc->rd"))
    input_part, first_gain_grad, first_shift_grad = norm_one_back(norm_one_grad)
    input_grad = hidden_grad + input_part
    input_grad = lax.dynamic_slice_in_dim(input_grad, model_index * share_rows, share_rows, 0)
    (
        qkv_weight_grad,
        out_weight_grad,
        up_weight_grad,
        down_weight_grad,
        proj_weight_grad,
        pos_grad,
    ) = (
        lax.psum_scatter(
            qkv_weight_grad.astype(jnp.bfloat16), "dp", scatter_dimension=0, tiled=True
        ).astype(jnp.float32),
        lax.psum_scatter(
            out_weight_grad.astype(jnp.bfloat16), "dp", scatter_dimension=1, tiled=True
        ).astype(jnp.float32),
        lax.psum_scatter(
            up_weight_grad.astype(jnp.bfloat16), "dp", scatter_dimension=0, tiled=True
        ).astype(jnp.float32),
        lax.psum_scatter(
            down_weight_grad.astype(jnp.bfloat16), "dp", scatter_dimension=1, tiled=True
        ).astype(jnp.float32),
        lax.psum_scatter(
            proj_weight_grad.astype(jnp.bfloat16), "dp", scatter_dimension=0, tiled=True
        ).astype(jnp.float32),
        lax.psum_scatter(
            pos_grad.astype(jnp.bfloat16), "dp", scatter_dimension=0, tiled=True
        ).astype(jnp.float32),
    )
    (
        query_bias_grad,
        value_bias_grad,
        up_bias_grad,
        proj_bias_grad,
        mask_grad,
        first_gain_grad,
        first_shift_grad,
        second_gain_grad,
        second_shift_grad,
        out_bias_grad,
        down_bias_grad,
    ) = lax.psum(
        (
            query_bias_grad,
            value_bias_grad,
            up_bias_grad,
            proj_bias_grad,
            mask_grad,
            first_gain_grad,
            first_shift_grad,
            second_gain_grad,
            second_shift_grad,
            out_bias_grad,
            down_bias_grad,
        ),
        "dp",
    )
    return (
        grid_out,
        input_grad.astype(low_type),
        qkv_weight_grad,
        query_bias_grad,
        value_bias_grad,
        out_weight_grad,
        out_bias_grad,
        first_gain_grad,
        first_shift_grad,
        second_gain_grad,
        second_shift_grad,
        up_weight_grad,
        up_bias_grad,
        down_weight_grad,
        down_bias_grad,
        proj_weight_grad,
        proj_bias_grad,
        mask_grad,
        pos_grad,
    )


def solution(mesh):
    return jax.shard_map(
        local,
        mesh=mesh,
        in_specs=(
            P("dp", None),
            P(),
            P(),
            P(),
            P(None, "mp"),
            P("mp"),
            P("mp"),
            P("mp", None),
            P(),
            P(),
            P(),
            P(),
            P(),
            P(None, "mp"),
            P("mp"),
            P("mp", None),
            P(),
            P(None, "mp"),
            P("mp"),
            P("mp"),
            P(None, "mp"),
            P("dp", None, "mp"),
        ),
        out_specs=(
            P("dp", None, "mp"),
            P(("dp", "mp"), None),
            P("dp", "mp"),
            P("mp"),
            P("mp"),
            P("mp", "dp"),
            P(),
            P(),
            P(),
            P(),
            P(),
            P("dp", "mp"),
            P("mp"),
            P("mp", "dp"),
            P(),
            P("dp", "mp"),
            P("mp"),
            P("mp"),
            P("dp", "mp"),
        ),
        check_vma=False,
    )
```

profile of v0, /device:TPU:0, one launch (start us, length us, event | category | flops | bytes accessed | tf_op | source)
XLA Modules:
  0.0 576.4 jit_solution(12643248955336218250)
XLA Ops:
  12.4 7.3 %all-to-all-start.1 = ((bf16[8,64,128]{2,1,0:T(8,128)(2,1)}), bf16[8,64,128]{2,1,0:T(8,128)(2,1)S(1)}, u32[]{:S(2)}, u32[]{:S(2)}) async-start(bf16[8,64,128]{2,1,0:T(8,128)(2,1)} %convolution_convert_fusion.13), calls=%async_computation.1 | async-start | bytes 262144 | tf_op jit(solution)/shard_map/all_to_all | solution.py:188
  29.1 2.8 reshape.348
  33.9 2.4 fusion.179
  57.5 41.5 %all-reduce.13.cloned.1.call-done = (bf16[512,768]{1,0:T(8,128)(2,1)}, bf16[512,768]{1,0:T(8,128)(2,1)}) async-done(((bf16[512,768]{1,0:T(8,128)(2,1)}, bf16[512,768]{1,0:T(8,128)(2,1)}), (bf16[512,768]{1,0:T(8,128)(2,1)}, bf16[512,768]{1,0:T(8,128)(2,1)})) %all-reduce.13.cloned.1.call-update) | async-done | bytes 1572880 | tf_op jit(solution)/shard_map/psum | solution.py:97
  102.2 5.8 %convert_reduce_fusion.4 = (f32[768]{0:T(1024)}, bf16[512,768]{1,0:T(8,128)(2,1)S(1)}, f32[512,768]{1,0:T(8,128)}) fusion(f32[512,768]{1,0:T(8,128)S(1)} %convolution_add_fusion, bf16[512,768]{1,0:T(8,128)(2,1)S(1)} %copy-done.22, bf16[768,768]{1,0:T(8,128)(2,1)S(1)} %copy-done), kind=kOutput, calls=%fused_computation.35 | convolution fusion | flops 633076992 | bytes 5901312 | tf_op jit(solution)/shard_map/rd,fd->rf/dot_general | solution.py:58
  115.5 30.0 %all-reduce.9.cloned.1.call-done = bf16[512,768]{1,0:T(8,128)(2,1)} async-done(((bf16[512,768]{1,0:T(8,128)(2,1)}), bf16[512,768]{1,0:T(8,128)(2,1)}) %all-reduce.9.cloned.1.call-update) | async-done | bytes 786448 | tf_op jit(solution)/shard_map/psum | solution.py:97
  145.5 2.5 convert_reduce_fusion.1
  163.9 2.7 copy.117
  166.5 2.7 reshape.356
  169.2 3.1 convolution_convert_fusion.5
  178.8 2.6 convolution_convert_fusion.10
  183.3 32.3 %all-reduce.11.cloned.1.call-done = (bf16[512,768]{1,0:T(8,128)(2,1)}, bf16[512,768]{1,0:T(8,128)(2,1)}) async-done(((bf16[512,768]{1,0:T(8,128)(2,1)}, bf16[512,768]{1,0:T(8,128)(2,1)}), (bf16[512,768]{1,0:T(8,128)(2,1)}, bf16[512,768]{1,0:T(8,128)(2,1)})) %all-reduce.11.cloned.1.call-update) | async-done | bytes 1572880 | tf_op jit(solution)/shard_map/psum | solution.py:97
  215.6 2.6 fusion.16
  218.2 2.7 fusion.178
  223.3 3.1 convolution_convert_fusion.2
  226.6 3.3 convolution_convert_fusion
  233.1 3.2 convolution_convert_fusion.1
  242.4 61.6 %reduce-scatter.19.cloned.1.call-done = bf16[96,192]{1,0:T(8,128)(2,1)} async-done(((bf16[768,192]{1,0:T(8,128)(2,1)}), bf16[96,192]{1,0:T(8,128)(2,1)}) %reduce-scatter.19.cloned.1.call-update) | async-done | bytes 36880
  307.1 3.6 all-to-all-start
  310.8 38.3 %all-reduce.2 = (f32[192]{0:T(256)}, f32[192]{0:T(256)}, f32[768]{0:T(1024)}, f32[768]{0:T(1024)}, f32[768]{0:T(1024)}, /*index=5*/f32[768]{0:T(1024)}, f32[768]...) all-reduce(f32[192]{0:T(256)S(1)} %reshape.357, ...), channel_id=1, replica_groups=mesh['dp'=8,'mp'=4] {'dp'}, use_global_device_ids=true, to_apply=%region_21.22 | all-reduce | flops 6016 | bytes 48128 | tf_op jit(solution)/shard_map/psum | solution.py:266
  352.6 15.3 %reduce-scatter.15.cloned.1.call-done = bf16[96,128]{1,0:T(8,128)(2,1)} async-done(((bf16[768,128]{1,0:T(8,128)(2,1)}), bf16[96,128]{1,0:T(8,128)(2,1)}) %reduce-scatter.15.cloned.1.call-update) | async-done | bytes 24592 | tf_op jit(solution)/shard_map/reduce_scatter | solution.py:247
  369.2 64.5 %reduce-scatter.9.cloned.1.call-done = bf16[96,576]{1,0:T(8,128)(2,1)} async-done(((bf16[768,576]{1,0:T(8,128)(2,1)}), bf16[96,576]{1,0:T(8,128)(2,1)}) %reduce-scatter.9.cloned.1.call-update) | async-done | bytes 110608 | tf_op jit(solution)/shard_map/reduce_scatter | solution.py:235
  435.3 65.4 %reduce-scatter.13.cloned.1.call-done = bf16[768,96]{0,1:T(8,128)(2,1)} async-done(((bf16[768,768]{0,1:T(8,128)(2,1)}), bf16[768,96]{0,1:T(8,128)(2,1)}) %reduce-scatter.13.cloned.1.call-update) | async-done | bytes 147472 | tf_op jit(solution)/shard_map/reduce_scatter | solution.py:244
  502.3 65.3 %reduce-scatter.11.cloned.1.call-done = bf16[96,768]{1,0:T(8,128)(2,1)} async-done(((bf16[768,768]{1,0:T(8,128)(2,1)}), bf16[96,768]{1,0:T(8,128)(2,1)}) %reduce-scatter.11.cloned.1.call-update) | async-done | bytes 147472 | tf_op jit(solution)/shard_map/reduce_scatter | solution.py:241
  (320 shorter events, 95.8 us)
Async XLA Ops:
  8.0 94.2 %copy-start = (bf16[768,768]{1,0:T(8,128)(2,1)S(1)}, bf16[768,768]{1,0:T(8,128)(2,1)}, u32[]{:S(2)}) copy-start(bf16[768,768]{1,0:T(8,128)(2,1)} %param.37) | copy-start | bytes 3538948
  12.4 40.0 %all-to-all-start.1 = ((bf16[8,64,128]{2,1,0:T(8,128)(2,1)}), bf16[8,64,128]{2,1,0:T(8,128)(2,1)S(1)}, u32[]{:S(2)}, u32[]{:S(2)}) async-start(bf16[8,64,128]{2,1,0:T(8,128)(2,1)} %convolution_convert_fusion.13), calls=%async_computation.1 | async-start | bytes 262144 | tf_op jit(solution)/shard_map/all_to_all | solution.py:188
  19.7 79.3 %all-reduce.13.cloned.1.call-start = ((), (), s32[]{:S(2)}) async-start(), calls=%async_computation.16 | async-start | bytes 3145728 | tf_op jit(solution)/shard_map/psum | solution.py:97
  54.4 91.1 %all-reduce.9.cloned.1.call-start = ((), (), s32[]{:S(2)}) async-start(), calls=%async_computation.8 | async-start | bytes 1572864 | tf_op jit(solution)/shard_map/psum | solution.py:97
  110.6 105.0 %all-reduce.11.cloned.1.call-start = ((), (), s32[]{:S(2)}) async-start(), calls=%async_computation.15 | async-start | bytes 3145728 | tf_op jit(solution)/shard_map/psum | solution.py:97
  172.4 68.4 %reduce-scatter.17.cloned.1.call-start = ((), (), s32[]{:S(2)}) async-start(), calls=%async_computation.13 | async-start | bytes 73728 | tf_op jit(solution)/shard_map/reduce_scatter | solution.py:250
  178.1 125.8 %reduce-scatter.19.cloned.1.call-start = ((), (), s32[]{:S(2)}) async-start(), calls=%async_computation.14 | async-start | bytes 442368
  178.8 36.8 %copy-start.37 = (f32[512]{0:T(512)S(1)}, f32[512]{0:T(512)}, u32[]{:S(2)}) copy-start(f32[512]{0:T(512)} %copy-done.36) | copy-start | bytes 6148
  181.4 36.8 %copy-start.39 = (f32[512]{0:T(512)S(1)}, f32[512]{0:T(512)}, u32[]{:S(2)}) copy-start(f32[512]{0:T(512)} %copy-done.38) | copy-start | bytes 6148
  183.3 184.6 %reduce-scatter.15.cloned.1.call-start = ((), (), s32[]{:S(2)}) async-start(), calls=%async_computation.12 | async-start | bytes 221184 | tf_op jit(solution)/shard_map/reduce_scatter | solution.py:247
  223.0 210.7 %reduce-scatter.9.cloned.1.call-start = ((), (), s32[]{:S(2)}) async-start(), calls=%async_computation.9 | async-start | bytes 1105920 | tf_op jit(solution)/shard_map/reduce_scatter | solution.py:235
  226.5 274.2 %reduce-scatter.13.cloned.1.call-start = ((), (), s32[]{:S(2)}) async-start(), calls=%async_computation.11 | async-start | bytes 1327104 | tf_op jit(solution)/shard_map/reduce_scatter | solution.py:244
  229.9 337.7 %reduce-scatter.11.cloned.1.call-start = ((), (), s32[]{:S(2)}) async-start(), calls=%async_computation.10 | async-start | bytes 1327104 | tf_op jit(solution)/shard_map/reduce_scatter | solution.py:241
  236.4 69.1 %copy-start.11 = (bf16[512,768]{1,0:T(8,128)(2,1)S(1)}, bf16[512,768]{1,0:T(8,128)(2,1)}, u32[]{:S(2)}) copy-start(bf16[512,768]{1,0:T(8,128)(2,1)} %copy-done.10) | copy-start | bytes 2359300
  236.4 69.1 %copy-start.27 = (bf16[768,128]{1,0:T(8,128)(2,1)S(1)}, bf16[768,128]{1,0:T(8,128)(2,1)}, u32[]{:S(2)}) copy-start(bf16[768,128]{1,0:T(8,128)(2,1)} %param.39) | copy-start | bytes 589828
  238.8 72.0 %copy-start.54 = (f32[512]{0:T(512)S(1)}, f32[512]{0:T(512)}, u32[]{:S(2)}) copy-start(f32[512]{0:T(512)} %get-tuple-element.48) | copy-start | bytes 6148
  238.9 71.9 %copy-start.42 = (f32[768]{0:T(1024)S(1)}, f32[768]{0:T(1024)}, u32[]{:S(2)}) copy-start(f32[768]{0:T(1024)} %get-tuple-element.23) | copy-start | bytes 9220
  239.0 71.8 %copy-start.43 = (f32[768]{0:T(1024)S(1)}, f32[768]{0:T(1024)}, u32[]{:S(2)}) copy-start(f32[768]{0:T(1024)} %get-tuple-element.19) | copy-start | bytes 9220
  239.0 71.8 %copy-start.44 = (f32[768]{0:T(1024)S(1)}, f32[768]{0:T(1024)}, u32[]{:S(2)}) copy-start(f32[768]{0:T(1024)} %get-tuple-element.46) | copy-start | bytes 9220
  239.0 71.8 %copy-start.45 = (f32[768]{0:T(1024)S(1)}, f32[768]{0:T(1024)}, u32[]{:S(2)}) copy-start(f32[768]{0:T(1024)} %get-tuple-element.54) | copy-start | bytes 9220
  239.0 71.8 %copy-start.46 = (f32[768]{0:T(1024)S(1)}, f32[768]{0:T(1024)}, u32[]{:S(2)}) copy-start(f32[768]{0:T(1024)} %get-tuple-element.21) | copy-start | bytes 9220
  239.0 71.8 %copy-start.47 = (f32[768]{0:T(1024)S(1)}, f32[768]{0:T(1024)}, u32[]{:S(2)}) copy-start(f32[768]{0:T(1024)} %get-tuple-element.25) | copy-start | bytes 9220
  239.0 71.8 %copy-start.60 = (f32[768]{0:T(1024)S(1)}, f32[768]{0:T(1024)}, u32[]{:S(2)}) copy-start(f32[768]{0:T(1024)} %get-tuple-element.43) | copy-start | bytes 9220
  307.1 43.9 %all-to-all-start = ((bf16[8,64,128]{2,1,0:T(8,128)(2,1)}), bf16[8,64,128]{2,1,0:T(8,128)(2,1)S(1)}, u32[]{:S(2)}, u32[]{:S(2)}) async-start(bf16[8,64,128]{2,1,0:T(8,128)(2,1)} %gather_fusion.1), calls=%async_computation | async-start | bytes 262144 | tf_op jit(solution)/shard_map/all_to_all | solution.py:158
  (79 other events, 315.0 us)
Sparse Core Ops, SparseCore 0:
  54.5 44.4 all-reduce.12
  110.8 34.6 all-reduce.8
  172.5 43.0 all-reduce.10
Sparse Core Ops, SparseCore 1:
  178.2 61.4 reduce-scatter.16
  243.3 60.5 reduce-scatter.18
  307.6 60.2 reduce-scatter.14
  371.2 62.4 reduce-scatter.8
  437.5 63.1 reduce-scatter.12
  504.5 63.1 reduce-scatter.10
where the time goes:
time: 578 us; the launch traced here: 576 us
  waiting for transfers between devices  376 us (65%)
  matrix products  56 us (10%)
  other arithmetic  40.1 us (7%)
  blocking collectives  38.3 us (7%)
  local copies, waits for them, and re-layouts  38.2 us (7%)
  between operations  16.3 us (3%)
  starting transfers between devices  11.7 us (2%)
    psum x3, waiting for transfers between devices, combine(): return lax.psum(partial_sum.astype(jnp.bfloat16), 'mp').astype(jnp.float32)  104 us
    reduce_scatter x1, waiting for transfers between devices, local(): lax.psum_scatter(down_weight_grad.astype(jnp.bfloat16), 'dp', scatter_dim...  65.4 us
    reduce_scatter x1, waiting for transfers between devices, local(): lax.psum_scatter(up_weight_grad.astype(jnp.bfloat16), 'dp', scatter_dimen...  65.3 us
    reduce_scatter x1, waiting for transfers between devices, local(): lax.psum_scatter(qkv_weight_grad.astype(jnp.bfloat16), 'dp', scatter_dime...  64.5 us
    unnamed x10, waiting for transfers between devices  61.7 us
    dot_general x27, matrix products, matmul(): jnp.einsum(pattern, left_op, right_op, preferred_element_type=jnp.float32)  45.2 us
    psum x1, blocking collectives, local(): lax.psum((query_bias_grad, value_bias_grad, up_bias_grad, proj_bias_grad,...  38.3 us
    reduce_scatter x1, waiting for transfers between devices, local(): lax.psum_scatter(proj_weight_grad.astype(jnp.bfloat16), 'dp', scatter_dim...  15.3 us
  transfers between devices with their start and end apart: 11, of which 8 were waited for; matrix products, arithmetic and copies ran while one was open for 15% of the time, Pallas kernels for 0%

commit v1 on v0

v1 whole, which is shorter than its diff:
```python
import math

import jax
import jax.numpy as jnp
import numpy as np
from jax import lax
from jax.experimental import pallas as pl
from jax.experimental.pallas import tpu as pltpu
from jax.sharding import PartitionSpec as P

HEAD_DIM = 64
GRID = 256
VIS = 64
PAIR = 2 * VIS
CHUNK = 512
LANES = 128

epsilon = 1e-06
low_type = jnp.bfloat16
wide_type = jnp.float32
scale_factor = HEAD_DIM ** (-0.5)

VMEM = pl.BlockSpec(memory_space=pltpu.VMEM)
SMEM = pl.BlockSpec(memory_space=pltpu.SMEM)


def grid_tables():
    grid_edge = math.isqrt(GRID)
    tables = []
    for side_cells in (10, 14):
        places = np.arange(side_cells)
        centers = ((2 * places + 1) * grid_edge - side_cells) / (2 * side_cells)
        lower = np.floor(centers).astype(np.int64)
        share = centers - lower
        lerp = np.zeros((side_cells, grid_edge))
        lerp[places, np.clip(lower, 0, grid_edge - 1)] += 1.0 - share
        lerp[places, np.clip(lower + 1, 0, grid_edge - 1)] += share
        table = np.zeros((GRID, GRID))
        table[: side_cells * side_cells] = np.kron(lerp, lerp)
        tables.append(table)
    return np.stack(tables).astype(np.float32)


def split_low(value):
    high = value.astype(low_type)
    return high, (value - high.astype(wide_type)).astype(low_type)


def dot(left, right):
    return lax.dot_general(left, right, (((1,), (0,)), ((), ())), preferred_element_type=wide_type)


def dot_right_t(left, right):
    return lax.dot_general(left, right, (((1,), (1,)), ((), ())), preferred_element_type=wide_type)


def dot_left_t(left, right):
    return lax.dot_general(left, right, (((0,), (0,)), ((), ())), preferred_element_type=wide_type)


def normalized(value):
    center = value - jnp.mean(value, axis=-1, keepdims=True)
    spread = lax.rsqrt(jnp.mean(center * center, axis=-1, keepdims=True) + epsilon)
    return center * spread, spread


def norm_back(grad, normed, spread, gain):
    scaled = grad * gain
    mean_one = jnp.mean(scaled, axis=-1, keepdims=True)
    mean_two = jnp.mean(scaled * normed, axis=-1, keepdims=True)
    return spread * (scaled - mean_one - normed * mean_two)


def row_sum(value):
    return jnp.sum(value, axis=0, keepdims=True)


def over_rows(total, size, body):
    size = min(size, total)
    if total == size:
        body(0, size)
        return

    def step(i, carry):
        body(pl.multiple_of(i * size, size), size)
        return carry

    lax.fori_loop(0, total // size, step, 0)


def call(kernel, outs, args, specs, scratch=(), flops=0, nbytes=0, out_specs=None):
    return pl.pallas_call(
        kernel,
        out_shape=tuple(jax.ShapeDtypeStruct(shape, kind) for shape, kind in outs),
        in_specs=list(specs),
        out_specs=tuple(VMEM for _ in outs) if out_specs is None else out_specs,
        scratch_shapes=list(scratch),
        compiler_params=pltpu.CompilerParams(vmem_limit_bytes=56 * 2**20),
        cost_estimate=pl.CostEstimate(flops=flops, bytes_accessed=nbytes, transcendentals=0),
    )(*args)


def cotangent_kernel(
    count, images, where_ref, owner_ref, patches_ref, visible_ref, cot_ref, table_high_ref, table_low_ref,
    send_ref, source_ref, mask_ref, sums_ref,
):
    me = where_ref[0]
    share = GRID // count
    cells = lax.broadcasted_iota(jnp.int32, (GRID, VIS), 0)
    cell_column = lax.broadcasted_iota(jnp.int32, (GRID, 1), 0)
    sums_ref[...] = jnp.zeros_like(sums_ref)
    mask_ref[...] = jnp.zeros_like(mask_ref)

    def one_slot(slot):
        def find(i, found):
            return jnp.where(owner_ref[slot * images + i] == me, slot * images + i, found)

        source = lax.fori_loop(0, images, find, slot * images)
        source_ref[slot] = source
        seen = visible_ref[pl.ds(source, 1), :] == cells
        cot = cot_ref[slot]
        send_ref[slot, :VIS, :] = dot_left_t(seen.astype(low_type), cot).astype(low_type)
        size = patches_ref[source]
        wide = cot.astype(wide_type)
        fill = (cell_column < size).astype(wide_type) - jnp.sum(
            seen.astype(wide_type), axis=1, keepdims=True
        )
        mask_ref[...] += row_sum(fill * wide)
        side = (size >= 196).astype(jnp.int32) + (size >= 256).astype(jnp.int32)
        sums_ref[side] += wide

    if count <= 8:
        for slot in range(count):
            one_slot(slot)
    else:
        lax.fori_loop(0, count, lambda slot, carry: (one_slot(slot), carry)[1], 0)
    total = sums_ref[2]
    for side in range(2):
        high, low = split_low(sums_ref[side])
        total += (
            dot(table_high_ref[side], high) + dot(table_high_ref[side], low) + dot(table_low_ref[side], high)
        )
    total = total.astype(low_type)
    for block in range(count):
        send_ref[block, VIS : VIS + share, :] = total[block * share : (block + 1) * share]


def enter_kernel(rows_ref, gain_ref, shift_ref, weight_ref, bias_ref, act_ref, qkv_ref):
    def body(start, size):
        rows = pl.ds(start, size)
        normed, _ = normalized(rows_ref[rows, :].astype(wide_type))
        act = (normed * gain_ref[...] + shift_ref[...]).astype(low_type)
        act_ref[rows, :] = act
        qkv_ref[rows, :] = (dot(act, weight_ref[...]) + bias_ref[...]).astype(low_type)

    over_rows(rows_ref.shape[0], CHUNK, body)


def attention_kernel(
    images, heads, where_ref, patches_ref, qkv_ref, weight_ref, prob_ref, attended_ref, keep_ref, sent_ref
):
    first_image = where_ref[0] * images
    row_half = lax.broadcasted_iota(jnp.int32, (PAIR, PAIR), 0) // VIS
    lane = lax.broadcasted_iota(jnp.int32, (PAIR, PAIR), 1)

    def body(start, size):
        for pair in range(size // PAIR):
            rows = pl.ds(start + pair * PAIR, PAIR)
            image = first_image + (start + pair * PAIR) // VIS
            limits = [patches_ref[image + i] // 4 for i in range(2)]
            last = jnp.where(row_half == 0, limits[0], VIS + limits[1])
            live = jnp.logical_and(lane >= row_half * VIS, lane < last)
            for head in range(heads):
                base = head * 3 * HEAD_DIM
                queries = qkv_ref[rows, base : base + HEAD_DIM]
                key_rows = qkv_ref[rows, base + HEAD_DIM : base + 2 * HEAD_DIM]
                value_rows = qkv_ref[rows, base + 2 * HEAD_DIM : base + 3 * HEAD_DIM]
                scores = jnp.where(live, dot_right_t(queries, key_rows) * scale_factor, -1e30)
                raised = jnp.exp(scores - jnp.max(scores, axis=-1, keepdims=True))
                probs = (raised / jnp.sum(raised, axis=-1, keepdims=True)).astype(low_type)
                prob_ref[rows, head * PAIR : (head + 1) * PAIR] = probs
                attended_ref[rows, head * HEAD_DIM : (head + 1) * HEAD_DIM] = dot(
                    probs, value_rows
                ).astype(low_type)

    over_rows(qkv_ref.shape[0], CHUNK, body)
    halves(where_ref[1] & 1, attended_ref, weight_ref, keep_ref, sent_ref, dot)


def halves(upper, left_ref, weight_ref, keep_ref, sent_ref, product):
    half = keep_ref.shape[0]
    for out_ref, which in ((sent_ref, 1 - upper), (keep_ref, upper)):

        def body(start, size, out_ref=out_ref, which=which):
            rows = pl.ds(pl.multiple_of(which * half + start, size), size)
            out_ref[pl.ds(start, size), :] = product(left_ref[rows, :], weight_ref[...]).astype(
                out_ref.dtype
            )

        over_rows(half, CHUNK, body)


def back_kernel(images, where_ref, owner_ref, back_ref, weight_ref, enc_ref, keep_ref, sent_ref):
    base = where_ref[0] * images
    for image in range(images):
        enc_ref[image * VIS : (image + 1) * VIS, :] = back_ref[owner_ref[base + image], :VIS, :]
    halves(where_ref[1] & 1, enc_ref, weight_ref, keep_ref, sent_ref, dot_right_t)


def gathered(upper, own_ref, other_ref, out_ref):
    half = own_ref.shape[0]
    out_ref[pl.ds(pl.multiple_of(upper * half, half), half), :] = own_ref[...]
    out_ref[pl.ds(pl.multiple_of((1 - upper) * half, half), half), :] = other_ref[...]


def forward_back_kernel(
    where_ref, rows_ref, sum_ref, sum_other_ref, grad_ref, grad_other_ref, vec_ref, up_ref, up_bias_ref, down_ref,
    hidden_ref, act_ref, acted_ref, up_low_ref, down_low_ref, bias_ref, keep_ref, sent_ref, fkeep_ref, fsent_ref,
    sums_ref,
):
    upper = where_ref[1] & 1
    gathered(upper, sum_ref, sum_other_ref, sums_ref)
    gathered(upper, grad_ref, grad_other_ref, down_low_ref)
    out_bias, gain, shift = vec_ref[2:3, :], vec_ref[3:4, :], vec_ref[4:5, :]

    def body(start, size):
        rows = pl.ds(start, size)
        hidden = rows_ref[rows, :].astype(wide_type) + sums_ref[rows, :].astype(wide_type) + out_bias
        hidden_ref[rows, :] = hidden
        normed, _ = normalized(hidden)
        act = (normed * gain + shift).astype(low_type)
        act_ref[rows, :] = act
        up_pre = dot(act, up_ref[...]) + up_bias_ref[...]
        cdf = 0.5 + 0.5 * lax.erf(up_pre * math.sqrt(0.5))
        acted_ref[rows, :] = (up_pre * cdf).astype(low_type)
        slope = cdf + up_pre * jnp.exp(-0.5 * up_pre * up_pre) * (1.0 / math.sqrt(2.0 * math.pi))
        up_low_ref[rows, :] = (dot_right_t(down_low_ref[rows, :], down_ref[...]) * slope).astype(low_type)

    over_rows(rows_ref.shape[0], 256, body)
    bias_ref[0:1, :] = row_sum(down_low_ref[...].astype(wide_type))
    bias_ref[1:2, :] = row_sum(up_low_ref[...].astype(wide_type))
    halves(upper, up_low_ref, up_ref, keep_ref, sent_ref, dot_right_t)
    halves(upper, acted_ref, down_ref, fkeep_ref, fsent_ref, dot)


def part_blocks(lower_bit, wide_ref, parts, keep_ref, sent_ref, first_tile):
    share = keep_ref.shape[2]
    for out_ref, which in ((sent_ref, 1 - lower_bit), (keep_ref, lower_bit)):
        for block in range(keep_ref.shape[0]):
            rows = pl.ds(pl.multiple_of((2 * block + which) * share, 8), share)
            for tile in range(parts):
                out_ref[block, first_tile + tile] = wide_ref[
                    rows, tile * LANES : (tile + 1) * LANES
                ].astype(out_ref.dtype)


def early_grads_kernel(where_ref, act_ref, up_low_ref, acted_ref, down_low_ref, keep_ref, sent_ref, wide_ref):
    lower_bit = where_ref[0] & 1
    tiles = wide_ref.shape[1] // LANES
    wide_ref[...] = dot_left_t(act_ref[...], up_low_ref[...])
    part_blocks(lower_bit, wide_ref, tiles, keep_ref, sent_ref, 0)
    wide_ref[...] = dot_left_t(down_low_ref[...], acted_ref[...])
    part_blocks(lower_bit, wide_ref, tiles, keep_ref, sent_ref, tiles)


def attention_back_kernel(
    heads, where_ref, sum_ref, sum_other_ref, hidden_ref, down_low_ref, vec_ref, weight_ref, qkv_ref, prob_ref,
    attended_ref, grads_ref, own_ref, weight_grad_ref, bias_ref, sums_ref, grad_ref, low_ref,
):
    gathered(where_ref[1] & 1, sum_ref, sum_other_ref, sums_ref)
    gain = vec_ref[3:4, :]
    bias_ref[...] = jnp.zeros_like(bias_ref)

    def body(start, size):
        rows = pl.ds(start, size)
        normed, spread = normalized(hidden_ref[rows, :])
        grad = sums_ref[rows, :].astype(wide_type)
        bias_ref[0:1, :] += row_sum(grad * normed)
        bias_ref[1:2, :] += row_sum(grad)
        hidden_grad = down_low_ref[rows, :].astype(wide_type) + norm_back(grad, normed, spread, gain)
        grad_ref[rows, :] = hidden_grad
        bias_ref[2:3, :] += row_sum(hidden_grad)
        attn_low = hidden_grad.astype(low_type)
        low_ref[rows, :] = attn_low
        attended_grad = dot_right_t(attn_low, weight_ref[...]).astype(low_type)
        for pair in range(size // PAIR):
            pair_rows = pl.ds(start + pair * PAIR, PAIR)
            for head in range(heads):
                base = head * 3 * HEAD_DIM
                queries = qkv_ref[pair_rows, base : base + HEAD_DIM]
                key_rows = qkv_ref[pair_rows, base + HEAD_DIM : base + 2 * HEAD_DIM]
                value_rows = qkv_ref[pair_rows, base + 2 * HEAD_DIM : base + 3 * HEAD_DIM]
                probs = prob_ref[pair_rows, head * PAIR : (head + 1) * PAIR]
                grad_rows = attended_grad[
                    pair * PAIR : (pair + 1) * PAIR, head * HEAD_DIM : (head + 1) * HEAD_DIM
                ]
                value_low = dot_left_t(probs, grad_rows).astype(low_type)
                prob_grad = dot_right_t(grad_rows, value_rows)
                wide_probs = probs.astype(wide_type)
                weighted = wide_probs * prob_grad
                score_low = (
                    weighted - wide_probs * jnp.sum(weighted, axis=-1, keepdims=True)
                ).astype(low_type)
                query_low = (dot(score_low, key_rows) * scale_factor).astype(low_type)
                key_low = (dot_left_t(score_low, queries) * scale_factor).astype(low_type)
                grads_ref[pair_rows, base : base + HEAD_DIM] = query_low
                grads_ref[pair_rows, base + HEAD_DIM : base + 2 * HEAD_DIM] = key_low
                grads_ref[pair_rows, base + 2 * HEAD_DIM : base + 3 * HEAD_DIM] = value_low

    over_rows(hidden_ref.shape[0], CHUNK, body)
    share = own_ref.shape[0]
    own_ref[...] = grad_ref[pl.ds(pl.multiple_of(where_ref[1] * share, share), share), :]
    weight_grad_ref[...] = dot_left_t(low_ref[...], attended_ref[...])


def late_grads_kernel(where_ref, act_ref, grads_ref, out_grad_ref, keep_ref, sent_ref, bias_ref, wide_ref):
    columns = grads_ref.shape[1]
    heads_columns = out_grad_ref.shape[1]
    bias_ref[...] = row_sum(grads_ref[...].astype(wide_type))
    wide_ref[:, :heads_columns] = out_grad_ref[...]
    wide_ref[:, heads_columns : heads_columns + columns] = dot_left_t(act_ref[...], grads_ref[...])
    part_blocks(
        where_ref[0] & 1, wide_ref, wide_ref.shape[1] // LANES, keep_ref, sent_ref, 0
    )


def input_part_kernel(
    where_ref, rows_ref, grads_ref, weight_ref, keep_ref, sent_ref, bias_ref, part_ref
):
    lower_bit = where_ref[1] & 1
    bias_ref[...] = jnp.zeros_like(bias_ref)

    def body(start, size):
        rows = pl.ds(start, size)
        grad = dot_right_t(grads_ref[rows, :], weight_ref[...])
        part_ref[rows, :] = grad
        normed, _ = normalized(rows_ref[rows, :].astype(wide_type))
        bias_ref[0:1, :] += row_sum(grad * normed)
        bias_ref[1:2, :] += row_sum(grad)

    over_rows(rows_ref.shape[0], CHUNK, body)
    share = keep_ref.shape[1]
    for out_ref, which in ((sent_ref, 1 - lower_bit), (keep_ref, lower_bit)):
        for block in range(keep_ref.shape[0]):
            rows = pl.ds(pl.multiple_of((2 * block + which) * share, share), share)
            out_ref[block] = part_ref[rows, :].astype(low_type)


def input_grad_kernel(where_ref, rows_ref, keep_ref, other_ref, own_ref, gain_ref, out_ref):
    share = out_ref.shape[0]
    rows = pl.ds(pl.multiple_of(where_ref[1] * share, share), share)
    normed, spread = normalized(rows_ref[rows, :].astype(wide_type))
    grad = keep_ref[...].astype(wide_type) + other_ref[...].astype(wide_type)
    out_ref[...] = (own_ref[...] + norm_back(grad, normed, spread, gain_ref[...])).astype(low_type)


def encoded_kernel(
    images, where_ref, owner_ref, hidden_ref, sum_ref, sum_other_ref, vec_ref, weight_ref, bias_ref, enc_ref,
    send_ref, bias_grad_ref, sums_ref, low_ref, wide_ref,
):
    gathered(where_ref[1] & 1, sum_ref, sum_other_ref, sums_ref)
    down_bias = vec_ref[5:6, :]
    base = where_ref[0] * images
    bias_grad_ref[...] = row_sum(enc_ref[...].astype(wide_type))

    def body(start, size):
        rows = pl.ds(start, size)
        out_low = (
            hidden_ref[rows, :] + sums_ref[rows, :].astype(wide_type) + down_bias
        ).astype(low_type)
        low_ref[rows, :] = out_low
        encoded = (dot(out_low, weight_ref[...]) + bias_ref[...]).astype(low_type)
        for image in range(size // VIS):
            send_ref[owner_ref[base + start // VIS + image], :VIS, :] = encoded[
                image * VIS : (image + 1) * VIS
            ]

    over_rows(hidden_ref.shape[0], CHUNK, body)
    wide_ref[...] = dot_left_t(low_ref[...], enc_ref[...])
    count = send_ref.shape[0]
    share = wide_ref.shape[0] // count
    for block in range(count):
        send_ref[block, VIS : VIS + share, :] = wide_ref[block * share : (block + 1) * share, :].astype(
            low_type
        )


def grids_kernel(
    source_ref, patches_ref, visible_ref, arrived_ref, mask_ref, pos_ref, table_high_ref, table_low_ref,
    grids_ref, weight_grad_ref, layout_ref,
):
    count = grids_ref.shape[0]
    share = weight_grad_ref.shape[0]
    cells = lax.broadcasted_iota(jnp.int32, (GRID, VIS), 0)
    cell_column = lax.broadcasted_iota(jnp.int32, (GRID, 1), 0)
    table = pos_ref[...]
    for side in range(2):
        layout_ref[side] = dot(table_high_ref[side], table) + dot(table_low_ref[side], table)
    layout_ref[2] = table.astype(wide_type)
    mask_row = mask_ref[...]

    def one_slot(slot):
        source = source_ref[slot]
        seen = visible_ref[pl.ds(source, 1), :] == cells
        size = patches_ref[source]
        fill = (cell_column < size).astype(wide_type) - jnp.sum(
            seen.astype(wide_type), axis=1, keepdims=True
        )
        side = (size >= 196).astype(jnp.int32) + (size >= 256).astype(jnp.int32)
        placed = dot(seen.astype(low_type), arrived_ref[slot, :VIS, :])
        grids_ref[slot] = (placed + fill * mask_row + layout_ref[side]).astype(low_type)

    if count <= 8:
        for slot in range(count):
            one_slot(slot)
    else:
        lax.fori_loop(0, count, lambda slot, carry: (one_slot(slot), carry)[1], 0)
    total = arrived_ref[0, VIS : VIS + share, :].astype(wide_type)
    for block in range(1, count):
        total += arrived_ref[block, VIS : VIS + share, :].astype(wide_type)
    weight_grad_ref[...] = total


def early_out_kernel(keep_ref, other_ref, up_ref, down_ref):
    tiles = keep_ref.shape[0] // 2
    for tile in range(2 * tiles):
        total = keep_ref[tile].astype(wide_type) + other_ref[tile].astype(wide_type)
        if tile < tiles:
            up_ref[:, tile * LANES : (tile + 1) * LANES] = total
        else:
            down_ref[(tile - tiles) * LANES : (tile - tiles + 1) * LANES, :] = total.T


def late_out_kernel(keep_ref, other_ref, out_ref, qkv_ref, wide_ref):
    tiles = keep_ref.shape[0]
    for tile in range(tiles):
        wide_ref[:, tile * LANES : (tile + 1) * LANES] = keep_ref[tile].astype(wide_type) + other_ref[
            tile
        ].astype(wide_type)
    columns = out_ref.shape[0]
    wide_out = -(-columns // LANES) * LANES
    out_ref[...] = wide_ref[:, :wide_out].T[:columns]
    qkv_ref[...] = wide_ref[:, columns:]


VECTOR_ROWS = 48


def vectors_kernel(
    mask_ref, proj_ref, down_up_ref, second_ref, qkv_ref, first_ref, first_other_ref, out_ref, rows_ref
):
    heads = qkv_ref.shape[1] // (3 * HEAD_DIM)
    qkv = qkv_ref[...]
    first = first_ref[...] + first_other_ref[...]
    empty = jnp.zeros((1, 2 * LANES - heads * HEAD_DIM), wide_type)
    spread = []
    for part in (0, 2):
        spread += [
            qkv[:, (3 * head + part) * HEAD_DIM : (3 * head + part + 1) * HEAD_DIM] for head in range(heads)
        ] + [empty]
    heads_row = jnp.concatenate(spread, axis=1)
    row = 0
    for value in (
        heads_row, down_up_ref[1:2, :], proj_ref[...], mask_ref[...], first[0:1], first[1:2],
        second_ref[0:1, :], second_ref[1:2, :], second_ref[2:3, :], down_up_ref[0:1, :],
    ):
        for tile in range(value.shape[1] // LANES):
            rows_ref[row : row + 1, :] = value[:, tile * LANES : (tile + 1) * LANES]
            row += 1
    for block in range(out_ref.shape[0]):
        out_ref[block] = rows_ref[...]


def vectors_sum_kernel(rows_ref, out_ref):
    total = rows_ref[0]
    for block in range(1, rows_ref.shape[0]):
        total += rows_ref[block]
    out_ref[...] = total


def swap(value, axis, bit):
    count = lax.axis_size(axis)
    return lax.ppermute(value, axis, [(i, i ^ bit) for i in range(count)])


def low_add(left, right):
    return (left.astype(wide_type) + right.astype(wide_type)).astype(low_type)


def model_sum(keep, sent):
    total = low_add(keep, swap(sent, "mp", 1))
    bit = 2
    while bit < lax.axis_size("mp"):
        total = low_add(total, swap(total, "mp", bit))
        bit *= 2
    return total, swap(total, "mp", 1)


def data_scatter(keep, sent, index):
    received = swap(sent, "dp", 1)
    bit = 2
    while keep.shape[0] > 1:
        blocks = low_add(keep, received)
        parted = blocks.reshape(-1, 2, *blocks.shape[1:])
        upper = (index & bit) != 0
        keep = jnp.where(upper, parted[:, 1], parted[:, 0])
        received = swap(jnp.where(upper, parted[:, 0], parted[:, 1]), "dp", bit)
        bit *= 2
    return keep[0], received[0]


def local(
    patch_rows, patches, visible, owner, qkv_weight, query_bias, value_bias, out_weight, out_bias, first_gain,
    first_shift, second_gain, second_shift, up_weight, up_bias, down_weight, down_bias, proj_weight, proj_bias,
    mask_token, decoder_pos, grid_cotangent,
):
    count = lax.axis_size("dp")
    parts = lax.axis_size("mp")
    data_index = lax.axis_index("dp")
    model_index = lax.axis_index("mp")
    where = jnp.stack([data_index, model_index]).astype(jnp.int32)
    rows, width = patch_rows.shape
    images = rows // VIS
    heads = qkv_weight.shape[1] // (3 * HEAD_DIM)
    units = up_weight.shape[1]
    columns = proj_weight.shape[1]
    share = width // count
    pos_share = GRID // count
    half = rows // 2
    pad = -(-share // 16) * 16
    pos_pad = -(-pos_share // 16) * 16

    tables = grid_tables()
    table_high = tables.astype(low_type)
    table_low = (tables - table_high.astype(np.float32)).astype(low_type)
    turned_high = jnp.asarray(np.ascontiguousarray(table_high.transpose(0, 2, 1)))
    turned_low = jnp.asarray(np.ascontiguousarray(table_low.transpose(0, 2, 1)))
    table_high, table_low = jnp.asarray(table_high), jnp.asarray(table_low)

    vec = jnp.stack(
        [first_gain, first_shift, out_bias, second_gain, second_shift, down_bias]
    ).astype(wide_type)
    nothing = jnp.zeros((heads, HEAD_DIM), wide_type)
    qkv_bias = jnp.stack(
        [
            query_bias.astype(wide_type).reshape(heads, HEAD_DIM),
            nothing,
            value_bias.astype(wide_type).reshape(heads, HEAD_DIM),
        ],
        axis=1,
    ).reshape(1, -1)
    up_bias_row = up_bias.astype(wide_type).reshape(1, -1)
    proj_bias_row = proj_bias.astype(wide_type).reshape(1, -1)
    mask_row = mask_token.astype(wide_type).reshape(1, -1)

    def low(*shape):
        return (shape, low_type)

    def wide(*shape):
        return (shape, wide_type)

    back_send, source, mask_grad = call(
        lambda *refs: cotangent_kernel(count, images, *refs),
        [low(count, VIS + pos_pad, columns), ((count,), jnp.int32), wide(1, columns)],
        (where, owner, patches, visible, grid_cotangent, turned_high, turned_low),
        (SMEM, SMEM, SMEM, VMEM, VMEM, VMEM, VMEM),
        scratch=[pltpu.VMEM((3, GRID, columns), wide_type)],
        out_specs=(VMEM, SMEM, VMEM),
        flops=10**8,
        nbytes=2 * 10**6,
    )
    returned = lax.all_to_all(back_send, "dp", split_axis=0, concat_axis=0, tiled=True)

    act_one, qkv = call(
        enter_kernel,
        [low(rows, width), low(rows, qkv_weight.shape[1])],
        (patch_rows, vec[0:1], vec[1:2], qkv_weight, qkv_bias),
        (VMEM,) * 5,
        flops=10**9,
        nbytes=3 * 10**6,
    )

    enc_grad, grad_keep, grad_sent = call(
        lambda *refs: back_kernel(images, *refs),
        [low(rows, columns), low(half, width), low(half, width)],
        (where, owner, returned, proj_weight),
        (SMEM, SMEM, VMEM, VMEM),
        flops=10**8,
        nbytes=10**6,
    )
    grad_sum, grad_other = model_sum(grad_keep, grad_sent)

    probs, attended, keep, sent = call(
        lambda *refs: attention_kernel(images, heads, *refs),
        [low(rows, heads * PAIR), low(rows, heads * HEAD_DIM), low(half, width), low(half, width)],
        (where, patches, qkv, out_weight),
        (SMEM, SMEM, VMEM, VMEM),
        flops=10**9,
        nbytes=3 * 10**6,
    )
    attn_sum, attn_other = model_sum(keep, sent)

    hidden, act_two, acted, up_low, down_low, bias_grads, keep, sent, fkeep, fsent = call(
        forward_back_kernel,
        [
            wide(rows, width), low(rows, width), low(rows, units), low(rows, units), low(rows, width),
            wide(2, width), low(half, width), low(half, width), low(half, width), low(half, width),
        ],
        (where, patch_rows, attn_sum, attn_other, grad_sum, grad_other, vec, up_weight, up_bias_row, down_weight),
        (SMEM,) + (VMEM,) * 9,
        scratch=[pltpu.VMEM((rows, width), low_type)],
        flops=3 * 10**9,
        nbytes=10**7,
    )
    second_sum, second_other = model_sum(keep, sent)
    out_sum, out_other = model_sum(fkeep, fsent)

    early_keep, early_sent = call(
        early_grads_kernel,
        [low(count // 2, 2 * units // LANES, share, LANES)] * 2,
        (where, act_two, up_low, acted, down_low),
        (SMEM,) + (VMEM,) * 4,
        scratch=[pltpu.VMEM((width, units), wide_type)],
        flops=2 * 10**9,
        nbytes=5 * 10**6,
    )
    early_keep, early_other = data_scatter(early_keep, early_sent, data_index)

    grads, own_grad, out_weight_grad, second_grads = call(
        lambda *refs: attention_back_kernel(heads, *refs),
        [low(rows, qkv_weight.shape[1]), wide(rows // parts, width), wide(width, heads * HEAD_DIM), wide(3, width)],
        (where, second_sum, second_other, hidden, down_low, vec, out_weight, qkv, probs, attended),
        (SMEM,) + (VMEM,) * 9,
        scratch=[
            pltpu.VMEM((rows, width), low_type),
            pltpu.VMEM((rows, width), wide_type),
            pltpu.VMEM((rows, width), low_type),
        ],
        flops=2 * 10**9,
        nbytes=8 * 10**6,
    )
    late_columns = qkv_weight.shape[1] + heads * HEAD_DIM
    late_keep, late_sent, qkv_bias_grad = call(
        late_grads_kernel,
        [low(count // 2, late_columns // LANES, share, LANES)] * 2 + [wide(1, qkv_weight.shape[1])],
        (where, act_one, grads, out_weight_grad),
        (SMEM,) + (VMEM,) * 3,
        scratch=[pltpu.VMEM((width, late_columns), wide_type)],
        flops=10**9,
        nbytes=4 * 10**6,
    )
    late_keep, late_other = data_scatter(late_keep, late_sent, data_index)

    in_keep, in_sent, first_grads = call(
        input_part_kernel,
        [low(parts // 2, rows // parts, width)] * 2 + [wide(2, width)],
        (where, patch_rows, grads, qkv_weight),
        (SMEM,) + (VMEM,) * 3,
        scratch=[pltpu.VMEM((rows, width), wide_type)],
        flops=10**9,
        nbytes=4 * 10**6,
    )
    received = swap(in_sent, "mp", 1)
    bit = 2
    while in_keep.shape[0] > 1:
        blocks = low_add(in_keep, received)
        parted = blocks.reshape(-1, 2, *blocks.shape[1:])
        upper = (model_index & bit) != 0
        in_keep = jnp.where(upper, parted[:, 1], parted[:, 0])
        received = swap(jnp.where(upper, parted[:, 0], parted[:, 1]), "mp", bit)
        bit *= 2
    bit = 1
    while 2 * bit < parts:
        first_grads = first_grads + swap(first_grads, "mp", bit)
        bit *= 2
    first_other = swap(first_grads, "mp", bit)

    (input_grad,) = call(
        input_grad_kernel,
        [low(rows // parts, width)],
        (where, patch_rows, in_keep[0], received[0], own_grad, vec[0:1]),
        (SMEM,) + (VMEM,) * 5,
        flops=10**7,
        nbytes=2 * 10**6,
    )

    send, proj_bias_grad = call(
        lambda *refs: encoded_kernel(images, *refs),
        [low(count, VIS + pad, columns), wide(1, columns)],
        (where, owner, hidden, out_sum, out_other, vec, proj_weight, proj_bias_row, enc_grad),
        (SMEM, SMEM) + (VMEM,) * 7,
        scratch=[
            pltpu.VMEM((rows, width), low_type),
            pltpu.VMEM((rows, width), low_type),
            pltpu.VMEM((width, columns), wide_type),
        ],
        flops=3 * 10**8,
        nbytes=4 * 10**6,
    )
    arrived = lax.all_to_all(send, "dp", split_axis=0, concat_axis=0, tiled=True)
    grids, proj_weight_grad = call(
        grids_kernel,
        [low(count, GRID, columns), wide(share, columns)],
        (source, patches, visible, arrived, mask_row, decoder_pos, table_high, table_low),
        (SMEM, SMEM) + (VMEM,) * 6,
        scratch=[pltpu.VMEM((3, GRID, columns), wide_type)],
        flops=10**8,
        nbytes=2 * 10**6,
    )

    (vector_rows,) = call(
        vectors_kernel,
        [wide(count, VECTOR_ROWS, LANES)],
        (mask_grad, proj_bias_grad, bias_grads, second_grads, qkv_bias_grad, first_grads, first_other),
        (VMEM,) * 7,
        scratch=[pltpu.VMEM((VECTOR_ROWS, LANES), wide_type)],
        nbytes=10**6,
    )
    vector_rows = lax.all_to_all(vector_rows, "dp", split_axis=0, concat_axis=0, tiled=True)
    (vectors,) = call(vectors_sum_kernel, [wide(VECTOR_ROWS, LANES)], (vector_rows,), (VMEM,), nbytes=10**6)
    flat = vectors.reshape(-1)
    pos_grad = jnp.sum(returned[:, VIS : VIS + pos_share, :].astype(wide_type), axis=0)

    up_weight_grad, down_weight_grad = call(
        early_out_kernel,
        [wide(share, units), wide(units, share)],
        (early_keep, early_other),
        (VMEM,) * 2,
        nbytes=2 * 10**6,
    )
    out_weight_grad, qkv_weight_grad = call(
        late_out_kernel,
        [wide(heads * HEAD_DIM, share), wide(share, qkv_weight.shape[1])],
        (late_keep, late_other),
        (VMEM,) * 2,
        scratch=[pltpu.VMEM((share, late_columns), wide_type)],
        nbytes=10**6,
    )

    tile = LANES
    head_columns = heads * HEAD_DIM
    return (
        grids,
        input_grad,
        qkv_weight_grad,
        flat[:head_columns],
        flat[2 * tile : 2 * tile + head_columns],
        out_weight_grad,
        flat[36 * tile : 42 * tile],
        flat[12 * tile : 18 * tile],
        flat[18 * tile : 24 * tile],
        flat[24 * tile : 30 * tile],
        flat[30 * tile : 36 * tile],
        up_weight_grad,
        flat[4 * tile : 10 * tile],
        down_weight_grad,
        flat[42 * tile : 48 * tile],
        proj_weight_grad,
        flat[10 * tile : 11 * tile],
        flat[11 * tile : 12 * tile],
        pos_grad,
    )


def solution(mesh):
    return jax.shard_map(
        local,
        mesh=mesh,
        in_specs=(
            P("dp", None), P(), P(), P(), P(None, "mp"), P("mp"), P("mp"), P("mp", None), P(), P(), P(), P(), P(),
            P(None, "mp"), P("mp"), P("mp", None), P(), P(None, "mp"), P("mp"), P("mp"), P(None, "mp"),
            P("dp", None, "mp"),
        ),
        out_specs=(
            P("dp", None, "mp"), P(("dp", "mp"), None), P("dp", "mp"), P("mp"), P("mp"), P("mp", "dp"), P(), P(),
            P(), P(), P(), P("dp", "mp"), P("mp"), P("mp", "dp"), P(), P("dp", "mp"), P("mp"), P("mp"),
            P("dp", "mp"),
        ),
        check_vma=False,
    )
```

time: 578 us -> 170 us (0.29)
  waiting for transfers between devices: 376 us -> 45 us
  Pallas kernels: 0 us -> 60.4 us
  matrix products: 56 us -> 0 us
  blocking collectives: 38.3 us -> 0 us
  other arithmetic: 40.1 us -> 11.9 us
  starting transfers between devices: 11.7 us -> 34 us
  local copies, waits for them, and re-layouts: 38.2 us -> 16 us
  between operations: 16.3 us -> 1.12 us
    reduce_scatter x5 -> x0, waiting for transfers between devices: 210 us -> none  [the longest x1 65.4 us: local(): lax.psum_scatter(down_weight_grad.astype(jnp.bfloat16), 'dp', scatter_dim...]
    psum x3 -> x0, waiting for transfers between devices: 104 us -> none  [combine(): return lax.psum(partial_sum.astype(jnp.bfloat16), 'mp').astype(jnp.float32)]
    unnamed x10 -> x0, waiting for transfers between devices: 61.7 us -> none
    pallas_call x0 -> x16, Pallas kernels: none -> 60.4 us  [call(): pl.pallas_call(kernel, out_shape=tuple((jax.ShapeDtypeStruct(shape, kind)...]
    dot_general x39 -> x0, matrix products: 56 us -> none  [the longest x27 45.2 us: matmul(): jnp.einsum(pattern, left_op, right_op, preferred_element_type=jnp.float32)]
    psum x1 -> x0, blocking collectives: 38.3 us -> none  [local(): lax.psum((query_bias_grad, value_bias_grad, up_bias_grad, proj_bias_grad,...]
    ppermute x0 -> x22, waiting for transfers between devices: none -> 38.2 us  [swap(): return lax.ppermute(value, axis, [(i, i ^ bit) for i in range(count)])]
    ppermute x0 -> x22, starting transfers between devices: none -> 18.5 us  [swap(): return lax.ppermute(value, axis, [(i, i ^ bit) for i in range(count)])]
  transfers between devices with their start and end apart: 11 -> 25, of which waited for: 8 -> 8; matrix products, arithmetic and copies ran while one was open for 15% -> 12% of each run, Pallas kernels for 0% -> 28%
where the time goes in v1:
time: 170 us; the launch traced here: 168 us
  Pallas kernels  60.4 us (36%)
  waiting for transfers between devices  45 us (26%)
  starting transfers between devices  34 us (20%)
  local copies, waits for them, and re-layouts  16 us (9%)
  other arithmetic  11.9 us (7%)
    pallas_call x16, Pallas kernels, call(): pl.pallas_call(kernel, out_shape=tuple((jax.ShapeDtypeStruct(shape, kind)...  60.4 us
    ppermute x22, waiting for transfers between devices, swap(): return lax.ppermute(value, axis, [(i, i ^ bit) for i in range(count)])  38.2 us
    ppermute x22, starting transfers between devices, swap(): return lax.ppermute(value, axis, [(i, i ^ bit) for i in range(count)])  18.5 us
    unnamed x68, local copies, waits for them, and re-layouts  9.82 us
    all_to_all x1, starting transfers between devices, local(): lax.all_to_all(back_send, 'dp', split_axis=0, concat_axis=0, tiled=True)  7.26 us
    all_to_all x1, waiting for transfers between devices, local(): lax.all_to_all(vector_rows, 'dp', split_axis=0, concat_axis=0, tiled=True)  6.75 us
    all_to_all x1, starting transfers between devices, local(): lax.all_to_all(vector_rows, 'dp', split_axis=0, concat_axis=0, tiled=True)  4.54 us
    convert_element_type x10, other arithmetic, low_add(): return (left.astype(wide_type) + right.astype(wide_type)).astype(low_type)  4.28 us
  transfers between devices with their start and end apart: 25, of which 8 were waited for; matrix products, arithmetic and copies ran while one was open for 12% of the time, Pallas kernels for 28%

profile of v1, /device:TPU:0, one launch (start us, length us, event | category | flops | bytes accessed | tf_op | source)
XLA Modules:
  0.0 168.4 jit_solution(3519676792897282839)
XLA Ops:
  1.3 4.1 %shard_map.393 = (bf16[8,96,128]{2,1,0:T(8,128)(2,1)}, s32[8]{0:T(128)}, f32[1,128]{1,0:T(1,128)}) custom-call(s32[2]{0:T(128)} %pad_add_fusion.refs_0_.where_ref, s32[64]{0:T(128)} %refs_1_.7, s32[64]{0:T(128)} %patches_ref.1, s32[64,64]{1,0:T(8,128)} %visible_ref.1, bf16[8,256,128]{2,1,0:T(8,128)(2,1)} %refs_4_.1, ...), custom_call_target="tpu_custom_call" | custom-call | flops 100000000 | bytes 2000000 | tf_op jit(solution)/shard_map/pallas_call | solution.py:92
  5.4 7.3 %all-to-all-start = ((bf16[8,96,128]{2,1,0:T(8,128)(2,1)}), bf16[8,96,128]{2,1,0:T(8,128)(2,1)S(1)}, u32[]{:S(2)}, u32[]{:S(2)}) async-start(bf16[8,96,128]{2,1,0:T(8,128)(2,1)} %get-tuple-element.65), calls=%async_computation | async-start | bytes 393216 | tf_op jit(solution)/shard_map/all_to_all | solution.py:572
  15.8 3.4 %shard_map.394 = (bf16[512,768]{1,0:T(8,128)(2,1)}, bf16[512,576]{1,0:T(8,128)(2,1)}) custom-call(bf16[512,768]{1,0:T(8,128)(2,1)} %rows_ref.7, f32[1,768]{1,0:T(1,128)} %get-tuple-element.159.gain_ref, f32[1,768]{1,0:T(1,128)} %get-tuple-element.158.shift_ref, bf16[768,576]{1,0:T(8,128)(2,1)} %copy.48.weight_ref, f32[1,576]{1,0:T(1,128)} %reshape.188.bias_ref), custom_call_target="tpu_custom_call" | custom-call | flops 1000000000 | bytes 3000000 | tf_op jit(solution)/shard_map/pallas_call | solution.py:92
  19.2 6.4 %shard_map.395 = (bf16[512,384]{1,0:T(8,128)(2,1)}, bf16[512,192]{1,0:T(8,128)(2,1)}, bf16[256,768]{1,0:T(8,128)(2,1)}, bf16[256,768]{1,0:T(8,128)(2,1)}) custom-call(s32[2]{0:T(128)} %pad_add_fusion.refs_0_.where_ref, s32[64]{0:T(128)} %patches_ref.1, bf16[512,576]{1,0:T(8,128)(2,1)} %get-tuple-element.62.refs_2_.refs_7_, bf16[192,768]{1,0:T(8,128)(2,1)} %refs_6_.4), custom_call_target="tpu_custom_call" | custom-call | flops 1000000000 | bytes 3000000 | tf_op jit(solution)/shard_map/pallas_call | solution.py:92
  26.3 2.3 %shard_map.396 = (bf16[512,128]{1,0:T(8,128)(2,1)}, bf16[256,768]{1,0:T(8,128)(2,1)}, bf16[256,768]{1,0:T(8,128)(2,1)}) custom-call(s32[2]{0:T(128)} %pad_add_fusion.refs_0_.where_ref, s32[64]{0:T(128)} %refs_1_.7, bf16[8,96,128]{2,1,0:T(8,128)(2,1)} %copy-done.3, bf16[768,128]{1,0:T(8,128)(2,1)} %refs_6_.3), custom_call_target="tpu_custom_call" | custom-call | flops 100000000 | bytes 1000000 | tf_op jit(solution)/shard_map/pallas_call | solution.py:92
  32.5 9.8 %collective-permute-done.1 = bf16[256,768]{1,0:T(8,128)(2,1)S(1)} collective-permute-done((bf16[256,768]{1,0:T(8,128)(2,1)S(1)}, bf16[256,768]{1,0:T(8,128)(2,1)S(1)}, u32[]{:S(2)}, u32[]{:S(2)}) %collective-permute-start.1) | collective-permute-done | bytes 393248 | tf_op jit(solution)/shard_map/ppermute | solution.py:483
  42.5 7.3 %collective-permute-done.4 = bf16[256,768]{1,0:T(8,128)(2,1)S(1)} collective-permute-done((bf16[256,768]{1,0:T(8,128)(2,1)S(1)}, bf16[256,768]{1,0:T(8,128)(2,1)S(1)}, u32[]{:S(2)}, u32[]{:S(2)}) %collective-permute-start.4) | collective-permute-done | bytes 393248 | tf_op jit(solution)/shard_map/ppermute | solution.py:483
  52.7 7.3 %shard_map.397 = (f32[512,768]{1,0:T(8,128)}, bf16[512,768]{1,0:T(8,128)(2,1)}, bf16[512,768]{1,0:T(8,128)(2,1)}, bf16[512,768]{1,0:T(8,128)(2,1)}, bf16[512,768...) custom-call(s32[2]{0:T(128)} %pad_add_fusion.refs_0_.where_ref, ...), custom_call_target="tpu_custom_call" | custom-call | flops 3000000000 | bytes 10000000 | tf_op jit(solution)/shard_map/pallas_call | solution.py:92
  64.9 5.3 %shard_map.407 = (bf16[4,12,96,128]{3,2,1,0:T(8,128)(2,1)}, bf16[4,12,96,128]{3,2,1,0:T(8,128)(2,1)}) custom-call(s32[2]{0:T(128)} %pad_add_fusion.refs_0_.where_ref, bf16[512,768]{1,0:T(8,128)(2,1)} %get-tuple-element.95.act_ref, bf16[512,768]{1,0:T(8,128)(2,1)} %get-tuple-element.96.up_low_ref, bf16[512,768]{1,0:T(8,128)(2,1)} %get-tuple-element.97.acted_ref, ...), custom_call_target="tpu_custom_call" | custom-call | flops 2000000000 | bytes 5000000 | tf_op jit(solution)/shard_map/pallas_call | solution.py:92
  70.2 2.0 %collective-permute-start.19 = (bf16[4,12,96,128]{3,2,1,0:T(8,128)(2,1)}, bf16[4,12,96,128]{3,2,1,0:T(8,128)(2,1)S(1)}, u32[]{:S(2)}, u32[]{:S(2)}) collective-permute-start(bf16[4,12,96,128]{3,2,1,0:T(8,128)(2,1)} %get-tuple-element.99), channel_id=1, source_target_pairs={{0,4},{4,0},{8,12},{12,8},{16,20},{20,16},{24,28},{28,24},{1,5},{5... | collective-permute-start | bytes 3538952 | tf_op jit(solution)/shard_map/ppermute | solution.py:483
  75.5 7.7 %collective-permute-done.7 = bf16[256,768]{1,0:T(8,128)(2,1)S(1)} collective-permute-done((bf16[256,768]{1,0:T(8,128)(2,1)S(1)}, bf16[256,768]{1,0:T(8,128)(2,1)S(1)}, u32[]{:S(2)}, u32[]{:S(2)}) %collective-permute-start.7) | collective-permute-done | bytes 393248 | tf_op jit(solution)/shard_map/ppermute | solution.py:483
  85.6 8.5 %shard_map.400 = (bf16[512,576]{1,0:T(8,128)(2,1)}, f32[128,768]{1,0:T(8,128)}, f32[768,192]{1,0:T(8,128)}, f32[3,768]{1,0:T(4,128)}) custom-call(s32[2]{0:T(128)} %pad_add_fusion.refs_0_.where_ref, bf16[256,768]{1,0:T(8,128)(2,1)} %copy-done.7, bf16[256,768]{1,0:T(8,128)(2,1)} %copy-done.28, f32[512,768]{1,0:T(8,128)} %get-tuple-element.68.refs_2_.refs_3_, ...), custom_call_target="tpu_custom_call" | custom-call | flops 2000000000 | bytes 8000000 | tf_op jit(solution)/shard_map/pallas_call | solution.py:92
  94.2 3.7 %shard_map.401 = (bf16[2,128,768]{2,1,0:T(8,128)(2,1)}, bf16[2,128,768]{2,1,0:T(8,128)(2,1)}, f32[2,768]{1,0:T(2,128)}) custom-call(s32[2]{0:T(128)} %pad_add_fusion.refs_0_.where_ref, bf16[512,768]{1,0:T(8,128)(2,1)} %rows_ref.7, bf16[512,576]{1,0:T(8,128)(2,1)} %get-tuple-element.79.grads_ref, bf16[768,576]{1,0:T(8,128)(2,1)} %copy.48.weight_ref), custom_call_target="tpu_custom_call" | custom-call | flops 1000000000 | bytes 4000000 | tf_op jit(solution)/shard_map/pallas_call | solution.py:92
  98.4 3.9 %shard_map.403 = (bf16[4,6,96,128]{3,2,1,0:T(8,128)(2,1)}, bf16[4,6,96,128]{3,2,1,0:T(8,128)(2,1)}, f32[1,576]{1,0:T(1,128)}) custom-call(s32[2]{0:T(128)} %pad_add_fusion.refs_0_.where_ref, bf16[512,768]{1,0:T(8,128)(2,1)} %get-tuple-element.83.act_ref, bf16[512,576]{1,0:T(8,128)(2,1)} %get-tuple-element.79.grads_ref, f32[768,192]{1,0:T(8,128)} %get-tuple-element.84.out_grad_ref), custom_call_target="tpu_custom_call" | custom-call | flops 1000000000 | bytes 4000000 | tf_op jit(solution)/shard_map/pallas_call | solution.py:92
  106.7 3.3 %shard_map.398 = (bf16[8,160,128]{2,1,0:T(8,128)(2,1)}, f32[1,128]{1,0:T(1,128)}) custom-call(s32[2]{0:T(128)} %pad_add_fusion.refs_0_.where_ref, s32[64]{0:T(128)} %refs_1_.7, f32[512,768]{1,0:T(8,128)} %get-tuple-element.68.refs_2_.refs_3_, bf16[256,768]{1,0:T(8,128)(2,1)} %copy-done, bf16[256,768]{1,0:T(8,128)(2,1)} %copy-done.12, ...), custom_call_target="tpu_custom_call" | custom-call | flops 300000000 | bytes 4000000 | tf_op jit(solution)/shard_map/pallas_call | solution.py:92
  112.2 4.5 %all-to-all-start.2 = ((f32[8,48,128]{2,1,0:T(8,128)}), f32[8,48,128]{2,1,0:T(8,128)}, u32[]{:S(2)}, u32[]{:S(2)}) async-start(f32[8,48,128]{2,1,0:T(8,128)} %shard_map.405), calls=%async_computation.2 | async-start | bytes 393216 | tf_op jit(solution)/shard_map/all_to_all | solution.py:719
  117.1 2.1 %collective-permute-start.20 = (bf16[2,12,96,128]{3,2,1,0:T(8,128)(2,1)S(1)}, bf16[2,12,96,128]{3,2,1,0:T(8,128)(2,1)S(1)}, u32[]{:S(2)}, u32[]{:S(2)}) collective-permute-start(bf16[2,12,96,128]{3,2,1,0:T(8,128)(2,1)S(1)} %select_bitcast_fusion), channel_id=1, source_target_pairs={{0,8},{4,12},{8,0},{12,4},{16,24},{20,28},{24,16},{28,20},{1,9},{5... | collective-permute-start | bytes 1769480 | tf_op jit(solution)/shard_map/ppermute | solution.py:483
  119.2 6.7 %all-to-all-done.2.rows_ref = f32[8,48,128]{2,1,0:T(8,128)} async-done(((f32[8,48,128]{2,1,0:T(8,128)}), f32[8,48,128]{2,1,0:T(8,128)}, u32[]{:S(2)}, u32[]{:S(2)}) %all-to-all-start.2) | async-done | bytes 196640 | tf_op jit(solution)/shard_map/all_to_all | solution.py:719
  125.9 3.7 %all-to-all-start.1 = ((bf16[8,160,128]{2,1,0:T(8,128)(2,1)}), bf16[8,160,128]{2,1,0:T(8,128)(2,1)S(1)}, u32[]{:S(2)}, u32[]{:S(2)}) async-start(bf16[8,160,128]{2,1,0:T(8,128)(2,1)} %get-tuple-element.72), calls=%async_computation.1 | async-start | bytes 655360 | tf_op jit(solution)/shard_map/all_to_all | solution.py:700
  140.3 2.4 %collective-permute-start.21 = (bf16[1,12,96,128]{3,2,1,0:T(8,128)(2,1)S(1)}, bf16[1,12,96,128]{3,2,1,0:T(8,128)(2,1)S(1)}, u32[]{:S(2)}, u32[]{:S(2)}) collective-permute-start(bf16[1,12,96,128]{3,2,1,0:T(8,128)(2,1)S(1)} %get-tuple-element.141), channel_id=1, source_target_pairs={{0,16},{4,20},{8,24},{12,28},{16,0},{20,4},{24,8},{28,12},{1,17},{... | collective-permute-start | bytes 884744 | tf_op jit(solution)/shard_map/ppermute | solution.py:483
  142.7 10.1 %collective-permute-done.15 = bf16[2,6,96,128]{3,2,1,0:T(8,128)(2,1)S(1)} collective-permute-done((bf16[2,6,96,128]{3,2,1,0:T(8,128)(2,1)S(1)}, bf16[2,6,96,128]{3,2,1,0:T(8,128)(2,1)S(1)}, u32[]{:S(2)}, u32[]{:S(2)}) %collective-permute-start.15) | collective-permute-done | bytes 294944 | tf_op jit(solution)/shard_map/ppermute | solution.py:483
  155.6 2.5 %shard_map.399 = (bf16[8,256,128]{2,1,0:T(8,128)(2,1)}, f32[96,128]{1,0:T(8,128)}) custom-call(s32[8]{0:T(128)} %get-tuple-element.61.source_ref, s32[64]{0:T(128)} %patches_ref.1, s32[64,64]{1,0:T(8,128)} %visible_ref.1, bf16[8,160,128]{2,1,0:T(8,128)(2,1)} %copy-done.1, f32[1,128]{1,0:T(1,128)} %bitcast_convert_fusion.mask_ref, bf16[256,128]{1,0:T(8,128)(2,1)} %pos_ref.1, ...), custom_call_target="tpu_custom_call" | custom-call | flops 100000000 | bytes 2000000 | tf_op jit(solution)/shard_map/pallas_call | solution.py:92
  158.9 2.4 %shard_map.402 = bf16[128,768]{1,0:T(8,128)(2,1)} custom-call(s32[2]{0:T(128)} %pad_add_fusion.refs_0_.where_ref, bf16[512,768]{1,0:T(8,128)(2,1)} %rows_ref.7, bf16[128,768]{1,0:T(8,128)(2,1)} %get-tuple-element.144.keep_ref, bf16[128,768]{1,0:T(8,128)(2,1)} %bitcast.90, f32[128,768]{1,0:T(8,128)} %get-tuple-element.82.own_ref, ...), custom_call_target="tpu_custom_call" | custom-call | flops 10000000 | bytes 2000000 | tf_op jit(solution)/shard_map/pallas_call | solution.py:92
  162.0 2.0 %shard_map.408 = (f32[96,768]{1,0:T(8,128)}, f32[768,96]{1,0:T(8,128)}) custom-call(bf16[12,96,128]{2,1,0:T(8,128)(2,1)} %get-tuple-element.142.keep_ref, bf16[12,96,128]{2,1,0:T(8,128)(2,1)} %bitcast.89), custom_call_target="tpu_custom_call" | custom-call | bytes 2000000 | tf_op jit(solution)/shard_map/pallas_call | solution.py:92
  (151 shorter events, 48.3 us)
Async XLA Ops:
  5.4 20.2 %all-to-all-start = ((bf16[8,96,128]{2,1,0:T(8,128)(2,1)}), bf16[8,96,128]{2,1,0:T(8,128)(2,1)S(1)}, u32[]{:S(2)}, u32[]{:S(2)}) async-start(bf16[8,96,128]{2,1,0:T(8,128)(2,1)} %get-tuple-element.65), calls=%async_computation | async-start | bytes 393216 | tf_op jit(solution)/shard_map/all_to_all | solution.py:572
  25.6 3.5 %collective-permute-start = (bf16[256,768]{1,0:T(8,128)(2,1)}, bf16[256,768]{1,0:T(8,128)(2,1)S(1)}, u32[]{:S(2)}, u32[]{:S(2)}) collective-permute-start(bf16[256,768]{1,0:T(8,128)(2,1)} %get-tuple-element.64), channel_id=1, source_target_pairs={{0,1},{1,0},{2,3},{3,2},{4,5},{5,4},{6,7},{7,6},{8,9},{9,8},{10,11... | collective-permute-start | bytes 1179656 | tf_op jit(solution)/shard_map/ppermute | solution.py:483
  28.7 3.2 %collective-permute-start.3 = (bf16[256,768]{1,0:T(8,128)(2,1)}, bf16[256,768]{1,0:T(8,128)(2,1)S(1)}, u32[]{:S(2)}, u32[]{:S(2)}) collective-permute-start(bf16[256,768]{1,0:T(8,128)(2,1)} %get-tuple-element.67), channel_id=1, source_target_pairs={{0,1},{1,0},{2,3},{3,2},{4,5},{5,4},{6,7},{7,6},{8,9},{9,8},{10,11... | collective-permute-start | bytes 1179656 | tf_op jit(solution)/shard_map/ppermute | solution.py:483
  30.3 12.0 %collective-permute-start.1 = (bf16[256,768]{1,0:T(8,128)(2,1)S(1)}, bf16[256,768]{1,0:T(8,128)(2,1)S(1)}, u32[]{:S(2)}, u32[]{:S(2)}) collective-permute-start(bf16[256,768]{1,0:T(8,128)(2,1)S(1)} %add_convert_fusion.10), channel_id=1, source_target_pairs={{0,2},{1,3},{2,0},{3,1},{4,6},{5,7},{6,4},{7,5},{8,10},{9,11},{10,... | collective-permute-start | bytes 1179656 | tf_op jit(solution)/shard_map/ppermute | solution.py:483
  32.0 17.9 %collective-permute-start.4 = (bf16[256,768]{1,0:T(8,128)(2,1)S(1)}, bf16[256,768]{1,0:T(8,128)(2,1)S(1)}, u32[]{:S(2)}, u32[]{:S(2)}) collective-permute-start(bf16[256,768]{1,0:T(8,128)(2,1)S(1)} %add_convert_fusion.8), channel_id=1, source_target_pairs={{0,2},{1,3},{2,0},{3,1},{4,6},{5,7},{6,4},{7,5},{8,10},{9,11},{10,... | collective-permute-start | bytes 1179656 | tf_op jit(solution)/shard_map/ppermute | solution.py:483
  42.4 8.8 %collective-permute-start.2 = (bf16[256,768]{1,0:T(8,128)(2,1)S(1)}, bf16[256,768]{1,0:T(8,128)(2,1)S(1)}, u32[]{:S(2)}, u32[]{:S(2)}) collective-permute-start(bf16[256,768]{1,0:T(8,128)(2,1)S(1)} %add_convert_fusion.9.sum_ref), channel_id=1, source_target_pairs={{0,1},{1,0},{2,3},{3,2},{4,5},{5,4},{6,7},{7,6},{8,9},{9,8},{10,11... | collective-permute-start | bytes 1179656 | tf_op jit(solution)/shard_map/ppermute | solution.py:483
  60.1 2.1 %collective-permute-start.9 = (bf16[256,768]{1,0:T(8,128)(2,1)}, bf16[256,768]{1,0:T(8,128)(2,1)S(1)}, u32[]{:S(2)}, u32[]{:S(2)}) collective-permute-start(bf16[256,768]{1,0:T(8,128)(2,1)} %get-tuple-element.75), channel_id=1, source_target_pairs={{0,1},{1,0},{2,3},{3,2},{4,5},{5,4},{6,7},{7,6},{8,9},{9,8},{10,11... | collective-permute-start | bytes 1179656 | tf_op jit(solution)/shard_map/ppermute | solution.py:483
  61.1 11.1 %collective-permute-start.6 = (bf16[256,768]{1,0:T(8,128)(2,1)}, bf16[256,768]{1,0:T(8,128)(2,1)S(1)}, u32[]{:S(2)}, u32[]{:S(2)}) collective-permute-start(bf16[256,768]{1,0:T(8,128)(2,1)} %get-tuple-element.70), channel_id=1, source_target_pairs={{0,1},{1,0},{2,3},{3,2},{4,5},{5,4},{6,7},{7,6},{8,9},{9,8},{10,11... | collective-permute-start | bytes 1179656 | tf_op jit(solution)/shard_map/ppermute | solution.py:483
  63.3 11.5 %collective-permute-start.10 = (bf16[256,768]{1,0:T(8,128)(2,1)S(1)}, bf16[256,768]{1,0:T(8,128)(2,1)S(1)}, u32[]{:S(2)}, u32[]{:S(2)}) collective-permute-start(bf16[256,768]{1,0:T(8,128)(2,1)S(1)} %add_convert_fusion.4), channel_id=1, source_target_pairs={{0,2},{1,3},{2,0},{3,1},{4,6},{5,7},{6,4},{7,5},{8,10},{9,11},{10,... | collective-permute-start | bytes 1179656 | tf_op jit(solution)/shard_map/ppermute | solution.py:483
  70.2 46.5 %collective-permute-start.19 = (bf16[4,12,96,128]{3,2,1,0:T(8,128)(2,1)}, bf16[4,12,96,128]{3,2,1,0:T(8,128)(2,1)S(1)}, u32[]{:S(2)}, u32[]{:S(2)}) collective-permute-start(bf16[4,12,96,128]{3,2,1,0:T(8,128)(2,1)} %get-tuple-element.99), channel_id=1, source_target_pairs={{0,4},{4,0},{8,12},{12,8},{16,20},{20,16},{24,28},{28,24},{1,5},{5... | collective-permute-start | bytes 3538952 | tf_op jit(solution)/shard_map/ppermute | solution.py:483
  72.3 10.9 %collective-permute-start.7 = (bf16[256,768]{1,0:T(8,128)(2,1)S(1)}, bf16[256,768]{1,0:T(8,128)(2,1)S(1)}, u32[]{:S(2)}, u32[]{:S(2)}) collective-permute-start(bf16[256,768]{1,0:T(8,128)(2,1)S(1)} %add_convert_fusion.6), channel_id=1, source_target_pairs={{0,2},{1,3},{2,0},{3,1},{4,6},{5,7},{6,4},{7,5},{8,10},{9,11},{10,... | collective-permute-start | bytes 1179656 | tf_op jit(solution)/shard_map/ppermute | solution.py:483
  74.8 10.0 %collective-permute-start.11 = (bf16[256,768]{1,0:T(8,128)(2,1)S(1)}, bf16[256,768]{1,0:T(8,128)(2,1)S(1)}, u32[]{:S(2)}, u32[]{:S(2)}) collective-permute-start(bf16[256,768]{1,0:T(8,128)(2,1)S(1)} %add_convert_fusion.3.refs_1_), channel_id=1, source_target_pairs={{0,1},{1,0},{2,3},{3,2},{4,5},{5,4},{6,7},{7,6},{8,9},{9,8},{10,11... | collective-permute-start | bytes 1179656 | tf_op jit(solution)/shard_map/ppermute | solution.py:483
  83.3 22.7 %collective-permute-start.8 = (bf16[256,768]{1,0:T(8,128)(2,1)S(1)}, bf16[256,768]{1,0:T(8,128)(2,1)S(1)}, u32[]{:S(2)}, u32[]{:S(2)}) collective-permute-start(bf16[256,768]{1,0:T(8,128)(2,1)S(1)} %add_convert_fusion.5.refs_3_), channel_id=1, source_target_pairs={{0,1},{1,0},{2,3},{3,2},{4,5},{5,4},{6,7},{7,6},{8,9},{9,8},{10,11... | collective-permute-start | bytes 1179656 | tf_op jit(solution)/shard_map/ppermute | solution.py:483
  97.9 36.1 %collective-permute-start.12 = (bf16[2,128,768]{2,1,0:T(8,128)(2,1)}, bf16[2,128,768]{2,1,0:T(8,128)(2,1)}, u32[]{:S(2)}, u32[]{:S(2)}) collective-permute-start(bf16[2,128,768]{2,1,0:T(8,128)(2,1)} %get-tuple-element.81), channel_id=1, source_target_pairs={{0,1},{1,0},{2,3},{3,2},{4,5},{5,4},{6,7},{7,6},{8,9},{9,8},{10,11... | collective-permute-start | bytes 1179656 | tf_op jit(solution)/shard_map/ppermute | solution.py:483
  98.3 6.0 %collective-permute-start.17 = (f32[2,768]{1,0:T(2,128)}, f32[2,768]{1,0:T(2,128)S(1)}, u32[]{:S(2)}, u32[]{:S(2)}) collective-permute-start(f32[2,768]{1,0:T(2,128)} %get-tuple-element.93), channel_id=1, source_target_pairs={{0,1},{1,0},{2,3},{3,2},{4,5},{5,4},{6,7},{7,6},{8,9},{9,8},{10,11... | collective-permute-start | bytes 18440 | tf_op jit(solution)/shard_map/ppermute | solution.py:483
  102.3 34.0 %collective-permute-start.14 = (bf16[4,6,96,128]{3,2,1,0:T(8,128)(2,1)}, bf16[4,6,96,128]{3,2,1,0:T(8,128)(2,1)}, u32[]{:S(2)}, u32[]{:S(2)}) collective-permute-start(bf16[4,6,96,128]{3,2,1,0:T(8,128)(2,1)} %get-tuple-element.86), channel_id=1, source_target_pairs={{0,4},{4,0},{8,12},{12,8},{16,20},{20,16},{24,28},{28,24},{1,5},{5... | collective-permute-start | bytes 1769480 | tf_op jit(solution)/shard_map/ppermute | solution.py:483
  104.4 5.7 %collective-permute-start.18 = (f32[2,768]{1,0:T(2,128)S(1)}, f32[2,768]{1,0:T(2,128)S(1)}, u32[]{:S(2)}, u32[]{:S(2)}) collective-permute-start(f32[2,768]{1,0:T(2,128)S(1)} %add.53.first_ref), channel_id=1, source_target_pairs={{0,2},{1,3},{2,0},{3,1},{4,6},{5,7},{6,4},{7,5},{8,10},{9,11},{10,... | collective-permute-start | bytes 18440 | tf_op jit(solution)/shard_map/ppermute | solution.py:483
  112.2 13.8 %all-to-all-start.2 = ((f32[8,48,128]{2,1,0:T(8,128)}), f32[8,48,128]{2,1,0:T(8,128)}, u32[]{:S(2)}, u32[]{:S(2)}) async-start(f32[8,48,128]{2,1,0:T(8,128)} %shard_map.405), calls=%async_computation.2 | async-start | bytes 393216 | tf_op jit(solution)/shard_map/all_to_all | solution.py:719
  117.1 22.2 %collective-permute-start.20 = (bf16[2,12,96,128]{3,2,1,0:T(8,128)(2,1)S(1)}, bf16[2,12,96,128]{3,2,1,0:T(8,128)(2,1)S(1)}, u32[]{:S(2)}, u32[]{:S(2)}) collective-permute-start(bf16[2,12,96,128]{3,2,1,0:T(8,128)(2,1)S(1)} %select_bitcast_fusion), channel_id=1, source_target_pairs={{0,8},{4,12},{8,0},{12,4},{16,24},{20,28},{24,16},{28,20},{1,9},{5... | collective-permute-start | bytes 1769480 | tf_op jit(solution)/shard_map/ppermute | solution.py:483
  125.9 28.9 %all-to-all-start.1 = ((bf16[8,160,128]{2,1,0:T(8,128)(2,1)}), bf16[8,160,128]{2,1,0:T(8,128)(2,1)S(1)}, u32[]{:S(2)}, u32[]{:S(2)}) async-start(bf16[8,160,128]{2,1,0:T(8,128)(2,1)} %get-tuple-element.72), calls=%async_computation.1 | async-start | bytes 655360 | tf_op jit(solution)/shard_map/all_to_all | solution.py:700
  135.8 22.4 %collective-permute-start.13 = (bf16[1,128,768]{2,1,0:T(8,128)(2,1)S(1)}, bf16[1,128,768]{2,1,0:T(8,128)(2,1)S(1)}, u32[]{:S(2)}, u32[]{:S(2)}) collective-permute-start(bf16[1,128,768]{2,1,0:T(8,128)(2,1)S(1)} %get-tuple-element.143), channel_id=1, source_target_pairs={{0,2},{1,3},{2,0},{3,1},{4,6},{5,7},{6,4},{7,5},{8,10},{9,11},{10,... | collective-permute-start | bytes 589832 | tf_op jit(solution)/shard_map/ppermute | solution.py:483
  137.6 15.2 %collective-permute-start.15 = (bf16[2,6,96,128]{3,2,1,0:T(8,128)(2,1)S(1)}, bf16[2,6,96,128]{3,2,1,0:T(8,128)(2,1)S(1)}, u32[]{:S(2)}, u32[]{:S(2)}) collective-permute-start(bf16[2,6,96,128]{3,2,1,0:T(8,128)(2,1)S(1)} %select_bitcast_fusion.3), channel_id=1, source_target_pairs={{0,8},{4,12},{8,0},{12,4},{16,24},{20,28},{24,16},{28,20},{1,9},{5... | collective-permute-start | bytes 884744 | tf_op jit(solution)/shard_map/ppermute | solution.py:483
  140.3 21.0 %collective-permute-start.21 = (bf16[1,12,96,128]{3,2,1,0:T(8,128)(2,1)S(1)}, bf16[1,12,96,128]{3,2,1,0:T(8,128)(2,1)S(1)}, u32[]{:S(2)}, u32[]{:S(2)}) collective-permute-start(bf16[1,12,96,128]{3,2,1,0:T(8,128)(2,1)S(1)} %get-tuple-element.141), channel_id=1, source_target_pairs={{0,16},{4,20},{8,24},{12,28},{16,0},{20,4},{24,8},{28,12},{1,17},{... | collective-permute-start | bytes 884744 | tf_op jit(solution)/shard_map/ppermute | solution.py:483
  153.6 12.3 %collective-permute-start.16 = (bf16[1,6,96,128]{3,2,1,0:T(8,128)(2,1)S(1)}, bf16[1,6,96,128]{3,2,1,0:T(8,128)(2,1)S(1)}, u32[]{:S(2)}, u32[]{:S(2)}) collective-permute-start(bf16[1,6,96,128]{3,2,1,0:T(8,128)(2,1)S(1)} %get-tuple-element.145), channel_id=1, source_target_pairs={{0,16},{4,20},{8,24},{12,28},{16,0},{20,4},{24,8},{28,12},{1,17},{... | collective-permute-start | bytes 442376 | tf_op jit(solution)/shard_map/ppermute | solution.py:483
  (34 other events, 231.5 us)

commit v2 on v1

v2 whole, which is shorter than its diff:
```python
import math

import jax
import jax.numpy as jnp
import numpy as np
from jax import lax
from jax.experimental import pallas as pl
from jax.experimental.pallas import tpu as pltpu
from jax.sharding import PartitionSpec as P

HEAD_DIM = 64
GRID = 256
VIS = 64
PAIR = 2 * VIS
CHUNK = 512
LANES = 128

epsilon = 1e-06
low_type = jnp.bfloat16
wide_type = jnp.float32
scale_factor = HEAD_DIM ** (-0.5)

VMEM = pl.BlockSpec(memory_space=pltpu.VMEM)
SMEM = pl.BlockSpec(memory_space=pltpu.SMEM)
ANY = pl.BlockSpec(memory_space=pl.ANY)
PINNED_ROWS = 512


def grid_tables():
    grid_edge = math.isqrt(GRID)
    tables = []
    for side_cells in (10, 14):
        places = np.arange(side_cells)
        centers = ((2 * places + 1) * grid_edge - side_cells) / (2 * side_cells)
        lower = np.floor(centers).astype(np.int64)
        share = centers - lower
        lerp = np.zeros((side_cells, grid_edge))
        lerp[places, np.clip(lower, 0, grid_edge - 1)] += 1.0 - share
        lerp[places, np.clip(lower + 1, 0, grid_edge - 1)] += share
        table = np.zeros((GRID, GRID))
        table[: side_cells * side_cells] = np.kron(lerp, lerp)
        tables.append(table)
    return np.stack(tables).astype(np.float32)


def split_low(value):
    high = value.astype(low_type)
    return high, (value - high.astype(wide_type)).astype(low_type)


def dot(left, right):
    return lax.dot_general(left, right, (((1,), (0,)), ((), ())), preferred_element_type=wide_type)


def dot_right_t(left, right):
    return lax.dot_general(left, right, (((1,), (1,)), ((), ())), preferred_element_type=wide_type)


def dot_left_t(left, right):
    return lax.dot_general(left, right, (((0,), (0,)), ((), ())), preferred_element_type=wide_type)


def normalized(value):
    center = value - jnp.mean(value, axis=-1, keepdims=True)
    spread = lax.rsqrt(jnp.mean(center * center, axis=-1, keepdims=True) + epsilon)
    return center * spread, spread


def norm_back(grad, normed, spread, gain):
    scaled = grad * gain
    mean_one = jnp.mean(scaled, axis=-1, keepdims=True)
    mean_two = jnp.mean(scaled * normed, axis=-1, keepdims=True)
    return spread * (scaled - mean_one - normed * mean_two)


def row_sum(value):
    return jnp.sum(value, axis=0, keepdims=True)


def over_rows(total, size, body):
    size = min(size, total)
    if total == size:
        body(0, size)
        return

    def step(i, carry):
        body(pl.multiple_of(i * size, size), size)
        return carry

    lax.fori_loop(0, total // size, step, 0)


def size_of(shape, kind):
    return math.prod(shape) * jnp.dtype(kind).itemsize


class Order:
    def __init__(self, pinned):
        self.pinned = pinned
        self.last = None
        self.held = []

    def keep(self, value):
        if not self.pinned:
            return value
        value = pltpu.with_memory_space_constraint(value, pltpu.VMEM)
        self.held.append(value)
        return value

    def __call__(self, kernel, outs, args, specs=None, scratch=(), out_specs=None, final=False):
        args = tuple(args)
        specs = [VMEM] * len(args) if specs is None else list(specs)
        count = len(args)
        needed = sum(size_of(ref.shape, ref.dtype) for ref in scratch)
        needed += sum(
            size_of(arg.shape, arg.dtype) for arg in args if not any(arg is held for held in self.held)
        )
        out_specs = [VMEM] * len(outs) if out_specs is None else list(out_specs)
        shapes = []
        for (shape, kind), spec in zip(outs, out_specs):
            if self.pinned and not final and spec is VMEM:
                shapes.append(pltpu.VMEM(shape, kind))
            else:
                shapes.append(jax.ShapeDtypeStruct(shape, kind))
                needed += size_of(shape, kind)
        body = kernel
        if self.last is not None:
            args += (self.last,)
            specs.append(ANY)

            def body(*refs):
                kernel(*refs[:count], *refs[count + 1 :])

        results = pl.pallas_call(
            body,
            out_shape=tuple(shapes),
            in_specs=specs,
            out_specs=tuple(out_specs),
            scratch_shapes=list(scratch),
            compiler_params=pltpu.CompilerParams(
                vmem_limit_bytes=min(needed + needed // 4 + 10 * 2**20, 60 * 2**20)
            ),
            cost_estimate=pl.CostEstimate(flops=1000, bytes_accessed=1000, transcendentals=0),
        )(*args)
        self.held += [
            result
            for result, shape in zip(results, shapes)
            if not isinstance(shape, jax.ShapeDtypeStruct)
        ]
        if not final:
            self.last = results[0]
        return results


def find_sources(count, images, me, owner_ref, source_ref):
    for slot in range(count):

        def find(i, found, slot=slot):
            return jnp.where(owner_ref[slot * images + i] == me, slot * images + i, found)

        source_ref[slot] = lax.fori_loop(0, images, find, slot * images, unroll=images <= 8)


def over_slots(count, one_slot):
    if count <= 8:
        for slot in range(count):
            one_slot(slot)
    else:
        lax.fori_loop(0, count, lambda slot, carry: (one_slot(slot), carry)[1], 0)


def side_of(size):
    return (size >= 196).astype(jnp.int32) + (size >= 256).astype(jnp.int32)


def cotangent_kernel(count, images, where_ref, owner_ref, visible_ref, cot_ref, send_ref, source_ref):
    find_sources(count, images, where_ref[0], owner_ref, source_ref)
    cells = lax.broadcasted_iota(jnp.int32, (GRID, VIS), 0)

    def one_slot(slot):
        seen = visible_ref[pl.ds(source_ref[slot], 1), :] == cells
        send_ref[slot] = dot_left_t(seen.astype(low_type), cot_ref[slot]).astype(low_type)

    over_slots(count, one_slot)


def position_kernel(
    count, source_ref, patches_ref, visible_ref, cot_ref, turned_high_ref, turned_low_ref, table_high_ref,
    table_low_ref, pos_ref, send_ref, mask_ref, layout_ref, sums_ref,
):
    share = GRID // count
    cells = lax.broadcasted_iota(jnp.int32, (GRID, VIS), 0)
    cell_column = lax.broadcasted_iota(jnp.int32, (GRID, 1), 0)
    sums_ref[...] = jnp.zeros_like(sums_ref)
    mask_ref[...] = jnp.zeros_like(mask_ref)

    def one_slot(slot):
        source = source_ref[slot]
        size = patches_ref[source]
        seen = visible_ref[pl.ds(source, 1), :] == cells
        fill = (cell_column < size).astype(wide_type) - jnp.sum(
            seen.astype(wide_type), axis=1, keepdims=True
        )
        wide = cot_ref[slot].astype(wide_type)
        mask_ref[...] += row_sum(fill * wide)
        sums_ref[side_of(size)] += wide

    over_slots(count, one_slot)
    total = sums_ref[2]
    for side in range(2):
        high, low = split_low(sums_ref[side])
        total += (
            dot(turned_high_ref[side], high) + dot(turned_high_ref[side], low) + dot(turned_low_ref[side], high)
        )
    send_ref[...] = jnp.zeros_like(send_ref)
    total = total.astype(low_type)
    for block in range(count):
        send_ref[block, :share, :] = total[block * share : (block + 1) * share]
    table = pos_ref[...]
    for side in range(2):
        layout_ref[side] = dot(table_high_ref[side], table) + dot(table_low_ref[side], table)
    layout_ref[2] = table.astype(wide_type)


def wide_row(ref):
    return ref[...].astype(wide_type).reshape(1, ref.shape[0])


def enter_kernel(rows_ref, gain_ref, shift_ref, weight_ref, query_ref, value_ref, act_ref, qkv_ref):
    gain, shift = wide_row(gain_ref), wide_row(shift_ref)
    query, value = wide_row(query_ref), wide_row(value_ref)
    nothing = jnp.zeros((1, HEAD_DIM), wide_type)
    pieces = []
    for start in range(0, query.shape[1], HEAD_DIM):
        pieces += [query[:, start : start + HEAD_DIM], nothing, value[:, start : start + HEAD_DIM]]
    bias = jnp.concatenate(pieces, axis=1)

    def body(start, size):
        rows = pl.ds(start, size)
        normed, _ = normalized(rows_ref[rows, :].astype(wide_type))
        act = (normed * gain + shift).astype(low_type)
        act_ref[rows, :] = act
        qkv_ref[rows, :] = (dot_right_t(act, weight_ref[...]) + bias).astype(low_type)

    over_rows(rows_ref.shape[0], CHUNK, body)


def attention_kernel(
    images, heads, where_ref, patches_ref, qkv_ref, weight_ref, keep_ref, sent_ref, prob_ref, attended_ref
):
    first_image = where_ref[0] * images
    row_half = lax.broadcasted_iota(jnp.int32, (PAIR, PAIR), 0) // VIS
    lane = lax.broadcasted_iota(jnp.int32, (PAIR, PAIR), 1)

    def body(start, size):
        for pair in range(size // PAIR):
            rows = pl.ds(start + pair * PAIR, PAIR)
            image = first_image + (start + pair * PAIR) // VIS
            limits = [patches_ref[image + i] // 4 for i in range(2)]
            last = jnp.where(row_half == 0, limits[0], VIS + limits[1])
            live = jnp.logical_and(lane >= row_half * VIS, lane < last)
            for head in range(heads):
                base = head * 3 * HEAD_DIM
                queries = qkv_ref[rows, base : base + HEAD_DIM]
                key_rows = qkv_ref[rows, base + HEAD_DIM : base + 2 * HEAD_DIM]
                value_rows = qkv_ref[rows, base + 2 * HEAD_DIM : base + 3 * HEAD_DIM]
                scores = jnp.where(live, dot_right_t(queries, key_rows) * scale_factor, -1e30)
                raised = jnp.exp(scores - jnp.max(scores, axis=-1, keepdims=True))
                probs = (raised / jnp.sum(raised, axis=-1, keepdims=True)).astype(low_type)
                prob_ref[rows, head * PAIR : (head + 1) * PAIR] = probs
                attended_ref[rows, head * HEAD_DIM : (head + 1) * HEAD_DIM] = dot(
                    probs, value_rows
                ).astype(low_type)

    over_rows(qkv_ref.shape[0], CHUNK, body)
    halves(where_ref[1] & 1, attended_ref, weight_ref, keep_ref, sent_ref, dot)


def halves(upper, left_ref, weight_ref, keep_ref, sent_ref, product):
    half = keep_ref.shape[0]
    for out_ref, which in ((sent_ref, 1 - upper), (keep_ref, upper)):

        def body(start, size, out_ref=out_ref, which=which):
            rows = pl.ds(pl.multiple_of(which * half + start, size), size)
            out_ref[pl.ds(start, size), :] = product(left_ref[rows, :], weight_ref[...]).astype(
                out_ref.dtype
            )

        over_rows(half, CHUNK, body)


def both_halves(upper, half, body):
    for source, which in enumerate((upper, 1 - upper)):

        def one(start, size, source=source, which=which):
            body(source, pl.ds(pl.multiple_of(which * half + start, size), size), pl.ds(start, size), size)

        over_rows(half, 256, one)


def back_kernel(images, where_ref, owner_ref, back_ref, weight_ref, keep_ref, sent_ref, enc_ref):
    base = where_ref[0] * images
    for image in range(images):
        enc_ref[image * VIS : (image + 1) * VIS, :] = back_ref[owner_ref[base + image]]
    halves(where_ref[1] & 1, enc_ref, weight_ref, keep_ref, sent_ref, dot_right_t)


def add_kernel(left_ref, right_ref, out_ref):
    out_ref[...] = (left_ref[...].astype(wide_type) + right_ref[...].astype(wide_type)).astype(low_type)


def forward_back_kernel(
    where_ref, rows_ref, sum_ref, sum_other_ref, grad_ref, grad_other_ref, out_bias_ref, gain_ref, shift_ref,
    up_ref, up_bias_ref, down_ref,
    keep_ref, sent_ref, hidden_ref, act_ref, acted_ref, up_low_ref, down_low_ref, bias_ref,
):
    upper = where_ref[1] & 1
    out_bias, gain, shift, up_bias = (
        wide_row(ref) for ref in (out_bias_ref, gain_ref, shift_ref, up_bias_ref)
    )

    def body(source, rows, part, size):
        total = (sum_ref, sum_other_ref)[source][part, :].astype(wide_type)
        hidden = rows_ref[rows, :].astype(wide_type) + total + out_bias
        hidden_ref[rows, :] = hidden
        normed, _ = normalized(hidden)
        act = (normed * gain + shift).astype(low_type)
        act_ref[rows, :] = act
        down_low = (grad_ref, grad_other_ref)[source][part, :]
        down_low_ref[rows, :] = down_low
        up_pre = dot(act, up_ref[...]) + up_bias
        cdf = 0.5 + 0.5 * lax.erf(up_pre * math.sqrt(0.5))
        acted_ref[rows, :] = (up_pre * cdf).astype(low_type)
        slope = cdf + up_pre * jnp.exp(-0.5 * up_pre * up_pre) * (1.0 / math.sqrt(2.0 * math.pi))
        up_low_ref[rows, :] = (dot_right_t(down_low, down_ref[...]) * slope).astype(low_type)

    both_halves(upper, sum_ref.shape[0], body)
    halves(upper, up_low_ref, up_ref, keep_ref, sent_ref, dot_right_t)
    bias_ref[0:1, :] = row_sum(down_low_ref[...].astype(wide_type))
    bias_ref[1:2, :] = row_sum(up_low_ref[...].astype(wide_type))


def part_blocks(lower_bit, wide_ref, parts, keep_ref, sent_ref, first_tile):
    share = keep_ref.shape[2]
    for out_ref, which in ((sent_ref, 1 - lower_bit), (keep_ref, lower_bit)):
        for block in range(keep_ref.shape[0]):
            rows = pl.ds(pl.multiple_of((2 * block + which) * share, 8), share)
            for tile in range(parts):
                out_ref[block, first_tile + tile] = wide_ref[
                    rows, tile * LANES : (tile + 1) * LANES
                ].astype(out_ref.dtype)


def early_grads_kernel(where_ref, act_ref, up_low_ref, acted_ref, down_low_ref, keep_ref, sent_ref, wide_ref):
    lower_bit = where_ref[0] & 1
    tiles = wide_ref.shape[1] // LANES
    wide_ref[...] = dot_left_t(act_ref[...], up_low_ref[...])
    part_blocks(lower_bit, wide_ref, tiles, keep_ref, sent_ref, 0)
    wide_ref[...] = dot_left_t(down_low_ref[...], acted_ref[...])
    part_blocks(lower_bit, wide_ref, tiles, keep_ref, sent_ref, tiles)


def forward_part_kernel(where_ref, acted_ref, down_ref, keep_ref, sent_ref):
    halves(where_ref[1] & 1, acted_ref, down_ref, keep_ref, sent_ref, dot)


def attention_back_kernel(
    heads, where_ref, sum_ref, sum_other_ref, hidden_ref, down_low_ref, gain_ref, weight_ref, qkv_ref, prob_ref,
    grads_ref, attn_low_ref, own_ref, bias_ref, grad_ref,
):
    gain = wide_row(gain_ref)
    bias_ref[...] = jnp.zeros_like(bias_ref)

    def body(source, rows, part, size):
        normed, spread = normalized(hidden_ref[rows, :])
        grad = (sum_ref, sum_other_ref)[source][part, :].astype(wide_type)
        bias_ref[0:1, :] += row_sum(grad * normed)
        bias_ref[1:2, :] += row_sum(grad)
        hidden_grad = down_low_ref[rows, :].astype(wide_type) + norm_back(grad, normed, spread, gain)
        grad_ref[rows, :] = hidden_grad
        bias_ref[2:3, :] += row_sum(hidden_grad)
        attn_low = hidden_grad.astype(low_type)
        attn_low_ref[rows, :] = attn_low
        attended_grad = dot_right_t(attn_low, weight_ref[...]).astype(low_type)
        for pair in range(size // PAIR):
            pair_rows = pl.ds(rows.start + pair * PAIR, PAIR)
            for head in range(heads):
                base = head * 3 * HEAD_DIM
                queries = qkv_ref[pair_rows, base : base + HEAD_DIM]
                key_rows = qkv_ref[pair_rows, base + HEAD_DIM : base + 2 * HEAD_DIM]
                value_rows = qkv_ref[pair_rows, base + 2 * HEAD_DIM : base + 3 * HEAD_DIM]
                probs = prob_ref[pair_rows, head * PAIR : (head + 1) * PAIR]
                grad_rows = attended_grad[
                    pair * PAIR : (pair + 1) * PAIR, head * HEAD_DIM : (head + 1) * HEAD_DIM
                ]
                value_low = dot_left_t(probs, grad_rows).astype(low_type)
                prob_grad = dot_right_t(grad_rows, value_rows)
                wide_probs = probs.astype(wide_type)
                weighted = wide_probs * prob_grad
                score_low = (
                    weighted - wide_probs * jnp.sum(weighted, axis=-1, keepdims=True)
                ).astype(low_type)
                query_low = (dot(score_low, key_rows) * scale_factor).astype(low_type)
                key_low = (dot_left_t(score_low, queries) * scale_factor).astype(low_type)
                grads_ref[pair_rows, base : base + HEAD_DIM] = query_low
                grads_ref[pair_rows, base + HEAD_DIM : base + 2 * HEAD_DIM] = key_low
                grads_ref[pair_rows, base + 2 * HEAD_DIM : base + 3 * HEAD_DIM] = value_low

    both_halves(where_ref[1] & 1, sum_ref.shape[0], body)
    share = own_ref.shape[0]
    own_ref[...] = grad_ref[pl.ds(pl.multiple_of(where_ref[1] * share, share), share), :]


def late_grads_kernel(
    where_ref, act_ref, grads_ref, attn_low_ref, attended_ref, keep_ref, sent_ref, bias_ref, wide_ref
):
    columns = grads_ref.shape[1]
    first = attended_ref.shape[1]
    wide_ref[:, :first] = dot_left_t(attn_low_ref[...], attended_ref[...])
    wide_ref[:, first : first + columns] = dot_left_t(act_ref[...], grads_ref[...])
    part_blocks(where_ref[0] & 1, wide_ref, wide_ref.shape[1] // LANES, keep_ref, sent_ref, 0)
    bias_ref[...] = row_sum(grads_ref[...].astype(wide_type))


EXTRA = 16


def put_extra(ref, start, gain, shift):
    rows = []
    for value in (gain, shift):
        rows += list(split_low(value))
    rows.append(jnp.zeros((EXTRA - 4, gain.shape[1]), low_type))
    ref[start : start + EXTRA, :] = jnp.concatenate(rows, axis=0)


def get_extra(ref, start):
    rows = ref[start : start + EXTRA, :].astype(wide_type)
    return rows[0:1] + rows[1:2], rows[2:3] + rows[3:4]


def input_part_kernel(where_ref, rows_ref, grads_ref, weight_ref, keep_ref, sent_ref, part_ref, bias_ref):
    lower_bit = where_ref[1] & 1
    bias_ref[...] = jnp.zeros_like(bias_ref)

    def body(start, size):
        rows = pl.ds(start, size)
        grad = dot(grads_ref[rows, :], weight_ref[...])
        part_ref[rows, :] = grad
        normed, _ = normalized(rows_ref[rows, :].astype(wide_type))
        bias_ref[0:1, :] += row_sum(grad * normed)
        bias_ref[1:2, :] += row_sum(grad)

    over_rows(rows_ref.shape[0], CHUNK, body)
    size = keep_ref.shape[0] - EXTRA
    share = size // (lax.axis_size("mp") // 2)
    for out_ref, which in ((sent_ref, 1 - lower_bit), (keep_ref, lower_bit)):
        for block in range(size // share):
            rows = pl.ds(pl.multiple_of((2 * block + which) * share, share), share)
            out_ref[block * share : (block + 1) * share, :] = part_ref[rows, :].astype(low_type)
        put_extra(out_ref, size, bias_ref[0:1, :], bias_ref[1:2, :])


def input_halve_kernel(bit, where_ref, keep_ref, other_ref, next_keep_ref, next_sent_ref, total_ref):
    upper = (where_ref[1] >> bit) & 1
    half = next_keep_ref.shape[0] - EXTRA
    size = 2 * half
    share = total_ref.shape[0] - size
    total_ref[:size, :] = keep_ref[:size, :].astype(wide_type) + other_ref[:size, :].astype(wide_type)
    own, other = get_extra(keep_ref, size), get_extra(other_ref, size)
    for out_ref, which in ((next_sent_ref, 1 - upper), (next_keep_ref, upper)):
        for block in range(half // share):
            rows = pl.ds(pl.multiple_of((2 * block + which) * share, share), share)
            out_ref[block * share : (block + 1) * share, :] = total_ref[rows, :].astype(low_type)
        put_extra(out_ref, half, own[0] + other[0], own[1] + other[1])


def input_grad_kernel(where_ref, rows_ref, keep_ref, other_ref, own_ref, gain_ref, out_ref):
    share = out_ref.shape[0]
    rows = pl.ds(pl.multiple_of(where_ref[1] * share, share), share)
    normed, spread = normalized(rows_ref[rows, :].astype(wide_type))
    grad = keep_ref[:share, :].astype(wide_type) + other_ref[:share, :].astype(wide_type)
    out_ref[...] = (own_ref[...] + norm_back(grad, normed, spread, wide_row(gain_ref))).astype(low_type)


VECTOR_ROWS = 48


def vector_rows(heads, mask_ref, down_up_ref, second_ref, qkv_ref, proj, gain, shift, rows_ref):
    qkv = qkv_ref[...]
    empty = jnp.zeros((1, 2 * LANES - heads * HEAD_DIM), wide_type)
    spread = []
    for part in (0, 2):
        spread += [
            qkv[:, (3 * head + part) * HEAD_DIM : (3 * head + part + 1) * HEAD_DIM] for head in range(heads)
        ] + [empty]
    row = 0
    for value in (
        jnp.concatenate(spread, axis=1), down_up_ref[1:2, :], proj, mask_ref[...], gain, shift,
        second_ref[0:1, :], second_ref[1:2, :], second_ref[2:3, :], down_up_ref[0:1, :],
    ):
        for tile in range(value.shape[1] // LANES):
            rows_ref[row : row + 1, :] = value[:, tile * LANES : (tile + 1) * LANES]
            row += 1


def encoded_kernel(
    images, heads, pad, where_ref, owner_ref, hidden_ref, sum_ref, sum_other_ref, down_bias_ref, weight_ref,
    bias_ref, enc_ref, mask_ref, down_up_ref, second_ref, qkv_ref, first_ref, first_other_ref,
    send_ref, low_ref, wide_ref, rows_ref,
):
    down_bias, bias = wide_row(down_bias_ref), wide_row(bias_ref)
    base = where_ref[0] * images

    def body(source, rows, part, size):
        total = (sum_ref, sum_other_ref)[source][part, :].astype(wide_type)
        out_low = (hidden_ref[rows, :] + total + down_bias).astype(low_type)
        low_ref[rows, :] = out_low
        encoded = (dot(out_low, weight_ref[...]) + bias).astype(low_type)
        for image in range(size // VIS):
            send_ref[owner_ref[base + rows.start // VIS + image], :VIS, :] = encoded[
                image * VIS : (image + 1) * VIS
            ]

    both_halves(where_ref[1] & 1, sum_ref.shape[0], body)
    wide_ref[...] = dot_left_t(low_ref[...], enc_ref[...])
    count = send_ref.shape[0]
    share = wide_ref.shape[0] // count
    own = get_extra(first_ref, first_ref.shape[0] - EXTRA)
    other = get_extra(first_other_ref, first_ref.shape[0] - EXTRA)
    proj = row_sum(enc_ref[...].astype(wide_type))
    vector_rows(
        heads, mask_ref, down_up_ref, second_ref, qkv_ref, proj, own[0] + other[0], own[1] + other[1], rows_ref
    )
    for block in range(count):
        send_ref[block, VIS : VIS + share, :] = wide_ref[block * share : (block + 1) * share, :].astype(
            low_type
        )
        if pad > share:
            send_ref[block, VIS + share : VIS + pad, :] = jnp.zeros((pad - share, LANES), low_type)
        send_ref[block, VIS + pad :, :] = rows_ref[...].astype(low_type)


def grids_kernel(
    pad, heads, source_ref, patches_ref, visible_ref, arrived_ref, mask_ref, layout_ref, moved_ref, grids_ref,
    weight_grad_ref, pos_grad_ref, *refs
):
    *vector_refs, rows_ref = refs
    count = grids_ref.shape[0]
    share = weight_grad_ref.shape[0]
    cells = lax.broadcasted_iota(jnp.int32, (GRID, VIS), 0)
    cell_column = lax.broadcasted_iota(jnp.int32, (GRID, 1), 0)
    mask_row = wide_row(mask_ref)

    def one_slot(slot):
        source = source_ref[slot]
        seen = visible_ref[pl.ds(source, 1), :] == cells
        size = patches_ref[source]
        fill = (cell_column < size).astype(wide_type) - jnp.sum(
            seen.astype(wide_type), axis=1, keepdims=True
        )
        placed = dot(seen.astype(low_type), arrived_ref[slot, :VIS, :])
        grids_ref[slot] = (placed + fill * mask_row + layout_ref[side_of(size)]).astype(low_type)

    over_slots(count, one_slot)

    def summed(ref, start, size):
        total = ref[0, start : start + size, :].astype(wide_type)
        for block in range(1, count):
            total += ref[block, start : start + size, :].astype(wide_type)
        return total

    weight_grad_ref[...] = summed(arrived_ref, VIS, share)
    pos_grad_ref[...] = summed(moved_ref, 0, pos_grad_ref.shape[0])
    rows_ref[...] = summed(arrived_ref, VIS + pad, VECTOR_ROWS)
    row = 0
    for ref in vector_refs:
        size = ref.shape[0]
        for tile in range(-(-size // LANES)):
            width = min(LANES, size - tile * LANES)
            ref[tile * LANES : tile * LANES + width] = rows_ref[row, :width]
            row += 1


def halve_kernel(bit, where_ref, keep_ref, other_ref, next_keep_ref, next_sent_ref):
    upper = (where_ref[0] >> bit) & 1
    for out_ref, which in ((next_sent_ref, 1 - upper), (next_keep_ref, upper)):
        for block in range(next_keep_ref.shape[0]):
            at = 2 * block + which
            out_ref[block] = (keep_ref[at].astype(wide_type) + other_ref[at].astype(wide_type)).astype(
                low_type
            )


def early_out_kernel(keep_ref, other_ref, up_ref, down_ref):
    tiles = keep_ref.shape[1] // 2
    for tile in range(2 * tiles):
        out_ref = up_ref if tile < tiles else down_ref
        at = (tile % tiles) * LANES
        out_ref[:, at : at + LANES] = keep_ref[0, tile].astype(wide_type) + other_ref[0, tile].astype(
            wide_type
        )


def late_out_kernel(keep_ref, other_ref, out_ref, qkv_ref, wide_ref):
    for tile in range(keep_ref.shape[1]):
        wide_ref[:, tile * LANES : (tile + 1) * LANES] = keep_ref[0, tile].astype(wide_type) + other_ref[
            0, tile
        ].astype(wide_type)
    columns = out_ref.shape[0]
    wide_out = -(-columns // LANES) * LANES
    out_ref[...] = wide_ref[:, :wide_out].T[:columns]
    qkv_ref[...] = wide_ref[:, columns:]


def swap(value, axis, bit):
    count = lax.axis_size(axis)
    return lax.ppermute(value, axis, [(i, i ^ bit) for i in range(count)])


def local(
    patch_rows, patches, visible, owner, qkv_weight, query_bias, value_bias, out_weight, out_bias, first_gain,
    first_shift, second_gain, second_shift, up_weight, up_bias, down_weight, down_bias, proj_weight, proj_bias,
    mask_token, decoder_pos, grid_cotangent,
):
    count = lax.axis_size("dp")
    parts = lax.axis_size("mp")
    where = jnp.stack([lax.axis_index("dp"), lax.axis_index("mp")]).astype(jnp.int32)
    rows, width = patch_rows.shape
    images = rows // VIS
    heads = qkv_weight.shape[1] // (3 * HEAD_DIM)
    head_columns = heads * HEAD_DIM
    qkv_columns = qkv_weight.shape[1]
    units = up_weight.shape[1]
    columns = proj_weight.shape[1]
    share = width // count
    pos_share = GRID // count
    half = rows // 2
    own_rows = rows // parts
    pad = -(-share // 16) * 16
    pos_pad = -(-pos_share // 16) * 16
    run = Order(rows <= PINNED_ROWS)

    tables = grid_tables()
    table_high = tables.astype(low_type)
    table_low = (tables - table_high.astype(np.float32)).astype(low_type)
    turned_high = jnp.asarray(np.ascontiguousarray(table_high.transpose(0, 2, 1)))
    turned_low = jnp.asarray(np.ascontiguousarray(table_low.transpose(0, 2, 1)))
    table_high, table_low = jnp.asarray(table_high), jnp.asarray(table_low)
    qkv_weight_t = qkv_weight.T

    def low(*shape):
        return (shape, low_type)

    def wide(*shape):
        return (shape, wide_type)

    def moved(value, axis, bit):
        return run.keep(swap(value, axis, bit))

    def spread(value):
        return run.keep(lax.all_to_all(value, "dp", split_axis=0, concat_axis=0, tiled=True))

    def model_steps(keep, sent):
        received = moved(sent, "mp", 1)
        yield
        (total,) = run(add_kernel, [low(half, width)], (keep, received))
        bit = 2
        while bit < parts:
            received = moved(total, "mp", bit)
            yield
            (total,) = run(add_kernel, [low(half, width)], (total, received))
            bit *= 2
        return total, moved(total, "mp", 1)

    def data_steps(keep, sent):
        received = moved(sent, "dp", 1)
        yield
        bit = 1
        while keep.shape[0] > 1:
            shape = (keep.shape[0] // 2,) + keep.shape[1:]
            keep, sent = run(
                lambda *refs, bit=bit: halve_kernel(bit, *refs),
                [low(*shape)] * 2,
                (where, keep, received),
                (SMEM, VMEM, VMEM),
            )
            received = moved(sent, "dp", 2**bit)
            yield
            bit += 1
        return keep, received

    def finish(steps):
        while True:
            try:
                next(steps)
            except StopIteration as stop:
                return stop.value

    back_send, source = run(
        lambda *refs: cotangent_kernel(count, images, *refs),
        [low(count, VIS, columns), ((count,), jnp.int32)],
        (where, owner, visible, grid_cotangent),
        (SMEM, SMEM, VMEM, VMEM),
        out_specs=(VMEM, SMEM),
    )
    returned = spread(back_send)
    act_one, qkv = run(
        enter_kernel,
        [low(rows, width), low(rows, qkv_columns)],
        (patch_rows, first_gain, first_shift, qkv_weight_t, query_bias, value_bias),
    )
    grad_keep, grad_sent, enc_grad = run(
        lambda *refs: back_kernel(images, *refs),
        [low(half, width), low(half, width), low(rows, columns)],
        (where, owner, returned, proj_weight),
        (SMEM, SMEM, VMEM, VMEM),
    )
    grad_steps = model_steps(grad_keep, grad_sent)
    next(grad_steps)
    next(grad_steps)
    keep, sent, probs, attended = run(
        lambda *refs: attention_kernel(images, heads, *refs),
        [low(half, width), low(half, width), low(rows, heads * PAIR), low(rows, head_columns)],
        (where, patches, qkv, out_weight),
        (SMEM, SMEM, VMEM, VMEM),
    )
    attn_steps = model_steps(keep, sent)
    next(attn_steps)
    next(attn_steps)
    grad_sum, grad_other = finish(grad_steps)
    pos_send, mask_grad, layouts = run(
        lambda *refs: position_kernel(count, *refs),
        [low(count, pos_pad, columns), wide(1, columns), wide(3, GRID, columns)],
        (source, patches, visible, grid_cotangent, turned_high, turned_low, table_high, table_low, decoder_pos),
        (SMEM, SMEM) + (VMEM,) * 7,
        scratch=[pltpu.VMEM((3, GRID, columns), wide_type)],
    )
    pos_moved = spread(pos_send)
    attn_sum, attn_other = finish(attn_steps)

    keep, sent, hidden, act_two, acted, up_low, down_low, bias_grads = run(
        forward_back_kernel,
        [
            low(half, width), low(half, width), wide(rows, width), low(rows, width), low(rows, units),
            low(rows, units), low(rows, width), wide(2, width),
        ],
        (
            where, patch_rows, attn_sum, attn_other, grad_sum, grad_other, out_bias, second_gain, second_shift,
            up_weight, up_bias, down_weight,
        ),
        (SMEM,) + (VMEM,) * 11,
    )
    second_steps = model_steps(keep, sent)
    next(second_steps)
    next(second_steps)
    early_keep, early_sent = run(
        early_grads_kernel,
        [low(count // 2, 2 * units // LANES, share, LANES)] * 2,
        (where, act_two, up_low, acted, down_low),
        (SMEM,) + (VMEM,) * 4,
        scratch=[pltpu.VMEM((width, units), wide_type)],
    )
    early_steps = data_steps(early_keep, early_sent)
    next(early_steps)
    keep, sent = run(
        forward_part_kernel,
        [low(half, width), low(half, width)],
        (where, acted, down_weight),
        (SMEM, VMEM, VMEM),
    )
    out_steps = model_steps(keep, sent)
    next(out_steps)
    second_sum, second_other = finish(second_steps)
    next(out_steps)
    grads, attn_low, own_grad, second_grads = run(
        lambda *refs: attention_back_kernel(heads, *refs),
        [low(rows, qkv_columns), low(rows, width), wide(own_rows, width), wide(3, width)],
        (where, second_sum, second_other, hidden, down_low, second_gain, out_weight, qkv, probs),
        (SMEM,) + (VMEM,) * 8,
        scratch=[pltpu.VMEM((rows, width), wide_type)],
    )
    late_columns = qkv_columns + head_columns
    late_keep, late_sent, qkv_bias_grad = run(
        late_grads_kernel,
        [low(count // 2, late_columns // LANES, share, LANES)] * 2 + [wide(1, qkv_columns)],
        (where, act_one, grads, attn_low, attended),
        (SMEM,) + (VMEM,) * 4,
        scratch=[pltpu.VMEM((width, late_columns), wide_type)],
    )
    late_steps = data_steps(late_keep, late_sent)
    next(late_steps)
    in_keep, in_sent = run(
        input_part_kernel,
        [low(half + EXTRA, width)] * 2,
        (where, patch_rows, grads, qkv_weight_t),
        (SMEM,) + (VMEM,) * 3,
        scratch=[pltpu.VMEM((rows, width), wide_type), pltpu.VMEM((2, width), wide_type)],
    )
    in_other = moved(in_sent, "mp", 1)
    out_sum, out_other = finish(out_steps)
    bit = 1
    size = half
    while 2**bit < parts:
        in_keep, in_sent = run(
            lambda *refs, bit=bit: input_halve_kernel(bit, *refs),
            [low(size // 2 + EXTRA, width)] * 2,
            (where, in_keep, in_other),
            (SMEM, VMEM, VMEM),
            scratch=[pltpu.VMEM((size + own_rows, width), wide_type)],
        )
        in_other = moved(in_sent, "mp", 2**bit)
        size //= 2
        bit += 1
    (send,) = run(
        lambda *refs: encoded_kernel(images, heads, pad, *refs),
        [low(count, VIS + pad + VECTOR_ROWS, columns)],
        (
            where, owner, hidden, out_sum, out_other, down_bias, proj_weight, proj_bias, enc_grad, mask_grad,
            bias_grads, second_grads, qkv_bias_grad, in_keep, in_other,
        ),
        (SMEM, SMEM) + (VMEM,) * 13,
        scratch=[
            pltpu.VMEM((rows, width), low_type),
            pltpu.VMEM((width, columns), wide_type),
            pltpu.VMEM((VECTOR_ROWS, LANES), wide_type),
        ],
    )
    arrived = spread(send)
    next(early_steps)
    (input_grad,) = run(
        input_grad_kernel,
        [low(own_rows, width)],
        (where, patch_rows, in_keep, in_other, own_grad, first_gain),
        (SMEM,) + (VMEM,) * 5,
        final=True,
    )
    next(late_steps)
    early_keep, early_other = finish(early_steps)
    late_keep, late_other = finish(late_steps)
    vector_sizes = [
        head_columns, head_columns, units, columns, columns, width, width, width, width, width, width
    ]
    (
        grids, proj_weight_grad, pos_grad, query_bias_grad, value_bias_grad, up_bias_grad, proj_bias_grad,
        mask_grad, first_gain_grad, first_shift_grad, second_gain_grad, second_shift_grad, out_bias_grad,
        down_bias_grad,
    ) = run(
        lambda *refs: grids_kernel(pad, heads, *refs),
        [low(count, GRID, columns), wide(share, columns), wide(pos_share, columns)]
        + [wide(size) for size in vector_sizes],
        (source, patches, visible, arrived, mask_token, layouts, pos_moved),
        (SMEM, SMEM) + (VMEM,) * 5,
        scratch=[pltpu.VMEM((VECTOR_ROWS, LANES), wide_type)],
        final=True,
    )
    up_weight_grad, down_weight_grad = run(
        early_out_kernel, [wide(share, units), wide(share, units)], (early_keep, early_other), final=True
    )
    out_weight_grad, qkv_weight_grad = run(
        late_out_kernel,
        [wide(head_columns, share), wide(share, qkv_columns)],
        (late_keep, late_other),
        scratch=[pltpu.VMEM((share, late_columns), wide_type)],
        final=True,
    )
    return (
        grids, input_grad, qkv_weight_grad, query_bias_grad, value_bias_grad, out_weight_grad, out_bias_grad,
        first_gain_grad, first_shift_grad, second_gain_grad, second_shift_grad, up_weight_grad, up_bias_grad,
        down_weight_grad.T, down_bias_grad, proj_weight_grad, proj_bias_grad, mask_grad, pos_grad,
    )


def solution(mesh):
    return jax.shard_map(
        local,
        mesh=mesh,
        in_specs=(
            P("dp", None), P(), P(), P(), P(None, "mp"), P("mp"), P("mp"), P("mp", None), P(), P(), P(), P(), P(),
            P(None, "mp"), P("mp"), P("mp", None), P(), P(None, "mp"), P("mp"), P("mp"), P(None, "mp"),
            P("dp", None, "mp"),
        ),
        out_specs=(
            P("dp", None, "mp"), P(("dp", "mp"), None), P("dp", "mp"), P("mp"), P("mp"), P("mp", "dp"), P(), P(),
            P(), P(), P(), P("dp", "mp"), P("mp"), P("mp", "dp"), P(), P("dp", "mp"), P("mp"), P("mp"),
            P("dp", "mp"),
        ),
        check_vma=False,
    )
```

time: 170 us -> 149 us (0.88)
  Pallas kernels: 60.4 us -> 43.1 us
  blocking collectives: 0 us -> 16.8 us
  other arithmetic: 11.9 us -> 0.08 us
  waiting for transfers between devices: 45 us -> 54.1 us
  starting transfers between devices: 34 us -> 25.3 us
  local copies, waits for them, and re-layouts: 16 us -> 7.46 us
    pallas_call x16 -> x29, Pallas kernels: 60.4 us -> 43.1 us  [__call__(): pl.pallas_call(body, out_shape=tuple(shapes), in_specs=specs, out_specs=t...]
    all_to_all x0 -> x1, blocking collectives: none -> 16.8 us  [spread(): lax.all_to_all(value, 'dp', split_axis=0, concat_axis=0, tiled=True)]
    ppermute x22 -> x20, waiting for transfers between devices: 38.2 us -> 51.8 us  [swap(): return lax.ppermute(value, axis, [(i, i ^ bit) for i in range(count)])]
    convert_element_type x11 -> x0, other arithmetic: 4.93 us -> none  [the longest x10 4.28 us: low_add(): return (left.astype(wide_type) + right.astype(wide_type)).astype(low_type)]
    all_to_all x3 -> x2, starting transfers between devices: 15.5 us -> 10.7 us  [spread(): lax.all_to_all(value, 'dp', split_axis=0, concat_axis=0, tiled=True)]
    slice x4 -> x0, local copies, waits for them, and re-layouts: 4.62 us -> none  [the longest x1 1.42 us: local(): flat[42 * tile:48 * tile]]
    all_to_all x3 -> x2, waiting for transfers between devices: 6.75 us -> 2.3 us  [spread(): lax.all_to_all(value, 'dp', split_axis=0, concat_axis=0, tiled=True)]
    ppermute x22 -> x20, starting transfers between devices: 18.5 us -> 14.5 us  [swap(): return lax.ppermute(value, axis, [(i, i ^ bit) for i in range(count)])]
  transfers between devices with their start and end apart: 25 -> 22, of which waited for: 8 -> 12; matrix products, arithmetic and copies ran while one was open for 12% -> 0% of each run, Pallas kernels for 28% -> 20%
where the time goes in v2:
time: 149 us; the launch traced here: 148 us
  waiting for transfers between devices  54.1 us (36%)
  Pallas kernels  43.1 us (29%)
  starting transfers between devices  25.3 us (17%)
  blocking collectives  16.8 us (11%)
  local copies, waits for them, and re-layouts  7.46 us (5%)
    ppermute x20, waiting for transfers between devices, swap(): return lax.ppermute(value, axis, [(i, i ^ bit) for i in range(count)])  51.8 us
    pallas_call x29, Pallas kernels, __call__(): pl.pallas_call(body, out_shape=tuple(shapes), in_specs=specs, out_specs=t...  43.1 us
    all_to_all x1, blocking collectives, spread(): lax.all_to_all(value, 'dp', split_axis=0, concat_axis=0, tiled=True)  16.8 us
    ppermute x20, starting transfers between devices, swap(): return lax.ppermute(value, axis, [(i, i ^ bit) for i in range(count)])  14.5 us
    all_to_all x2, starting transfers between devices, spread(): lax.all_to_all(value, 'dp', split_axis=0, concat_axis=0, tiled=True)  10.7 us
    unnamed x66, local copies, waits for them, and re-layouts  7.46 us
  transfers between devices with their start and end apart: 22, of which 12 were waited for; matrix products, arithmetic and copies ran while one was open for 0% of the time, Pallas kernels for 20%

profile of v2, /device:TPU:0, one launch (start us, length us, event | category | flops | bytes accessed | tf_op | source)
XLA Modules:
  0.0 147.9 jit_solution(6282517134174943981)
XLA Ops:
  4.8 7.3 %all-to-all-start = ((bf16[8,64,128]{2,1,0:T(8,128)(2,1)}), bf16[8,64,128]{2,1,0:T(8,128)(2,1)S(1)}, u32[]{:S(2)}, u32[]{:S(2)}) async-start(bf16[8,64,128]{2,1,0:T(8,128)(2,1)} %get-tuple-element.83.refs_6_), calls=%async_computation | async-start | bytes 262144 | tf_op jit(solution)/shard_map/all_to_all | solution.py:661
  17.1 2.3 %all-to-all-done.refs_2_ = bf16[8,64,128]{2,1,0:T(8,128)(2,1)S(1)} async-done(((bf16[8,64,128]{2,1,0:T(8,128)(2,1)}), bf16[8,64,128]{2,1,0:T(8,128)(2,1)S(1)}, u32[]{:S(2)}, u32[]{:S(2)}) %all-to-all-start) | async-done | bytes 131104 | tf_op jit(solution)/shard_map/all_to_all | solution.py:661
  20.4 1.7 %collective-permute-done.refs_1_ = bf16[256,768]{1,0:T(8,128)(2,1)S(1)} collective-permute-done((bf16[256,768]{1,0:T(8,128)(2,1)S(1)}, bf16[256,768]{1,0:T(8,128)(2,1)S(1)}, u32[]{:S(2)}, u32[]{:S(2)}) %collective-permute-start) | collective-permute-done | bytes 393248 | tf_op jit(solution)/shard_map/ppermute | solution.py:617
  22.3 5.0 %shard_map.397 = (bf16[256,768]{1,0:T(8,128)(2,1)S(1)}, bf16[256,768]{1,0:T(8,128)(2,1)S(1)}, bf16[512,384]{1,0:T(8,128)(2,1)S(1)}, bf16[512,192]{1,0:T(8,128)(2,1)S(1)}) custom-call(s32[2]{0:T(128)S(1)} %pad_add_fusion.refs_0_, s32[64]{0:T(128)S(1)} %copy-done.23, bf16[512,576]{1,0:T(8,128)(2,1)S(1)} %get-tuple-element.84.refs_2_.refs_7_, ...), custom_call_target="tpu_custom_call" | custom-call | flops 1000 | bytes 1000 | tf_op jit(solution)/shard_map/pallas_call | solution.py:134
  30.8 8.6 %collective-permute-done.3.refs_1_ = bf16[256,768]{1,0:T(8,128)(2,1)S(1)} collective-permute-done((bf16[256,768]{1,0:T(8,128)(2,1)S(1)}, bf16[256,768]{1,0:T(8,128)(2,1)S(1)}, u32[]{:S(2)}, u32[]{:S(2)}) %collective-permute-start.3) | collective-permute-done | bytes 393248 | tf_op jit(solution)/shard_map/ppermute | solution.py:617
  41.2 6.1 %collective-permute-done.2.refs_1_ = bf16[256,768]{1,0:T(8,128)(2,1)S(1)} collective-permute-done((bf16[256,768]{1,0:T(8,128)(2,1)S(1)}, bf16[256,768]{1,0:T(8,128)(2,1)S(1)}, u32[]{:S(2)}, u32[]{:S(2)}) %collective-permute-start.2) | collective-permute-done | bytes 393248 | tf_op jit(solution)/shard_map/ppermute | solution.py:617
  47.5 1.7 %collective-permute-done.4.refs_3_ = bf16[256,768]{1,0:T(8,128)(2,1)S(1)} collective-permute-done((bf16[256,768]{1,0:T(8,128)(2,1)S(1)}, bf16[256,768]{1,0:T(8,128)(2,1)S(1)}, u32[]{:S(2)}, u32[]{:S(2)}) %collective-permute-start.4) | collective-permute-done | bytes 393248 | tf_op jit(solution)/shard_map/ppermute | solution.py:617
  49.2 3.5 %shard_map.402 = (bf16[256,768]{1,0:T(8,128)(2,1)S(1)}, bf16[256,768]{1,0:T(8,128)(2,1)S(1)}, f32[512,768]{1,0:T(8,128)S(1)}, bf16[512,768]{1,0:T(8,128)(2,1)S(1...) custom-call(s32[2]{0:T(128)S(1)} %pad_add_fusion.refs_0_, ...), custom_call_target="tpu_custom_call" | custom-call | flops 1000 | bytes 1000 | tf_op jit(solution)/shard_map/pallas_call | solution.py:134
  56.2 2.5 %shard_map.404 = (bf16[4,12,96,128]{3,2,1,0:T(8,128)(2,1)S(1)}, bf16[4,12,96,128]{3,2,1,0:T(8,128)(2,1)S(1)}) custom-call(s32[2]{0:T(128)S(1)} %pad_add_fusion.refs_0_, bf16[512,768]{1,0:T(8,128)(2,1)S(1)} %get-tuple-element.93.refs_1_, bf16[512,768]{1,0:T(8,128)(2,1)S(1)} %get-tuple-element.94.refs_2_, ...), custom_call_target="tpu_custom_call" | custom-call | flops 1000 | bytes 1000 | tf_op jit(solution)/shard_map/pallas_call | solution.py:134
  60.4 5.4 %collective-permute-done.8.refs_1_ = bf16[256,768]{1,0:T(8,128)(2,1)S(1)} collective-permute-done((bf16[256,768]{1,0:T(8,128)(2,1)S(1)}, bf16[256,768]{1,0:T(8,128)(2,1)S(1)}, u32[]{:S(2)}, u32[]{:S(2)}) %collective-permute-start.8) | collective-permute-done | bytes 393248 | tf_op jit(solution)/shard_map/ppermute | solution.py:617
  67.8 6.0 %shard_map.408 = (bf16[512,576]{1,0:T(8,128)(2,1)S(1)}, bf16[512,768]{1,0:T(8,128)(2,1)S(1)}, f32[128,768]{1,0:T(8,128)S(1)}, f32[3,768]{1,0:T(4,128)S(1)}) custom-call(s32[2]{0:T(128)S(1)} %pad_add_fusion.refs_0_, bf16[256,768]{1,0:T(8,128)(2,1)S(1)} %shard_map.406.refs_2_.refs_1_, bf16[256,768]{1,0:T(8,128)(2,1)S(1)} %collective-permute-done.10.refs_2_, ...), custom_call_target="tpu_custom_call" | custom-call | flops 1000 | bytes 1000 | tf_op jit(solution)/shard_map/pallas_call | solution.py:134
  73.8 3.0 %shard_map.409 = (bf16[4,6,96,128]{3,2,1,0:T(8,128)(2,1)S(1)}, bf16[4,6,96,128]{3,2,1,0:T(8,128)(2,1)}, f32[1,576]{1,0:T(1,128)S(1)}) custom-call(s32[2]{0:T(128)S(1)} %pad_add_fusion.refs_0_, bf16[512,768]{1,0:T(8,128)(2,1)S(1)} %get-tuple-element.85.refs_4_.refs_1_, bf16[512,576]{1,0:T(8,128)(2,1)S(1)} %get-tuple-element.102.refs_2_.refs_5_, ...), custom_call_target="tpu_custom_call" | custom-call | flops 1000 | bytes 1000 | tf_op jit(solution)/shard_map/pallas_call | solution.py:134
  76.7 1.8 %shard_map.410 = (bf16[272,768]{1,0:T(8,128)(2,1)S(1)}, bf16[272,768]{1,0:T(8,128)(2,1)S(1)}) custom-call(s32[2]{0:T(128)S(1)} %pad_add_fusion.refs_0_, bf16[512,768]{1,0:T(8,128)(2,1)S(1)} %copy-done, bf16[512,576]{1,0:T(8,128)(2,1)S(1)} %get-tuple-element.102.refs_2_.refs_5_, bf16[576,768]{1,0:T(8,128)(2,1)S(1)} %bitcast.5, ...), custom_call_target="tpu_custom_call" | custom-call | flops 1000 | bytes 1000 | tf_op jit(solution)/shard_map/pallas_call | solution.py:134
  82.9 5.8 %collective-permute-done.13.refs_14_.refs_3_ = bf16[144,768]{1,0:T(8,128)(2,1)S(1)} collective-permute-done((bf16[144,768]{1,0:T(8,128)(2,1)S(1)}, bf16[144,768]{1,0:T(8,128)(2,1)S(1)}, u32[]{:S(2)}, u32[]{:S(2)}) %collective-permute-start.13) | collective-permute-done | bytes 221216 | tf_op jit(solution)/shard_map/ppermute | solution.py:617
  88.7 2.0 %shard_map.413.refs_3_ = bf16[8,208,128]{2,1,0:T(8,128)(2,1)} custom-call(s32[2]{0:T(128)S(1)} %pad_add_fusion.refs_0_, s32[64]{0:T(128)S(1)} %copy-done.22, f32[512,768]{1,0:T(8,128)S(1)} %get-tuple-element.91.refs_3_.refs_2_, bf16[256,768]{1,0:T(8,128)(2,1)S(1)} %shard_map.411.refs_3_, bf16[256,768]{1,0:T(8,128)(2,1)S(1)} %collective-permute-done.11.refs_4_, ...), custom_call_target="tpu_custom_call" | custom-call | flops 1000 | bytes 1000 | tf_op jit(solution)/shard_map/pallas_call | solution.py:134
  92.3 16.8 %all_to_all.15.refs_6_ = bf16[8,32,128]{2,1,0:T(8,128)(2,1)S(1)} all-to-all(bf16[8,32,128]{2,1,0:T(8,128)(2,1)S(1)} %get-tuple-element.90.refs_2_), channel_id=1, replica_groups=mesh['dp'=8,'mp'=4] {'dp'}, dimensions={0} | all-to-all | bytes 131072 | tf_op jit(solution)/shard_map/all_to_all | solution.py:661
  109.0 3.5 %all-to-all-start.1 = ((bf16[8,208,128]{2,1,0:T(8,128)(2,1)}), bf16[8,208,128]{2,1,0:T(8,128)(2,1)S(1)}, u32[]{:S(2)}, u32[]{:S(2)}) async-start(bf16[8,208,128]{2,1,0:T(8,128)(2,1)} %shard_map.413.refs_3_), calls=%async_computation.1 | async-start | bytes 851968 | tf_op jit(solution)/shard_map/all_to_all | solution.py:661
  113.8 2.0 %collective-permute-start.16 = (bf16[2,6,96,128]{3,2,1,0:T(8,128)(2,1)S(1)}, bf16[2,6,96,128]{3,2,1,0:T(8,128)(2,1)S(1)}, u32[]{:S(2)}, u32[]{:S(2)}) collective-permute-start(bf16[2,6,96,128]{3,2,1,0:T(8,128)(2,1)S(1)} %get-tuple-element.120), channel_id=1, source_target_pairs={{0,8},{4,12},{8,0},{12,4},{16,24},{20,28},{24,16},{28,20},{1,9},{5... | collective-permute-start | bytes 884744 | tf_op jit(solution)/shard_map/ppermute | solution.py:617
  115.7 1.9 %shard_map.416 = (bf16[1,12,96,128]{3,2,1,0:T(8,128)(2,1)S(1)}, bf16[1,12,96,128]{3,2,1,0:T(8,128)(2,1)}) custom-call(s32[2]{0:T(128)S(1)} %pad_add_fusion.refs_0_, bf16[2,12,96,128]{3,2,1,0:T(8,128)(2,1)S(1)} %get-tuple-element.118.refs_3_.refs_1_.refs_6_, bf16[2,12,96,128]{3,2,1,0:T(8,128)(2,1)} %collective-permute-done.17.refs_2_, ...), custom_call_target="tpu_custom_call" | custom-call | flops 1000 | bytes 1000 | tf_op jit(solution)/shard_map/pallas_call | solution.py:134
  117.6 2.4 %collective-permute-start.19 = (bf16[1,12,96,128]{3,2,1,0:T(8,128)(2,1)}, bf16[1,12,96,128]{3,2,1,0:T(8,128)(2,1)}, u32[]{:S(2)}, u32[]{:S(2)}) collective-permute-start(bf16[1,12,96,128]{3,2,1,0:T(8,128)(2,1)} %get-tuple-element.136), channel_id=1, source_target_pairs={{0,16},{4,20},{8,24},{12,28},{16,0},{20,4},{24,8},{28,12},{1,17},{... | collective-permute-start | bytes 884744 | tf_op jit(solution)/shard_map/ppermute | solution.py:617
  120.0 11.5 %collective-permute-done.16.refs_2_ = bf16[2,6,96,128]{3,2,1,0:T(8,128)(2,1)S(1)} collective-permute-done((bf16[2,6,96,128]{3,2,1,0:T(8,128)(2,1)S(1)}, bf16[2,6,96,128]{3,2,1,0:T(8,128)(2,1)S(1)}, u32[]{:S(2)}, u32[]{:S(2)}) %collective-permute-start.16) | collective-permute-done | bytes 294944 | tf_op jit(solution)/shard_map/ppermute | solution.py:617
  134.1 8.3 %collective-permute-done.18.refs_1_ = bf16[1,6,96,128]{3,2,1,0:T(8,128)(2,1)S(1)} collective-permute-done((bf16[1,6,96,128]{3,2,1,0:T(8,128)(2,1)S(1)}, bf16[1,6,96,128]{3,2,1,0:T(8,128)(2,1)S(1)}, u32[]{:S(2)}, u32[]{:S(2)}) %collective-permute-start.18) | collective-permute-done | bytes 147488 | tf_op jit(solution)/shard_map/ppermute | solution.py:617
  144.2 1.8 %shard_map.418 = (bf16[8,256,128]{2,1,0:T(8,128)(2,1)}, f32[96,128]{1,0:T(8,128)}, f32[32,128]{1,0:T(8,128)}, f32[192]{0:T(256)}, f32[192]{0:T(256)}, /*index=5*...) custom-call(s32[8]{0:T(128)S(1)} %get-tuple-element.82.refs_0_, ...), custom_call_target="tpu_custom_call" | custom-call | flops 1000 | bytes 1000 | tf_op jit(solution)/shard_map/pallas_call | solution.py:134
  146.1 1.8 %shard_map.421 = (f32[96,768]{1,0:T(8,128)}, f32[96,768]{1,0:T(8,128)}) custom-call(bf16[1,12,96,128]{3,2,1,0:T(8,128)(2,1)S(1)} %get-tuple-element.122.refs_3_.refs_0_, bf16[1,12,96,128]{3,2,1,0:T(8,128)(2,1)} %collective-permute-done.19.refs_1_, bf16[1,6,96,128]{3,2,1,0:T(8,128)(2,1)S(1)} %get-tuple-element.123.refs_7_.refs_0_.refs_2_), custom_call_target="tpu_custom_call" | custom-call | flops 1000 | bytes 1000 | tf_op jit(solution)/shard_map/pallas_call | solution.py:134
  (117 shorter events, 34.2 us)
Async XLA Ops:
  3.3 16.2 %copy-start.22 = (s32[64]{0:T(128)S(1)}, s32[64]{0:T(128)}, u32[]{:S(2)}) copy-start(s32[64]{0:T(128)} %refs_1_.17) | copy-start | bytes 772
  4.8 14.6 %all-to-all-start = ((bf16[8,64,128]{2,1,0:T(8,128)(2,1)}), bf16[8,64,128]{2,1,0:T(8,128)(2,1)S(1)}, u32[]{:S(2)}, u32[]{:S(2)}) async-start(bf16[8,64,128]{2,1,0:T(8,128)(2,1)} %get-tuple-element.83.refs_6_), calls=%async_computation | async-start | bytes 262144 | tf_op jit(solution)/shard_map/all_to_all | solution.py:661
  20.4 1.8 %collective-permute-start = (bf16[256,768]{1,0:T(8,128)(2,1)S(1)}, bf16[256,768]{1,0:T(8,128)(2,1)S(1)}, u32[]{:S(2)}, u32[]{:S(2)}) collective-permute-start(bf16[256,768]{1,0:T(8,128)(2,1)S(1)} %get-tuple-element.87), channel_id=1, source_target_pairs={{0,1},{1,0},{2,3},{3,2},{4,5},{5,4},{6,7},{7,6},{8,9},{9,8},{10,11... | collective-permute-start | bytes 1179656 | tf_op jit(solution)/shard_map/ppermute | solution.py:617
  27.3 1.8 %collective-permute-start.1 = (bf16[256,768]{1,0:T(8,128)(2,1)S(1)}, bf16[256,768]{1,0:T(8,128)(2,1)S(1)}, u32[]{:S(2)}, u32[]{:S(2)}) collective-permute-start(bf16[256,768]{1,0:T(8,128)(2,1)S(1)} %get-tuple-element.89), channel_id=1, source_target_pairs={{0,1},{1,0},{2,3},{3,2},{4,5},{5,4},{6,7},{7,6},{8,9},{9,8},{10,11... | collective-permute-start | bytes 1179656 | tf_op jit(solution)/shard_map/ppermute | solution.py:617
  27.5 11.9 %collective-permute-start.3 = (bf16[256,768]{1,0:T(8,128)(2,1)S(1)}, bf16[256,768]{1,0:T(8,128)(2,1)S(1)}, u32[]{:S(2)}, u32[]{:S(2)}) collective-permute-start(bf16[256,768]{1,0:T(8,128)(2,1)S(1)} %shard_map.396.refs_4_.refs_0_), channel_id=1, source_target_pairs={{0,2},{1,3},{2,0},{3,1},{4,6},{5,7},{6,4},{7,5},{8,10},{9,11},{10,... | collective-permute-start | bytes 1179656 | tf_op jit(solution)/shard_map/ppermute | solution.py:617
  29.2 18.1 %collective-permute-start.2 = (bf16[256,768]{1,0:T(8,128)(2,1)S(1)}, bf16[256,768]{1,0:T(8,128)(2,1)S(1)}, u32[]{:S(2)}, u32[]{:S(2)}) collective-permute-start(bf16[256,768]{1,0:T(8,128)(2,1)S(1)} %shard_map.398.refs_2_.refs_0_), channel_id=1, source_target_pairs={{0,2},{1,3},{2,0},{3,1},{4,6},{5,7},{6,4},{7,5},{8,10},{9,11},{10,... | collective-permute-start | bytes 1179656 | tf_op jit(solution)/shard_map/ppermute | solution.py:617
  39.5 8.0 %collective-permute-start.5 = (bf16[256,768]{1,0:T(8,128)(2,1)S(1)}, bf16[256,768]{1,0:T(8,128)(2,1)S(1)}, u32[]{:S(2)}, u32[]{:S(2)}) collective-permute-start(bf16[256,768]{1,0:T(8,128)(2,1)S(1)} %shard_map.399.refs_9_.refs_4_), channel_id=1, source_target_pairs={{0,1},{1,0},{2,3},{3,2},{4,5},{5,4},{6,7},{7,6},{8,9},{9,8},{10,11... | collective-permute-start | bytes 1179656 | tf_op jit(solution)/shard_map/ppermute | solution.py:617
  47.4 1.8 %collective-permute-start.4 = (bf16[256,768]{1,0:T(8,128)(2,1)S(1)}, bf16[256,768]{1,0:T(8,128)(2,1)S(1)}, u32[]{:S(2)}, u32[]{:S(2)}) collective-permute-start(bf16[256,768]{1,0:T(8,128)(2,1)S(1)} %shard_map.401.refs_2_.refs_12_), channel_id=1, source_target_pairs={{0,1},{1,0},{2,3},{3,2},{4,5},{5,4},{6,7},{7,6},{8,9},{9,8},{10,11... | collective-permute-start | bytes 1179656 | tf_op jit(solution)/shard_map/ppermute | solution.py:617
  52.7 1.8 %collective-permute-start.6 = (bf16[256,768]{1,0:T(8,128)(2,1)S(1)}, bf16[256,768]{1,0:T(8,128)(2,1)S(1)}, u32[]{:S(2)}, u32[]{:S(2)}) collective-permute-start(bf16[256,768]{1,0:T(8,128)(2,1)S(1)} %get-tuple-element.97), channel_id=1, source_target_pairs={{0,1},{1,0},{2,3},{3,2},{4,5},{5,4},{6,7},{7,6},{8,9},{9,8},{10,11... | collective-permute-start | bytes 1179656 | tf_op jit(solution)/shard_map/ppermute | solution.py:617
  54.6 11.2 %collective-permute-start.8 = (bf16[256,768]{1,0:T(8,128)(2,1)S(1)}, bf16[256,768]{1,0:T(8,128)(2,1)S(1)}, u32[]{:S(2)}, u32[]{:S(2)}) collective-permute-start(bf16[256,768]{1,0:T(8,128)(2,1)S(1)} %shard_map.403.refs_5_.refs_0_), channel_id=1, source_target_pairs={{0,2},{1,3},{2,0},{3,1},{4,6},{5,7},{6,4},{7,5},{8,10},{9,11},{10,... | collective-permute-start | bytes 1179656 | tf_op jit(solution)/shard_map/ppermute | solution.py:617
  60.1 6.0 %collective-permute-start.7 = (bf16[256,768]{1,0:T(8,128)(2,1)S(1)}, bf16[256,768]{1,0:T(8,128)(2,1)S(1)}, u32[]{:S(2)}, u32[]{:S(2)}) collective-permute-start(bf16[256,768]{1,0:T(8,128)(2,1)S(1)} %get-tuple-element.100), channel_id=1, source_target_pairs={{0,1},{1,0},{2,3},{3,2},{4,5},{5,4},{6,7},{7,6},{8,9},{9,8},{10,11... | collective-permute-start | bytes 1179656 | tf_op jit(solution)/shard_map/ppermute | solution.py:617
  60.1 30.6 %collective-permute-start.15 = (bf16[4,12,96,128]{3,2,1,0:T(8,128)(2,1)S(1)}, bf16[4,12,96,128]{3,2,1,0:T(8,128)(2,1)S(1)}, u32[]{:S(2)}, u32[]{:S(2)}) collective-permute-start(bf16[4,12,96,128]{3,2,1,0:T(8,128)(2,1)S(1)} %get-tuple-element.117), channel_id=1, source_target_pairs={{0,4},{4,0},{8,12},{12,8},{16,20},{20,16},{24,28},{28,24},{1,5},{5... | collective-permute-start | bytes 3538952 | tf_op jit(solution)/shard_map/ppermute | solution.py:617
  66.0 1.8 %collective-permute-start.10 = (bf16[256,768]{1,0:T(8,128)(2,1)S(1)}, bf16[256,768]{1,0:T(8,128)(2,1)S(1)}, u32[]{:S(2)}, u32[]{:S(2)}) collective-permute-start(bf16[256,768]{1,0:T(8,128)(2,1)S(1)} %shard_map.406.refs_2_.refs_1_), channel_id=1, source_target_pairs={{0,1},{1,0},{2,3},{3,2},{4,5},{5,4},{6,7},{7,6},{8,9},{9,8},{10,11... | collective-permute-start | bytes 1179656 | tf_op jit(solution)/shard_map/ppermute | solution.py:617
  66.2 12.7 %collective-permute-start.9 = (bf16[256,768]{1,0:T(8,128)(2,1)S(1)}, bf16[256,768]{1,0:T(8,128)(2,1)S(1)}, u32[]{:S(2)}, u32[]{:S(2)}) collective-permute-start(bf16[256,768]{1,0:T(8,128)(2,1)S(1)} %shard_map.407.refs_9_.refs_0_), channel_id=1, source_target_pairs={{0,2},{1,3},{2,0},{3,1},{4,6},{5,7},{6,4},{7,5},{8,10},{9,11},{10,... | collective-permute-start | bytes 1179656 | tf_op jit(solution)/shard_map/ppermute | solution.py:617
  78.6 1.8 %collective-permute-start.12 = (bf16[272,768]{1,0:T(8,128)(2,1)S(1)}, bf16[272,768]{1,0:T(8,128)(2,1)S(1)}, u32[]{:S(2)}, u32[]{:S(2)}) collective-permute-start(bf16[272,768]{1,0:T(8,128)(2,1)S(1)} %get-tuple-element.112), channel_id=1, source_target_pairs={{0,1},{1,0},{2,3},{3,2},{4,5},{5,4},{6,7},{7,6},{8,9},{9,8},{10,11... | collective-permute-start | bytes 1253384 | tf_op jit(solution)/shard_map/ppermute | solution.py:617
  78.9 4.0 %collective-permute-start.11 = (bf16[256,768]{1,0:T(8,128)(2,1)S(1)}, bf16[256,768]{1,0:T(8,128)(2,1)S(1)}, u32[]{:S(2)}, u32[]{:S(2)}) collective-permute-start(bf16[256,768]{1,0:T(8,128)(2,1)S(1)} %shard_map.411.refs_3_), channel_id=1, source_target_pairs={{0,1},{1,0},{2,3},{3,2},{4,5},{5,4},{6,7},{7,6},{8,9},{9,8},{10,11... | collective-permute-start | bytes 1179656 | tf_op jit(solution)/shard_map/ppermute | solution.py:617
  81.1 7.6 %collective-permute-start.13 = (bf16[144,768]{1,0:T(8,128)(2,1)S(1)}, bf16[144,768]{1,0:T(8,128)(2,1)S(1)}, u32[]{:S(2)}, u32[]{:S(2)}) collective-permute-start(bf16[144,768]{1,0:T(8,128)(2,1)S(1)} %get-tuple-element.114), channel_id=1, source_target_pairs={{0,2},{1,3},{2,0},{3,1},{4,6},{5,7},{6,4},{7,5},{8,10},{9,11},{10,... | collective-permute-start | bytes 663560 | tf_op jit(solution)/shard_map/ppermute | solution.py:617
  82.7 29.8 %collective-permute-start.14 = (bf16[4,6,96,128]{3,2,1,0:T(8,128)(2,1)}, bf16[4,6,96,128]{3,2,1,0:T(8,128)(2,1)}, u32[]{:S(2)}, u32[]{:S(2)}) collective-permute-start(bf16[4,6,96,128]{3,2,1,0:T(8,128)(2,1)} %get-tuple-element.116), channel_id=1, source_target_pairs={{0,4},{4,0},{8,12},{12,8},{16,20},{20,16},{24,28},{28,24},{1,5},{5... | collective-permute-start | bytes 1769480 | tf_op jit(solution)/shard_map/ppermute | solution.py:617
  92.3 23.4 %collective-permute-start.17 = (bf16[2,12,96,128]{3,2,1,0:T(8,128)(2,1)}, bf16[2,12,96,128]{3,2,1,0:T(8,128)(2,1)}, u32[]{:S(2)}, u32[]{:S(2)}) collective-permute-start(bf16[2,12,96,128]{3,2,1,0:T(8,128)(2,1)} %get-tuple-element.121), channel_id=1, source_target_pairs={{0,8},{4,12},{8,0},{12,4},{16,24},{20,28},{24,16},{28,20},{1,9},{5... | collective-permute-start | bytes 1769480 | tf_op jit(solution)/shard_map/ppermute | solution.py:617
  109.0 34.2 %all-to-all-start.1 = ((bf16[8,208,128]{2,1,0:T(8,128)(2,1)}), bf16[8,208,128]{2,1,0:T(8,128)(2,1)S(1)}, u32[]{:S(2)}, u32[]{:S(2)}) async-start(bf16[8,208,128]{2,1,0:T(8,128)(2,1)} %shard_map.413.refs_3_), calls=%async_computation.1 | async-start | bytes 851968 | tf_op jit(solution)/shard_map/all_to_all | solution.py:661
  113.8 17.8 %collective-permute-start.16 = (bf16[2,6,96,128]{3,2,1,0:T(8,128)(2,1)S(1)}, bf16[2,6,96,128]{3,2,1,0:T(8,128)(2,1)S(1)}, u32[]{:S(2)}, u32[]{:S(2)}) collective-permute-start(bf16[2,6,96,128]{3,2,1,0:T(8,128)(2,1)S(1)} %get-tuple-element.120), channel_id=1, source_target_pairs={{0,8},{4,12},{8,0},{12,4},{16,24},{20,28},{24,16},{28,20},{1,9},{5... | collective-permute-start | bytes 884744 | tf_op jit(solution)/shard_map/ppermute | solution.py:617
  115.7 16.8 %copy-start.20 = (bf16[768]{0:T(1024)(128)(2,1)S(1)}, bf16[768]{0:T(1024)(128)(2,1)}, u32[]{:S(2)}) copy-start(bf16[768]{0:T(1024)(128)(2,1)} %refs_5_.8) | copy-start | bytes 4612
  117.6 28.4 %collective-permute-start.19 = (bf16[1,12,96,128]{3,2,1,0:T(8,128)(2,1)}, bf16[1,12,96,128]{3,2,1,0:T(8,128)(2,1)}, u32[]{:S(2)}, u32[]{:S(2)}) collective-permute-start(bf16[1,12,96,128]{3,2,1,0:T(8,128)(2,1)} %get-tuple-element.136), channel_id=1, source_target_pairs={{0,16},{4,20},{8,24},{12,28},{16,0},{20,4},{24,8},{28,12},{1,17},{... | collective-permute-start | bytes 884744 | tf_op jit(solution)/shard_map/ppermute | solution.py:617
  132.1 10.2 %collective-permute-start.18 = (bf16[1,6,96,128]{3,2,1,0:T(8,128)(2,1)S(1)}, bf16[1,6,96,128]{3,2,1,0:T(8,128)(2,1)S(1)}, u32[]{:S(2)}, u32[]{:S(2)}) collective-permute-start(bf16[1,6,96,128]{3,2,1,0:T(8,128)(2,1)S(1)} %get-tuple-element.126), channel_id=1, source_target_pairs={{0,16},{4,20},{8,24},{12,28},{16,0},{20,4},{24,8},{28,12},{1,17},{... | collective-permute-start | bytes 442376 | tf_op jit(solution)/shard_map/ppermute | solution.py:617
  (31 other events, 197.8 us)

commit v3 on v2

v3 whole, which is shorter than its diff:
```python
import math

import jax
import jax.numpy as jnp
import numpy as np
from jax import lax
from jax.experimental import pallas as pl
from jax.experimental.pallas import tpu as pltpu
from jax.sharding import PartitionSpec as P

HEAD_DIM = 64
GRID = 256
VIS = 64
PAIR = 2 * VIS
CHUNK = 512
LANES = 128

epsilon = 1e-06
low_type = jnp.bfloat16
wide_type = jnp.float32
scale_factor = HEAD_DIM ** (-0.5)

VMEM = pl.BlockSpec(memory_space=pltpu.VMEM)
SMEM = pl.BlockSpec(memory_space=pltpu.SMEM)
ANY = pl.BlockSpec(memory_space=pl.ANY)
PINNED_ROWS = 512


def grid_tables():
    grid_edge = math.isqrt(GRID)
    tables = []
    for side_cells in (10, 14):
        places = np.arange(side_cells)
        centers = ((2 * places + 1) * grid_edge - side_cells) / (2 * side_cells)
        lower = np.floor(centers).astype(np.int64)
        share = centers - lower
        lerp = np.zeros((side_cells, grid_edge))
        lerp[places, np.clip(lower, 0, grid_edge - 1)] += 1.0 - share
        lerp[places, np.clip(lower + 1, 0, grid_edge - 1)] += share
        table = np.zeros((GRID, GRID))
        table[: side_cells * side_cells] = np.kron(lerp, lerp)
        tables.append(table)
    return np.stack(tables).astype(np.float32)


def split_low(value):
    high = value.astype(low_type)
    return high, (value - high.astype(wide_type)).astype(low_type)


def dot(left, right):
    return lax.dot_general(left, right, (((1,), (0,)), ((), ())), preferred_element_type=wide_type)


def dot_right_t(left, right):
    return lax.dot_general(left, right, (((1,), (1,)), ((), ())), preferred_element_type=wide_type)


def dot_left_t(left, right):
    return lax.dot_general(left, right, (((0,), (0,)), ((), ())), preferred_element_type=wide_type)


def normalized(value):
    center = value - jnp.mean(value, axis=-1, keepdims=True)
    spread = lax.rsqrt(jnp.mean(center * center, axis=-1, keepdims=True) + epsilon)
    return center * spread, spread


def norm_back(grad, normed, spread, gain):
    scaled = grad * gain
    mean_one = jnp.mean(scaled, axis=-1, keepdims=True)
    mean_two = jnp.mean(scaled * normed, axis=-1, keepdims=True)
    return spread * (scaled - mean_one - normed * mean_two)


def row_sum(value):
    return jnp.sum(value, axis=0, keepdims=True)


def over_rows(total, size, body):
    size = min(size, total)
    if total <= 2 * size:
        for start in range(0, total, size):
            body(start, size)
        return

    def step(i, carry):
        body(pl.multiple_of(i * size, size), size)
        return carry

    lax.fori_loop(0, total // size, step, 0)


def size_of(shape, kind):
    return math.prod(shape) * jnp.dtype(kind).itemsize


RATE = 10**9
COST_SHARE = 20.0


class Order:
    def __init__(self, pinned):
        self.pinned = pinned
        self.last = None
        self.near = []
        self.far = []

    def keep(self, value):
        if self.pinned:
            self.near.append((value, pltpu.VMEM))
        return value

    def leave(self, *values):
        self.far += values

    def placed(self, value):
        for near, space in self.near:
            if value is near:
                return pltpu.with_memory_space_constraint(value, space)
        if any(value is far for far in self.far):
            return pltpu.with_memory_space_constraint(value, pltpu.HBM)
        return value

    def __call__(
        self, kernel, outs, args, specs=None, scratch=(), out_specs=None, final=False, stage=(), cost=1.0
    ):
        args = tuple(args)
        specs = [VMEM] * len(args) if specs is None else list(specs)
        out_specs = [VMEM] * len(outs) if out_specs is None else list(out_specs)
        count, results_count = len(args), len(outs)
        staged = list(stage) if self.pinned else []
        self.leave(*staged)
        needed = sum(size_of(ref.shape, ref.dtype) for ref in scratch)
        needed += sum(
            size_of(arg.shape, arg.dtype) for arg in args if not any(arg is near for near, _ in self.near)
        )
        shapes = []
        for (shape, kind), spec in zip(outs, out_specs):
            if self.pinned and not final:
                shapes.append((pltpu.SMEM if spec is SMEM else pltpu.VMEM)(shape, kind))
            else:
                shapes.append(jax.ShapeDtypeStruct(shape, kind))
                needed += size_of(shape, kind)
        tail = len(staged)
        args += tuple(staged)
        specs += [ANY] * tail
        skipped = 0
        if self.last is not None:
            args += (self.last,)
            specs.append(ANY)
            skipped = 1

        def body(*refs):
            own, sources, refs = refs[:count], refs[count : count + tail], refs[count + tail + skipped :]
            results, targets, refs = (
                refs[:results_count], refs[results_count : results_count + tail], refs[results_count + tail :]
            )
            copies = []
            if tail:
                *refs, sems = refs
                copies = [
                    pltpu.make_async_copy(source, target, sems.at[at])
                    for at, (source, target) in enumerate(zip(sources, targets))
                ]
            for copy in copies:
                copy.start()
            kernel(*own, *results, *refs)
            for copy in copies:
                copy.wait()

        results = pl.pallas_call(
            body,
            out_shape=tuple(shapes) + tuple(pltpu.VMEM(array.shape, array.dtype) for array in staged),
            in_specs=specs,
            out_specs=tuple(out_specs) + (VMEM,) * tail,
            scratch_shapes=list(scratch) + ([pltpu.SemaphoreType.DMA((tail,))] if tail else []),
            compiler_params=pltpu.CompilerParams(
                vmem_limit_bytes=min(needed + needed // 4 + 10 * 2**20, 60 * 2**20)
            ),
            cost_estimate=pl.CostEstimate(
                flops=int(cost * RATE * COST_SHARE), bytes_accessed=0, transcendentals=0
            ),
        )(*(self.placed(arg) for arg in args))
        if self.pinned and not final:
            for result, spec in zip(results, out_specs + [VMEM] * tail):
                self.near.append((result, pltpu.SMEM if spec is SMEM else pltpu.VMEM))
        if not final:
            self.last = results[0]
        if stage and not self.pinned:
            return (*results, *stage)
        return results


class Info:
    def __init__(self, count):
        self.count = count
        self.size = 2 + 5 * count

    def dp(self, ref):
        return ref[0]

    def mp(self, ref):
        return ref[1]

    def owner(self, ref, image):
        return ref[2 + image]

    def live(self, ref, image):
        return ref[2 + self.count + image]

    def source(self, ref, slot):
        return ref[2 + 2 * self.count + slot]

    def cells(self, ref, slot):
        return ref[2 + 3 * self.count + slot]

    def image(self, ref, owner):
        return ref[2 + 4 * self.count + owner]


def fill_info(count, where_ref, owner_ref, patches_ref, info_ref):
    me = where_ref[0]
    info_ref[0] = me
    info_ref[1] = where_ref[1]

    def one(at):
        own = me * count + at
        info_ref[2 + at] = owner_ref[own]
        info_ref[2 + 4 * count + owner_ref[own]] = at
        info_ref[2 + count + at] = patches_ref[own] // 4

        def find(i, found):
            return jnp.where(owner_ref[at * count + i] == me, at * count + i, found)

        source = lax.fori_loop(0, count, find, at * count, unroll=count <= 8)
        info_ref[2 + 2 * count + at] = source
        info_ref[2 + 3 * count + at] = patches_ref[source]

    over_slots(count, one)


def over_slots(count, one_slot):
    if count <= 8:
        for slot in range(count):
            one_slot(slot)
    else:
        lax.fori_loop(0, count, lambda slot, carry: (one_slot(slot), carry)[1], 0)


def side_of(size):
    return (size >= 196).astype(jnp.int32) + (size >= 256).astype(jnp.int32)


def block_at(rest, place, bit):
    low = rest & ((1 << place) - 1)
    return ((rest - low) << 1) + (bit << place) + low


class Exchange:
    def __init__(self, count, bits, block, moved=0, shared=0):
        self.count, self.bits, self.block, self.moved, self.shared = count, bits, block, moved, shared

    def blocks(self, step):
        return self.count >> (step + 1)

    def place(self, step):
        bit = self.bits[step]
        return bit - sum(done < bit for done in self.bits[:step])

    def moved_at(self, step):
        return self.blocks(step) * self.block

    def shared_at(self, step):
        return self.moved_at(step) + self.count // 2 * self.moved

    def rows(self, step):
        return self.shared_at(step) + self.shared

    def own_bit(self, step, info_ref):
        return (info_ref[0] >> self.bits[step]) & 1

    def targets(self, step, info_ref, keep_ref, sent_ref):
        own = self.own_bit(step, info_ref)
        place = self.place(step)
        for ref, which in ((sent_ref, 1 - own), (keep_ref, own)):
            yield ref, [block_at(block, place, which) for block in range(self.blocks(step))]

    def kernel(self, step, parts, info_ref, *refs):
        *from_refs, next_keep_ref, next_sent_ref = refs
        pairs = list(zip(parts, from_refs[::2], from_refs[1::2]))
        sources = 1 << (step - 1)
        rests = self.blocks(step - 1)
        for ref, indices in self.targets(step, info_ref, next_keep_ref, next_sent_ref):
            first, moved_at, shared_at = 0, self.moved_at(step), self.shared_at(step)
            for part, keep_ref, other_ref in pairs:
                for block, index in enumerate(indices if part.block else ()):
                    rows = pl.ds(pl.multiple_of(index * part.block, 16), part.block)
                    at = block * self.block + first
                    ref[at : at + part.block, :] = (
                        keep_ref[rows, :].astype(wide_type) + other_ref[rows, :].astype(wide_type)
                    ).astype(low_type)
                first += part.block
                for from_ref in (keep_ref, other_ref) if part.moved else ():
                    for source in range(sources):
                        for index in indices:
                            rows = part.moved_at(step - 1) + (source * rests + index) * part.moved
                            ref[moved_at : moved_at + part.moved, :] = from_ref[
                                pl.ds(pl.multiple_of(rows, 16), part.moved), :
                            ]
                            moved_at += part.moved
                if part.shared:
                    at = part.shared_at(step - 1)
                    rows = slice(at, at + part.shared)
                    ref[shared_at : shared_at + part.shared, :] = (
                        keep_ref[rows, :].astype(wide_type) + other_ref[rows, :].astype(wide_type)
                    ).astype(low_type)

    def arrived(self, keep_ref, other_ref):
        last = len(self.bits) - 1
        sources = 1 << last
        for half, ref in enumerate((keep_ref, other_ref)):
            for source in range(sources):
                relative = 0
                for step, bit in enumerate(self.bits):
                    relative |= (((source + half * sources) >> step) & 1) << bit
                yield relative, ref, self.moved_at(last) + source * self.moved

    def total(self, keep_ref, other_ref, start, size):
        rows = slice(start, start + size)
        return keep_ref[rows, :].astype(wide_type) + other_ref[rows, :].astype(wide_type)

    def shared_total(self, keep_ref, other_ref):
        return self.total(keep_ref, other_ref, self.shared_at(len(self.bits) - 1), self.shared)


def cotangent_kernel(
    info, exchange, where_ref, owner_ref, patches_ref, visible_ref, cot_ref, keep_ref, sent_ref, info_ref, seen_ref,
    turned_ref,
):
    count = info.count
    fill_info(count, where_ref, owner_ref, patches_ref, info_ref)

    def take(slot):
        seen_ref[pl.ds(slot, 1), :] = visible_ref[pl.ds(info.source(info_ref, slot), 1), :]

    over_slots(count, take)
    turned_ref[...] = seen_ref[...].astype(wide_type).T
    cells = lax.broadcasted_iota(jnp.int32, (VIS, GRID), 1).astype(wide_type)
    own = exchange.own_bit(0, info_ref)
    place = exchange.place(0)
    for slot in range(count):
        onehot = (turned_ref[:, slot : slot + 1] == cells).astype(wide_type).astype(low_type)
        rows = dot(onehot, cot_ref[slot]).astype(low_type)
        rest = (slot & ((1 << place) - 1)) | ((slot >> (place + 1)) << place)
        kept = ((slot >> place) & 1) == own

        @pl.when(kept)
        def _(rest=rest, rows=rows):
            keep_ref[rest * VIS : (rest + 1) * VIS, :] = rows

        @pl.when(jnp.logical_not(kept))
        def _(rest=rest, rows=rows):
            sent_ref[rest * VIS : (rest + 1) * VIS, :] = rows


def position_kernel(
    info, info_ref, visible_ref, cot_ref, turned_high_ref, turned_low_ref, table_high_ref, table_low_ref, pos_ref,
    grad_ref, mask_ref, layout_ref, sums_ref,
):
    cells = lax.broadcasted_iota(jnp.int32, (GRID, VIS), 0)
    cell_column = lax.broadcasted_iota(jnp.int32, (GRID, 1), 0)
    sums_ref[...] = jnp.zeros_like(sums_ref)
    mask_ref[...] = jnp.zeros_like(mask_ref)

    def one_slot(slot):
        size = info.cells(info_ref, slot)
        seen = visible_ref[pl.ds(slot, 1), :] == cells
        fill = (cell_column < size).astype(wide_type) - jnp.sum(
            seen.astype(wide_type), axis=1, keepdims=True
        )
        wide = cot_ref[slot].astype(wide_type)
        mask_ref[...] += row_sum(fill * wide)
        sums_ref[side_of(size)] += wide

    over_slots(info.count, one_slot)
    total = sums_ref[2]
    for side in range(2):
        high, low = split_low(sums_ref[side])
        total += (
            dot(turned_high_ref[side], high) + dot(turned_high_ref[side], low) + dot(turned_low_ref[side], high)
        )
    grad_ref[...] = total
    table = pos_ref[...]
    for side in range(2):
        layout_ref[side] = dot(table_high_ref[side], table) + dot(table_low_ref[side], table)
    layout_ref[2] = table.astype(wide_type)


def wide_row(ref):
    return ref[...].astype(wide_type).reshape(1, ref.shape[0])


def enter_kernel(
    rows_ref, gain_ref, shift_ref, weight_ref, query_ref, value_ref, out_ref, proj_ref, weights_ref, act_ref, qkv_ref
):
    weights_ref[: out_ref.shape[0], :] = out_ref[...]
    weights_ref[out_ref.shape[0] :, :] = proj_ref[...].astype(wide_type).T.astype(low_type)
    gain, shift = wide_row(gain_ref), wide_row(shift_ref)
    query, value = wide_row(query_ref), wide_row(value_ref)
    nothing = jnp.zeros((1, HEAD_DIM), wide_type)
    pieces = []
    for start in range(0, query.shape[1], HEAD_DIM):
        pieces += [query[:, start : start + HEAD_DIM], nothing, value[:, start : start + HEAD_DIM]]
    bias = jnp.concatenate(pieces, axis=1)

    def body(start, size):
        rows = pl.ds(start, size)
        normed, _ = normalized(rows_ref[rows, :].astype(wide_type))
        act = (normed * gain + shift).astype(low_type)
        act_ref[rows, :] = act
        qkv_ref[rows, :] = (dot_right_t(act, weight_ref[...]) + bias).astype(low_type)

    over_rows(rows_ref.shape[0], CHUNK, body)


PACKED = 256


def attention_kernel(info, heads, first, info_ref, qkv_ref, packed_ref, prob_ref, attended_ref):
    row_half = lax.broadcasted_iota(jnp.int32, (PAIR, PAIR), 0) // VIS
    lane = lax.broadcasted_iota(jnp.int32, (PAIR, PAIR), 1)
    columns = heads * HEAD_DIM
    full = columns // LANES * LANES
    rest = PACKED * (columns - full) // LANES

    def body(start, size):
        for pair in range(size // PAIR):
            rows = pl.ds(start + pair * PAIR, PAIR)
            from_rows = pl.ds(first + start + pair * PAIR, PAIR)
            image = (first + start + pair * PAIR) // VIS
            limits = [info.live(info_ref, image + i) for i in range(2)]
            last = jnp.where(row_half == 0, limits[0], VIS + limits[1])
            live = jnp.logical_and(lane >= row_half * VIS, lane < last)
            for head in range(heads):
                base = head * 3 * HEAD_DIM
                queries = qkv_ref[from_rows, base : base + HEAD_DIM]
                key_rows = qkv_ref[from_rows, base + HEAD_DIM : base + 2 * HEAD_DIM]
                value_rows = qkv_ref[from_rows, base + 2 * HEAD_DIM : base + 3 * HEAD_DIM]
                scores = jnp.where(live, dot_right_t(queries, key_rows) * scale_factor, -1e30)
                raised = jnp.exp(scores - jnp.max(scores, axis=-1, keepdims=True))
                probs = (raised / jnp.sum(raised, axis=-1, keepdims=True)).astype(low_type)
                prob_ref[rows, head * PAIR : (head + 1) * PAIR] = probs
                attended_ref[rows, head * HEAD_DIM : (head + 1) * HEAD_DIM] = dot(
                    probs, value_rows
                ).astype(low_type)
        at = start // PACKED * (full // LANES * PACKED + rest)
        rows = pl.ds(start, PACKED)
        for tile in range(full // LANES):
            packed_ref[pl.ds(at, PACKED), :] = attended_ref[rows, tile * LANES : (tile + 1) * LANES]
            at += PACKED
        pieces = [
            attended_ref[pl.ds(start + piece * rest, rest), full:].astype(wide_type)
            for piece in range(PACKED // rest)
        ]
        packed_ref[pl.ds(at, rest), :] = jnp.concatenate(pieces, axis=1).astype(low_type)

    over_rows(prob_ref.shape[0], PACKED, body)


def packed_product(packed_ref, weight_ref, start, columns):
    full = columns // LANES * LANES
    width = columns - full
    rest = PACKED * width // LANES
    at = start // PACKED * (full // LANES * PACKED + rest)
    total = None
    for tile in range(full // LANES):
        part = dot(packed_ref[pl.ds(at, PACKED), :], weight_ref[tile * LANES : (tile + 1) * LANES, :])
        total = part if total is None else total + part
        at += PACKED
    rows = packed_ref[pl.ds(at, rest), :].astype(wide_type)
    left = jnp.concatenate(
        [rows[:, piece * width : (piece + 1) * width] for piece in range(PACKED // rest)], axis=0
    ).astype(low_type)
    return total + dot(left, weight_ref[full:columns, :])


def halves(upper, left_ref, weight_ref, keep_ref, sent_ref, product):
    half = keep_ref.shape[0]
    for out_ref, which in ((sent_ref, 1 - upper), (keep_ref, upper)):

        def body(start, size, out_ref=out_ref, which=which):
            rows = pl.ds(pl.multiple_of(which * half + start, size), size)
            out_ref[pl.ds(start, size), :] = product(left_ref[rows, :], weight_ref[...]).astype(
                out_ref.dtype
            )

        over_rows(half, CHUNK, body)


def both_halves(upper, half, body):
    for source, which in enumerate((upper, 1 - upper)):

        def one(start, size, source=source, which=which):
            body(source, pl.ds(pl.multiple_of(which * half + start, size), size), pl.ds(start, size), size)

        over_rows(half, 256, one)


def back_kernel(info, exchange, info_ref, back_ref, back_other_ref, enc_ref):
    for relative, ref, start in exchange.arrived(back_ref, back_other_ref):
        image = info.image(info_ref, info_ref[0] ^ relative)
        enc_ref[pl.ds(pl.multiple_of(image * VIS, VIS), VIS), :] = ref[start : start + VIS, :]


def paired_sum(sums):
    while len(sums) > 1:
        sums = [left + right for left, right in zip(sums[::2], sums[1::2])]
    return sums[0]


def add_kernel(left_ref, right_ref, out_ref):
    out_ref[...] = (left_ref[...].astype(wide_type) + right_ref[...].astype(wide_type)).astype(low_type)


def forward_kernel(
    parts, proj_columns, rows_ref, out_bias_ref, gain_ref, shift_ref, up_ref, up_bias_ref, *refs
):
    attended_refs = (refs[:parts], refs[parts : 2 * parts])
    weight_refs = refs[2 * parts : 3 * parts]
    hidden_ref, act_ref, acted_ref, slope_ref = refs[3 * parts :]
    columns = weight_refs[0].shape[0] - proj_columns
    half = rows_ref.shape[0] // 2
    out_bias, gain, shift, up_bias = (
        wide_row(ref) for ref in (out_bias_ref, gain_ref, shift_ref, up_bias_ref)
    )

    def body(which, start, size):
        rows = pl.ds(which * half + start, size)
        total = paired_sum(
            [
                packed_product(attended_ref, weight_ref, start, columns)
                for attended_ref, weight_ref in zip(attended_refs[which], weight_refs)
            ]
        )
        hidden = rows_ref[rows, :].astype(wide_type) + total + out_bias
        hidden_ref[rows, :] = hidden
        normed, _ = normalized(hidden)
        act = (normed * gain + shift).astype(low_type)
        act_ref[rows, :] = act
        up_pre = dot(act, up_ref[...]) + up_bias
        cdf = 0.5 + 0.5 * lax.erf(up_pre * math.sqrt(0.5))
        acted_ref[rows, :] = (up_pre * cdf).astype(low_type)
        slope_ref[rows, :] = cdf + up_pre * jnp.exp(-0.5 * up_pre * up_pre) * (
            1.0 / math.sqrt(2.0 * math.pi)
        )

    for which in range(2):
        over_rows(half, PACKED, lambda start, size, which=which: body(which, start, size))


def forward_part_kernel(info_ref, acted_ref, down_ref, keep_ref, sent_ref):
    halves(info_ref[1] & 1, acted_ref, down_ref, keep_ref, sent_ref, dot)


def forward_grad_kernel(parts, first, info_ref, slope_ref, up_ref, down_ref, *refs):
    enc_refs, weight_refs = refs[:parts], refs[parts : 2 * parts]
    keep_ref, sent_ref, up_low_ref, down_low_ref, bias_ref = refs[2 * parts :]
    bias_ref[...] = jnp.zeros_like(bias_ref)

    def body(start, size):
        rows = pl.ds(start, size)
        out_grad = paired_sum(
            [
                dot(enc_ref[rows, :], weight_ref[first:, :])
                for enc_ref, weight_ref in zip(enc_refs, weight_refs)
            ]
        )
        bias_ref[0:1, :] += row_sum(out_grad)
        down_low = out_grad.astype(low_type)
        down_low_ref[rows, :] = down_low
        up_low_ref[rows, :] = (dot_right_t(down_low, down_ref[...]) * slope_ref[rows, :]).astype(low_type)

    over_rows(slope_ref.shape[0], 256, body)
    halves(info_ref[1] & 1, up_low_ref, up_ref, keep_ref, sent_ref, dot_right_t)
    bias_ref[1:2, :] = row_sum(up_low_ref[...].astype(wide_type))


def put_blocks(exchange, info_ref, keep_ref, sent_ref, wide_ref, pad, first=0):
    share = wide_ref.shape[0] // exchange.count
    for ref, indices in exchange.targets(0, info_ref, keep_ref, sent_ref):
        for block, index in enumerate(indices):
            rows = pl.ds(pl.multiple_of(index * share, 8), share)
            for tile in range(wide_ref.shape[1] // LANES):
                at = block * exchange.block + first + tile * pad
                ref[at : at + share, :] = wide_ref[rows, tile * LANES : (tile + 1) * LANES].astype(low_type)


def weight_grad_kernel(exchange, pad, info_ref, left_ref, right_ref, *refs):
    *pos_refs, keep_ref, sent_ref, wide_ref = refs
    wide_ref[...] = dot_left_t(left_ref[...], right_ref[...])
    put_blocks(exchange, info_ref, keep_ref, sent_ref, wide_ref, pad)
    for pos_ref in pos_refs:
        put_blocks(exchange, info_ref, keep_ref, sent_ref, pos_ref, 0, wide_ref.shape[1] // LANES * pad)


def attention_back_kernel(
    heads, info_ref, sum_ref, sum_other_ref, hidden_ref, down_low_ref, gain_ref, weight_ref, qkv_ref, prob_ref,
    prob_last_ref, grads_ref, attn_low_ref, own_ref, bias_ref, grad_ref, probs_ref,
):
    gain = wide_row(gain_ref)
    bias_ref[...] = jnp.zeros_like(bias_ref)
    probs_ref[: prob_ref.shape[0], :] = prob_ref[...]
    probs_ref[prob_ref.shape[0] :, :] = prob_last_ref[...]

    def body(source, rows, part, size):
        normed, spread = normalized(hidden_ref[rows, :])
        grad = (sum_ref, sum_other_ref)[source][part, :].astype(wide_type)
        bias_ref[0:1, :] += row_sum(grad * normed)
        bias_ref[1:2, :] += row_sum(grad)
        hidden_grad = down_low_ref[rows, :].astype(wide_type) + norm_back(grad, normed, spread, gain)
        grad_ref[rows, :] = hidden_grad
        bias_ref[2:3, :] += row_sum(hidden_grad)
        attn_low = hidden_grad.astype(low_type)
        attn_low_ref[rows, :] = attn_low
        attended_grad = dot_right_t(attn_low, weight_ref[...]).astype(low_type)
        for pair in range(size // PAIR):
            pair_rows = pl.ds(rows.start + pair * PAIR, PAIR)
            for head in range(heads):
                base = head * 3 * HEAD_DIM
                queries = qkv_ref[pair_rows, base : base + HEAD_DIM]
                key_rows = qkv_ref[pair_rows, base + HEAD_DIM : base + 2 * HEAD_DIM]
                value_rows = qkv_ref[pair_rows, base + 2 * HEAD_DIM : base + 3 * HEAD_DIM]
                probs = probs_ref[pair_rows, head * PAIR : (head + 1) * PAIR]
                grad_rows = attended_grad[
                    pair * PAIR : (pair + 1) * PAIR, head * HEAD_DIM : (head + 1) * HEAD_DIM
                ]
                value_low = dot_left_t(probs, grad_rows).astype(low_type)
                prob_grad = dot_right_t(grad_rows, value_rows)
                wide_probs = probs.astype(wide_type)
                weighted = wide_probs * prob_grad
                score_low = (
                    weighted - wide_probs * jnp.sum(weighted, axis=-1, keepdims=True)
                ).astype(low_type)
                query_low = (dot(score_low, key_rows) * scale_factor).astype(low_type)
                key_low = (dot_left_t(score_low, queries) * scale_factor).astype(low_type)
                grads_ref[pair_rows, base : base + HEAD_DIM] = query_low
                grads_ref[pair_rows, base + HEAD_DIM : base + 2 * HEAD_DIM] = key_low
                grads_ref[pair_rows, base + 2 * HEAD_DIM : base + 3 * HEAD_DIM] = value_low

    both_halves(info_ref[1] & 1, sum_ref.shape[0], body)
    share = own_ref.shape[0]
    own_ref[...] = grad_ref[pl.ds(pl.multiple_of(info_ref[1] * share, share), share), :]


def late_grads_kernel(
    exchange, pad, info_ref, act_ref, grads_ref, attn_low_ref, first_ref, last_ref, keep_ref, sent_ref, bias_ref,
    wide_ref,
):
    columns = grads_ref.shape[1]
    half, first = first_ref.shape
    wide_ref[:, :first] = dot_left_t(attn_low_ref[:half, :], first_ref[...]) + dot_left_t(
        attn_low_ref[half:, :], last_ref[...]
    )
    wide_ref[:, first : first + columns] = dot_left_t(act_ref[...], grads_ref[...])
    put_blocks(exchange, info_ref, keep_ref, sent_ref, wide_ref, pad)
    bias_ref[...] = row_sum(grads_ref[...].astype(wide_type))


EXTRA = 16


def put_extra(ref, start, gain, shift):
    rows = []
    for value in (gain, shift):
        rows += list(split_low(value))
    rows.append(jnp.zeros((EXTRA - 4, gain.shape[1]), low_type))
    ref[start : start + EXTRA, :] = jnp.concatenate(rows, axis=0)


def get_extra(ref, start):
    rows = ref[start : start + EXTRA, :].astype(wide_type)
    return rows[0:1] + rows[1:2], rows[2:3] + rows[3:4]


def input_part_kernel(info_ref, rows_ref, grads_ref, weight_ref, keep_ref, sent_ref, part_ref, bias_ref):
    lower_bit = info_ref[1] & 1
    bias_ref[...] = jnp.zeros_like(bias_ref)

    def body(start, size):
        rows = pl.ds(start, size)
        grad = dot(grads_ref[rows, :], weight_ref[...])
        part_ref[rows, :] = grad
        normed, _ = normalized(rows_ref[rows, :].astype(wide_type))
        bias_ref[0:1, :] += row_sum(grad * normed)
        bias_ref[1:2, :] += row_sum(grad)

    over_rows(rows_ref.shape[0], CHUNK, body)
    size = keep_ref.shape[0] - EXTRA
    share = size // (lax.axis_size("mp") // 2)
    for out_ref, which in ((sent_ref, 1 - lower_bit), (keep_ref, lower_bit)):
        for block in range(size // share):
            rows = pl.ds(pl.multiple_of((2 * block + which) * share, share), share)
            out_ref[block * share : (block + 1) * share, :] = part_ref[rows, :].astype(low_type)
        put_extra(out_ref, size, bias_ref[0:1, :], bias_ref[1:2, :])


def input_halve_kernel(bit, info_ref, keep_ref, other_ref, next_keep_ref, next_sent_ref, total_ref):
    upper = (info_ref[1] >> bit) & 1
    half = next_keep_ref.shape[0] - EXTRA
    size = 2 * half
    share = total_ref.shape[0] - size
    total_ref[:size, :] = keep_ref[:size, :].astype(wide_type) + other_ref[:size, :].astype(wide_type)
    own, other = get_extra(keep_ref, size), get_extra(other_ref, size)
    for out_ref, which in ((next_sent_ref, 1 - upper), (next_keep_ref, upper)):
        for block in range(half // share):
            rows = pl.ds(pl.multiple_of((2 * block + which) * share, share), share)
            out_ref[block * share : (block + 1) * share, :] = total_ref[rows, :].astype(low_type)
        put_extra(out_ref, half, own[0] + other[0], own[1] + other[1])


def input_grad_kernel(info_ref, rows_ref, keep_ref, other_ref, own_ref, gain_ref, out_ref):
    share = out_ref.shape[0]
    rows = pl.ds(pl.multiple_of(info_ref[1] * share, share), share)
    normed, spread = normalized(rows_ref[rows, :].astype(wide_type))
    grad = keep_ref[:share, :].astype(wide_type) + other_ref[:share, :].astype(wide_type)
    out_ref[...] = (own_ref[...] + norm_back(grad, normed, spread, wide_row(gain_ref))).astype(low_type)


VECTOR_ROWS = 48


def put_rows(values, rows_ref):
    row = 0
    for value in values:
        for tile in range(value.shape[1] // LANES):
            rows_ref[row : row + 1, :] = value[:, tile * LANES : (tile + 1) * LANES]
            row += 1


def take_rows(rows_ref, refs):
    row = 0
    for ref in refs:
        size = ref.shape[0]
        for tile in range(-(-size // LANES)):
            width = min(LANES, size - tile * LANES)
            ref[tile * LANES : tile * LANES + width] = rows_ref[row, :width]
            row += 1


def encoded_kernel(
    info, exchange, heads, info_ref, hidden_ref, sum_ref, sum_other_ref, down_bias_ref, weight_ref, bias_ref, enc_ref,
    mask_ref, grads_ref, second_ref, qkv_ref, first_ref, first_other_ref, keep_ref, sent_ref, low_ref, wide_ref,
    encoded_ref, rows_ref,
):
    down_bias, bias = wide_row(down_bias_ref), wide_row(bias_ref)

    def body(source, rows, part, size):
        total = (sum_ref, sum_other_ref)[source][part, :].astype(wide_type)
        out_low = (hidden_ref[rows, :] + total + down_bias).astype(low_type)
        low_ref[rows, :] = out_low
        encoded_ref[rows, :] = (dot(out_low, weight_ref[...]) + bias).astype(low_type)

    both_halves(info_ref[1] & 1, sum_ref.shape[0], body)
    wide_ref[...] = dot_left_t(low_ref[...], enc_ref[...])
    put_blocks(exchange, info_ref, keep_ref, sent_ref, wide_ref, 0)
    for ref, indices in exchange.targets(0, info_ref, keep_ref, sent_ref):
        at = exchange.moved_at(0)
        for index in indices:
            image = info.image(info_ref, index)
            ref[at : at + VIS, :] = encoded_ref[pl.ds(pl.multiple_of(image * VIS, VIS), VIS), :]
            at += VIS
    qkv = qkv_ref[...]
    empty = jnp.zeros((1, 2 * LANES - heads * HEAD_DIM), wide_type)
    spread = []
    for part in (0, 2):
        spread += [
            qkv[:, (3 * head + part) * HEAD_DIM : (3 * head + part + 1) * HEAD_DIM] for head in range(heads)
        ] + [empty]
    own = get_extra(first_ref, first_ref.shape[0] - EXTRA)
    other = get_extra(first_other_ref, first_ref.shape[0] - EXTRA)
    put_rows(
        (
            jnp.concatenate(spread, axis=1), grads_ref[1:2, :], row_sum(enc_ref[...].astype(wide_type)),
            mask_ref[...], own[0] + other[0], own[1] + other[1], second_ref[0:1, :], second_ref[1:2, :],
            second_ref[2:3, :], grads_ref[0:1, :],
        ),
        rows_ref,
    )
    for ref in (keep_ref, sent_ref):
        ref[exchange.shared_at(0) :, :] = rows_ref[...].astype(low_type)


def late_out_kernel(
    info, exchange, pad, info_ref, seen_ref, keep_ref, other_ref, mask_ref, layout_ref, grids_ref, out_ref, qkv_ref,
    proj_ref, *refs
):
    *vector_refs, wide_ref, rows_ref = refs
    cells = lax.broadcasted_iota(jnp.int32, (GRID, VIS), 0)
    cell_column = lax.broadcasted_iota(jnp.int32, (GRID, 1), 0)
    mask_row = wide_row(mask_ref)
    for relative, ref, start in exchange.arrived(keep_ref, other_ref):
        slot = info_ref[0] ^ relative
        seen = seen_ref[pl.ds(slot, 1), :] == cells
        size = info.cells(info_ref, slot)
        fill = (cell_column < size).astype(wide_type) - jnp.sum(
            seen.astype(wide_type), axis=1, keepdims=True
        )
        placed = dot(seen.astype(low_type), ref[start : start + VIS, :])
        grids_ref[slot] = (placed + fill * mask_row + layout_ref[side_of(size)]).astype(low_type)
    share = proj_ref.shape[0]
    tiles = wide_ref.shape[1] // LANES
    for tile in range(tiles):
        wide_ref[:, tile * LANES : (tile + 1) * LANES] = exchange.total(keep_ref, other_ref, tile * pad, share)
    columns = out_ref.shape[0]
    wide_out = -(-columns // LANES) * LANES
    out_ref[...] = wide_ref[:, :wide_out].T[:columns]
    qkv_ref[...] = wide_ref[:, columns:]
    proj_ref[...] = exchange.total(keep_ref, other_ref, tiles * pad, share)
    rows_ref[...] = exchange.shared_total(keep_ref, other_ref)
    take_rows(rows_ref, vector_refs)


def early_out_kernel(exchange, pad, keep_ref, other_ref, out_ref, *pos_refs):
    tiles = out_ref.shape[1] // LANES
    for tile in range(tiles):
        out_ref[:, tile * LANES : (tile + 1) * LANES] = exchange.total(
            keep_ref, other_ref, tile * pad, out_ref.shape[0]
        )
    for pos_ref in pos_refs:
        pos_ref[...] = exchange.total(keep_ref, other_ref, tiles * pad, pos_ref.shape[0])


def swap(value, axis, bit):
    count = lax.axis_size(axis)
    return lax.ppermute(value, axis, [(i, i ^ bit) for i in range(count)])


def local(
    patch_rows, patches, visible, owner, qkv_weight, query_bias, value_bias, out_weight, out_bias, first_gain,
    first_shift, second_gain, second_shift, up_weight, up_bias, down_weight, down_bias, proj_weight, proj_bias,
    mask_token, decoder_pos, grid_cotangent,
):
    count = lax.axis_size("dp")
    parts = lax.axis_size("mp")
    where = jnp.stack([lax.axis_index("dp"), lax.axis_index("mp")]).astype(jnp.int32)
    rows, width = patch_rows.shape
    images = rows // VIS
    heads = qkv_weight.shape[1] // (3 * HEAD_DIM)
    head_columns = heads * HEAD_DIM
    qkv_columns = qkv_weight.shape[1]
    units = up_weight.shape[1]
    columns = proj_weight.shape[1]
    share = width // count
    pos_share = GRID // count
    half = rows // 2
    own_rows = rows // parts
    pads = (-(-share // 16) * 16, -(-pos_share // 16) * 16)
    run = Order(rows <= PINNED_ROWS)

    tables = grid_tables()
    table_high = tables.astype(low_type)
    table_low = (tables - table_high.astype(np.float32)).astype(low_type)
    turned_high = jnp.asarray(np.ascontiguousarray(table_high.transpose(0, 2, 1)))
    turned_low = jnp.asarray(np.ascontiguousarray(table_low.transpose(0, 2, 1)))
    table_high, table_low = jnp.asarray(table_high), jnp.asarray(table_low)
    qkv_weight_t = qkv_weight.T
    run.leave(owner, visible, patches, grid_cotangent)
    info = Info(count)
    bits = tuple(range(count.bit_length() - 1))
    late_columns = qkv_columns + head_columns
    turned = (1, 0) + bits[2:]
    back_exchange = Exchange(count, bits, 0, moved=VIS)
    up_exchange = Exchange(count, bits, units // LANES * pads[0] + pads[1])
    down_exchange = Exchange(count, turned, units // LANES * pads[0])
    late_exchange = Exchange(count, turned, late_columns // LANES * pads[0])
    last_exchange = Exchange(count, turned, pads[0], moved=VIS, shared=VECTOR_ROWS)
    joint_exchange = Exchange(
        count, turned, late_exchange.block + last_exchange.block, moved=VIS, shared=VECTOR_ROWS
    )

    def low(*shape):
        return (shape, low_type)

    def wide(*shape):
        return (shape, wide_type)

    def moved(value, axis, bit):
        return run.keep(swap(value, axis, bit))

    def model_steps(keep, sent):
        received = moved(sent, "mp", 1)
        yield
        (total,) = run(add_kernel, [low(half, width)], (keep, received), cost=0.6)
        bit = 2
        while bit < parts:
            received = moved(total, "mp", bit)
            yield
            (total,) = run(add_kernel, [low(half, width)], (total, received), cost=0.6)
            bit *= 2
        other = moved(total, "mp", 1)
        yield
        return total, other

    def model_gather(value):
        values = {0: value}
        bit = parts // 2
        while bit:
            values.update({other | bit: moved(values[other], "mp", bit) for other in tuple(values)})
            bit //= 2
        return tuple(values[at] for at in range(parts))

    def data_step(step, exchange, pairs):
        keep, sent = run(
            lambda *refs: exchange.kernel(step, [part for part, _, _ in pairs], *refs),
            [low(exchange.rows(step), LANES)] * 2,
            (facts,) + tuple(array for _, *arrays in pairs for array in arrays),
            (SMEM,) + (VMEM,) * (2 * len(pairs)),
            cost=1.2,
        )
        return keep, moved(sent, "dp", 2 ** exchange.bits[step])

    def data_steps(exchange, keep, sent):
        received = moved(sent, "dp", 2 ** exchange.bits[0])
        yield keep, received
        for step in range(1, len(exchange.bits)):
            keep, received = data_step(step, exchange, [(exchange, keep, received)])
            yield keep, received

    def finish_pair(steps):
        *_, last = steps
        return last

    def finish(steps):
        while True:
            try:
                next(steps)
            except StopIteration as stop:
                return stop.value

    (
        back_keep, back_sent, facts, seen, patch_rows, qkv_weight_t, first_gain, first_shift, query_bias, value_bias,
        out_weight, proj_weight,
    ) = run(
        lambda *refs: cotangent_kernel(info, back_exchange, *refs),
        [
            low(back_exchange.rows(0), columns), low(back_exchange.rows(0), columns), ((info.size,), jnp.int32),
            ((count, VIS), jnp.int32),
        ],
        (where, owner, patches, visible, grid_cotangent),
        (SMEM, SMEM, SMEM, VMEM, VMEM),
        out_specs=(VMEM, VMEM, SMEM, VMEM),
        scratch=[pltpu.VMEM((VIS, count), wide_type)],
        stage=(
            patch_rows, qkv_weight_t, first_gain, first_shift, query_bias, value_bias, out_weight, proj_weight
        ),
        cost=3.0,
    )
    back_steps = data_steps(back_exchange, back_keep, back_sent)
    next(back_steps)
    weights, act_one, qkv = run(
        enter_kernel,
        [low(head_columns + columns, width), low(rows, width), low(rows, qkv_columns)],
        (
            patch_rows, first_gain, first_shift, qkv_weight_t, query_bias, value_bias, out_weight, proj_weight
        ),
        cost=1.2,
    )
    weights = model_gather(weights)
    next(back_steps)
    packed_rows = half * head_columns // LANES
    packed, first_probs, first_attended, out_bias, second_gain, second_shift, up_weight, up_bias = run(
        lambda *refs: attention_kernel(info, heads, 0, *refs),
        [low(packed_rows, LANES), low(half, heads * PAIR), low(half, head_columns)],
        (facts, qkv),
        (SMEM, VMEM),
        stage=(out_bias, second_gain, second_shift, up_weight, up_bias),
        cost=2.8,
    )
    first_all = model_gather(packed)
    back_own, back_other = finish_pair(back_steps)
    packed, last_probs, last_attended, down_weight, down_bias, proj_bias = run(
        lambda *refs: attention_kernel(info, heads, half, *refs),
        [low(packed_rows, LANES), low(half, heads * PAIR), low(half, head_columns)],
        (facts, qkv),
        (SMEM, VMEM),
        stage=(down_weight, down_bias, proj_bias),
        cost=2.5,
    )
    last_all = model_gather(packed)
    (enc_grad,) = run(
        lambda *refs: back_kernel(info, back_exchange, *refs),
        [low(rows, columns)],
        (facts, back_own, back_other),
        (SMEM, VMEM, VMEM),
        cost=0.4,
    )
    enc_all = model_gather(enc_grad)
    (
        hidden, act_two, acted, slope, turned_high, turned_low, table_high, table_low, decoder_pos, grid_cotangent
    ) = run(
        lambda *refs: forward_kernel(parts, columns, *refs),
        [wide(rows, width), low(rows, width), low(rows, units), wide(rows, units)],
        (patch_rows, out_bias, second_gain, second_shift, up_weight, up_bias) + first_all + last_all + weights,
        stage=(turned_high, turned_low, table_high, table_low, decoder_pos, grid_cotangent),
        cost=2.6,
    )
    keep, sent, up_low, down_low, bias_grads = run(
        lambda *refs: forward_grad_kernel(parts, head_columns, *refs),
        [low(half, width), low(half, width), low(rows, units), low(rows, width), wide(2, width)],
        (facts, slope, up_weight, down_weight) + enc_all + weights,
        (SMEM,) + (VMEM,) * (3 + 2 * parts),
        cost=2.0,
    )
    second_steps = model_steps(keep, sent)
    next(second_steps)
    keep, sent = run(
        forward_part_kernel,
        [low(half, width), low(half, width)],
        (facts, acted, down_weight),
        (SMEM, VMEM, VMEM),
        cost=0.7,
    )
    next(second_steps)
    out_steps = model_steps(keep, sent)
    next(out_steps)

    def weight_grad(exchange, left, right, *pos):
        keep, sent = run(
            lambda *refs: weight_grad_kernel(exchange, pads[0], *refs),
            [low(exchange.rows(0), LANES)] * 2,
            (facts, left, right) + pos,
            (SMEM,) + (VMEM,) * (2 + len(pos)),
            scratch=[pltpu.VMEM((width, right.shape[1]), wide_type)],
            cost=1.9,
        )
        steps = data_steps(exchange, keep, sent)
        next(steps)
        return steps

    down_steps = weight_grad(down_exchange, down_low, acted)
    pos_grad_own, mask_grad, layouts = run(
        lambda *refs: position_kernel(info, *refs),
        [wide(GRID, columns), wide(1, columns), wide(3, GRID, columns)],
        (facts, seen, grid_cotangent, turned_high, turned_low, table_high, table_low, decoder_pos),
        (SMEM,) + (VMEM,) * 7,
        scratch=[pltpu.VMEM((3, GRID, columns), wide_type)],
        cost=1.0,
    )
    up_steps = weight_grad(up_exchange, act_two, up_low, pos_grad_own)
    next(second_steps)
    next(out_steps)
    second_sum, second_other = finish(second_steps)
    grads, attn_low, own_grad, second_grads = run(
        lambda *refs: attention_back_kernel(heads, *refs),
        [low(rows, qkv_columns), low(rows, width), wide(own_rows, width), wide(3, width)],
        (
            facts, second_sum, second_other, hidden, down_low, second_gain, out_weight, qkv, first_probs, last_probs
        ),
        (SMEM,) + (VMEM,) * 9,
        scratch=[pltpu.VMEM((rows, width), wide_type), pltpu.VMEM((rows, heads * PAIR), low_type)],
        cost=5.5,
    )
    in_keep, in_sent = run(
        input_part_kernel,
        [low(half + EXTRA, width)] * 2,
        (facts, patch_rows, grads, qkv_weight_t),
        (SMEM,) + (VMEM,) * 3,
        scratch=[pltpu.VMEM((rows, width), wide_type), pltpu.VMEM((2, width), wide_type)],
        cost=2.0,
    )
    in_other = moved(in_sent, "mp", 1)
    keep, sent, qkv_bias_grad = run(
        lambda *refs: late_grads_kernel(late_exchange, pads[0], *refs),
        [low(late_exchange.rows(0), LANES)] * 2 + [wide(1, qkv_columns)],
        (facts, act_one, grads, attn_low, first_attended, last_attended),
        (SMEM,) + (VMEM,) * 5,
        scratch=[pltpu.VMEM((width, late_columns), wide_type)],
        cost=2.5,
    )
    late_keep, late_other = next(data_steps(late_exchange, keep, sent))
    bit = 1
    size = half
    while 2**bit < parts:
        in_keep, in_sent = run(
            lambda *refs, bit=bit: input_halve_kernel(bit, *refs),
            [low(size // 2 + EXTRA, width)] * 2,
            (facts, in_keep, in_other),
            (SMEM, VMEM, VMEM),
            scratch=[pltpu.VMEM((size + own_rows, width), wide_type)],
            cost=1.1,
        )
        in_other = moved(in_sent, "mp", 2**bit)
        size //= 2
        bit += 1
    next(out_steps)
    next(down_steps)
    out_sum, out_other = finish(out_steps)
    keep, sent = run(
        lambda *refs: encoded_kernel(info, last_exchange, heads, *refs),
        [low(last_exchange.rows(0), LANES)] * 2,
        (
            facts, hidden, out_sum, out_other, down_bias, proj_weight, proj_bias, enc_grad, mask_grad, bias_grads,
            second_grads, qkv_bias_grad, in_keep, in_other,
        ),
        (SMEM,) + (VMEM,) * 13,
        scratch=[
            pltpu.VMEM((rows, width), low_type),
            pltpu.VMEM((width, columns), wide_type),
            pltpu.VMEM((rows, columns), low_type),
            pltpu.VMEM((VECTOR_ROWS, LANES), wide_type),
        ],
        cost=2.2,
    )
    last_keep, last_other = next(data_steps(last_exchange, keep, sent))
    next(up_steps)
    (input_grad,) = run(
        input_grad_kernel,
        [low(own_rows, width)],
        (facts, patch_rows, in_keep, in_other, own_grad, first_gain),
        (SMEM,) + (VMEM,) * 5,
        final=True,
        cost=0.8,
    )
    late_keep, late_other = data_step(
        1, joint_exchange, [(late_exchange, late_keep, late_other), (last_exchange, last_keep, last_other)]
    )
    down_keep, down_other = finish_pair(down_steps)
    up_keep, up_other = finish_pair(up_steps)
    for step in range(2, len(bits)):
        late_keep, late_other = data_step(step, joint_exchange, [(joint_exchange, late_keep, late_other)])
    (down_weight_grad,) = run(
        lambda *refs: early_out_kernel(down_exchange, pads[0], *refs),
        [wide(share, units)],
        (down_keep, down_other),
        final=True,
        cost=0.8,
    )
    up_weight_grad, pos_grad = run(
        lambda *refs: early_out_kernel(up_exchange, pads[0], *refs),
        [wide(share, units), wide(pos_share, columns)],
        (up_keep, up_other),
        final=True,
        cost=0.8,
    )
    (
        grids, out_weight_grad, qkv_weight_grad, proj_weight_grad, query_bias_grad, value_bias_grad, up_bias_grad,
        proj_bias_grad, mask_token_grad, first_gain_grad, first_shift_grad, second_gain_grad, second_shift_grad,
        out_bias_grad, down_bias_grad,
    ) = run(
        lambda *refs: late_out_kernel(info, joint_exchange, pads[0], *refs),
        [
            low(count, GRID, columns), wide(head_columns, share), wide(share, qkv_columns), wide(share, columns)
        ]
        + [wide(size) for size in (head_columns, head_columns, units, columns, columns) + (width,) * 6],
        (facts, seen, late_keep, late_other, mask_token, layouts),
        (SMEM,) + (VMEM,) * 5,
        scratch=[pltpu.VMEM((share, late_columns), wide_type), pltpu.VMEM((VECTOR_ROWS, LANES), wide_type)],
        final=True,
        cost=2.5,
    )
    return (
        grids, input_grad, qkv_weight_grad, query_bias_grad, value_bias_grad, out_weight_grad, out_bias_grad,
        first_gain_grad, first_shift_grad, second_gain_grad, second_shift_grad, up_weight_grad, up_bias_grad,
        down_weight_grad.T, down_bias_grad, proj_weight_grad, proj_bias_grad, mask_token_grad, pos_grad,
    )


def solution(mesh):
    return jax.shard_map(
        local,
        mesh=mesh,
        in_specs=(
            P("dp", None), P(), P(), P(), P(None, "mp"), P("mp"), P("mp"), P("mp", None), P(), P(), P(), P(), P(),
            P(None, "mp"), P("mp"), P("mp", None), P(), P(None, "mp"), P("mp"), P("mp"), P(None, "mp"),
            P("dp", None, "mp"),
        ),
        out_specs=(
            P("dp", None, "mp"), P(("dp", "mp"), None), P("dp", "mp"), P("mp"), P("mp"), P("mp", "dp"), P(), P(),
            P(), P(), P(), P("dp", "mp"), P("mp"), P("mp", "dp"), P(), P("dp", "mp"), P("mp"), P("mp"),
            P("dp", "mp"),
        ),
        check_vma=False,
    )
```

time: 149 us -> 118 us (0.79)
  blocking collectives: 16.8 us -> 0 us
  waiting for transfers between devices: 54.1 us -> 42.1 us
  local copies, waits for them, and re-layouts: 7.46 us -> 0.11 us
  starting transfers between devices: 25.3 us -> 29.1 us
  Pallas kernels: 43.1 us -> 44.6 us
    all_to_all x1 -> x0, blocking collectives: 16.8 us -> none  [spread(): lax.all_to_all(value, 'dp', split_axis=0, concat_axis=0, tiled=True)]
    ppermute x20 -> x33, starting transfers between devices: 14.5 us -> 29.1 us  [swap(): return lax.ppermute(value, axis, [(i, i ^ bit) for i in range(count)])]
    all_to_all x2 -> x0, starting transfers between devices: 10.7 us -> none  [spread(): lax.all_to_all(value, 'dp', split_axis=0, concat_axis=0, tiled=True)]
    ppermute x20 -> x33, waiting for transfers between devices: 51.8 us -> 42.1 us  [swap(): return lax.ppermute(value, axis, [(i, i ^ bit) for i in range(count)])]
    unnamed x66 -> x44, local copies, waits for them, and re-layouts: 7.46 us -> 0.11 us
    all_to_all x2 -> x0, waiting for transfers between devices: 2.3 us -> none  [spread(): lax.all_to_all(value, 'dp', split_axis=0, concat_axis=0, tiled=True)]
    pallas_call x29 -> x32, Pallas kernels: 43.1 us -> 44.6 us  [__call__(): pl.pallas_call(body, out_shape=tuple(shapes) + tuple((pltpu.VMEM(array.sh...]
  transfers between devices with their start and end apart: 22 -> 33, of which waited for: 12 -> 13; matrix products, arithmetic and copies ran while one was open for 0% -> 0% of each run, Pallas kernels for 20% -> 31%
where the time goes in v3:
time: 118 us; the launch traced here: 117 us
  Pallas kernels  44.6 us (38%)
  waiting for transfers between devices  42.1 us (36%)
  starting transfers between devices  29.1 us (25%)
  between operations  1.24 us (1%)
    pallas_call x32, Pallas kernels, __call__(): pl.pallas_call(body, out_shape=tuple(shapes) + tuple((pltpu.VMEM(array.sh...  44.6 us
    ppermute x33, waiting for transfers between devices, swap(): return lax.ppermute(value, axis, [(i, i ^ bit) for i in range(count)])  42.1 us
    ppermute x33, starting transfers between devices, swap(): return lax.ppermute(value, axis, [(i, i ^ bit) for i in range(count)])  29.1 us
  transfers between devices with their start and end apart: 33, of which 13 were waited for; matrix products, arithmetic and copies ran while one was open for 0% of the time, Pallas kernels for 31%

profile of v3, /device:TPU:0, one launch (start us, length us, event | category | flops | bytes accessed | tf_op | source)
XLA Modules:
  0.0 117.2 jit_solution(365389772674320479)
XLA Ops:
  0.7 3.0 %shard_map.393 = (bf16[256,128]{1,0:T(8,128)(2,1)S(1)}, bf16[256,128]{1,0:T(8,128)(2,1)S(1)}, s32[42]{0:T(128)S(4)}, s32[8,64]{1,0:T(8,128)S(1)}, bf16[512,768]{...) custom-call(s32[2]{0:T(128)S(1)} %pad_add_fusion.refs_0_, ...), custom_call_target="tpu_custom_call" | custom-call | flops 60000002048 | tf_op jit(solution)/shard_map/pallas_call | solution.py:172
  3.8 3.0 %collective-permute-start = (bf16[256,128]{1,0:T(8,128)(2,1)S(1)}, bf16[256,128]{1,0:T(8,128)(2,1)S(1)}, u32[]{:S(2)}, u32[]{:S(2)}) collective-permute-start(bf16[256,128]{1,0:T(8,128)(2,1)S(1)} %get-tuple-element.131), channel_id=1, source_target_pairs={{0,4},{4,0},{8,12},{12,8},{16,20},{20,16},{24,28},{28,24},{1,5},{5... | collective-permute-start | bytes 196616 | tf_op jit(solution)/shard_map/ppermute | solution.py:836
  6.8 1.9 %shard_map.394 = (bf16[320,768]{1,0:T(8,128)(2,1)}, bf16[512,768]{1,0:T(8,128)(2,1)S(1)}, bf16[512,576]{1,0:T(8,128)(2,1)S(1)}) custom-call(bf16[512,768]{1,0:T(8,128)(2,1)S(1)} %get-tuple-element.120.refs_0_.refs_1_, bf16[768]{0:T(1024)(128)(2,1)S(1)} %get-tuple-element.121.refs_1_.refs_5_, bf16[768]{0:T(1024)(128)(2,1)S(1)} %get-tuple-element.122.refs_2_, ...), custom_call_target="tpu_custom_call" | custom-call | flops 24000000000 | tf_op jit(solution)/shard_map/pallas_call | solution.py:172
  10.3 1.6 %collective-permute-start.4 = (bf16[256,128]{1,0:T(8,128)(2,1)S(1)}, bf16[256,128]{1,0:T(8,128)(2,1)S(1)}, u32[]{:S(2)}, u32[]{:S(2)}) collective-permute-start(bf16[256,128]{1,0:T(8,128)(2,1)S(1)} %get-tuple-element.140), channel_id=1, source_target_pairs={{0,8},{4,12},{8,0},{12,4},{16,24},{20,28},{24,16},{28,20},{1,9},{5... | collective-permute-start | bytes 196616 | tf_op jit(solution)/shard_map/ppermute | solution.py:836
  12.0 3.3 %shard_map.396 = (bf16[384,128]{1,0:T(8,128)(2,1)S(1)}, bf16[256,384]{1,0:T(8,128)(2,1)S(1)}, bf16[256,192]{1,0:T(8,128)(2,1)S(1)}, bf16[768]{0:T(1024)(128)(2,1...) custom-call(s32[42]{0:T(128)S(4)} %get-tuple-element.118.refs_0_, ...), custom_call_target="tpu_custom_call" | custom-call | flops 56000000000 | tf_op jit(solution)/shard_map/pallas_call | solution.py:172
  16.1 2.7 %collective-permute-start.11 = (bf16[256,128]{1,0:T(8,128)(2,1)S(1)}, bf16[256,128]{1,0:T(8,128)(2,1)S(1)}, u32[]{:S(2)}, u32[]{:S(2)}) collective-permute-start(bf16[256,128]{1,0:T(8,128)(2,1)S(1)} %get-tuple-element.143), channel_id=1, source_target_pairs={{0,16},{4,20},{8,24},{12,28},{16,0},{20,4},{24,8},{28,12},{1,17},{... | collective-permute-start | bytes 196616 | tf_op jit(solution)/shard_map/ppermute | solution.py:836
  18.8 2.3 %shard_map.398 = (bf16[384,128]{1,0:T(8,128)(2,1)S(1)}, bf16[256,384]{1,0:T(8,128)(2,1)S(1)}, bf16[256,192]{1,0:T(8,128)(2,1)S(1)}, bf16[768,768]{1,0:T(8,128)(2...) custom-call(s32[42]{0:T(128)S(4)} %get-tuple-element.118.refs_0_, ...), custom_call_target="tpu_custom_call" | custom-call | flops 49999998976 | tf_op jit(solution)/shard_map/pallas_call | solution.py:172
  21.0 2.7 %collective-permute-done.2.refs_8_ = bf16[384,128]{1,0:T(8,128)(2,1)S(1)} collective-permute-done((bf16[384,128]{1,0:T(8,128)(2,1)S(1)}, bf16[384,128]{1,0:T(8,128)(2,1)S(1)}, u32[]{:S(2)}, u32[]{:S(2)}) %collective-permute-start.2) | collective-permute-done | bytes 98336 | tf_op jit(solution)/shard_map/ppermute | solution.py:836
  26.4 2.0 %collective-permute-done.6.refs_12_ = bf16[384,128]{1,0:T(8,128)(2,1)S(1)} collective-permute-done((bf16[384,128]{1,0:T(8,128)(2,1)S(1)}, bf16[384,128]{1,0:T(8,128)(2,1)S(1)}, u32[]{:S(2)}, u32[]{:S(2)}) %collective-permute-start.6) | collective-permute-done | bytes 98336 | tf_op jit(solution)/shard_map/ppermute | solution.py:836
  31.4 6.2 %shard_map.400 = (f32[512,768]{1,0:T(8,128)S(1)}, bf16[512,768]{1,0:T(8,128)(2,1)S(1)}, bf16[512,768]{1,0:T(8,128)(2,1)S(1)}, f32[512,768]{1,0:T(8,128)S(1)}, bf...) custom-call(bf16[512,768]{1,0:T(8,128)(2,1)S(1)} %copy-done.4, ...), custom_call_target="tpu_custom_call" | custom-call | flops 51999997952 | tf_op jit(solution)/shard_map/pallas_call | solution.py:172
  37.7 4.0 %shard_map.401 = (bf16[256,768]{1,0:T(8,128)(2,1)S(1)}, bf16[256,768]{1,0:T(8,128)(2,1)S(1)}, bf16[512,768]{1,0:T(8,128)(2,1)S(1)}, bf16[512,768]{1,0:T(8,128)(2,1)S(1)}, f32[2,768]{1,0:T(2,128)S(1)}) custom-call(s32[42]{0:T(128)S(4)} %get-tuple-element.118.refs_0_, f32[512,768]{1,0:T(8,128)S(1)} %get-tuple-element.144.refs_1_, ...), custom_call_target="tpu_custom_call" | custom-call | flops 40000000000 | tf_op jit(solution)/shard_map/pallas_call | solution.py:172
  45.1 2.0 %shard_map.404 = (bf16[2304,128]{1,0:T(8,128)(2,1)S(1)}, bf16[2304,128]{1,0:T(8,128)(2,1)}) custom-call(s32[42]{0:T(128)S(4)} %get-tuple-element.118.refs_0_, bf16[512,768]{1,0:T(8,128)(2,1)S(1)} %get-tuple-element.159.refs_1_.refs_4_, bf16[512,768]{1,0:T(8,128)(2,1)S(1)} %get-tuple-element.149.refs_1_.refs_2_, bf16[256,768]{1,0:T(8,128)(2,1)S(1)} %shard_map.403.refs_3_.refs_0_), custom_call_target="tpu_custom_call" | custom-call | flops 38000001024 | tf_op jit(solution)/shard_map/pallas_call | solution.py:172
  49.6 2.2 %shard_map.406 = (bf16[2432,128]{1,0:T(8,128)(2,1)S(1)}, bf16[2432,128]{1,0:T(8,128)(2,1)}) custom-call(s32[42]{0:T(128)S(4)} %get-tuple-element.118.refs_0_, bf16[512,768]{1,0:T(8,128)(2,1)S(1)} %get-tuple-element.151.refs_1_, bf16[512,768]{1,0:T(8,128)(2,1)S(1)} %get-tuple-element.152.refs_2_, f32[256,128]{1,0:T(8,128)S(1)} %get-tuple-element.161.refs_3_.refs_4_, ...), custom_call_target="tpu_custom_call" | custom-call | flops 38000001024 | tf_op jit(solution)/shard_map/pallas_call | solution.py:172
  52.3 2.8 %collective-permute-done.16.refs_1_ = bf16[256,768]{1,0:T(8,128)(2,1)S(1)} collective-permute-done((bf16[256,768]{1,0:T(8,128)(2,1)S(1)}, bf16[256,768]{1,0:T(8,128)(2,1)S(1)}, u32[]{:S(2)}, u32[]{:S(2)}) %collective-permute-start.16) | collective-permute-done | bytes 393248 | tf_op jit(solution)/shard_map/ppermute | solution.py:836
  57.6 5.3 %shard_map.409 = (bf16[512,576]{1,0:T(8,128)(2,1)S(1)}, bf16[512,768]{1,0:T(8,128)(2,1)S(1)}, f32[128,768]{1,0:T(8,128)S(1)}, f32[3,768]{1,0:T(4,128)S(1)}) custom-call(s32[42]{0:T(128)S(4)} %get-tuple-element.118.refs_0_, bf16[256,768]{1,0:T(8,128)(2,1)S(1)} %shard_map.407.refs_2_.refs_1_, bf16[256,768]{1,0:T(8,128)(2,1)S(1)} %collective-permute-done.17.refs_2_, ...), custom_call_target="tpu_custom_call" | custom-call | flops 109999996928 | tf_op jit(solution)/shard_map/pallas_call | solution.py:172
  71.8 3.4 %collective-permute-done.23.refs_13_.refs_3_ = bf16[144,768]{1,0:T(8,128)(2,1)S(1)} collective-permute-done((bf16[144,768]{1,0:T(8,128)(2,1)S(1)}, bf16[144,768]{1,0:T(8,128)(2,1)S(1)}, u32[]{:S(2)}, u32[]{:S(2)}) %collective-permute-start.23) | collective-permute-done | bytes 221216 | tf_op jit(solution)/shard_map/ppermute | solution.py:836
  77.7 1.7 %collective-permute-start.28 = (bf16[1216,128]{1,0:T(8,128)(2,1)S(1)}, bf16[1216,128]{1,0:T(8,128)(2,1)S(1)}, u32[]{:S(2)}, u32[]{:S(2)}) collective-permute-start(bf16[1216,128]{1,0:T(8,128)(2,1)S(1)} %get-tuple-element.190), channel_id=1, source_target_pairs={{0,8},{4,12},{8,0},{12,4},{16,24},{20,28},{24,16},{28,20},{1,9},{5... | collective-permute-start | bytes 933896 | tf_op jit(solution)/shard_map/ppermute | solution.py:836
  80.4 1.8 %collective-permute-done.19.refs_2_ = bf16[2304,128]{1,0:T(8,128)(2,1)S(1)} collective-permute-done((bf16[2304,128]{1,0:T(8,128)(2,1)S(1)}, bf16[2304,128]{1,0:T(8,128)(2,1)S(1)}, u32[]{:S(2)}, u32[]{:S(2)}) %collective-permute-start.19) | collective-permute-done | bytes 589856 | tf_op jit(solution)/shard_map/ppermute | solution.py:836
  82.2 3.8 %collective-permute-done.25.refs_4_ = bf16[688,128]{1,0:T(8,128)(2,1)S(1)} collective-permute-done((bf16[688,128]{1,0:T(8,128)(2,1)S(1)}, bf16[688,128]{1,0:T(8,128)(2,1)S(1)}, u32[]{:S(2)}, u32[]{:S(2)}) %collective-permute-start.25) | collective-permute-done | bytes 176160 | tf_op jit(solution)/shard_map/ppermute | solution.py:836
  86.2 2.6 %collective-permute-start.32 = (bf16[576,128]{1,0:T(8,128)(2,1)S(1)}, bf16[576,128]{1,0:T(8,128)(2,1)S(1)}, u32[]{:S(2)}, u32[]{:S(2)}) collective-permute-start(bf16[576,128]{1,0:T(8,128)(2,1)S(1)} %get-tuple-element.211), channel_id=1, source_target_pairs={{0,16},{4,20},{8,24},{12,28},{16,0},{20,4},{24,8},{28,12},{1,17},{... | collective-permute-start | bytes 442376 | tf_op jit(solution)/shard_map/ppermute | solution.py:836
  89.4 5.7 %collective-permute-done.28.refs_2_ = bf16[1216,128]{1,0:T(8,128)(2,1)S(1)} collective-permute-done((bf16[1216,128]{1,0:T(8,128)(2,1)S(1)}, bf16[1216,128]{1,0:T(8,128)(2,1)S(1)}, u32[]{:S(2)}, u32[]{:S(2)}) %collective-permute-start.28) | collective-permute-done | bytes 311328 | tf_op jit(solution)/shard_map/ppermute | solution.py:836
  96.5 2.6 %collective-permute-done.27.refs_2_ = bf16[1648,128]{1,0:T(8,128)(2,1)S(1)} collective-permute-done((bf16[1648,128]{1,0:T(8,128)(2,1)S(1)}, bf16[1648,128]{1,0:T(8,128)(2,1)S(1)}, u32[]{:S(2)}, u32[]{:S(2)}) %collective-permute-start.27) | collective-permute-done | bytes 421920 | tf_op jit(solution)/shard_map/ppermute | solution.py:836
  100.4 10.6 %collective-permute-done.31.refs_1_ = bf16[608,128]{1,0:T(8,128)(2,1)S(1)} collective-permute-done((bf16[608,128]{1,0:T(8,128)(2,1)S(1)}, bf16[608,128]{1,0:T(8,128)(2,1)S(1)}, u32[]{:S(2)}, u32[]{:S(2)}) %collective-permute-start.31) | collective-permute-done | bytes 155680 | tf_op jit(solution)/shard_map/ppermute | solution.py:836
  111.7 3.9 %collective-permute-done.30.refs_3_ = bf16[976,128]{1,0:T(8,128)(2,1)S(1)} collective-permute-done((bf16[976,128]{1,0:T(8,128)(2,1)S(1)}, bf16[976,128]{1,0:T(8,128)(2,1)S(1)}, u32[]{:S(2)}, u32[]{:S(2)}) %collective-permute-start.30) | collective-permute-done | bytes 249888 | tf_op jit(solution)/shard_map/ppermute | solution.py:836
  (119 shorter events, 35.1 us)
Async XLA Ops:
  3.8 6.5 %collective-permute-start = (bf16[256,128]{1,0:T(8,128)(2,1)S(1)}, bf16[256,128]{1,0:T(8,128)(2,1)S(1)}, u32[]{:S(2)}, u32[]{:S(2)}) collective-permute-start(bf16[256,128]{1,0:T(8,128)(2,1)S(1)} %get-tuple-element.131), channel_id=1, source_target_pairs={{0,4},{4,0},{8,12},{12,8},{16,20},{20,16},{24,28},{28,24},{1,5},{5... | collective-permute-start | bytes 196616 | tf_op jit(solution)/shard_map/ppermute | solution.py:836
  8.7 16.6 %collective-permute-start.9 = (bf16[320,768]{1,0:T(8,128)(2,1)}, bf16[320,768]{1,0:T(8,128)(2,1)}, u32[]{:S(2)}, u32[]{:S(2)}) collective-permute-start(bf16[320,768]{1,0:T(8,128)(2,1)} %get-tuple-element.132.refs_3_.refs_14_.refs_8_), channel_id=1, source_target_pairs={{0,2},{1,3},{2,0},{3,1},{4,6},{5,7},{6,4},{7,5},{8,10},{9,11},{10,... | collective-permute-start | bytes 1474568 | tf_op jit(solution)/shard_map/ppermute | solution.py:836
  10.3 21.1 %collective-permute-start.8 = (bf16[320,768]{1,0:T(8,128)(2,1)}, bf16[320,768]{1,0:T(8,128)(2,1)}, u32[]{:S(2)}, u32[]{:S(2)}) collective-permute-start(bf16[320,768]{1,0:T(8,128)(2,1)} %get-tuple-element.132.refs_3_.refs_14_.refs_8_), channel_id=1, source_target_pairs={{0,1},{1,0},{2,3},{3,2},{4,5},{5,4},{6,7},{7,6},{8,9},{9,8},{10,11... | collective-permute-start | bytes 1474568 | tf_op jit(solution)/shard_map/ppermute | solution.py:836
  10.3 5.8 %collective-permute-start.4 = (bf16[256,128]{1,0:T(8,128)(2,1)S(1)}, bf16[256,128]{1,0:T(8,128)(2,1)S(1)}, u32[]{:S(2)}, u32[]{:S(2)}) collective-permute-start(bf16[256,128]{1,0:T(8,128)(2,1)S(1)} %get-tuple-element.140), channel_id=1, source_target_pairs={{0,8},{4,12},{8,0},{12,4},{16,24},{20,28},{24,16},{28,20},{1,9},{5... | collective-permute-start | bytes 196616 | tf_op jit(solution)/shard_map/ppermute | solution.py:836
  15.3 8.5 %collective-permute-start.2 = (bf16[384,128]{1,0:T(8,128)(2,1)S(1)}, bf16[384,128]{1,0:T(8,128)(2,1)S(1)}, u32[]{:S(2)}, u32[]{:S(2)}) collective-permute-start(bf16[384,128]{1,0:T(8,128)(2,1)S(1)} %get-tuple-element.139.refs_3_.refs_6_), channel_id=1, source_target_pairs={{0,2},{1,3},{2,0},{3,1},{4,6},{5,7},{6,4},{7,5},{8,10},{9,11},{10,... | collective-permute-start | bytes 294920 | tf_op jit(solution)/shard_map/ppermute | solution.py:836
  16.1 9.8 %collective-permute-start.1 = (bf16[384,128]{1,0:T(8,128)(2,1)S(1)}, bf16[384,128]{1,0:T(8,128)(2,1)S(1)}, u32[]{:S(2)}, u32[]{:S(2)}) collective-permute-start(bf16[384,128]{1,0:T(8,128)(2,1)S(1)} %get-tuple-element.139.refs_3_.refs_6_), channel_id=1, source_target_pairs={{0,1},{1,0},{2,3},{3,2},{4,5},{5,4},{6,7},{7,6},{8,9},{9,8},{10,11... | collective-permute-start | bytes 294920 | tf_op jit(solution)/shard_map/ppermute | solution.py:836
  16.1 9.2 %collective-permute-start.11 = (bf16[256,128]{1,0:T(8,128)(2,1)S(1)}, bf16[256,128]{1,0:T(8,128)(2,1)S(1)}, u32[]{:S(2)}, u32[]{:S(2)}) collective-permute-start(bf16[256,128]{1,0:T(8,128)(2,1)S(1)} %get-tuple-element.143), channel_id=1, source_target_pairs={{0,16},{4,20},{8,24},{12,28},{16,0},{20,4},{24,8},{28,12},{1,17},{... | collective-permute-start | bytes 196616 | tf_op jit(solution)/shard_map/ppermute | solution.py:836
  25.3 6.1 %collective-permute-start.10 = (bf16[320,768]{1,0:T(8,128)(2,1)}, bf16[320,768]{1,0:T(8,128)(2,1)S(1)}, u32[]{:S(2)}, u32[]{:S(2)}) collective-permute-start(bf16[320,768]{1,0:T(8,128)(2,1)} %collective-permute-done.9.refs_16_.refs_10_), channel_id=1, source_target_pairs={{0,1},{1,0},{2,3},{3,2},{4,5},{5,4},{6,7},{7,6},{8,9},{9,8},{10,11... | collective-permute-start | bytes 1474568 | tf_op jit(solution)/shard_map/ppermute | solution.py:836
  29.7 7.9 %collective-permute-start.12 = (bf16[512,128]{1,0:T(8,128)(2,1)S(1)}, bf16[512,128]{1,0:T(8,128)(2,1)S(1)}, u32[]{:S(2)}, u32[]{:S(2)}) collective-permute-start(bf16[512,128]{1,0:T(8,128)(2,1)S(1)} %shard_map.399.refs_24_.refs_4_.refs_7_), channel_id=1, source_target_pairs={{0,1},{1,0},{2,3},{3,2},{4,5},{5,4},{6,7},{7,6},{8,9},{9,8},{10,11... | collective-permute-start | bytes 393224 | tf_op jit(solution)/shard_map/ppermute | solution.py:836
  31.4 6.3 %collective-permute-start.14 = (bf16[512,128]{1,0:T(8,128)(2,1)S(1)}, bf16[512,128]{1,0:T(8,128)(2,1)S(1)}, u32[]{:S(2)}, u32[]{:S(2)}) collective-permute-start(bf16[512,128]{1,0:T(8,128)(2,1)S(1)} %collective-permute-done.13.refs_6_), channel_id=1, source_target_pairs={{0,1},{1,0},{2,3},{3,2},{4,5},{5,4},{6,7},{7,6},{8,9},{9,8},{10,11... | collective-permute-start | bytes 393224 | tf_op jit(solution)/shard_map/ppermute | solution.py:836
  43.0 12.3 %collective-permute-start.18 = (bf16[256,768]{1,0:T(8,128)(2,1)S(1)}, bf16[256,768]{1,0:T(8,128)(2,1)S(1)}, u32[]{:S(2)}, u32[]{:S(2)}) collective-permute-start(bf16[256,768]{1,0:T(8,128)(2,1)S(1)} %get-tuple-element.165), channel_id=1, source_target_pairs={{0,1},{1,0},{2,3},{3,2},{4,5},{5,4},{6,7},{7,6},{8,9},{9,8},{10,11... | collective-permute-start | bytes 1179656 | tf_op jit(solution)/shard_map/ppermute | solution.py:836
  43.7 11.5 %collective-permute-start.16 = (bf16[256,768]{1,0:T(8,128)(2,1)S(1)}, bf16[256,768]{1,0:T(8,128)(2,1)S(1)}, u32[]{:S(2)}, u32[]{:S(2)}) collective-permute-start(bf16[256,768]{1,0:T(8,128)(2,1)S(1)} %shard_map.403.refs_3_.refs_0_), channel_id=1, source_target_pairs={{0,2},{1,3},{2,0},{3,1},{4,6},{5,7},{6,4},{7,5},{8,10},{9,11},{10,... | collective-permute-start | bytes 1179656 | tf_op jit(solution)/shard_map/ppermute | solution.py:836
  47.1 22.9 %collective-permute-start.24 = (bf16[2304,128]{1,0:T(8,128)(2,1)}, bf16[2304,128]{1,0:T(8,128)(2,1)}, u32[]{:S(2)}, u32[]{:S(2)}) collective-permute-start(bf16[2304,128]{1,0:T(8,128)(2,1)} %get-tuple-element.182), channel_id=1, source_target_pairs={{0,8},{4,12},{8,0},{12,4},{16,24},{20,28},{24,16},{28,20},{1,9},{5... | collective-permute-start | bytes 1769480 | tf_op jit(solution)/shard_map/ppermute | solution.py:836
  51.8 24.7 %collective-permute-start.26 = (bf16[2432,128]{1,0:T(8,128)(2,1)}, bf16[2432,128]{1,0:T(8,128)(2,1)}, u32[]{:S(2)}, u32[]{:S(2)}) collective-permute-start(bf16[2432,128]{1,0:T(8,128)(2,1)} %get-tuple-element.186), channel_id=1, source_target_pairs={{0,4},{4,0},{8,12},{12,8},{16,20},{20,16},{24,28},{28,24},{1,5},{5... | collective-permute-start | bytes 1867784 | tf_op jit(solution)/shard_map/ppermute | solution.py:836
  56.2 12.4 %collective-permute-start.20 = (bf16[256,768]{1,0:T(8,128)(2,1)}, bf16[256,768]{1,0:T(8,128)(2,1)}, u32[]{:S(2)}, u32[]{:S(2)}) collective-permute-start(bf16[256,768]{1,0:T(8,128)(2,1)} %shard_map.408.refs_10_.refs_0_), channel_id=1, source_target_pairs={{0,2},{1,3},{2,0},{3,1},{4,6},{5,7},{6,4},{7,5},{8,10},{9,11},{10,... | collective-permute-start | bytes 1179656 | tf_op jit(solution)/shard_map/ppermute | solution.py:836
  66.0 16.2 %collective-permute-start.19 = (bf16[2304,128]{1,0:T(8,128)(2,1)S(1)}, bf16[2304,128]{1,0:T(8,128)(2,1)S(1)}, u32[]{:S(2)}, u32[]{:S(2)}) collective-permute-start(bf16[2304,128]{1,0:T(8,128)(2,1)S(1)} %get-tuple-element.172), channel_id=1, source_target_pairs={{0,8},{4,12},{8,0},{12,4},{16,24},{20,28},{24,16},{28,20},{1,9},{5... | collective-permute-start | bytes 1769480 | tf_op jit(solution)/shard_map/ppermute | solution.py:836
  67.8 7.4 %collective-permute-start.23 = (bf16[144,768]{1,0:T(8,128)(2,1)S(1)}, bf16[144,768]{1,0:T(8,128)(2,1)S(1)}, u32[]{:S(2)}, u32[]{:S(2)}) collective-permute-start(bf16[144,768]{1,0:T(8,128)(2,1)S(1)} %get-tuple-element.181), channel_id=1, source_target_pairs={{0,2},{1,3},{2,0},{3,1},{4,6},{5,7},{6,4},{7,5},{8,10},{9,11},{10,... | collective-permute-start | bytes 663560 | tf_op jit(solution)/shard_map/ppermute | solution.py:836
  71.2 14.9 %collective-permute-start.29 = (bf16[1152,128]{1,0:T(8,128)(2,1)S(1)}, bf16[1152,128]{1,0:T(8,128)(2,1)S(1)}, u32[]{:S(2)}, u32[]{:S(2)}) collective-permute-start(bf16[1152,128]{1,0:T(8,128)(2,1)S(1)} %get-tuple-element.191), channel_id=1, source_target_pairs={{0,4},{4,0},{8,12},{12,8},{16,20},{20,16},{24,28},{28,24},{1,5},{5... | collective-permute-start | bytes 884744 | tf_op jit(solution)/shard_map/ppermute | solution.py:836
  76.0 10.0 %collective-permute-start.25 = (bf16[688,128]{1,0:T(8,128)(2,1)S(1)}, bf16[688,128]{1,0:T(8,128)(2,1)S(1)}, u32[]{:S(2)}, u32[]{:S(2)}) collective-permute-start(bf16[688,128]{1,0:T(8,128)(2,1)S(1)} %get-tuple-element.185), channel_id=1, source_target_pairs={{0,8},{4,12},{8,0},{12,4},{16,24},{20,28},{24,16},{28,20},{1,9},{5... | collective-permute-start | bytes 528392 | tf_op jit(solution)/shard_map/ppermute | solution.py:836
  77.7 17.4 %collective-permute-start.28 = (bf16[1216,128]{1,0:T(8,128)(2,1)S(1)}, bf16[1216,128]{1,0:T(8,128)(2,1)S(1)}, u32[]{:S(2)}, u32[]{:S(2)}) collective-permute-start(bf16[1216,128]{1,0:T(8,128)(2,1)S(1)} %get-tuple-element.190), channel_id=1, source_target_pairs={{0,8},{4,12},{8,0},{12,4},{16,24},{20,28},{24,16},{28,20},{1,9},{5... | collective-permute-start | bytes 933896 | tf_op jit(solution)/shard_map/ppermute | solution.py:836
  86.2 13.4 %collective-permute-start.32 = (bf16[576,128]{1,0:T(8,128)(2,1)S(1)}, bf16[576,128]{1,0:T(8,128)(2,1)S(1)}, u32[]{:S(2)}, u32[]{:S(2)}) collective-permute-start(bf16[576,128]{1,0:T(8,128)(2,1)S(1)} %get-tuple-element.211), channel_id=1, source_target_pairs={{0,16},{4,20},{8,24},{12,28},{16,0},{20,4},{24,8},{28,12},{1,17},{... | collective-permute-start | bytes 442376 | tf_op jit(solution)/shard_map/ppermute | solution.py:836
  88.9 10.2 %collective-permute-start.27 = (bf16[1648,128]{1,0:T(8,128)(2,1)S(1)}, bf16[1648,128]{1,0:T(8,128)(2,1)S(1)}, u32[]{:S(2)}, u32[]{:S(2)}) collective-permute-start(bf16[1648,128]{1,0:T(8,128)(2,1)S(1)} %get-tuple-element.189), channel_id=1, source_target_pairs={{0,4},{4,0},{8,12},{12,8},{16,20},{20,16},{24,28},{28,24},{1,5},{5... | collective-permute-start | bytes 1265672 | tf_op jit(solution)/shard_map/ppermute | solution.py:836
  95.2 15.8 %collective-permute-start.31 = (bf16[608,128]{1,0:T(8,128)(2,1)S(1)}, bf16[608,128]{1,0:T(8,128)(2,1)S(1)}, u32[]{:S(2)}, u32[]{:S(2)}) collective-permute-start(bf16[608,128]{1,0:T(8,128)(2,1)S(1)} %get-tuple-element.208), channel_id=1, source_target_pairs={{0,16},{4,20},{8,24},{12,28},{16,0},{20,4},{24,8},{28,12},{1,17},{... | collective-permute-start | bytes 466952 | tf_op jit(solution)/shard_map/ppermute | solution.py:836
  99.2 16.4 %collective-permute-start.30 = (bf16[976,128]{1,0:T(8,128)(2,1)S(1)}, bf16[976,128]{1,0:T(8,128)(2,1)S(1)}, u32[]{:S(2)}, u32[]{:S(2)}) collective-permute-start(bf16[976,128]{1,0:T(8,128)(2,1)S(1)} %get-tuple-element.195), channel_id=1, source_target_pairs={{0,16},{4,20},{8,24},{12,28},{16,0},{20,4},{24,8},{28,12},{1,17},{... | collective-permute-start | bytes 749576 | tf_op jit(solution)/shard_map/ppermute | solution.py:836
  (31 other events, 198.8 us)

commit v4 on v3

--- a/solution.py
+++ b/solution.py
@@ -11,7 +11,6 @@
 HEAD_DIM = 64
 GRID = 256
 VIS = 64
-PAIR = 2 * VIS
 CHUNK = 512
 LANES = 128
 
@@ -96,7 +95,8 @@
 
 
 RATE = 10**9
-COST_SHARE = 20.0
+COST_SHARE = 1.0
+BYTES = 0
 
 
 class Order:
@@ -105,6 +105,7 @@
         self.last = None
         self.near = []
         self.far = []
+        self.share = COST_SHARE
 
     def keep(self, value):
         if self.pinned:
@@ -179,7 +180,7 @@
                 vmem_limit_bytes=min(needed + needed // 4 + 10 * 2**20, 60 * 2**20)
             ),
             cost_estimate=pl.CostEstimate(
-                flops=int(cost * RATE * COST_SHARE), bytes_accessed=0, transcendentals=0
+                flops=int(cost * RATE * self.share), bytes_accessed=int(cost * BYTES), transcendentals=0
             ),
         )(*(self.placed(arg) for arg in args))
         if self.pinned and not final:
@@ -402,10 +403,8 @@
 
 
 def enter_kernel(
-    rows_ref, gain_ref, shift_ref, weight_ref, query_ref, value_ref, out_ref, proj_ref, weights_ref, act_ref, qkv_ref
+    rows_ref, gain_ref, shift_ref, weight_ref, query_ref, value_ref, act_ref, qkv_ref
 ):
-    weights_ref[: out_ref.shape[0], :] = out_ref[...]
-    weights_ref[out_ref.shape[0] :, :] = proj_ref[...].astype(wide_type).T.astype(low_type)
     gain, shift = wide_row(gain_ref), wide_row(shift_ref)
     query, value = wide_row(query_ref), wide_row(value_ref)
     nothing = jnp.zeros((1, HEAD_DIM), wide_type)
@@ -424,65 +423,92 @@
     over_rows(rows_ref.shape[0], CHUNK, body)
 
 
-PACKED = 256
+BLOCK = 4 * VIS
 
 
 def attention_kernel(info, heads, first, info_ref, qkv_ref, packed_ref, prob_ref, attended_ref):
-    row_half = lax.broadcasted_iota(jnp.int32, (PAIR, PAIR), 0) // VIS
-    lane = lax.broadcasted_iota(jnp.int32, (PAIR, PAIR), 1)
+    key_image = lax.broadcasted_iota(jnp.int32, (BLOCK, BLOCK), 0) // VIS
+    key_slot = lax.broadcasted_iota(jnp.int32, (BLOCK, BLOCK), 0) % VIS
+    own_image = key_image == lax.broadcasted_iota(jnp.int32, (BLOCK, BLOCK), 1) // VIS
     columns = heads * HEAD_DIM
     full = columns // LANES * LANES
-    rest = PACKED * (columns - full) // LANES
+    rest = BLOCK * (columns - full) // LANES
 
     def body(start, size):
-        for pair in range(size // PAIR):
-            rows = pl.ds(start + pair * PAIR, PAIR)
-            from_rows = pl.ds(first + start + pair * PAIR, PAIR)
-            image = (first + start + pair * PAIR) // VIS
-            limits = [info.live(info_ref, image + i) for i in range(2)]
-            last = jnp.where(row_half == 0, limits[0], VIS + limits[1])
-            live = jnp.logical_and(lane >= row_half * VIS, lane < last)
-            for head in range(heads):
-                base = head * 3 * HEAD_DIM
-                queries = qkv_ref[from_rows, base : base + HEAD_DIM]
-                key_rows = qkv_ref[from_rows, base + HEAD_DIM : base + 2 * HEAD_DIM]
-                value_rows = qkv_ref[from_rows, base + 2 * HEAD_DIM : base + 3 * HEAD_DIM]
-                scores = jnp.where(live, dot_right_t(queries, key_rows) * scale_factor, -1e30)
-                raised = jnp.exp(scores - jnp.max(scores, axis=-1, keepdims=True))
-                probs = (raised / jnp.sum(raised, axis=-1, keepdims=True)).astype(low_type)
-                prob_ref[rows, head * PAIR : (head + 1) * PAIR] = probs
-                attended_ref[rows, head * HEAD_DIM : (head + 1) * HEAD_DIM] = dot(
-                    probs, value_rows
-                ).astype(low_type)
-        at = start // PACKED * (full // LANES * PACKED + rest)
-        rows = pl.ds(start, PACKED)
+        rows = pl.ds(start, size)
+        from_rows = pl.ds(first + start, size)
+        limit = jnp.zeros((size, size), jnp.int32)
+        for image in range(size // VIS):
+            limit = jnp.where(key_image == image, info.live(info_ref, (first + start) // VIS + image), limit)
+        live = jnp.logical_and(own_image, key_slot < limit)
+        for head in range(heads):
+            base = head * 3 * HEAD_DIM
+            queries = qkv_ref[from_rows, base : base + HEAD_DIM]
+            key_rows = qkv_ref[from_rows, base + HEAD_DIM : base + 2 * HEAD_DIM]
+            value_rows = qkv_ref[from_rows, base + 2 * HEAD_DIM : base + 3 * HEAD_DIM]
+            scores = jnp.where(live, dot_right_t(key_rows, queries) * scale_factor, -1e30)
+            raised = jnp.exp(scores - jnp.max(scores, axis=0, keepdims=True))
+            probs = (raised / jnp.sum(raised, axis=0, keepdims=True)).astype(low_type)
+            prob_ref[rows, head * BLOCK : (head + 1) * BLOCK] = probs
+            attended_ref[rows, head * HEAD_DIM : (head + 1) * HEAD_DIM] = dot_left_t(
+                probs, value_rows
+            ).astype(low_type)
+        at = start // BLOCK * (full // LANES * BLOCK + rest)
         for tile in range(full // LANES):
-            packed_ref[pl.ds(at, PACKED), :] = attended_ref[rows, tile * LANES : (tile + 1) * LANES]
-            at += PACKED
+            packed_ref[pl.ds(at, BLOCK), :] = attended_ref[rows, tile * LANES : (tile + 1) * LANES]
+            at += BLOCK
         pieces = [
             attended_ref[pl.ds(start + piece * rest, rest), full:].astype(wide_type)
-            for piece in range(PACKED // rest)
+            for piece in range(BLOCK // rest)
         ]
         packed_ref[pl.ds(at, rest), :] = jnp.concatenate(pieces, axis=1).astype(low_type)
 
-    over_rows(prob_ref.shape[0], PACKED, body)
-
-
-def packed_product(packed_ref, weight_ref, start, columns):
+    over_rows(prob_ref.shape[0], BLOCK, body)
+
+
+def unpack(own, packed_refs, start, columns, out_ref):
     full = columns // LANES * LANES
     width = columns - full
-    rest = PACKED * width // LANES
-    at = start // PACKED * (full // LANES * PACKED + rest)
-    total = None
+    rest = BLOCK * width // LANES
+    at = start // BLOCK * (full // LANES * BLOCK + rest)
+    count = len(packed_refs)
     for tile in range(full // LANES):
-        part = dot(packed_ref[pl.ds(at, PACKED), :], weight_ref[tile * LANES : (tile + 1) * LANES, :])
-        total = part if total is None else total + part
-        at += PACKED
-    rows = packed_ref[pl.ds(at, rest), :].astype(wide_type)
-    left = jnp.concatenate(
-        [rows[:, piece * width : (piece + 1) * width] for piece in range(PACKED // rest)], axis=0
-    ).astype(low_type)
-    return total + dot(left, weight_ref[full:columns, :])
+        for relative, ref in enumerate(packed_refs):
+            lane = (tile * count + (own ^ relative)) * LANES
+            out_ref[:, pl.ds(pl.multiple_of(lane, LANES), LANES)] = ref[pl.ds(at, BLOCK), :]
+        at += BLOCK
+    lane = full * count
+    for other in range(0, count, LANES // width):
+        pieces = []
+        for part in range(other, other + LANES // width):
+            rows = None
+            for relative, ref in enumerate(packed_refs):
+                here = ref[pl.ds(at, rest), :].astype(wide_type)
+                rows = here if rows is None else jnp.where((own ^ relative) == part, here, rows)
+            pieces.append(
+                jnp.concatenate(
+                    [rows[:, piece * width : (piece + 1) * width] for piece in range(BLOCK // rest)], axis=0
+                )
+            )
+        out_ref[:, lane : lane + LANES] = jnp.concatenate(pieces, axis=1).astype(low_type)
+        lane += LANES
+
+
+def weights_kernel(parts, info_ref, *refs):
+    out_refs, proj_refs, (out_ref, proj_ref) = refs[:parts], refs[parts : 2 * parts], refs[2 * parts :]
+    own = info_ref[1]
+    columns = out_refs[0].shape[0]
+    full = columns // LANES * LANES
+    width = columns - full
+    for relative, (out_part_ref, proj_part_ref) in enumerate(zip(out_refs, proj_refs)):
+        part = own ^ relative
+        for tile in range(full // LANES):
+            at = pl.multiple_of((tile * parts + part) * LANES, LANES)
+            out_ref[pl.ds(at, LANES), :] = out_part_ref[tile * LANES : (tile + 1) * LANES, :]
+        at = pl.multiple_of(full * parts + part * width, 16)
+        out_ref[pl.ds(at, width), :] = out_part_ref[full:, :]
+        size = proj_part_ref.shape[1]
+        proj_ref[:, pl.ds(pl.multiple_of(part * size, LANES), size)] = proj_part_ref[...]
 
 
 def halves(upper, left_ref, weight_ref, keep_ref, sent_ref, product):
@@ -513,23 +539,15 @@
         enc_ref[pl.ds(pl.multiple_of(image * VIS, VIS), VIS), :] = ref[start : start + VIS, :]
 
 
-def paired_sum(sums):
-    while len(sums) > 1:
-        sums = [left + right for left, right in zip(sums[::2], sums[1::2])]
-    return sums[0]
-
-
 def add_kernel(left_ref, right_ref, out_ref):
     out_ref[...] = (left_ref[...].astype(wide_type) + right_ref[...].astype(wide_type)).astype(low_type)
 
 
 def forward_kernel(
-    parts, proj_columns, rows_ref, out_bias_ref, gain_ref, shift_ref, up_ref, up_bias_ref, *refs
+    parts, columns, info_ref, rows_ref, out_bias_ref, gain_ref, shift_ref, up_ref, up_bias_ref, weight_ref, *refs
 ):
     attended_refs = (refs[:parts], refs[parts : 2 * parts])
-    weight_refs = refs[2 * parts : 3 * parts]
-    hidden_ref, act_ref, acted_ref, slope_ref = refs[3 * parts :]
-    columns = weight_refs[0].shape[0] - proj_columns
+    hidden_ref, act_ref, acted_ref, slope_ref, all_ref = refs[2 * parts :]
     half = rows_ref.shape[0] // 2
     out_bias, gain, shift, up_bias = (
         wide_row(ref) for ref in (out_bias_ref, gain_ref, shift_ref, up_bias_ref)
@@ -537,12 +555,8 @@
 
     def body(which, start, size):
         rows = pl.ds(which * half + start, size)
-        total = paired_sum(
-            [
-                packed_product(attended_ref, weight_ref, start, columns)
-                for attended_ref, weight_ref in zip(attended_refs[which], weight_refs)
-            ]
-        )
+        unpack(info_ref[1], attended_refs[which], start, columns, all_ref)
+        total = dot(all_ref[...], weight_ref[...])
         hidden = rows_ref[rows, :].astype(wide_type) + total + out_bias
         hidden_ref[rows, :] = hidden
         normed, _ = normalized(hidden)
@@ -556,34 +570,40 @@
         )
 
     for which in range(2):
-        over_rows(half, PACKED, lambda start, size, which=which: body(which, start, size))
+        over_rows(half, BLOCK, lambda start, size, which=which: body(which, start, size))
 
 
 def forward_part_kernel(info_ref, acted_ref, down_ref, keep_ref, sent_ref):
     halves(info_ref[1] & 1, acted_ref, down_ref, keep_ref, sent_ref, dot)
 
 
-def forward_grad_kernel(parts, first, info_ref, slope_ref, up_ref, down_ref, *refs):
-    enc_refs, weight_refs = refs[:parts], refs[parts : 2 * parts]
-    keep_ref, sent_ref, up_low_ref, down_low_ref, bias_ref = refs[2 * parts :]
+def forward_grad_kernel(
+    parts, own, info_ref, slope_ref, up_ref, down_ref, weight_ref, *refs
+):
+    enc_refs = refs[:parts]
+    part_ref, up_low_ref, down_low_ref, bias_ref, all_ref = refs[parts:]
+    upper = info_ref[1] & 1
+    half = part_ref.shape[0]
+    first = (upper if own else 1 - upper) * half
     bias_ref[...] = jnp.zeros_like(bias_ref)
 
     def body(start, size):
+        from_rows = pl.ds(pl.multiple_of(first + start, size), size)
         rows = pl.ds(start, size)
-        out_grad = paired_sum(
-            [
-                dot(enc_ref[rows, :], weight_ref[first:, :])
-                for enc_ref, weight_ref in zip(enc_refs, weight_refs)
-            ]
-        )
-        bias_ref[0:1, :] += row_sum(out_grad)
+        for relative, enc_ref in enumerate(enc_refs):
+            columns = enc_ref.shape[1]
+            lane = pl.multiple_of((info_ref[1] ^ relative) * columns, LANES)
+            all_ref[:, pl.ds(lane, columns)] = enc_ref[from_rows, :]
+        out_grad = dot_right_t(all_ref[...], weight_ref[...])
         down_low = out_grad.astype(low_type)
         down_low_ref[rows, :] = down_low
-        up_low_ref[rows, :] = (dot_right_t(down_low, down_ref[...]) * slope_ref[rows, :]).astype(low_type)
-
-    over_rows(slope_ref.shape[0], 256, body)
-    halves(info_ref[1] & 1, up_low_ref, up_ref, keep_ref, sent_ref, dot_right_t)
-    bias_ref[1:2, :] = row_sum(up_low_ref[...].astype(wide_type))
+        up_low = dot_right_t(down_low, down_ref[...]) * slope_ref[from_rows, :]
+        up_low_ref[rows, :] = up_low.astype(low_type)
+        bias_ref[0:1, :] += row_sum(out_grad)
+        bias_ref[1:2, :] += row_sum(up_low_ref[rows, :].astype(wide_type))
+        part_ref[rows, :] = dot_right_t(up_low_ref[rows, :], up_ref[...]).astype(low_type)
+
+    over_rows(half, BLOCK, body)
 
 
 def put_blocks(exchange, info_ref, keep_ref, sent_ref, wide_ref, pad, first=0):
@@ -596,66 +616,92 @@
                 ref[at : at + share, :] = wide_ref[rows, tile * LANES : (tile + 1) * LANES].astype(low_type)
 
 
-def weight_grad_kernel(exchange, pad, info_ref, left_ref, right_ref, *refs):
-    *pos_refs, keep_ref, sent_ref, wide_ref = refs
-    wide_ref[...] = dot_left_t(left_ref[...], right_ref[...])
-    put_blocks(exchange, info_ref, keep_ref, sent_ref, wide_ref, pad)
-    for pos_ref in pos_refs:
-        put_blocks(exchange, info_ref, keep_ref, sent_ref, pos_ref, 0, wide_ref.shape[1] // LANES * pad)
+def halves_of(info_ref, refs):
+    if len(refs) == 2:
+        return refs[0][...], refs[1][...]
+    half = refs[0].shape[0] // 2
+    upper = info_ref[1] & 1
+    return tuple(
+        refs[0][pl.ds(pl.multiple_of(which * half, half), half), :] for which in (upper, 1 - upper)
+    )
+
+
+def early_grads_kernel(
+    exchanges, pad, info_ref, low_ref, low_other_ref, acted_ref, act_ref, up_ref, up_other_ref, down_keep_ref,
+    down_sent_ref, up_keep_ref, up_sent_ref, wide_ref,
+):
+    left, right = halves_of(info_ref, (low_ref, low_other_ref)), halves_of(info_ref, (acted_ref,))
+    wide_ref[...] = dot_left_t(left[0], right[0]) + dot_left_t(left[1], right[1])
+    put_blocks(exchanges[0], info_ref, down_keep_ref, down_sent_ref, wide_ref, pad)
+    left, right = halves_of(info_ref, (act_ref,)), halves_of(info_ref, (up_ref, up_other_ref))
+    wide_ref[...] = dot_left_t(left[0], right[0]) + dot_left_t(left[1], right[1])
+    put_blocks(exchanges[1], info_ref, up_keep_ref, up_sent_ref, wide_ref, pad)
 
 
 def attention_back_kernel(
-    heads, info_ref, sum_ref, sum_other_ref, hidden_ref, down_low_ref, gain_ref, weight_ref, qkv_ref, prob_ref,
-    prob_last_ref, grads_ref, attn_low_ref, own_ref, bias_ref, grad_ref, probs_ref,
+    heads, info_ref, sum_ref, sum_other_ref, hidden_ref, low_ref, low_other_ref, gain_ref, weight_ref, qkv_ref,
+    prob_ref, prob_last_ref, grads_ref, attn_low_ref, own_ref, bias_ref, grad_ref, probs_ref,
 ):
     gain = wide_row(gain_ref)
     bias_ref[...] = jnp.zeros_like(bias_ref)
-    probs_ref[: prob_ref.shape[0], :] = prob_ref[...]
-    probs_ref[prob_ref.shape[0] :, :] = prob_last_ref[...]
+    half = prob_ref.shape[0]
+    probs_ref[:half, :] = prob_ref[...]
+    probs_ref[half:, :] = prob_last_ref[...]
 
     def body(source, rows, part, size):
         normed, spread = normalized(hidden_ref[rows, :])
         grad = (sum_ref, sum_other_ref)[source][part, :].astype(wide_type)
         bias_ref[0:1, :] += row_sum(grad * normed)
         bias_ref[1:2, :] += row_sum(grad)
-        hidden_grad = down_low_ref[rows, :].astype(wide_type) + norm_back(grad, normed, spread, gain)
+        down_low = (low_ref, low_other_ref)[source][part, :].astype(wide_type)
+        hidden_grad = down_low + norm_back(grad, normed, spread, gain)
         grad_ref[rows, :] = hidden_grad
         bias_ref[2:3, :] += row_sum(hidden_grad)
         attn_low = hidden_grad.astype(low_type)
         attn_low_ref[rows, :] = attn_low
         attended_grad = dot_right_t(attn_low, weight_ref[...]).astype(low_type)
-        for pair in range(size // PAIR):
-            pair_rows = pl.ds(rows.start + pair * PAIR, PAIR)
-            for head in range(heads):
-                base = head * 3 * HEAD_DIM
-                queries = qkv_ref[pair_rows, base : base + HEAD_DIM]
-                key_rows = qkv_ref[pair_rows, base + HEAD_DIM : base + 2 * HEAD_DIM]
-                value_rows = qkv_ref[pair_rows, base + 2 * HEAD_DIM : base + 3 * HEAD_DIM]
-                probs = probs_ref[pair_rows, head * PAIR : (head + 1) * PAIR]
-                grad_rows = attended_grad[
-                    pair * PAIR : (pair + 1) * PAIR, head * HEAD_DIM : (head + 1) * HEAD_DIM
-                ]
-                value_low = dot_left_t(probs, grad_rows).astype(low_type)
-                prob_grad = dot_right_t(grad_rows, value_rows)
-                wide_probs = probs.astype(wide_type)
-                weighted = wide_probs * prob_grad
-                score_low = (
-                    weighted - wide_probs * jnp.sum(weighted, axis=-1, keepdims=True)
-                ).astype(low_type)
-                query_low = (dot(score_low, key_rows) * scale_factor).astype(low_type)
-                key_low = (dot_left_t(score_low, queries) * scale_factor).astype(low_type)
-                grads_ref[pair_rows, base : base + HEAD_DIM] = query_low
-                grads_ref[pair_rows, base + HEAD_DIM : base + 2 * HEAD_DIM] = key_low
-                grads_ref[pair_rows, base + 2 * HEAD_DIM : base + 3 * HEAD_DIM] = value_low
+        for head in range(heads):
+            base = head * 3 * HEAD_DIM
+            queries = qkv_ref[rows, base : base + HEAD_DIM]
+            key_rows = qkv_ref[rows, base + HEAD_DIM : base + 2 * HEAD_DIM]
+            value_rows = qkv_ref[rows, base + 2 * HEAD_DIM : base + 3 * HEAD_DIM]
+            probs = probs_ref[rows, head * BLOCK : (head + 1) * BLOCK]
+            grad_rows = attended_grad[:, head * HEAD_DIM : (head + 1) * HEAD_DIM]
+            value_low = dot(probs, grad_rows).astype(low_type)
+            prob_grad = dot_right_t(value_rows, grad_rows)
+            wide_probs = probs.astype(wide_type)
+            weighted = wide_probs * prob_grad
+            score_low = (
+                weighted - wide_probs * jnp.sum(weighted, axis=0, keepdims=True)
+            ).astype(low_type)
+            query_low = (dot_left_t(score_low, key_rows) * scale_factor).astype(low_type)
+            key_low = (dot(score_low, queries) * scale_factor).astype(low_type)
+            grads_ref[rows, base : base + HEAD_DIM] = query_low
+            grads_ref[rows, base + HEAD_DIM : base + 2 * HEAD_DIM] = key_low
+            grads_ref[rows, base + 2 * HEAD_DIM : base + 3 * HEAD_DIM] = value_low
 
     both_halves(info_ref[1] & 1, sum_ref.shape[0], body)
     share = own_ref.shape[0]
     own_ref[...] = grad_ref[pl.ds(pl.multiple_of(info_ref[1] * share, share), share), :]
 
 
+def views(ref, sizes):
+    starts = [sum(sizes[:at]) for at in range(len(sizes))]
+    return [ref.at[pl.ds(start, size), :] for start, size in zip(starts, sizes)]
+
+
+def step_kernel(moves, sizes, info_ref, *refs):
+    parted = [None if size is None else views(ref, size) for ref, size in zip(refs, sizes)]
+    for exchange, step, sources, kept, (sent, place) in moves:
+        pairs = []
+        for _, keep, (came, at) in sources:
+            pairs += [refs[keep], parted[came][at]]
+        exchange.kernel(step, [part for part, _, _ in sources], info_ref, *pairs, refs[kept], parted[sent][place])
+
+
 def late_grads_kernel(
-    exchange, pad, info_ref, act_ref, grads_ref, attn_low_ref, first_ref, last_ref, keep_ref, sent_ref, bias_ref,
-    wide_ref,
+    exchanges, pad, middle, info_ref, act_ref, grads_ref, attn_low_ref, first_ref, last_ref, keep_ref, sent_ref,
+    turned_keep_ref, turned_sent_ref, bias_ref, wide_ref,
 ):
     columns = grads_ref.shape[1]
     half, first = first_ref.shape
@@ -663,7 +709,11 @@
         attn_low_ref[half:, :], last_ref[...]
     )
     wide_ref[:, first : first + columns] = dot_left_t(act_ref[...], grads_ref[...])
-    put_blocks(exchange, info_ref, keep_ref, sent_ref, wide_ref, pad)
+    put_blocks(exchanges[0], info_ref, keep_ref, sent_ref, wide_ref.at[:, pl.ds(0, middle)], pad)
+    put_blocks(
+        exchanges[1], info_ref, turned_keep_ref, turned_sent_ref,
+        wide_ref.at[:, pl.ds(middle, wide_ref.shape[1] - middle)], pad,
+    )
     bias_ref[...] = row_sum(grads_ref[...].astype(wide_type))
 
 
@@ -683,7 +733,15 @@
     return rows[0:1] + rows[1:2], rows[2:3] + rows[3:4]
 
 
-def input_part_kernel(info_ref, rows_ref, grads_ref, weight_ref, keep_ref, sent_ref, part_ref, bias_ref):
+def norm_kernel(rows_ref, normed_ref):
+    def body(start, size):
+        rows = pl.ds(start, size)
+        normed_ref[rows, :] = normalized(rows_ref[rows, :].astype(wide_type))[0].astype(low_type)
+
+    over_rows(rows_ref.shape[0], CHUNK, body)
+
+
+def input_part_kernel(info_ref, normed_ref, grads_ref, weight_ref, keep_ref, sent_ref, part_ref, bias_ref):
     lower_bit = info_ref[1] & 1
     bias_ref[...] = jnp.zeros_like(bias_ref)
 
@@ -691,11 +749,10 @@
         rows = pl.ds(start, size)
         grad = dot(grads_ref[rows, :], weight_ref[...])
         part_ref[rows, :] = grad
-        normed, _ = normalized(rows_ref[rows, :].astype(wide_type))
-        bias_ref[0:1, :] += row_sum(grad * normed)
+        bias_ref[0:1, :] += row_sum(grad * normed_ref[rows, :].astype(wide_type))
         bias_ref[1:2, :] += row_sum(grad)
 
-    over_rows(rows_ref.shape[0], CHUNK, body)
+    over_rows(normed_ref.shape[0], CHUNK, body)
     size = keep_ref.shape[0] - EXTRA
     share = size // (lax.axis_size("mp") // 2)
     for out_ref, which in ((sent_ref, 1 - lower_bit), (keep_ref, lower_bit)):
@@ -749,9 +806,8 @@
 
 
 def encoded_kernel(
-    info, exchange, heads, info_ref, hidden_ref, sum_ref, sum_other_ref, down_bias_ref, weight_ref, bias_ref, enc_ref,
-    mask_ref, grads_ref, second_ref, qkv_ref, first_ref, first_other_ref, keep_ref, sent_ref, low_ref, wide_ref,
-    encoded_ref, rows_ref,
+    info_ref, hidden_ref, sum_ref, sum_other_ref, down_bias_ref, weight_ref, bias_ref, enc_ref, encoded_ref, wide_ref,
+    low_ref,
 ):
     down_bias, bias = wide_row(down_bias_ref), wide_row(bias_ref)
 
@@ -763,14 +819,21 @@
 
     both_halves(info_ref[1] & 1, sum_ref.shape[0], body)
     wide_ref[...] = dot_left_t(low_ref[...], enc_ref[...])
+
+
+def last_kernel(
+    info, exchange, heads, pad, info_ref, encoded_ref, wide_ref, enc_ref, pos_ref, mask_ref, grads_ref, grads_other_ref,
+    second_ref, qkv_ref, first_ref, first_other_ref, keep_ref, sent_ref, rows_ref,
+):
     put_blocks(exchange, info_ref, keep_ref, sent_ref, wide_ref, 0)
+    put_blocks(exchange, info_ref, keep_ref, sent_ref, pos_ref, 0, pad)
     for ref, indices in exchange.targets(0, info_ref, keep_ref, sent_ref):
         at = exchange.moved_at(0)
         for index in indices:
             image = info.image(info_ref, index)
             ref[at : at + VIS, :] = encoded_ref[pl.ds(pl.multiple_of(image * VIS, VIS), VIS), :]
             at += VIS
-    qkv = qkv_ref[...]
+    qkv, early = qkv_ref[...], grads_ref[...] + grads_other_ref[...]
     empty = jnp.zeros((1, 2 * LANES - heads * HEAD_DIM), wide_type)
     spread = []
     for part in (0, 2):
@@ -781,9 +844,9 @@
     other = get_extra(first_other_ref, first_ref.shape[0] - EXTRA)
     put_rows(
         (
-            jnp.concatenate(spread, axis=1), grads_ref[1:2, :], row_sum(enc_ref[...].astype(wide_type)),
-            mask_ref[...], own[0] + other[0], own[1] + other[1], second_ref[0:1, :], second_ref[1:2, :],
-            second_ref[2:3, :], grads_ref[0:1, :],
+            jnp.concatenate(spread, axis=1), early[1:2], row_sum(enc_ref[...].astype(wide_type)), mask_ref[...],
+            own[0] + other[0], own[1] + other[1], second_ref[0:1, :], second_ref[1:2, :], second_ref[2:3, :],
+            early[0:1],
         ),
         rows_ref,
     )
@@ -792,10 +855,11 @@
 
 
 def late_out_kernel(
-    info, exchange, pad, info_ref, seen_ref, keep_ref, other_ref, mask_ref, layout_ref, grids_ref, out_ref, qkv_ref,
-    proj_ref, *refs
+    info, exchange, turned_exchange, pad, middle, sizes, info_ref, seen_ref, keep_ref, turned_ref, came_ref, mask_ref,
+    layout_ref, grids_ref, out_ref, qkv_ref, proj_ref, pos_ref, *refs
 ):
     *vector_refs, wide_ref, rows_ref = refs
+    other_ref, turned_other_ref = views(came_ref, sizes)
     cells = lax.broadcasted_iota(jnp.int32, (GRID, VIS), 0)
     cell_column = lax.broadcasted_iota(jnp.int32, (GRID, 1), 0)
     mask_row = wide_row(mask_ref)
@@ -811,24 +875,26 @@
     share = proj_ref.shape[0]
     tiles = wide_ref.shape[1] // LANES
     for tile in range(tiles):
-        wide_ref[:, tile * LANES : (tile + 1) * LANES] = exchange.total(keep_ref, other_ref, tile * pad, share)
+        here = (exchange, keep_ref, other_ref, tile) if tile < middle else (
+            turned_exchange, turned_ref, turned_other_ref, tile - middle
+        )
+        wide_ref[:, tile * LANES : (tile + 1) * LANES] = here[0].total(here[1], here[2], here[3] * pad, share)
     columns = out_ref.shape[0]
     wide_out = -(-columns // LANES) * LANES
     out_ref[...] = wide_ref[:, :wide_out].T[:columns]
     qkv_ref[...] = wide_ref[:, columns:]
-    proj_ref[...] = exchange.total(keep_ref, other_ref, tiles * pad, share)
+    proj_ref[...] = exchange.total(keep_ref, other_ref, middle * pad, share)
+    pos_ref[...] = exchange.total(keep_ref, other_ref, (middle + 1) * pad, pos_ref.shape[0])
     rows_ref[...] = exchange.shared_total(keep_ref, other_ref)
     take_rows(rows_ref, vector_refs)
 
 
-def early_out_kernel(exchange, pad, keep_ref, other_ref, out_ref, *pos_refs):
-    tiles = out_ref.shape[1] // LANES
-    for tile in range(tiles):
-        out_ref[:, tile * LANES : (tile + 1) * LANES] = exchange.total(
-            keep_ref, other_ref, tile * pad, out_ref.shape[0]
-        )
-    for pos_ref in pos_refs:
-        pos_ref[...] = exchange.total(keep_ref, other_ref, tiles * pad, pos_ref.shape[0])
+def early_out_kernel(exchanges, pad, *refs):
+    for exchange, keep_ref, other_ref, out_ref in zip(exchanges, refs[:2], refs[2:4], refs[4:]):
+        for tile in range(out_ref.shape[1] // LANES):
+            out_ref[:, tile * LANES : (tile + 1) * LANES] = exchange.total(
+                keep_ref, other_ref, tile * pad, out_ref.shape[0]
+            )
 
 
 def swap(value, axis, bit):
@@ -865,18 +931,22 @@
     turned_low = jnp.asarray(np.ascontiguousarray(table_low.transpose(0, 2, 1)))
     table_high, table_low = jnp.asarray(table_high), jnp.asarray(table_low)
     qkv_weight_t = qkv_weight.T
-    run.leave(owner, visible, patches, grid_cotangent)
+    run.leave(owner, visible, patches, grid_cotangent, turned_high, turned_low, table_high, table_low, decoder_pos)
     info = Info(count)
     bits = tuple(range(count.bit_length() - 1))
     late_columns = qkv_columns + head_columns
     turned = (1, 0) + bits[2:]
     back_exchange = Exchange(count, bits, 0, moved=VIS)
-    up_exchange = Exchange(count, bits, units // LANES * pads[0] + pads[1])
+    far = (0, 2, 1) + bits[3:]
+    up_exchange = Exchange(count, far, units // LANES * pads[0])
     down_exchange = Exchange(count, turned, units // LANES * pads[0])
-    late_exchange = Exchange(count, turned, late_columns // LANES * pads[0])
-    last_exchange = Exchange(count, turned, pads[0], moved=VIS, shared=VECTOR_ROWS)
+    tiles = late_columns // LANES
+    middle = tiles // 3
+    late_exchange = Exchange(count, bits, middle * pads[0])
+    turned_exchange = Exchange(count, turned, (tiles - middle) * pads[0])
+    last_exchange = Exchange(count, bits, sum(pads), moved=VIS, shared=VECTOR_ROWS)
     joint_exchange = Exchange(
-        count, turned, late_exchange.block + last_exchange.block, moved=VIS, shared=VECTOR_ROWS
+        count, bits, late_exchange.block + last_exchange.block, moved=VIS, shared=VECTOR_ROWS
     )
 
     def low(*shape):
@@ -888,9 +958,7 @@
     def moved(value, axis, bit):
         return run.keep(swap(value, axis, bit))
 
-    def model_steps(keep, sent):
-        received = moved(sent, "mp", 1)
-        yield
+    def model_steps(keep, received):
         (total,) = run(add_kernel, [low(half, width)], (keep, received), cost=0.6)
         bit = 2
         while bit < parts:
@@ -927,6 +995,26 @@
             keep, received = data_step(step, exchange, [(exchange, keep, received)])
             yield keep, received
 
+    def steps(kept, arrays, moves, sends):
+        first = len(kept) + len(arrays)
+        sizes = [None] * len(kept) + [size for _, size in arrays] + [None] * len(moves)
+        sizes += [size for _, size in sends]
+        placed = [
+            (exchange, step, sources, first + at, (first + len(moves) + to[0], to[1]))
+            for at, (exchange, step, sources, to) in enumerate(moves)
+        ]
+        results = run(
+            lambda *refs: step_kernel(placed, sizes, *refs),
+            [low(exchange.rows(step), LANES) for exchange, step, _, _ in moves]
+            + [low(sum(size), LANES) for _, size in sends],
+            (facts, *kept) + tuple(array for array, _ in arrays),
+            (SMEM,) + (VMEM,) * first,
+            cost=1.0,
+        )
+        return results[: len(moves)], [
+            moved(sent, "dp", 2**bit) for sent, (bit, _) in zip(results[len(moves) :], sends)
+        ]
+
     def finish_pair(steps):
         *_, last = steps
         return last
@@ -938,6 +1026,8 @@
             except StopIteration as stop:
                 return stop.value
 
+    out_all = model_gather(out_weight)
+    proj_all = model_gather(proj_weight)
     (
         back_keep, back_sent, facts, seen, patch_rows, qkv_weight_t, first_gain, first_shift, query_bias, value_bias,
         out_weight, proj_weight,
@@ -958,20 +1048,17 @@
     )
     back_steps = data_steps(back_exchange, back_keep, back_sent)
     next(back_steps)
-    weights, act_one, qkv = run(
+    act_one, qkv = run(
         enter_kernel,
-        [low(head_columns + columns, width), low(rows, width), low(rows, qkv_columns)],
-        (
-            patch_rows, first_gain, first_shift, qkv_weight_t, query_bias, value_bias, out_weight, proj_weight
-        ),
+        [low(rows, width), low(rows, qkv_columns)],
+        (patch_rows, first_gain, first_shift, qkv_weight_t, query_bias, value_bias),
         cost=1.2,
     )
-    weights = model_gather(weights)
     next(back_steps)
     packed_rows = half * head_columns // LANES
     packed, first_probs, first_attended, out_bias, second_gain, second_shift, up_weight, up_bias = run(
         lambda *refs: attention_kernel(info, heads, 0, *refs),
-        [low(packed_rows, LANES), low(half, heads * PAIR), low(half, head_columns)],
+        [low(packed_rows, LANES), low(half, heads * BLOCK), low(half, head_columns)],
         (facts, qkv),
         (SMEM, VMEM),
         stage=(out_bias, second_gain, second_shift, up_weight, up_bias),
@@ -981,13 +1068,20 @@
     back_own, back_other = finish_pair(back_steps)
     packed, last_probs, last_attended, down_weight, down_bias, proj_bias = run(
         lambda *refs: attention_kernel(info, heads, half, *refs),
-        [low(packed_rows, LANES), low(half, heads * PAIR), low(half, head_columns)],
+        [low(packed_rows, LANES), low(half, heads * BLOCK), low(half, head_columns)],
         (facts, qkv),
         (SMEM, VMEM),
         stage=(down_weight, down_bias, proj_bias),
         cost=2.5,
     )
     last_all = model_gather(packed)
+    out_whole, proj_whole = run(
+        lambda *refs: weights_kernel(parts, *refs),
+        [low(parts * head_columns, width), low(width, parts * columns)],
+        (facts,) + out_all + proj_all,
+        (SMEM,) + (VMEM,) * (2 * parts),
+        cost=0.0,
+    )
     (enc_grad,) = run(
         lambda *refs: back_kernel(info, back_exchange, *refs),
         [low(rows, columns)],
@@ -996,23 +1090,31 @@
         cost=0.4,
     )
     enc_all = model_gather(enc_grad)
-    (
-        hidden, act_two, acted, slope, turned_high, turned_low, table_high, table_low, decoder_pos, grid_cotangent
-    ) = run(
-        lambda *refs: forward_kernel(parts, columns, *refs),
+    hidden, act_two, acted, slope = run(
+        lambda *refs: forward_kernel(parts, head_columns, *refs),
         [wide(rows, width), low(rows, width), low(rows, units), wide(rows, units)],
-        (patch_rows, out_bias, second_gain, second_shift, up_weight, up_bias) + first_all + last_all + weights,
-        stage=(turned_high, turned_low, table_high, table_low, decoder_pos, grid_cotangent),
+        (facts, patch_rows, out_bias, second_gain, second_shift, up_weight, up_bias, out_whole)
+        + first_all
+        + last_all,
+        (SMEM,) + (VMEM,) * (7 + 2 * parts),
+        scratch=[pltpu.VMEM((BLOCK, parts * head_columns), low_type)],
         cost=2.6,
     )
-    keep, sent, up_low, down_low, bias_grads = run(
-        lambda *refs: forward_grad_kernel(parts, head_columns, *refs),
-        [low(half, width), low(half, width), low(rows, units), low(rows, width), wide(2, width)],
-        (facts, slope, up_weight, down_weight) + enc_all + weights,
-        (SMEM,) + (VMEM,) * (3 + 2 * parts),
-        cost=2.0,
-    )
-    second_steps = model_steps(keep, sent)
+
+    def forward_grad(own):
+        return run(
+            lambda *refs: forward_grad_kernel(parts, own, *refs),
+            [low(half, width), low(half, units), low(half, width), wide(2, width)],
+            (facts, slope, up_weight, down_weight, proj_whole) + enc_all,
+            (SMEM,) + (VMEM,) * (4 + parts),
+            scratch=[pltpu.VMEM((BLOCK, parts * columns), low_type)],
+            cost=1.2,
+        )
+
+    sent, up_low_other, down_low_other, bias_grads_other = forward_grad(False)
+    second_other = moved(sent, "mp", 1)
+    keep, up_low, down_low, bias_grads = forward_grad(True)
+    second_steps = model_steps(keep, second_other)
     next(second_steps)
     keep, sent = run(
         forward_part_kernel,
@@ -1021,64 +1123,64 @@
         (SMEM, VMEM, VMEM),
         cost=0.7,
     )
-    next(second_steps)
-    out_steps = model_steps(keep, sent)
-    next(out_steps)
-
-    def weight_grad(exchange, left, right, *pos):
-        keep, sent = run(
-            lambda *refs: weight_grad_kernel(exchange, pads[0], *refs),
-            [low(exchange.rows(0), LANES)] * 2,
-            (facts, left, right) + pos,
-            (SMEM,) + (VMEM,) * (2 + len(pos)),
-            scratch=[pltpu.VMEM((width, right.shape[1]), wide_type)],
-            cost=1.9,
-        )
-        steps = data_steps(exchange, keep, sent)
-        next(steps)
-        return steps
-
-    down_steps = weight_grad(down_exchange, down_low, acted)
+    out_steps = model_steps(keep, moved(sent, "mp", 1))
+
+    down_keep, down_sent, up_keep, up_sent = run(
+        lambda *refs: early_grads_kernel((down_exchange, up_exchange), pads[0], *refs),
+        [low(down_exchange.rows(0), LANES)] * 2 + [low(up_exchange.rows(0), LANES)] * 2,
+        (facts, down_low, down_low_other, acted, act_two, up_low, up_low_other),
+        (SMEM,) + (VMEM,) * 6,
+        scratch=[pltpu.VMEM((width, units), wide_type)],
+        cost=2.2,
+    )
+    down_pair = (down_keep, moved(down_sent, "dp", 2 ** turned[0]))
+    up_pair = (up_keep, moved(up_sent, "dp", 2 ** bits[0]))
     pos_grad_own, mask_grad, layouts = run(
         lambda *refs: position_kernel(info, *refs),
         [wide(GRID, columns), wide(1, columns), wide(3, GRID, columns)],
         (facts, seen, grid_cotangent, turned_high, turned_low, table_high, table_low, decoder_pos),
         (SMEM,) + (VMEM,) * 7,
         scratch=[pltpu.VMEM((3, GRID, columns), wide_type)],
-        cost=1.0,
-    )
-    up_steps = weight_grad(up_exchange, act_two, up_low, pos_grad_own)
+        cost=20.0,
+    )
+    next(out_steps)
     next(second_steps)
-    next(out_steps)
     second_sum, second_other = finish(second_steps)
+    (normed_low,) = run(norm_kernel, [low(rows, width)], (patch_rows,), cost=40.0)
+    run.share = 3.0
     grads, attn_low, own_grad, second_grads = run(
         lambda *refs: attention_back_kernel(heads, *refs),
         [low(rows, qkv_columns), low(rows, width), wide(own_rows, width), wide(3, width)],
         (
-            facts, second_sum, second_other, hidden, down_low, second_gain, out_weight, qkv, first_probs, last_probs
+            facts, second_sum, second_other, hidden, down_low, down_low_other, second_gain, out_weight, qkv,
+            first_probs, last_probs,
         ),
-        (SMEM,) + (VMEM,) * 9,
-        scratch=[pltpu.VMEM((rows, width), wide_type), pltpu.VMEM((rows, heads * PAIR), low_type)],
+        (SMEM,) + (VMEM,) * 10,
+        scratch=[pltpu.VMEM((rows, width), wide_type), pltpu.VMEM((rows, heads * BLOCK), low_type)],
         cost=5.5,
     )
     in_keep, in_sent = run(
         input_part_kernel,
         [low(half + EXTRA, width)] * 2,
-        (facts, patch_rows, grads, qkv_weight_t),
+        (facts, normed_low, grads, qkv_weight_t),
         (SMEM,) + (VMEM,) * 3,
         scratch=[pltpu.VMEM((rows, width), wide_type), pltpu.VMEM((2, width), wide_type)],
         cost=2.0,
     )
     in_other = moved(in_sent, "mp", 1)
-    keep, sent, qkv_bias_grad = run(
-        lambda *refs: late_grads_kernel(late_exchange, pads[0], *refs),
-        [low(late_exchange.rows(0), LANES)] * 2 + [wide(1, qkv_columns)],
+    in_other = moved(in_sent, "mp", 1)
+    late_keep, late_sent, turned_keep, turned_sent, qkv_bias_grad = run(
+        lambda *refs: late_grads_kernel((late_exchange, turned_exchange), pads[0], middle * LANES, *refs),
+        [low(late_exchange.rows(0), LANES)] * 2
+        + [low(turned_exchange.rows(0), LANES)] * 2
+        + [wide(1, qkv_columns)],
         (facts, act_one, grads, attn_low, first_attended, last_attended),
         (SMEM,) + (VMEM,) * 5,
         scratch=[pltpu.VMEM((width, late_columns), wide_type)],
-        cost=2.5,
-    )
-    late_keep, late_other = next(data_steps(late_exchange, keep, sent))
+        cost=40.0,
+    )
+    turned_came = moved(turned_sent, "dp", 2 ** turned[0])
+    late_came = moved(late_sent, "dp", 2 ** bits[0])
     bit = 1
     size = half
     while 2**bit < parts:
@@ -1094,26 +1196,37 @@
         size //= 2
         bit += 1
     next(out_steps)
-    next(down_steps)
+    early_sizes = [[exchange.rows(1)] for exchange in (up_exchange, down_exchange)]
+    (up_keep, down_keep), (up_came, down_came) = steps(
+        (up_pair[0], down_pair[0]),
+        ((up_pair[1], [up_exchange.rows(0)]), (down_pair[1], [down_exchange.rows(0)])),
+        [
+            (up_exchange, 1, [(up_exchange, 0, (2, 0))], (0, 0)),
+            (down_exchange, 1, [(down_exchange, 1, (3, 0))], (1, 0)),
+        ],
+        [(far[1], early_sizes[0]), (turned[1], early_sizes[1])],
+    )
     out_sum, out_other = finish(out_steps)
-    keep, sent = run(
-        lambda *refs: encoded_kernel(info, last_exchange, heads, *refs),
+    encoded, proj_grad = run(
+        encoded_kernel,
+        [low(rows, columns), wide(width, columns)],
+        (facts, hidden, out_sum, out_other, down_bias, proj_weight, proj_bias, enc_grad),
+        (SMEM,) + (VMEM,) * 7,
+        scratch=[pltpu.VMEM((rows, width), low_type)],
+        cost=1.0,
+    )
+    last_keep, last_sent = run(
+        lambda *refs: last_kernel(info, last_exchange, heads, pads[0], *refs),
         [low(last_exchange.rows(0), LANES)] * 2,
         (
-            facts, hidden, out_sum, out_other, down_bias, proj_weight, proj_bias, enc_grad, mask_grad, bias_grads,
-            second_grads, qkv_bias_grad, in_keep, in_other,
+            facts, encoded, proj_grad, enc_grad, pos_grad_own, mask_grad, bias_grads, bias_grads_other, second_grads,
+            qkv_bias_grad, in_keep, in_other,
         ),
-        (SMEM,) + (VMEM,) * 13,
-        scratch=[
-            pltpu.VMEM((rows, width), low_type),
-            pltpu.VMEM((width, columns), wide_type),
-            pltpu.VMEM((rows, columns), low_type),
-            pltpu.VMEM((VECTOR_ROWS, LANES), wide_type),
-        ],
-        cost=2.2,
-    )
-    last_keep, last_other = next(data_steps(last_exchange, keep, sent))
-    next(up_steps)
+        (SMEM,) + (VMEM,) * 11,
+        scratch=[pltpu.VMEM((VECTOR_ROWS, LANES), wide_type)],
+        cost=0.6,
+    )
+    last_came = moved(last_sent, "dp", 2 ** bits[0])
     (input_grad,) = run(
         input_grad_kernel,
         [low(own_rows, width)],
@@ -1122,39 +1235,77 @@
         final=True,
         cost=0.8,
     )
-    late_keep, late_other = data_step(
-        1, joint_exchange, [(late_exchange, late_keep, late_other), (last_exchange, last_keep, last_other)]
-    )
-    down_keep, down_other = finish_pair(down_steps)
-    up_keep, up_other = finish_pair(up_steps)
-    for step in range(2, len(bits)):
-        late_keep, late_other = data_step(step, joint_exchange, [(joint_exchange, late_keep, late_other)])
-    (down_weight_grad,) = run(
-        lambda *refs: early_out_kernel(down_exchange, pads[0], *refs),
-        [wide(share, units)],
-        (down_keep, down_other),
+
+    early = (up_exchange, down_exchange)
+    late = (joint_exchange, turned_exchange)
+    joint_sizes = [[exchange.rows(1)] for exchange in late]
+    (late_keep, turned_keep), late_came = steps(
+        (late_keep, last_keep, turned_keep),
+        (
+            (late_came, [late_exchange.rows(0)]), (last_came, [last_exchange.rows(0)]),
+            (turned_came, [turned_exchange.rows(0)]),
+        ),
+        [
+            (joint_exchange, 1, [(late_exchange, 0, (3, 0)), (last_exchange, 1, (4, 0))], (0, 0)),
+            (turned_exchange, 1, [(turned_exchange, 2, (5, 0))], (1, 0)),
+        ],
+        [(bits[1], joint_sizes[0]), (turned[1], joint_sizes[1])],
+    )
+    old_sizes, early_sizes = early_sizes, [[exchange.rows(2)] for exchange in early]
+    (up_keep, down_keep), early_came = steps(
+        (up_keep, down_keep),
+        ((up_came, old_sizes[0]), (down_came, old_sizes[1])),
+        [
+            (up_exchange, 2, [(up_exchange, 0, (2, 0))], (0, 0)),
+            (down_exchange, 2, [(down_exchange, 1, (3, 0))], (1, 0)),
+        ],
+        [(far[2], early_sizes[0]), (turned[2], early_sizes[1])],
+    )
+    last_sizes = [exchange.rows(2) for exchange in late]
+    (late_keep, turned_keep), (late_came,) = steps(
+        (late_keep, turned_keep),
+        ((late_came[0], joint_sizes[0]), (late_came[1], joint_sizes[1])),
+        [
+            (joint_exchange, 2, [(joint_exchange, 0, (2, 0))], (0, 0)),
+            (turned_exchange, 2, [(turned_exchange, 1, (3, 0))], (0, 1)),
+        ],
+        [(2, last_sizes)],
+    )
+    for step in range(3, len(bits)):
+        old_sizes, early_sizes = early_sizes, [[exchange.rows(step)] for exchange in early]
+        (up_keep, down_keep), early_came = steps(
+            (up_keep, down_keep),
+            ((early_came[0], old_sizes[0]), (early_came[1], old_sizes[1])),
+            [(exchange, step, [(exchange, at, (2 + at, 0))], (at, 0)) for at, exchange in enumerate(early)],
+            [(step, early_sizes[0]), (step, early_sizes[1])],
+        )
+        old_sizes, last_sizes = last_sizes, [exchange.rows(step) for exchange in late]
+        (late_keep, turned_keep), (late_came,) = steps(
+            (late_keep, turned_keep),
+            ((late_came, old_sizes),),
+            [(exchange, step, [(exchange, at, (2, at))], (0, at)) for at, exchange in enumerate(late)],
+            [(step, last_sizes)],
+        )
+    up_weight_grad, down_weight_grad = run(
+        lambda *refs: early_out_kernel(early, pads[0], *refs),
+        [wide(share, units)] * 2,
+        (up_keep, down_keep, *early_came),
         final=True,
-        cost=0.8,
-    )
-    up_weight_grad, pos_grad = run(
-        lambda *refs: early_out_kernel(up_exchange, pads[0], *refs),
-        [wide(share, units), wide(pos_share, columns)],
-        (up_keep, up_other),
-        final=True,
-        cost=0.8,
+        cost=1.0,
     )
     (
-        grids, out_weight_grad, qkv_weight_grad, proj_weight_grad, query_bias_grad, value_bias_grad, up_bias_grad,
-        proj_bias_grad, mask_token_grad, first_gain_grad, first_shift_grad, second_gain_grad, second_shift_grad,
-        out_bias_grad, down_bias_grad,
+        grids, out_weight_grad, qkv_weight_grad, proj_weight_grad, pos_grad, query_bias_grad, value_bias_grad,
+        up_bias_grad, proj_bias_grad, mask_token_grad, first_gain_grad, first_shift_grad, second_gain_grad,
+        second_shift_grad, out_bias_grad, down_bias_grad,
     ) = run(
-        lambda *refs: late_out_kernel(info, joint_exchange, pads[0], *refs),
+        lambda *refs: late_out_kernel(info, joint_exchange, turned_exchange, pads[0], middle, last_sizes, *refs),
         [
-            low(count, GRID, columns), wide(head_columns, share), wide(share, qkv_columns), wide(share, columns)
+            low(count, GRID, columns), wide(head_columns, share), wide(share, qkv_columns), wide(share, columns),
+            wide(pos_share, columns),
         ]
         + [wide(size) for size in (head_columns, head_columns, units, columns, columns) + (width,) * 6],
-        (facts, seen, late_keep, late_other, mask_token, layouts),
-        (SMEM,) + (VMEM,) * 5,
+        (facts, seen, late_keep, turned_keep, late_came, mask_token, layouts),
+        (SMEM,) + (VMEM,) * 6,
         scratch=[pltpu.VMEM((share, late_columns), wide_type), pltpu.VMEM((VECTOR_ROWS, LANES), wide_type)],
         final=True,
         cost=2.5,

time: 118 us -> 105 us (0.89)
  Pallas kernels: 44.6 us -> 36.3 us
  waiting for transfers between devices: 42.1 us -> 36.6 us
  starting transfers between devices: 29.1 us -> 30.3 us
    pallas_call x32, Pallas kernels: 44.6 us -> 36.3 us  [__call__(): pl.pallas_call(body, out_shape=tuple(shapes) + tuple((pltpu.VMEM(array.sh...]
    ppermute x33 -> x38, waiting for transfers between devices: 42.1 us -> 36.6 us  [swap(): return lax.ppermute(value, axis, [(i, i ^ bit) for i in range(count)])]
    ppermute x33 -> x38, starting transfers between devices: 29.1 us -> 30.3 us  [swap(): return lax.ppermute(value, axis, [(i, i ^ bit) for i in range(count)])]
  transfers between devices with their start and end apart: 33 -> 38, of which waited for: 13 -> 15; matrix products, arithmetic and copies ran while one was open for 0% -> 0% of each run, Pallas kernels for 31% -> 32%
where the time goes in v4:
time: 105 us
  waiting for transfers between devices  36.6 us (35%)
  Pallas kernels  36.3 us (35%)
  starting transfers between devices  30.3 us (29%)
  between operations  1.15 us (1%)
    ppermute x38, waiting for transfers between devices, swap(): return lax.ppermute(value, axis, [(i, i ^ bit) for i in range(count)])  36.6 us
    pallas_call x32, Pallas kernels, __call__(): pl.pallas_call(body, out_shape=tuple(shapes) + tuple((pltpu.VMEM(array.sh...  36.3 us
    ppermute x38, starting transfers between devices, swap(): return lax.ppermute(value, axis, [(i, i ^ bit) for i in range(count)])  30.3 us
  transfers between devices with their start and end apart: 38, of which 15 were waited for; matrix products, arithmetic and copies ran while one was open for 0% of the time, Pallas kernels for 32%

profile of v4, /device:TPU:0, one launch (start us, length us, event | category | flops | bytes accessed | tf_op | source)
XLA Modules:
  0.0 104.5 jit_solution(16833712047033900301)
XLA Ops:
  1.2 2.6 %collective-permute-start.5 = (bf16[768,128]{1,0:T(8,128)(2,1)}, bf16[768,128]{1,0:T(8,128)(2,1)S(1)}, u32[]{:S(2)}, u32[]{:S(2)}) collective-permute-start(bf16[768,128]{1,0:T(8,128)(2,1)} %refs_5_.7), channel_id=1, source_target_pairs={{0,2},{1,3},{2,0},{3,1},{4,6},{5,7},{6,4},{7,5},{8,10},{9,11},{10,... | collective-permute-start | bytes 589832 | tf_op jit(solution)/shard_map/ppermute | solution.py:902
  4.3 3.0 %shard_map.393 = (bf16[256,128]{1,0:T(8,128)(2,1)S(1)}, bf16[256,128]{1,0:T(8,128)(2,1)S(1)}, s32[42]{0:T(128)S(4)}, s32[8,64]{1,0:T(8,128)S(1)}, bf16[512,768]{...) custom-call(s32[2]{0:T(128)S(1)} %pad_add_fusion.refs_0_, ...), custom_call_target="tpu_custom_call" | custom-call | flops 3000000000 | tf_op jit(solution)/shard_map/pallas_call | solution.py:173
  7.3 1.8 %collective-permute-start = (bf16[256,128]{1,0:T(8,128)(2,1)S(1)}, bf16[256,128]{1,0:T(8,128)(2,1)S(1)}, u32[]{:S(2)}, u32[]{:S(2)}) collective-permute-start(bf16[256,128]{1,0:T(8,128)(2,1)S(1)} %get-tuple-element.135), channel_id=1, source_target_pairs={{0,4},{4,0},{8,12},{12,8},{16,20},{20,16},{24,28},{28,24},{1,5},{5... | collective-permute-start | bytes 196616 | tf_op jit(solution)/shard_map/ppermute | solution.py:902
  11.6 1.9 %collective-permute-start.7 = (bf16[256,128]{1,0:T(8,128)(2,1)S(1)}, bf16[256,128]{1,0:T(8,128)(2,1)S(1)}, u32[]{:S(2)}, u32[]{:S(2)}) collective-permute-start(bf16[256,128]{1,0:T(8,128)(2,1)S(1)} %get-tuple-element.142), channel_id=1, source_target_pairs={{0,8},{4,12},{8,0},{12,4},{16,24},{20,28},{24,16},{28,20},{1,9},{5... | collective-permute-start | bytes 196616 | tf_op jit(solution)/shard_map/ppermute | solution.py:902
  13.5 2.4 %shard_map.396 = (bf16[384,128]{1,0:T(8,128)(2,1)S(1)}, bf16[256,768]{1,0:T(8,128)(2,1)S(1)}, bf16[256,192]{1,0:T(8,128)(2,1)S(1)}, bf16[768]{0:T(1024)(128)(2,1...) custom-call(s32[42]{0:T(128)S(4)} %get-tuple-element.124.refs_0_, ...), custom_call_target="tpu_custom_call" | custom-call | flops 2800000000 | tf_op jit(solution)/shard_map/pallas_call | solution.py:173
  16.0 2.8 %collective-permute-start.14 = (bf16[256,128]{1,0:T(8,128)(2,1)S(1)}, bf16[256,128]{1,0:T(8,128)(2,1)S(1)}, u32[]{:S(2)}, u32[]{:S(2)}) collective-permute-start(bf16[256,128]{1,0:T(8,128)(2,1)S(1)} %get-tuple-element.147), channel_id=1, source_target_pairs={{0,16},{4,20},{8,24},{12,28},{16,0},{20,4},{24,8},{28,12},{1,17},{... | collective-permute-start | bytes 196616 | tf_op jit(solution)/shard_map/ppermute | solution.py:902
  18.9 1.8 %shard_map.398 = (bf16[384,128]{1,0:T(8,128)(2,1)S(1)}, bf16[256,768]{1,0:T(8,128)(2,1)S(1)}, bf16[256,192]{1,0:T(8,128)(2,1)S(1)}, bf16[768,768]{1,0:T(8,128)(2...) custom-call(s32[42]{0:T(128)S(4)} %get-tuple-element.124.refs_0_, ...), custom_call_target="tpu_custom_call" | custom-call | flops 2500000000 | tf_op jit(solution)/shard_map/pallas_call | solution.py:173
  20.8 1.6 %collective-permute-start.9 = (bf16[384,128]{1,0:T(8,128)(2,1)S(1)}, bf16[384,128]{1,0:T(8,128)(2,1)S(1)}, u32[]{:S(2)}, u32[]{:S(2)}) collective-permute-start(bf16[384,128]{1,0:T(8,128)(2,1)S(1)} %get-tuple-element.143.refs_3_.refs_8_), channel_id=1, source_target_pairs={{0,2},{1,3},{2,0},{3,1},{4,6},{5,7},{6,4},{7,5},{8,10},{9,11},{10,... | collective-permute-start | bytes 294920 | tf_op jit(solution)/shard_map/ppermute | solution.py:902
  24.1 1.6 %collective-permute-start.16 = (bf16[512,128]{1,0:T(8,128)(2,1)S(1)}, bf16[512,128]{1,0:T(8,128)(2,1)S(1)}, u32[]{:S(2)}, u32[]{:S(2)}) collective-permute-start(bf16[512,128]{1,0:T(8,128)(2,1)S(1)} %shard_map.400.refs_16_.refs_5_.refs_7_.refs_3_), channel_id=1, source_target_pairs={{0,2},{1,3},{2,0},{3,1},{4,6},{5,7},{6,4},{7,5},{8,10},{9,11},{10,... | collective-permute-start | bytes 393224 | tf_op jit(solution)/shard_map/ppermute | solution.py:902
  26.4 2.1 %collective-permute-done.12.refs_14_ = bf16[384,128]{1,0:T(8,128)(2,1)S(1)} collective-permute-done((bf16[384,128]{1,0:T(8,128)(2,1)S(1)}, bf16[384,128]{1,0:T(8,128)(2,1)S(1)}, u32[]{:S(2)}, u32[]{:S(2)}) %collective-permute-start.12) | collective-permute-done | bytes 98336 | tf_op jit(solution)/shard_map/ppermute | solution.py:902
  29.0 1.9 %collective-permute-done.16.refs_7_ = bf16[512,128]{1,0:T(8,128)(2,1)S(1)} collective-permute-done((bf16[512,128]{1,0:T(8,128)(2,1)S(1)}, bf16[512,128]{1,0:T(8,128)(2,1)S(1)}, u32[]{:S(2)}, u32[]{:S(2)}) %collective-permute-start.16) | collective-permute-done | bytes 131104 | tf_op jit(solution)/shard_map/ppermute | solution.py:902
  30.9 2.7 %shard_map.401 = (f32[512,768]{1,0:T(8,128)S(1)}, bf16[512,768]{1,0:T(8,128)(2,1)S(1)}, bf16[512,768]{1,0:T(8,128)(2,1)S(1)}, f32[512,768]{1,0:T(8,128)S(1)}) custom-call(s32[42]{0:T(128)S(4)} %get-tuple-element.124.refs_0_, bf16[512,768]{1,0:T(8,128)(2,1)S(1)} %get-tuple-element.126.refs_0_.refs_1_, bf16[768]{0:T(1024)(128)(2,1)S(1)} %get-tuple-element.137.refs_2_, ...), custom_call_target="tpu_custom_call" | custom-call | flops 2600000000 | tf_op jit(solution)/shard_map/pallas_call | solution.py:173
  36.8 1.6 %collective-permute-start.19 = (bf16[256,768]{1,0:T(8,128)(2,1)S(1)}, bf16[256,768]{1,0:T(8,128)(2,1)S(1)}, u32[]{:S(2)}, u32[]{:S(2)}) collective-permute-start(bf16[256,768]{1,0:T(8,128)(2,1)S(1)} %shard_map.404.refs_3_.refs_0_), channel_id=1, source_target_pairs={{0,2},{1,3},{2,0},{3,1},{4,6},{5,7},{6,4},{7,5},{8,10},{9,11},{10,... | collective-permute-start | bytes 1179656 | tf_op jit(solution)/shard_map/ppermute | solution.py:902
  39.4 2.9 %shard_map.406 = (bf16[2304,128]{1,0:T(8,128)(2,1)S(1)}, bf16[2304,128]{1,0:T(8,128)(2,1)}, bf16[2304,128]{1,0:T(8,128)(2,1)S(1)}, bf16[2304,128]{1,0:T(8,128)(2,1)}) custom-call(s32[42]{0:T(128)S(4)} %get-tuple-element.124.refs_0_, bf16[256,768]{1,0:T(8,128)(2,1)S(1)} %get-tuple-element.157.refs_1_.refs_4_, ...), custom_call_target="tpu_custom_call" | custom-call | flops 2200000000 | tf_op jit(solution)/shard_map/pallas_call | solution.py:173
  45.4 2.3 %shard_map.407 = (f32[256,128]{1,0:T(8,128)S(1)}, f32[1,128]{1,0:T(1,128)S(1)}, f32[3,256,128]{2,1,0:T(8,128)S(1)}) custom-call(s32[42]{0:T(128)S(4)} %get-tuple-element.124.refs_0_, s32[8,64]{1,0:T(8,128)S(1)} %get-tuple-element.125.refs_1_, bf16[8,256,128]{2,1,0:T(8,128)(2,1)} %refs_2_.7, bf16[2,256,256]{2,1,0:T(8,128)(2,1)} %constant.17.clone.refs_3_, ...), custom_call_target="tpu_custom_call" | custom-call | flops 20000000000 | tf_op jit(solution)/shard_map/pallas_call | solution.py:173
  50.9 4.0 %shard_map.411 = (bf16[512,576]{1,0:T(8,128)(2,1)S(1)}, bf16[512,768]{1,0:T(8,128)(2,1)S(1)}, f32[128,768]{1,0:T(8,128)S(1)}, f32[3,768]{1,0:T(4,128)S(1)}) custom-call(s32[42]{0:T(128)S(4)} %get-tuple-element.124.refs_0_, bf16[256,768]{1,0:T(8,128)(2,1)S(1)} %shard_map.409.refs_1_, bf16[256,768]{1,0:T(8,128)(2,1)S(1)} %collective-permute-done.21.refs_2_, ...), custom_call_target="tpu_custom_call" | custom-call | flops 16499999744 | tf_op jit(solution)/shard_map/pallas_call | solution.py:173
  58.0 1.7 %collective-permute-done.22.refs_1_ = bf16[256,768]{1,0:T(8,128)(2,1)} collective-permute-done((bf16[256,768]{1,0:T(8,128)(2,1)}, bf16[256,768]{1,0:T(8,128)(2,1)}, u32[]{:S(2)}, u32[]{:S(2)}) %collective-permute-start.22) | collective-permute-done | bytes 393248 | tf_op jit(solution)/shard_map/ppermute | solution.py:902
  62.1 1.6 %collective-permute-start.27 = (bf16[144,768]{1,0:T(8,128)(2,1)S(1)}, bf16[144,768]{1,0:T(8,128)(2,1)S(1)}, u32[]{:S(2)}, u32[]{:S(2)}) collective-permute-start(bf16[144,768]{1,0:T(8,128)(2,1)S(1)} %get-tuple-element.189), channel_id=1, source_target_pairs={{0,2},{1,3},{2,0},{3,1},{4,6},{5,7},{6,4},{7,5},{8,10},{9,11},{10,... | collective-permute-start | bytes 663560 | tf_op jit(solution)/shard_map/ppermute | solution.py:902
  66.8 2.5 %collective-permute-done.27.refs_11_.refs_3_ = bf16[144,768]{1,0:T(8,128)(2,1)S(1)} collective-permute-done((bf16[144,768]{1,0:T(8,128)(2,1)S(1)}, bf16[144,768]{1,0:T(8,128)(2,1)S(1)}, u32[]{:S(2)}, u32[]{:S(2)}) %collective-permute-start.27) | collective-permute-done | bytes 221216 | tf_op jit(solution)/shard_map/ppermute | solution.py:902
  72.0 5.4 %collective-permute-done.30.refs_6_ = bf16[1536,128]{1,0:T(8,128)(2,1)S(1)} collective-permute-done((bf16[1536,128]{1,0:T(8,128)(2,1)S(1)}, bf16[1536,128]{1,0:T(8,128)(2,1)S(1)}, u32[]{:S(2)}, u32[]{:S(2)}) %collective-permute-start.30) | collective-permute-done | bytes 393248 | tf_op jit(solution)/shard_map/ppermute | solution.py:902
  77.4 1.8 %collective-permute-done.29.refs_5_ = bf16[816,128]{1,0:T(8,128)(2,1)S(1)} collective-permute-done((bf16[816,128]{1,0:T(8,128)(2,1)S(1)}, bf16[816,128]{1,0:T(8,128)(2,1)S(1)}, u32[]{:S(2)}, u32[]{:S(2)}) %collective-permute-start.29) | collective-permute-done | bytes 208928 | tf_op jit(solution)/shard_map/ppermute | solution.py:902
  82.2 1.7 %collective-permute-start.37 = (bf16[576,128]{1,0:T(8,128)(2,1)S(1)}, bf16[576,128]{1,0:T(8,128)(2,1)S(1)}, u32[]{:S(2)}, u32[]{:S(2)}) collective-permute-start(bf16[576,128]{1,0:T(8,128)(2,1)S(1)} %get-tuple-element.220), channel_id=1, source_target_pairs={{0,16},{4,20},{8,24},{12,28},{16,0},{20,4},{24,8},{28,12},{1,17},{... | collective-permute-start | bytes 442376 | tf_op jit(solution)/shard_map/ppermute | solution.py:902
  85.2 7.7 %collective-permute-done.31.refs_3_ = bf16[944,128]{1,0:T(8,128)(2,1)S(1)} collective-permute-done((bf16[944,128]{1,0:T(8,128)(2,1)S(1)}, bf16[944,128]{1,0:T(8,128)(2,1)S(1)}, u32[]{:S(2)}, u32[]{:S(2)}) %collective-permute-start.31) | collective-permute-done | bytes 241696 | tf_op jit(solution)/shard_map/ppermute | solution.py:902
  95.5 7.4 %collective-permute-done.35.refs_4_ = bf16[1008,128]{1,0:T(8,128)(2,1)S(1)} collective-permute-done((bf16[1008,128]{1,0:T(8,128)(2,1)S(1)}, bf16[1008,128]{1,0:T(8,128)(2,1)S(1)}, u32[]{:S(2)}, u32[]{:S(2)}) %collective-permute-start.35) | collective-permute-done | bytes 258080 | tf_op jit(solution)/shard_map/ppermute | solution.py:902
  (107 shorter events, 36.8 us)
Async XLA Ops:
  0.7 20.1 %collective-permute-start.4 = (bf16[768,128]{1,0:T(8,128)(2,1)}, bf16[768,128]{1,0:T(8,128)(2,1)S(1)}, u32[]{:S(2)}, u32[]{:S(2)}) collective-permute-start(bf16[768,128]{1,0:T(8,128)(2,1)} %refs_5_.7), channel_id=1, source_target_pairs={{0,1},{1,0},{2,3},{3,2},{4,5},{5,4},{6,7},{7,6},{8,9},{9,8},{10,11... | collective-permute-start | bytes 589832 | tf_op jit(solution)/shard_map/ppermute | solution.py:902
  1.2 17.7 %collective-permute-start.5 = (bf16[768,128]{1,0:T(8,128)(2,1)}, bf16[768,128]{1,0:T(8,128)(2,1)S(1)}, u32[]{:S(2)}, u32[]{:S(2)}) collective-permute-start(bf16[768,128]{1,0:T(8,128)(2,1)} %refs_5_.7), channel_id=1, source_target_pairs={{0,2},{1,3},{2,0},{3,1},{4,6},{5,7},{6,4},{7,5},{8,10},{9,11},{10,... | collective-permute-start | bytes 589832 | tf_op jit(solution)/shard_map/ppermute | solution.py:902
  3.8 18.6 %collective-permute-start.1 = (bf16[192,768]{1,0:T(8,128)(2,1)}, bf16[192,768]{1,0:T(8,128)(2,1)S(1)}, u32[]{:S(2)}, u32[]{:S(2)}) collective-permute-start(bf16[192,768]{1,0:T(8,128)(2,1)} %refs_1_.3), channel_id=1, source_target_pairs={{0,1},{1,0},{2,3},{3,2},{4,5},{5,4},{6,7},{7,6},{8,9},{9,8},{10,11... | collective-permute-start | bytes 884744 | tf_op jit(solution)/shard_map/ppermute | solution.py:902
  3.9 12.0 %collective-permute-start.2 = (bf16[192,768]{1,0:T(8,128)(2,1)}, bf16[192,768]{1,0:T(8,128)(2,1)S(1)}, u32[]{:S(2)}, u32[]{:S(2)}) collective-permute-start(bf16[192,768]{1,0:T(8,128)(2,1)} %refs_1_.3), channel_id=1, source_target_pairs={{0,2},{1,3},{2,0},{3,1},{4,6},{5,7},{6,4},{7,5},{8,10},{9,11},{10,... | collective-permute-start | bytes 884744 | tf_op jit(solution)/shard_map/ppermute | solution.py:902
  15.9 6.9 %collective-permute-start.3 = (bf16[192,768]{1,0:T(8,128)(2,1)S(1)}, bf16[192,768]{1,0:T(8,128)(2,1)S(1)}, u32[]{:S(2)}, u32[]{:S(2)}) collective-permute-start(bf16[192,768]{1,0:T(8,128)(2,1)S(1)} %collective-permute-done.2.refs_3_), channel_id=1, source_target_pairs={{0,1},{1,0},{2,3},{3,2},{4,5},{5,4},{6,7},{7,6},{8,9},{9,8},{10,11... | collective-permute-start | bytes 884744 | tf_op jit(solution)/shard_map/ppermute | solution.py:902
  16.0 8.0 %collective-permute-start.14 = (bf16[256,128]{1,0:T(8,128)(2,1)S(1)}, bf16[256,128]{1,0:T(8,128)(2,1)S(1)}, u32[]{:S(2)}, u32[]{:S(2)}) collective-permute-start(bf16[256,128]{1,0:T(8,128)(2,1)S(1)} %get-tuple-element.147), channel_id=1, source_target_pairs={{0,16},{4,20},{8,24},{12,28},{16,0},{20,4},{24,8},{28,12},{1,17},{... | collective-permute-start | bytes 196616 | tf_op jit(solution)/shard_map/ppermute | solution.py:902
  22.3 6.2 %collective-permute-start.12 = (bf16[384,128]{1,0:T(8,128)(2,1)S(1)}, bf16[384,128]{1,0:T(8,128)(2,1)S(1)}, u32[]{:S(2)}, u32[]{:S(2)}) collective-permute-start(bf16[384,128]{1,0:T(8,128)(2,1)S(1)} %get-tuple-element.145.refs_9_.refs_12_), channel_id=1, source_target_pairs={{0,2},{1,3},{2,0},{3,1},{4,6},{5,7},{6,4},{7,5},{8,10},{9,11},{10,... | collective-permute-start | bytes 294920 | tf_op jit(solution)/shard_map/ppermute | solution.py:902
  24.1 6.8 %collective-permute-start.16 = (bf16[512,128]{1,0:T(8,128)(2,1)S(1)}, bf16[512,128]{1,0:T(8,128)(2,1)S(1)}, u32[]{:S(2)}, u32[]{:S(2)}) collective-permute-start(bf16[512,128]{1,0:T(8,128)(2,1)S(1)} %shard_map.400.refs_16_.refs_5_.refs_7_.refs_3_), channel_id=1, source_target_pairs={{0,2},{1,3},{2,0},{3,1},{4,6},{5,7},{6,4},{7,5},{8,10},{9,11},{10,... | collective-permute-start | bytes 393224 | tf_op jit(solution)/shard_map/ppermute | solution.py:902
  36.8 12.1 %collective-permute-start.19 = (bf16[256,768]{1,0:T(8,128)(2,1)S(1)}, bf16[256,768]{1,0:T(8,128)(2,1)S(1)}, u32[]{:S(2)}, u32[]{:S(2)}) collective-permute-start(bf16[256,768]{1,0:T(8,128)(2,1)S(1)} %shard_map.404.refs_3_.refs_0_), channel_id=1, source_target_pairs={{0,2},{1,3},{2,0},{3,1},{4,6},{5,7},{6,4},{7,5},{8,10},{9,11},{10,... | collective-permute-start | bytes 1179656 | tf_op jit(solution)/shard_map/ppermute | solution.py:902
  39.2 8.4 %collective-permute-start.20 = (bf16[256,768]{1,0:T(8,128)(2,1)S(1)}, bf16[256,768]{1,0:T(8,128)(2,1)S(1)}, u32[]{:S(2)}, u32[]{:S(2)}) collective-permute-start(bf16[256,768]{1,0:T(8,128)(2,1)S(1)} %get-tuple-element.156), channel_id=1, source_target_pairs={{0,1},{1,0},{2,3},{3,2},{4,5},{5,4},{6,7},{7,6},{8,9},{9,8},{10,11... | collective-permute-start | bytes 1179656 | tf_op jit(solution)/shard_map/ppermute | solution.py:902
  42.3 19.8 %collective-permute-start.25 = (bf16[2304,128]{1,0:T(8,128)(2,1)}, bf16[2304,128]{1,0:T(8,128)(2,1)}, u32[]{:S(2)}, u32[]{:S(2)}) collective-permute-start(bf16[2304,128]{1,0:T(8,128)(2,1)} %get-tuple-element.179), channel_id=1, source_target_pairs={{0,4},{4,0},{8,12},{12,8},{16,20},{20,16},{24,28},{28,24},{1,5},{5... | collective-permute-start | bytes 1769480 | tf_op jit(solution)/shard_map/ppermute | solution.py:902
  43.8 20.0 %collective-permute-start.26 = (bf16[2304,128]{1,0:T(8,128)(2,1)}, bf16[2304,128]{1,0:T(8,128)(2,1)}, u32[]{:S(2)}, u32[]{:S(2)}) collective-permute-start(bf16[2304,128]{1,0:T(8,128)(2,1)} %get-tuple-element.180), channel_id=1, source_target_pairs={{0,8},{4,12},{8,0},{12,4},{16,24},{20,28},{24,16},{28,20},{1,9},{5... | collective-permute-start | bytes 1769480 | tf_op jit(solution)/shard_map/ppermute | solution.py:902
  48.5 11.2 %collective-permute-start.22 = (bf16[256,768]{1,0:T(8,128)(2,1)}, bf16[256,768]{1,0:T(8,128)(2,1)}, u32[]{:S(2)}, u32[]{:S(2)}) collective-permute-start(bf16[256,768]{1,0:T(8,128)(2,1)} %shard_map.408.refs_2_.refs_0_), channel_id=1, source_target_pairs={{0,2},{1,3},{2,0},{3,1},{4,6},{5,7},{6,4},{7,5},{8,10},{9,11},{10,... | collective-permute-start | bytes 1179656 | tf_op jit(solution)/shard_map/ppermute | solution.py:902
  61.0 11.0 %collective-permute-start.28 = (bf16[768,128]{1,0:T(8,128)(2,1)S(1)}, bf16[768,128]{1,0:T(8,128)(2,1)S(1)}, u32[]{:S(2)}, u32[]{:S(2)}) collective-permute-start(bf16[768,128]{1,0:T(8,128)(2,1)S(1)} %get-tuple-element.192), channel_id=1, source_target_pairs={{0,4},{4,0},{8,12},{12,8},{16,20},{20,16},{24,28},{28,24},{1,5},{5... | collective-permute-start | bytes 589832 | tf_op jit(solution)/shard_map/ppermute | solution.py:902
  61.7 15.7 %collective-permute-start.30 = (bf16[1536,128]{1,0:T(8,128)(2,1)S(1)}, bf16[1536,128]{1,0:T(8,128)(2,1)S(1)}, u32[]{:S(2)}, u32[]{:S(2)}) collective-permute-start(bf16[1536,128]{1,0:T(8,128)(2,1)S(1)} %get-tuple-element.194), channel_id=1, source_target_pairs={{0,8},{4,12},{8,0},{12,4},{16,24},{20,28},{24,16},{28,20},{1,9},{5... | collective-permute-start | bytes 1179656 | tf_op jit(solution)/shard_map/ppermute | solution.py:902
  62.1 7.2 %collective-permute-start.27 = (bf16[144,768]{1,0:T(8,128)(2,1)S(1)}, bf16[144,768]{1,0:T(8,128)(2,1)S(1)}, u32[]{:S(2)}, u32[]{:S(2)}) collective-permute-start(bf16[144,768]{1,0:T(8,128)(2,1)S(1)} %get-tuple-element.189), channel_id=1, source_target_pairs={{0,2},{1,3},{2,0},{3,1},{4,6},{5,7},{6,4},{7,5},{8,10},{9,11},{10,... | collective-permute-start | bytes 663560 | tf_op jit(solution)/shard_map/ppermute | solution.py:902
  65.3 15.6 %collective-permute-start.33 = (bf16[1152,128]{1,0:T(8,128)(2,1)S(1)}, bf16[1152,128]{1,0:T(8,128)(2,1)S(1)}, u32[]{:S(2)}, u32[]{:S(2)}) collective-permute-start(bf16[1152,128]{1,0:T(8,128)(2,1)S(1)} %get-tuple-element.200), channel_id=1, source_target_pairs={{0,16},{4,20},{8,24},{12,28},{16,0},{20,4},{24,8},{28,12},{1,17},{... | collective-permute-start | bytes 884744 | tf_op jit(solution)/shard_map/ppermute | solution.py:902
  65.8 15.0 %collective-permute-start.34 = (bf16[1152,128]{1,0:T(8,128)(2,1)S(1)}, bf16[1152,128]{1,0:T(8,128)(2,1)S(1)}, u32[]{:S(2)}, u32[]{:S(2)}) collective-permute-start(bf16[1152,128]{1,0:T(8,128)(2,1)S(1)} %get-tuple-element.201), channel_id=1, source_target_pairs={{0,4},{4,0},{8,12},{12,8},{16,20},{20,16},{24,28},{28,24},{1,5},{5... | collective-permute-start | bytes 884744 | tf_op jit(solution)/shard_map/ppermute | solution.py:902
  69.4 9.7 %collective-permute-start.29 = (bf16[816,128]{1,0:T(8,128)(2,1)S(1)}, bf16[816,128]{1,0:T(8,128)(2,1)S(1)}, u32[]{:S(2)}, u32[]{:S(2)}) collective-permute-start(bf16[816,128]{1,0:T(8,128)(2,1)S(1)} %get-tuple-element.193), channel_id=1, source_target_pairs={{0,4},{4,0},{8,12},{12,8},{16,20},{20,16},{24,28},{28,24},{1,5},{5... | collective-permute-start | bytes 626696 | tf_op jit(solution)/shard_map/ppermute | solution.py:902
  79.3 5.9 %collective-permute-start.32 = (bf16[768,128]{1,0:T(8,128)(2,1)S(1)}, bf16[768,128]{1,0:T(8,128)(2,1)S(1)}, u32[]{:S(2)}, u32[]{:S(2)}) collective-permute-start(bf16[768,128]{1,0:T(8,128)(2,1)S(1)} %get-tuple-element.198), channel_id=1, source_target_pairs={{0,4},{4,0},{8,12},{12,8},{16,20},{20,16},{24,28},{28,24},{1,5},{5... | collective-permute-start | bytes 589832 | tf_op jit(solution)/shard_map/ppermute | solution.py:902
  80.0 12.9 %collective-permute-start.31 = (bf16[944,128]{1,0:T(8,128)(2,1)S(1)}, bf16[944,128]{1,0:T(8,128)(2,1)S(1)}, u32[]{:S(2)}, u32[]{:S(2)}) collective-permute-start(bf16[944,128]{1,0:T(8,128)(2,1)S(1)} %get-tuple-element.197), channel_id=1, source_target_pairs={{0,8},{4,12},{8,0},{12,4},{16,24},{20,28},{24,16},{28,20},{1,9},{5... | collective-permute-start | bytes 725000 | tf_op jit(solution)/shard_map/ppermute | solution.py:902
  81.0 13.6 %collective-permute-start.36 = (bf16[576,128]{1,0:T(8,128)(2,1)S(1)}, bf16[576,128]{1,0:T(8,128)(2,1)S(1)}, u32[]{:S(2)}, u32[]{:S(2)}) collective-permute-start(bf16[576,128]{1,0:T(8,128)(2,1)S(1)} %get-tuple-element.219), channel_id=1, source_target_pairs={{0,8},{4,12},{8,0},{12,4},{16,24},{20,28},{24,16},{28,20},{1,9},{5... | collective-permute-start | bytes 442376 | tf_op jit(solution)/shard_map/ppermute | solution.py:902
  82.2 12.4 %collective-permute-start.37 = (bf16[576,128]{1,0:T(8,128)(2,1)S(1)}, bf16[576,128]{1,0:T(8,128)(2,1)S(1)}, u32[]{:S(2)}, u32[]{:S(2)}) collective-permute-start(bf16[576,128]{1,0:T(8,128)(2,1)S(1)} %get-tuple-element.220), channel_id=1, source_target_pairs={{0,16},{4,20},{8,24},{12,28},{16,0},{20,4},{24,8},{28,12},{1,17},{... | collective-permute-start | bytes 442376 | tf_op jit(solution)/shard_map/ppermute | solution.py:902
  93.0 9.9 %collective-permute-start.35 = (bf16[1008,128]{1,0:T(8,128)(2,1)S(1)}, bf16[1008,128]{1,0:T(8,128)(2,1)S(1)}, u32[]{:S(2)}, u32[]{:S(2)}) collective-permute-start(bf16[1008,128]{1,0:T(8,128)(2,1)S(1)} %get-tuple-element.205), channel_id=1, source_target_pairs={{0,16},{4,20},{8,24},{12,28},{16,0},{20,4},{24,8},{28,12},{1,17},{... | collective-permute-start | bytes 774152 | tf_op jit(solution)/shard_map/ppermute | solution.py:902
  (25 other events, 138.4 us)

commit v5 on v4

--- a/solution.py
+++ b/solution.py
@@ -124,7 +124,7 @@
         return value
 
     def __call__(
-        self, kernel, outs, args, specs=None, scratch=(), out_specs=None, final=False, stage=(), cost=1.0
+        self, kernel, outs, args, specs=None, scratch=(), out_specs=None, final=False, stage=(), cost=1.0, after=()
     ):
         args = tuple(args)
         specs = [VMEM] * len(args) if specs is None else list(specs)
@@ -146,11 +146,10 @@
         tail = len(staged)
         args += tuple(staged)
         specs += [ANY] * tail
-        skipped = 0
-        if self.last is not None:
-            args += (self.last,)
-            specs.append(ANY)
-            skipped = 1
+        unread = tuple(after) if self.last is None else (*after, self.last)
+        skipped = len(unread)
+        args += unread
+        specs += [ANY] * skipped
 
         def body(*refs):
             own, sources, refs = refs[:count], refs[count : count + tail], refs[count + tail + skipped :]
@@ -941,7 +940,7 @@
     up_exchange = Exchange(count, far, units // LANES * pads[0])
     down_exchange = Exchange(count, turned, units // LANES * pads[0])
     tiles = late_columns // LANES
-    middle = tiles // 3
+    middle = 3 * tiles // 6
     late_exchange = Exchange(count, bits, middle * pads[0])
     turned_exchange = Exchange(count, turned, (tiles - middle) * pads[0])
     last_exchange = Exchange(count, bits, sum(pads), moved=VIS, shared=VECTOR_ROWS)
@@ -995,7 +994,7 @@
             keep, received = data_step(step, exchange, [(exchange, keep, received)])
             yield keep, received
 
-    def steps(kept, arrays, moves, sends):
+    def steps(kept, arrays, moves, sends, cost=1.0):
         first = len(kept) + len(arrays)
         sizes = [None] * len(kept) + [size for _, size in arrays] + [None] * len(moves)
         sizes += [size for _, size in sends]
@@ -1009,7 +1008,7 @@
             + [low(sum(size), LANES) for _, size in sends],
             (facts, *kept) + tuple(array for array, _ in arrays),
             (SMEM,) + (VMEM,) * first,
-            cost=1.0,
+            cost=cost,
         )
         return results[: len(moves)], [
             moved(sent, "dp", 2**bit) for sent, (bit, _) in zip(results[len(moves) :], sends)
@@ -1030,7 +1029,6 @@
     proj_all = model_gather(proj_weight)
     (
         back_keep, back_sent, facts, seen, patch_rows, qkv_weight_t, first_gain, first_shift, query_bias, value_bias,
-        out_weight, proj_weight,
     ) = run(
         lambda *refs: cotangent_kernel(info, back_exchange, *refs),
         [
@@ -1041,9 +1039,7 @@
         (SMEM, SMEM, SMEM, VMEM, VMEM),
         out_specs=(VMEM, VMEM, SMEM, VMEM),
         scratch=[pltpu.VMEM((VIS, count), wide_type)],
-        stage=(
-            patch_rows, qkv_weight_t, first_gain, first_shift, query_bias, value_bias, out_weight, proj_weight
-        ),
+        stage=(patch_rows, qkv_weight_t, first_gain, first_shift, query_bias, value_bias),
         cost=3.0,
     )
     back_steps = data_steps(back_exchange, back_keep, back_sent)
@@ -1053,6 +1049,7 @@
         [low(rows, width), low(rows, qkv_columns)],
         (patch_rows, first_gain, first_shift, qkv_weight_t, query_bias, value_bias),
         cost=1.2,
+        after=(out_all[1], proj_all[1]),
     )
     next(back_steps)
     packed_rows = half * head_columns // LANES
@@ -1066,19 +1063,22 @@
     )
     first_all = model_gather(packed)
     back_own, back_other = finish_pair(back_steps)
-    packed, last_probs, last_attended, down_weight, down_bias, proj_bias = run(
+    (
+        packed, last_probs, last_attended, down_weight, down_bias, proj_bias, out_near, proj_near, out_core, proj_core
+    ) = run(
         lambda *refs: attention_kernel(info, heads, half, *refs),
         [low(packed_rows, LANES), low(half, heads * BLOCK), low(half, head_columns)],
         (facts, qkv),
         (SMEM, VMEM),
-        stage=(down_weight, down_bias, proj_bias),
+        stage=(down_weight, down_bias, proj_bias, out_weight, proj_weight, out_all[1], proj_all[1]),
         cost=2.5,
+        after=(out_all[parts // 2], proj_all[parts // 2]),
     )
     last_all = model_gather(packed)
     out_whole, proj_whole = run(
         lambda *refs: weights_kernel(parts, *refs),
         [low(parts * head_columns, width), low(width, parts * columns)],
-        (facts,) + out_all + proj_all,
+        (facts, out_near, out_core) + out_all[2:] + (proj_near, proj_core) + proj_all[2:],
         (SMEM,) + (VMEM,) * (2 * parts),
         cost=0.0,
     )
@@ -1116,15 +1116,6 @@
     keep, up_low, down_low, bias_grads = forward_grad(True)
     second_steps = model_steps(keep, second_other)
     next(second_steps)
-    keep, sent = run(
-        forward_part_kernel,
-        [low(half, width), low(half, width)],
-        (facts, acted, down_weight),
-        (SMEM, VMEM, VMEM),
-        cost=0.7,
-    )
-    out_steps = model_steps(keep, moved(sent, "mp", 1))
-
     down_keep, down_sent, up_keep, up_sent = run(
         lambda *refs: early_grads_kernel((down_exchange, up_exchange), pads[0], *refs),
         [low(down_exchange.rows(0), LANES)] * 2 + [low(up_exchange.rows(0), LANES)] * 2,
@@ -1135,6 +1126,15 @@
     )
     down_pair = (down_keep, moved(down_sent, "dp", 2 ** turned[0]))
     up_pair = (up_keep, moved(up_sent, "dp", 2 ** bits[0]))
+    keep, sent = run(
+        forward_part_kernel,
+        [low(half, width), low(half, width)],
+        (facts, acted, down_weight),
+        (SMEM, VMEM, VMEM),
+        cost=0.7,
+    )
+    out_steps = model_steps(keep, moved(sent, "mp", 1))
+
     pos_grad_own, mask_grad, layouts = run(
         lambda *refs: position_kernel(info, *refs),
         [wide(GRID, columns), wide(1, columns), wide(3, GRID, columns)],
@@ -1152,7 +1152,7 @@
         lambda *refs: attention_back_kernel(heads, *refs),
         [low(rows, qkv_columns), low(rows, width), wide(own_rows, width), wide(3, width)],
         (
-            facts, second_sum, second_other, hidden, down_low, down_low_other, second_gain, out_weight, qkv,
+            facts, second_sum, second_other, hidden, down_low, down_low_other, second_gain, out_near, qkv,
             first_probs, last_probs,
         ),
         (SMEM,) + (VMEM,) * 10,
@@ -1191,26 +1191,25 @@
             (SMEM, VMEM, VMEM),
             scratch=[pltpu.VMEM((size + own_rows, width), wide_type)],
             cost=1.1,
+            after=(up_pair[1], down_pair[1]),
         )
         in_other = moved(in_sent, "mp", 2**bit)
         size //= 2
         bit += 1
     next(out_steps)
     early_sizes = [[exchange.rows(1)] for exchange in (up_exchange, down_exchange)]
-    (up_keep, down_keep), (up_came, down_came) = steps(
-        (up_pair[0], down_pair[0]),
-        ((up_pair[1], [up_exchange.rows(0)]), (down_pair[1], [down_exchange.rows(0)])),
-        [
-            (up_exchange, 1, [(up_exchange, 0, (2, 0))], (0, 0)),
-            (down_exchange, 1, [(down_exchange, 1, (3, 0))], (1, 0)),
-        ],
-        [(far[1], early_sizes[0]), (turned[1], early_sizes[1])],
+    (up_keep,), (up_came,) = steps(
+        (up_pair[0],),
+        ((up_pair[1], [up_exchange.rows(0)]),),
+        [(up_exchange, 1, [(up_exchange, 0, (1, 0))], (0, 0))],
+        [(far[1], early_sizes[0])],
+        cost=40.0,
     )
     out_sum, out_other = finish(out_steps)
     encoded, proj_grad = run(
         encoded_kernel,
         [low(rows, columns), wide(width, columns)],
-        (facts, hidden, out_sum, out_other, down_bias, proj_weight, proj_bias, enc_grad),
+        (facts, hidden, out_sum, out_other, down_bias, proj_near, proj_bias, enc_grad),
         (SMEM,) + (VMEM,) * 7,
         scratch=[pltpu.VMEM((rows, width), low_type)],
         cost=1.0,
@@ -1227,6 +1226,12 @@
         cost=0.6,
     )
     last_came = moved(last_sent, "dp", 2 ** bits[0])
+    (down_keep,), (down_came,) = steps(
+        (down_pair[0],),
+        ((down_pair[1], [down_exchange.rows(0)]),),
+        [(down_exchange, 1, [(down_exchange, 0, (1, 0))], (0, 0))],
+        [(turned[1], early_sizes[1])],
+    )
     (input_grad,) = run(
         input_grad_kernel,
         [low(own_rows, width)],
@@ -1251,16 +1256,20 @@
         ],
         [(bits[1], joint_sizes[0]), (turned[1], joint_sizes[1])],
     )
-    old_sizes, early_sizes = early_sizes, [[exchange.rows(2)] for exchange in early]
-    (up_keep, down_keep), early_came = steps(
-        (up_keep, down_keep),
-        ((up_came, old_sizes[0]), (down_came, old_sizes[1])),
-        [
-            (up_exchange, 2, [(up_exchange, 0, (2, 0))], (0, 0)),
-            (down_exchange, 2, [(down_exchange, 1, (3, 0))], (1, 0)),
-        ],
-        [(far[2], early_sizes[0]), (turned[2], early_sizes[1])],
-    )
+    (down_keep,), (down_came,) = steps(
+        (down_keep,),
+        ((down_came, early_sizes[1]),),
+        [(down_exchange, 2, [(down_exchange, 0, (1, 0))], (0, 0))],
+        [(turned[2], [down_exchange.rows(2)])],
+    )
+    (up_keep,), (up_came,) = steps(
+        (up_keep,),
+        ((up_came, early_sizes[0]),),
+        [(up_exchange, 2, [(up_exchange, 0, (1, 0))], (0, 0))],
+        [(far[2], [up_exchange.rows(2)])],
+    )
+    early_came = (up_came, down_came)
+    early_sizes = [[exchange.rows(2)] for exchange in early]
     last_sizes = [exchange.rows(2) for exchange in late]
     (late_keep, turned_keep), (late_came,) = steps(
         (late_keep, turned_keep),

time: 105 us -> 102 us (0.971)
  waiting for transfers between devices: 36.6 us -> 33.2 us
    ppermute x38, waiting for transfers between devices: 36.6 us -> 33.2 us  [swap(): return lax.ppermute(value, axis, [(i, i ^ bit) for i in range(count)])]
    pallas_call x32 -> x34, Pallas kernels: 36.3 us -> 36.3 us  [__call__(): pl.pallas_call(body, out_shape=tuple(shapes) + tuple((pltpu.VMEM(array.sh...]
  transfers between devices with their start and end apart: 38 -> 38, of which waited for: 15 -> 15; matrix products, arithmetic and copies ran while one was open for 0% -> 0% of each run, Pallas kernels for 32% -> 33%
where the time goes in v5:
time: 102 us
  Pallas kernels  36.3 us (36%)
  waiting for transfers between devices  33.2 us (33%)
  starting transfers between devices  31 us (30%)
  between operations  1.18 us (1%)
    pallas_call x34, Pallas kernels, __call__(): pl.pallas_call(body, out_shape=tuple(shapes) + tuple((pltpu.VMEM(array.sh...  36.3 us
    ppermute x38, waiting for transfers between devices, swap(): return lax.ppermute(value, axis, [(i, i ^ bit) for i in range(count)])  33.2 us
    ppermute x38, starting transfers between devices, swap(): return lax.ppermute(value, axis, [(i, i ^ bit) for i in range(count)])  31 us
  transfers between devices with their start and end apart: 38, of which 15 were waited for; matrix products, arithmetic and copies ran while one was open for 0% of the time, Pallas kernels for 33%

profile of v5, /device:TPU:0, one launch (start us, length us, event | category | flops | bytes accessed | tf_op | source)
XLA Modules:
  0.0 102.0 jit_solution(3381661637409382199)
XLA Ops:
  1.2 2.6 %collective-permute-start.4 = (bf16[768,128]{1,0:T(8,128)(2,1)}, bf16[768,128]{1,0:T(8,128)(2,1)S(1)}, u32[]{:S(2)}, u32[]{:S(2)}) collective-permute-start(bf16[768,128]{1,0:T(8,128)(2,1)} %refs_6_.4), channel_id=1, source_target_pairs={{0,2},{1,3},{2,0},{3,1},{4,6},{5,7},{6,4},{7,5},{8,10},{9,11},{10,... | collective-permute-start | bytes 589832 | tf_op jit(solution)/shard_map/ppermute | solution.py:901
  4.3 3.0 %shard_map.393 = (bf16[256,128]{1,0:T(8,128)(2,1)S(1)}, bf16[256,128]{1,0:T(8,128)(2,1)S(1)}, s32[42]{0:T(128)S(4)}, s32[8,64]{1,0:T(8,128)S(1)}, bf16[512,768]{...) custom-call(s32[2]{0:T(128)S(1)} %pad_add_fusion.refs_0_, ...), custom_call_target="tpu_custom_call" | custom-call | flops 3000000000 | tf_op jit(solution)/shard_map/pallas_call | solution.py:172
  7.3 1.8 %collective-permute-start.2 = (bf16[256,128]{1,0:T(8,128)(2,1)S(1)}, bf16[256,128]{1,0:T(8,128)(2,1)S(1)}, u32[]{:S(2)}, u32[]{:S(2)}) collective-permute-start(bf16[256,128]{1,0:T(8,128)(2,1)S(1)} %get-tuple-element.137), channel_id=1, source_target_pairs={{0,4},{4,0},{8,12},{12,8},{16,20},{20,16},{24,28},{28,24},{1,5},{5... | collective-permute-start | bytes 196616 | tf_op jit(solution)/shard_map/ppermute | solution.py:901
  11.6 1.9 %collective-permute-start.5 = (bf16[256,128]{1,0:T(8,128)(2,1)S(1)}, bf16[256,128]{1,0:T(8,128)(2,1)S(1)}, u32[]{:S(2)}, u32[]{:S(2)}) collective-permute-start(bf16[256,128]{1,0:T(8,128)(2,1)S(1)} %get-tuple-element.144), channel_id=1, source_target_pairs={{0,8},{4,12},{8,0},{12,4},{16,24},{20,28},{24,16},{28,20},{1,9},{5... | collective-permute-start | bytes 196616 | tf_op jit(solution)/shard_map/ppermute | solution.py:901
  13.5 2.4 %shard_map.396 = (bf16[384,128]{1,0:T(8,128)(2,1)S(1)}, bf16[256,768]{1,0:T(8,128)(2,1)S(1)}, bf16[256,192]{1,0:T(8,128)(2,1)S(1)}, bf16[768]{0:T(1024)(128)(2,1...) custom-call(s32[42]{0:T(128)S(4)} %get-tuple-element.126.refs_0_, ...), custom_call_target="tpu_custom_call" | custom-call | flops 2800000000 | tf_op jit(solution)/shard_map/pallas_call | solution.py:172
  15.9 1.6 %collective-permute-start.9 = (bf16[384,128]{1,0:T(8,128)(2,1)S(1)}, bf16[384,128]{1,0:T(8,128)(2,1)S(1)}, u32[]{:S(2)}, u32[]{:S(2)}) collective-permute-start(bf16[384,128]{1,0:T(8,128)(2,1)S(1)} %get-tuple-element.145.refs_3_.refs_8_), channel_id=1, source_target_pairs={{0,2},{1,3},{2,0},{3,1},{4,6},{5,7},{6,4},{7,5},{8,10},{9,11},{10,... | collective-permute-start | bytes 294920 | tf_op jit(solution)/shard_map/ppermute | solution.py:901
  17.5 2.7 %collective-permute-start.14 = (bf16[256,128]{1,0:T(8,128)(2,1)S(1)}, bf16[256,128]{1,0:T(8,128)(2,1)S(1)}, u32[]{:S(2)}, u32[]{:S(2)}) collective-permute-start(bf16[256,128]{1,0:T(8,128)(2,1)S(1)} %get-tuple-element.153), channel_id=1, source_target_pairs={{0,16},{4,20},{8,24},{12,28},{16,0},{20,4},{24,8},{28,12},{1,17},{... | collective-permute-start | bytes 196616 | tf_op jit(solution)/shard_map/ppermute | solution.py:901
  20.2 1.8 %shard_map.398 = (bf16[384,128]{1,0:T(8,128)(2,1)S(1)}, bf16[256,768]{1,0:T(8,128)(2,1)S(1)}, bf16[256,192]{1,0:T(8,128)(2,1)S(1)}, bf16[768,768]{1,0:T(8,128)(2...) custom-call(s32[42]{0:T(128)S(4)} %get-tuple-element.126.refs_0_, ...), custom_call_target="tpu_custom_call" | custom-call | flops 2500000000 | tf_op jit(solution)/shard_map/pallas_call | solution.py:172
  22.7 1.5 %collective-permute-done.14.refs_2_ = bf16[256,128]{1,0:T(8,128)(2,1)S(1)} collective-permute-done((bf16[256,128]{1,0:T(8,128)(2,1)S(1)}, bf16[256,128]{1,0:T(8,128)(2,1)S(1)}, u32[]{:S(2)}, u32[]{:S(2)}) %collective-permute-start.14) | collective-permute-done | bytes 65568 | tf_op jit(solution)/shard_map/ppermute | solution.py:901
  27.4 2.4 %collective-permute-done.16.refs_7_ = bf16[512,128]{1,0:T(8,128)(2,1)S(1)} collective-permute-done((bf16[512,128]{1,0:T(8,128)(2,1)S(1)}, bf16[512,128]{1,0:T(8,128)(2,1)S(1)}, u32[]{:S(2)}, u32[]{:S(2)}) %collective-permute-start.16) | collective-permute-done | bytes 131104 | tf_op jit(solution)/shard_map/ppermute | solution.py:901
  29.9 2.7 %shard_map.401 = (f32[512,768]{1,0:T(8,128)S(1)}, bf16[512,768]{1,0:T(8,128)(2,1)S(1)}, bf16[512,768]{1,0:T(8,128)(2,1)S(1)}, f32[512,768]{1,0:T(8,128)S(1)}) custom-call(s32[42]{0:T(128)S(4)} %get-tuple-element.126.refs_0_, bf16[512,768]{1,0:T(8,128)(2,1)S(1)} %get-tuple-element.128.refs_0_.refs_1_, bf16[768]{0:T(1024)(128)(2,1)S(1)} %get-tuple-element.139.refs_2_, ...), custom_call_target="tpu_custom_call" | custom-call | flops 2600000000 | tf_op jit(solution)/shard_map/pallas_call | solution.py:172
  36.3 2.9 %shard_map.405 = (bf16[2304,128]{1,0:T(8,128)(2,1)S(1)}, bf16[2304,128]{1,0:T(8,128)(2,1)}, bf16[2304,128]{1,0:T(8,128)(2,1)S(1)}, bf16[2304,128]{1,0:T(8,128)(2,1)}) custom-call(s32[42]{0:T(128)S(4)} %get-tuple-element.126.refs_0_, bf16[256,768]{1,0:T(8,128)(2,1)S(1)} %get-tuple-element.161.refs_1_.refs_4_, ...), custom_call_target="tpu_custom_call" | custom-call | flops 2200000000 | tf_op jit(solution)/shard_map/pallas_call | solution.py:172
  40.1 1.5 %collective-permute-start.24 = (bf16[2304,128]{1,0:T(8,128)(2,1)}, bf16[2304,128]{1,0:T(8,128)(2,1)}, u32[]{:S(2)}, u32[]{:S(2)}) collective-permute-start(bf16[2304,128]{1,0:T(8,128)(2,1)} %get-tuple-element.179), channel_id=1, source_target_pairs={{0,4},{4,0},{8,12},{12,8},{16,20},{20,16},{24,28},{28,24},{1,5},{5... | collective-permute-start | bytes 1769480 | tf_op jit(solution)/shard_map/ppermute | solution.py:901
  42.7 2.3 %shard_map.407 = (f32[256,128]{1,0:T(8,128)S(1)}, f32[1,128]{1,0:T(1,128)S(1)}, f32[3,256,128]{2,1,0:T(8,128)S(1)}) custom-call(s32[42]{0:T(128)S(4)} %get-tuple-element.126.refs_0_, s32[8,64]{1,0:T(8,128)S(1)} %get-tuple-element.127.refs_1_, bf16[8,256,128]{2,1,0:T(8,128)(2,1)} %refs_2_.7, bf16[2,256,256]{2,1,0:T(8,128)(2,1)} %constant.17.clone.refs_3_, ...), custom_call_target="tpu_custom_call" | custom-call | flops 20000000000 | tf_op jit(solution)/shard_map/pallas_call | solution.py:172
  49.1 4.2 %shard_map.411 = (bf16[512,576]{1,0:T(8,128)(2,1)S(1)}, bf16[512,768]{1,0:T(8,128)(2,1)S(1)}, f32[128,768]{1,0:T(8,128)S(1)}, f32[3,768]{1,0:T(4,128)S(1)}) custom-call(s32[42]{0:T(128)S(4)} %get-tuple-element.126.refs_0_, bf16[256,768]{1,0:T(8,128)(2,1)S(1)} %shard_map.409.refs_1_, bf16[256,768]{1,0:T(8,128)(2,1)S(1)} %collective-permute-done.21.refs_2_, ...), custom_call_target="tpu_custom_call" | custom-call | flops 16499999744 | tf_op jit(solution)/shard_map/pallas_call | solution.py:172
  54.6 1.6 %shard_map.413 = (bf16[1152,128]{1,0:T(8,128)(2,1)S(1)}, bf16[1152,128]{1,0:T(8,128)(2,1)S(1)}, bf16[1152,128]{1,0:T(8,128)(2,1)S(1)}, bf16[1152,128]{1,0:T(8,128)(2,1)S(1)}, f32[1,576]{1,0:T(1,128)S(1)}) custom-call(s32[42]{0:T(128)S(4)} %get-tuple-element.126.refs_0_, bf16[512,768]{1,0:T(8,128)(2,1)S(1)} %get-tuple-element.135.refs_3_.refs_1_, ...), custom_call_target="tpu_custom_call" | custom-call | flops 120000004096 | tf_op jit(solution)/shard_map/pallas_call | solution.py:172
  56.2 1.6 %collective-permute-start.28 = (bf16[1152,128]{1,0:T(8,128)(2,1)S(1)}, bf16[1152,128]{1,0:T(8,128)(2,1)S(1)}, u32[]{:S(2)}, u32[]{:S(2)}) collective-permute-start(bf16[1152,128]{1,0:T(8,128)(2,1)S(1)} %get-tuple-element.196), channel_id=1, source_target_pairs={{0,4},{4,0},{8,12},{12,8},{16,20},{20,16},{24,28},{28,24},{1,5},{5... | collective-permute-start | bytes 884744 | tf_op jit(solution)/shard_map/ppermute | solution.py:901
  62.2 2.7 %collective-permute-start.33 = (bf16[1152,128]{1,0:T(8,128)(2,1)S(1)}, bf16[1152,128]{1,0:T(8,128)(2,1)S(1)}, u32[]{:S(2)}, u32[]{:S(2)}) collective-permute-start(bf16[1152,128]{1,0:T(8,128)(2,1)S(1)} %get-tuple-element.204), channel_id=1, source_target_pairs={{0,16},{4,20},{8,24},{12,28},{16,0},{20,4},{24,8},{28,12},{1,17},{... | collective-permute-start | bytes 884744 | tf_op jit(solution)/shard_map/ppermute | solution.py:901
  70.3 3.7 %collective-permute-done.29.refs_5_ = bf16[816,128]{1,0:T(8,128)(2,1)S(1)} collective-permute-done((bf16[816,128]{1,0:T(8,128)(2,1)S(1)}, bf16[816,128]{1,0:T(8,128)(2,1)S(1)}, u32[]{:S(2)}, u32[]{:S(2)}) %collective-permute-start.29) | collective-permute-done | bytes 208928 | tf_op jit(solution)/shard_map/ppermute | solution.py:901
  76.2 4.0 %collective-permute-done.34.refs_2_ = bf16[1152,128]{1,0:T(8,128)(2,1)S(1)} collective-permute-done((bf16[1152,128]{1,0:T(8,128)(2,1)S(1)}, bf16[1152,128]{1,0:T(8,128)(2,1)S(1)}, u32[]{:S(2)}, u32[]{:S(2)}) %collective-permute-start.34) | collective-permute-done | bytes 294944 | tf_op jit(solution)/shard_map/ppermute | solution.py:901
  82.7 5.3 %collective-permute-done.31.refs_3_ = bf16[1136,128]{1,0:T(8,128)(2,1)S(1)} collective-permute-done((bf16[1136,128]{1,0:T(8,128)(2,1)S(1)}, bf16[1136,128]{1,0:T(8,128)(2,1)S(1)}, u32[]{:S(2)}, u32[]{:S(2)}) %collective-permute-start.31) | collective-permute-done | bytes 290848 | tf_op jit(solution)/shard_map/ppermute | solution.py:901
  88.2 3.2 %collective-permute-done.36.refs_2_ = bf16[576,128]{1,0:T(8,128)(2,1)S(1)} collective-permute-done((bf16[576,128]{1,0:T(8,128)(2,1)S(1)}, bf16[576,128]{1,0:T(8,128)(2,1)S(1)}, u32[]{:S(2)}, u32[]{:S(2)}) %collective-permute-start.36) | collective-permute-done | bytes 147488 | tf_op jit(solution)/shard_map/ppermute | solution.py:901
  91.4 3.5 %collective-permute-done.37.refs_3_ = bf16[576,128]{1,0:T(8,128)(2,1)S(1)} collective-permute-done((bf16[576,128]{1,0:T(8,128)(2,1)S(1)}, bf16[576,128]{1,0:T(8,128)(2,1)S(1)}, u32[]{:S(2)}, u32[]{:S(2)}) %collective-permute-start.37) | collective-permute-done | bytes 147488 | tf_op jit(solution)/shard_map/ppermute | solution.py:901
  95.7 4.6 %collective-permute-done.35.refs_4_ = bf16[1008,128]{1,0:T(8,128)(2,1)S(1)} collective-permute-done((bf16[1008,128]{1,0:T(8,128)(2,1)S(1)}, bf16[1008,128]{1,0:T(8,128)(2,1)S(1)}, u32[]{:S(2)}, u32[]{:S(2)}) %collective-permute-start.35) | collective-permute-done | bytes 258080 | tf_op jit(solution)/shard_map/ppermute | solution.py:901
  (105 shorter events, 35.6 us)
Async XLA Ops:
  0.7 9.1 %collective-permute-start.1 = (bf16[768,128]{1,0:T(8,128)(2,1)}, bf16[768,128]{1,0:T(8,128)(2,1)S(1)}, u32[]{:S(2)}, u32[]{:S(2)}) collective-permute-start(bf16[768,128]{1,0:T(8,128)(2,1)} %refs_6_.4), channel_id=1, source_target_pairs={{0,1},{1,0},{2,3},{3,2},{4,5},{5,4},{6,7},{7,6},{8,9},{9,8},{10,11... | collective-permute-start | bytes 589832 | tf_op jit(solution)/shard_map/ppermute | solution.py:901
  1.2 8.6 %collective-permute-start.4 = (bf16[768,128]{1,0:T(8,128)(2,1)}, bf16[768,128]{1,0:T(8,128)(2,1)S(1)}, u32[]{:S(2)}, u32[]{:S(2)}) collective-permute-start(bf16[768,128]{1,0:T(8,128)(2,1)} %refs_6_.4), channel_id=1, source_target_pairs={{0,2},{1,3},{2,0},{3,1},{4,6},{5,7},{6,4},{7,5},{8,10},{9,11},{10,... | collective-permute-start | bytes 589832 | tf_op jit(solution)/shard_map/ppermute | solution.py:901
  3.8 6.0 %collective-permute-start = (bf16[192,768]{1,0:T(8,128)(2,1)}, bf16[192,768]{1,0:T(8,128)(2,1)S(1)}, u32[]{:S(2)}, u32[]{:S(2)}) collective-permute-start(bf16[192,768]{1,0:T(8,128)(2,1)} %refs_5_.7), channel_id=1, source_target_pairs={{0,1},{1,0},{2,3},{3,2},{4,5},{5,4},{6,7},{7,6},{8,9},{9,8},{10,11... | collective-permute-start | bytes 884744 | tf_op jit(solution)/shard_map/ppermute | solution.py:901
  3.9 13.5 %collective-permute-start.3 = (bf16[192,768]{1,0:T(8,128)(2,1)}, bf16[192,768]{1,0:T(8,128)(2,1)S(1)}, u32[]{:S(2)}, u32[]{:S(2)}) collective-permute-start(bf16[192,768]{1,0:T(8,128)(2,1)} %refs_5_.7), channel_id=1, source_target_pairs={{0,2},{1,3},{2,0},{3,1},{4,6},{5,7},{6,4},{7,5},{8,10},{9,11},{10,... | collective-permute-start | bytes 884744 | tf_op jit(solution)/shard_map/ppermute | solution.py:901
  9.7 12.8 %collective-permute-start.7 = (bf16[768,128]{1,0:T(8,128)(2,1)S(1)}, bf16[768,128]{1,0:T(8,128)(2,1)S(1)}, u32[]{:S(2)}, u32[]{:S(2)}) collective-permute-start(bf16[768,128]{1,0:T(8,128)(2,1)S(1)} %collective-permute-done.4.refs_10_.refs_7_), channel_id=1, source_target_pairs={{0,1},{1,0},{2,3},{3,2},{4,5},{5,4},{6,7},{7,6},{8,9},{9,8},{10,11... | collective-permute-start | bytes 589832 | tf_op jit(solution)/shard_map/ppermute | solution.py:901
  11.6 5.9 %collective-permute-start.5 = (bf16[256,128]{1,0:T(8,128)(2,1)S(1)}, bf16[256,128]{1,0:T(8,128)(2,1)S(1)}, u32[]{:S(2)}, u32[]{:S(2)}) collective-permute-start(bf16[256,128]{1,0:T(8,128)(2,1)S(1)} %get-tuple-element.144), channel_id=1, source_target_pairs={{0,8},{4,12},{8,0},{12,4},{16,24},{20,28},{24,16},{28,20},{1,9},{5... | collective-permute-start | bytes 196616 | tf_op jit(solution)/shard_map/ppermute | solution.py:901
  15.9 9.6 %collective-permute-start.9 = (bf16[384,128]{1,0:T(8,128)(2,1)S(1)}, bf16[384,128]{1,0:T(8,128)(2,1)S(1)}, u32[]{:S(2)}, u32[]{:S(2)}) collective-permute-start(bf16[384,128]{1,0:T(8,128)(2,1)S(1)} %get-tuple-element.145.refs_3_.refs_8_), channel_id=1, source_target_pairs={{0,2},{1,3},{2,0},{3,1},{4,6},{5,7},{6,4},{7,5},{8,10},{9,11},{10,... | collective-permute-start | bytes 294920 | tf_op jit(solution)/shard_map/ppermute | solution.py:901
  17.5 6.7 %collective-permute-start.14 = (bf16[256,128]{1,0:T(8,128)(2,1)S(1)}, bf16[256,128]{1,0:T(8,128)(2,1)S(1)}, u32[]{:S(2)}, u32[]{:S(2)}) collective-permute-start(bf16[256,128]{1,0:T(8,128)(2,1)S(1)} %get-tuple-element.153), channel_id=1, source_target_pairs={{0,16},{4,20},{8,24},{12,28},{16,0},{20,4},{24,8},{28,12},{1,17},{... | collective-permute-start | bytes 196616 | tf_op jit(solution)/shard_map/ppermute | solution.py:901
  26.9 5.7 %collective-permute-start.15 = (bf16[512,128]{1,0:T(8,128)(2,1)S(1)}, bf16[512,128]{1,0:T(8,128)(2,1)S(1)}, u32[]{:S(2)}, u32[]{:S(2)}) collective-permute-start(bf16[512,128]{1,0:T(8,128)(2,1)S(1)} %shard_map.400.refs_16_.refs_5_.refs_7_.refs_3_), channel_id=1, source_target_pairs={{0,1},{1,0},{2,3},{3,2},{4,5},{5,4},{6,7},{7,6},{8,9},{9,8},{10,11... | collective-permute-start | bytes 393224 | tf_op jit(solution)/shard_map/ppermute | solution.py:901
  35.8 11.5 %collective-permute-start.19 = (bf16[256,768]{1,0:T(8,128)(2,1)S(1)}, bf16[256,768]{1,0:T(8,128)(2,1)S(1)}, u32[]{:S(2)}, u32[]{:S(2)}) collective-permute-start(bf16[256,768]{1,0:T(8,128)(2,1)S(1)} %shard_map.404.refs_7_.refs_0_), channel_id=1, source_target_pairs={{0,2},{1,3},{2,0},{3,1},{4,6},{5,7},{6,4},{7,5},{8,10},{9,11},{10,... | collective-permute-start | bytes 1179656 | tf_op jit(solution)/shard_map/ppermute | solution.py:901
  40.1 17.7 %collective-permute-start.24 = (bf16[2304,128]{1,0:T(8,128)(2,1)}, bf16[2304,128]{1,0:T(8,128)(2,1)}, u32[]{:S(2)}, u32[]{:S(2)}) collective-permute-start(bf16[2304,128]{1,0:T(8,128)(2,1)} %get-tuple-element.179), channel_id=1, source_target_pairs={{0,4},{4,0},{8,12},{12,8},{16,20},{20,16},{24,28},{28,24},{1,5},{5... | collective-permute-start | bytes 1769480 | tf_op jit(solution)/shard_map/ppermute | solution.py:901
  41.6 16.6 %collective-permute-start.25 = (bf16[2304,128]{1,0:T(8,128)(2,1)}, bf16[2304,128]{1,0:T(8,128)(2,1)}, u32[]{:S(2)}, u32[]{:S(2)}) collective-permute-start(bf16[2304,128]{1,0:T(8,128)(2,1)} %get-tuple-element.180), channel_id=1, source_target_pairs={{0,8},{4,12},{8,0},{12,4},{16,24},{20,28},{24,16},{28,20},{1,9},{5... | collective-permute-start | bytes 1769480 | tf_op jit(solution)/shard_map/ppermute | solution.py:901
  45.8 13.8 %collective-permute-start.22 = (bf16[256,768]{1,0:T(8,128)(2,1)}, bf16[256,768]{1,0:T(8,128)(2,1)}, u32[]{:S(2)}, u32[]{:S(2)}) collective-permute-start(bf16[256,768]{1,0:T(8,128)(2,1)} %shard_map.408.refs_2_.refs_0_), channel_id=1, source_target_pairs={{0,2},{1,3},{2,0},{3,1},{4,6},{5,7},{6,4},{7,5},{8,10},{9,11},{10,... | collective-permute-start | bytes 1179656 | tf_op jit(solution)/shard_map/ppermute | solution.py:901
  56.2 14.0 %collective-permute-start.28 = (bf16[1152,128]{1,0:T(8,128)(2,1)S(1)}, bf16[1152,128]{1,0:T(8,128)(2,1)S(1)}, u32[]{:S(2)}, u32[]{:S(2)}) collective-permute-start(bf16[1152,128]{1,0:T(8,128)(2,1)S(1)} %get-tuple-element.196), channel_id=1, source_target_pairs={{0,4},{4,0},{8,12},{12,8},{16,20},{20,16},{24,28},{28,24},{1,5},{5... | collective-permute-start | bytes 884744 | tf_op jit(solution)/shard_map/ppermute | solution.py:901
  57.8 12.5 %collective-permute-start.30 = (bf16[1152,128]{1,0:T(8,128)(2,1)S(1)}, bf16[1152,128]{1,0:T(8,128)(2,1)S(1)}, u32[]{:S(2)}, u32[]{:S(2)}) collective-permute-start(bf16[1152,128]{1,0:T(8,128)(2,1)S(1)} %get-tuple-element.198), channel_id=1, source_target_pairs={{0,8},{4,12},{8,0},{12,4},{16,24},{20,28},{24,16},{28,20},{1,9},{5... | collective-permute-start | bytes 884744 | tf_op jit(solution)/shard_map/ppermute | solution.py:901
  58.3 7.3 %collective-permute-start.27 = (bf16[144,768]{1,0:T(8,128)(2,1)S(1)}, bf16[144,768]{1,0:T(8,128)(2,1)S(1)}, u32[]{:S(2)}, u32[]{:S(2)}) collective-permute-start(bf16[144,768]{1,0:T(8,128)(2,1)S(1)} %get-tuple-element.193), channel_id=1, source_target_pairs={{0,2},{1,3},{2,0},{3,1},{4,6},{5,7},{6,4},{7,5},{8,10},{9,11},{10,... | collective-permute-start | bytes 663560 | tf_op jit(solution)/shard_map/ppermute | solution.py:901
  62.2 18.2 %collective-permute-start.33 = (bf16[1152,128]{1,0:T(8,128)(2,1)S(1)}, bf16[1152,128]{1,0:T(8,128)(2,1)S(1)}, u32[]{:S(2)}, u32[]{:S(2)}) collective-permute-start(bf16[1152,128]{1,0:T(8,128)(2,1)S(1)} %get-tuple-element.204), channel_id=1, source_target_pairs={{0,16},{4,20},{8,24},{12,28},{16,0},{20,4},{24,8},{28,12},{1,17},{... | collective-permute-start | bytes 884744 | tf_op jit(solution)/shard_map/ppermute | solution.py:901
  65.9 8.1 %collective-permute-start.29 = (bf16[816,128]{1,0:T(8,128)(2,1)S(1)}, bf16[816,128]{1,0:T(8,128)(2,1)S(1)}, u32[]{:S(2)}, u32[]{:S(2)}) collective-permute-start(bf16[816,128]{1,0:T(8,128)(2,1)S(1)} %get-tuple-element.197), channel_id=1, source_target_pairs={{0,4},{4,0},{8,12},{12,8},{16,20},{20,16},{24,28},{28,24},{1,5},{5... | collective-permute-start | bytes 626696 | tf_op jit(solution)/shard_map/ppermute | solution.py:901
  68.2 12.0 %collective-permute-start.34 = (bf16[1152,128]{1,0:T(8,128)(2,1)S(1)}, bf16[1152,128]{1,0:T(8,128)(2,1)S(1)}, u32[]{:S(2)}, u32[]{:S(2)}) collective-permute-start(bf16[1152,128]{1,0:T(8,128)(2,1)S(1)} %get-tuple-element.205), channel_id=1, source_target_pairs={{0,4},{4,0},{8,12},{12,8},{16,20},{20,16},{24,28},{28,24},{1,5},{5... | collective-permute-start | bytes 884744 | tf_op jit(solution)/shard_map/ppermute | solution.py:901
  74.1 8.6 %collective-permute-start.32 = (bf16[576,128]{1,0:T(8,128)(2,1)S(1)}, bf16[576,128]{1,0:T(8,128)(2,1)S(1)}, u32[]{:S(2)}, u32[]{:S(2)}) collective-permute-start(bf16[576,128]{1,0:T(8,128)(2,1)S(1)} %get-tuple-element.203), channel_id=1, source_target_pairs={{0,4},{4,0},{8,12},{12,8},{16,20},{20,16},{24,28},{28,24},{1,5},{5... | collective-permute-start | bytes 442376 | tf_op jit(solution)/shard_map/ppermute | solution.py:901
  75.4 12.6 %collective-permute-start.31 = (bf16[1136,128]{1,0:T(8,128)(2,1)S(1)}, bf16[1136,128]{1,0:T(8,128)(2,1)S(1)}, u32[]{:S(2)}, u32[]{:S(2)}) collective-permute-start(bf16[1136,128]{1,0:T(8,128)(2,1)S(1)} %get-tuple-element.202), channel_id=1, source_target_pairs={{0,8},{4,12},{8,0},{12,4},{16,24},{20,28},{24,16},{28,20},{1,9},{5... | collective-permute-start | bytes 872456 | tf_op jit(solution)/shard_map/ppermute | solution.py:901
  80.4 11.0 %collective-permute-start.36 = (bf16[576,128]{1,0:T(8,128)(2,1)S(1)}, bf16[576,128]{1,0:T(8,128)(2,1)S(1)}, u32[]{:S(2)}, u32[]{:S(2)}) collective-permute-start(bf16[576,128]{1,0:T(8,128)(2,1)S(1)} %get-tuple-element.223), channel_id=1, source_target_pairs={{0,8},{4,12},{8,0},{12,4},{16,24},{20,28},{24,16},{28,20},{1,9},{5... | collective-permute-start | bytes 442376 | tf_op jit(solution)/shard_map/ppermute | solution.py:901
  81.5 13.4 %collective-permute-start.37 = (bf16[576,128]{1,0:T(8,128)(2,1)S(1)}, bf16[576,128]{1,0:T(8,128)(2,1)S(1)}, u32[]{:S(2)}, u32[]{:S(2)}) collective-permute-start(bf16[576,128]{1,0:T(8,128)(2,1)S(1)} %get-tuple-element.224), channel_id=1, source_target_pairs={{0,16},{4,20},{8,24},{12,28},{16,0},{20,4},{24,8},{28,12},{1,17},{... | collective-permute-start | bytes 442376 | tf_op jit(solution)/shard_map/ppermute | solution.py:901
  88.1 12.3 %collective-permute-start.35 = (bf16[1008,128]{1,0:T(8,128)(2,1)S(1)}, bf16[1008,128]{1,0:T(8,128)(2,1)S(1)}, u32[]{:S(2)}, u32[]{:S(2)}) collective-permute-start(bf16[1008,128]{1,0:T(8,128)(2,1)S(1)} %get-tuple-element.210), channel_id=1, source_target_pairs={{0,16},{4,20},{8,24},{12,28},{16,0},{20,4},{24,8},{28,12},{1,17},{... | collective-permute-start | bytes 774152 | tf_op jit(solution)/shard_map/ppermute | solution.py:901
  (23 other events, 88.2 us)

commit v6 on v5

--- a/solution.py
+++ b/solution.py
@@ -96,6 +96,7 @@
 
 RATE = 10**9
 COST_SHARE = 1.0
+COVER = 40.0
 BYTES = 0
 
 
@@ -638,33 +639,42 @@
 
 
 def attention_back_kernel(
-    heads, info_ref, sum_ref, sum_other_ref, hidden_ref, low_ref, low_other_ref, gain_ref, weight_ref, qkv_ref,
-    prob_ref, prob_last_ref, grads_ref, attn_low_ref, own_ref, bias_ref, grad_ref, probs_ref,
+    heads, own, info_ref, sum_ref, hidden_ref, low_ref, gain_ref, weight_ref, qkv_ref, prob_ref, prob_last_ref,
+    grads_ref, attn_low_ref, grad_ref, bias_ref, probs_ref,
 ):
     gain = wide_row(gain_ref)
     bias_ref[...] = jnp.zeros_like(bias_ref)
-    half = prob_ref.shape[0]
-    probs_ref[:half, :] = prob_ref[...]
-    probs_ref[half:, :] = prob_last_ref[...]
-
-    def body(source, rows, part, size):
+    half = sum_ref.shape[0]
+    upper = info_ref[1] & 1
+    which = upper if own else 1 - upper
+
+    @pl.when(which == 0)
+    def _():
+        probs_ref[...] = prob_ref[...]
+
+    @pl.when(which == 1)
+    def _():
+        probs_ref[...] = prob_last_ref[...]
+
+    def body(start, size):
+        part = pl.ds(start, size)
+        rows = pl.ds(pl.multiple_of(which * half + start, size), size)
         normed, spread = normalized(hidden_ref[rows, :])
-        grad = (sum_ref, sum_other_ref)[source][part, :].astype(wide_type)
+        grad = sum_ref[part, :].astype(wide_type)
         bias_ref[0:1, :] += row_sum(grad * normed)
         bias_ref[1:2, :] += row_sum(grad)
-        down_low = (low_ref, low_other_ref)[source][part, :].astype(wide_type)
-        hidden_grad = down_low + norm_back(grad, normed, spread, gain)
-        grad_ref[rows, :] = hidden_grad
+        hidden_grad = low_ref[part, :].astype(wide_type) + norm_back(grad, normed, spread, gain)
+        grad_ref[part, :] = hidden_grad
         bias_ref[2:3, :] += row_sum(hidden_grad)
         attn_low = hidden_grad.astype(low_type)
-        attn_low_ref[rows, :] = attn_low
+        attn_low_ref[part, :] = attn_low
         attended_grad = dot_right_t(attn_low, weight_ref[...]).astype(low_type)
         for head in range(heads):
             base = head * 3 * HEAD_DIM
             queries = qkv_ref[rows, base : base + HEAD_DIM]
             key_rows = qkv_ref[rows, base + HEAD_DIM : base + 2 * HEAD_DIM]
             value_rows = qkv_ref[rows, base + 2 * HEAD_DIM : base + 3 * HEAD_DIM]
-            probs = probs_ref[rows, head * BLOCK : (head + 1) * BLOCK]
+            probs = probs_ref[part, head * BLOCK : (head + 1) * BLOCK]
             grad_rows = attended_grad[:, head * HEAD_DIM : (head + 1) * HEAD_DIM]
             value_low = dot(probs, grad_rows).astype(low_type)
             prob_grad = dot_right_t(value_rows, grad_rows)
@@ -675,13 +685,11 @@
             ).astype(low_type)
             query_low = (dot_left_t(score_low, key_rows) * scale_factor).astype(low_type)
             key_low = (dot(score_low, queries) * scale_factor).astype(low_type)
-            grads_ref[rows, base : base + HEAD_DIM] = query_low
-            grads_ref[rows, base + HEAD_DIM : base + 2 * HEAD_DIM] = key_low
-            grads_ref[rows, base + 2 * HEAD_DIM : base + 3 * HEAD_DIM] = value_low
-
-    both_halves(info_ref[1] & 1, sum_ref.shape[0], body)
-    share = own_ref.shape[0]
-    own_ref[...] = grad_ref[pl.ds(pl.multiple_of(info_ref[1] * share, share), share), :]
+            grads_ref[part, base : base + HEAD_DIM] = query_low
+            grads_ref[part, base + HEAD_DIM : base + 2 * HEAD_DIM] = key_low
+            grads_ref[part, base + 2 * HEAD_DIM : base + 3 * HEAD_DIM] = value_low
+
+    over_rows(half, BLOCK, body)
 
 
 def views(ref, sizes):
@@ -699,21 +707,28 @@
 
 
 def late_grads_kernel(
-    exchanges, pad, middle, info_ref, act_ref, grads_ref, attn_low_ref, first_ref, last_ref, keep_ref, sent_ref,
-    turned_keep_ref, turned_sent_ref, bias_ref, wide_ref,
+    exchanges, pad, middle, info_ref, act_ref, grads_ref, grads_other_ref, low_ref, low_other_ref, first_ref, last_ref,
+    keep_ref, sent_ref, turned_keep_ref, turned_sent_ref, bias_ref, wide_ref,
 ):
     columns = grads_ref.shape[1]
-    half, first = first_ref.shape
-    wide_ref[:, :first] = dot_left_t(attn_low_ref[:half, :], first_ref[...]) + dot_left_t(
-        attn_low_ref[half:, :], last_ref[...]
-    )
-    wide_ref[:, first : first + columns] = dot_left_t(act_ref[...], grads_ref[...])
+    first = first_ref.shape[1]
+    lower = (info_ref[1] & 1) == 0
+    attended = (first_ref[...].astype(wide_type), last_ref[...].astype(wide_type))
+    attended_own = jnp.where(lower, attended[0], attended[1]).astype(low_type)
+    attended_other = jnp.where(lower, attended[1], attended[0]).astype(low_type)
+    act_own, act_other = halves_of(info_ref, (act_ref,))
+    wide_ref[:, :first] = dot_left_t(low_ref[...], attended_own) + dot_left_t(
+        low_other_ref[...], attended_other
+    )
+    wide_ref[:, first : first + columns] = dot_left_t(act_own, grads_ref[...]) + dot_left_t(
+        act_other, grads_other_ref[...]
+    )
     put_blocks(exchanges[0], info_ref, keep_ref, sent_ref, wide_ref.at[:, pl.ds(0, middle)], pad)
     put_blocks(
         exchanges[1], info_ref, turned_keep_ref, turned_sent_ref,
         wide_ref.at[:, pl.ds(middle, wide_ref.shape[1] - middle)], pad,
     )
-    bias_ref[...] = row_sum(grads_ref[...].astype(wide_type))
+    bias_ref[...] = row_sum(grads_ref[...].astype(wide_type)) + row_sum(grads_other_ref[...].astype(wide_type))
 
 
 EXTRA = 16
@@ -740,18 +755,19 @@
     over_rows(rows_ref.shape[0], CHUNK, body)
 
 
-def input_part_kernel(info_ref, normed_ref, grads_ref, weight_ref, keep_ref, sent_ref, part_ref, bias_ref):
+def input_part_kernel(
+    info_ref, normed_ref, grads_ref, grads_other_ref, weight_ref, keep_ref, sent_ref, part_ref, bias_ref
+):
     lower_bit = info_ref[1] & 1
     bias_ref[...] = jnp.zeros_like(bias_ref)
 
-    def body(start, size):
-        rows = pl.ds(start, size)
-        grad = dot(grads_ref[rows, :], weight_ref[...])
+    def body(source, rows, part, size):
+        grad = dot((grads_ref, grads_other_ref)[source][part, :], weight_ref[...])
         part_ref[rows, :] = grad
         bias_ref[0:1, :] += row_sum(grad * normed_ref[rows, :].astype(wide_type))
         bias_ref[1:2, :] += row_sum(grad)
 
-    over_rows(normed_ref.shape[0], CHUNK, body)
+    both_halves(lower_bit, grads_ref.shape[0], body)
     size = keep_ref.shape[0] - EXTRA
     share = size // (lax.axis_size("mp") // 2)
     for out_ref, which in ((sent_ref, 1 - lower_bit), (keep_ref, lower_bit)):
@@ -775,12 +791,17 @@
         put_extra(out_ref, half, own[0] + other[0], own[1] + other[1])
 
 
-def input_grad_kernel(info_ref, rows_ref, keep_ref, other_ref, own_ref, gain_ref, out_ref):
+def input_grad_kernel(info_ref, rows_ref, keep_ref, other_ref, grad_ref, grad_other_ref, gain_ref, out_ref):
     share = out_ref.shape[0]
-    rows = pl.ds(pl.multiple_of(info_ref[1] * share, share), share)
+    half = grad_ref.shape[0]
+    start = info_ref[1] * share
+    rows = pl.ds(pl.multiple_of(start, share), share)
+    part = pl.ds(pl.multiple_of(start % half, share), share)
+    own = start // half == (info_ref[1] & 1)
     normed, spread = normalized(rows_ref[rows, :].astype(wide_type))
     grad = keep_ref[:share, :].astype(wide_type) + other_ref[:share, :].astype(wide_type)
-    out_ref[...] = (own_ref[...] + norm_back(grad, normed, spread, wide_row(gain_ref))).astype(low_type)
+    hidden_grad = jnp.where(own, grad_ref[part, :], grad_other_ref[part, :])
+    out_ref[...] = (hidden_grad + norm_back(grad, normed, spread, wide_row(gain_ref))).astype(low_type)
 
 
 VECTOR_ROWS = 48
@@ -822,7 +843,7 @@
 
 def last_kernel(
     info, exchange, heads, pad, info_ref, encoded_ref, wide_ref, enc_ref, pos_ref, mask_ref, grads_ref, grads_other_ref,
-    second_ref, qkv_ref, first_ref, first_other_ref, keep_ref, sent_ref, rows_ref,
+    second_ref, second_other_ref, qkv_ref, first_ref, first_other_ref, keep_ref, sent_ref, rows_ref,
 ):
     put_blocks(exchange, info_ref, keep_ref, sent_ref, wide_ref, 0)
     put_blocks(exchange, info_ref, keep_ref, sent_ref, pos_ref, 0, pad)
@@ -833,6 +854,7 @@
             ref[at : at + VIS, :] = encoded_ref[pl.ds(pl.multiple_of(image * VIS, VIS), VIS), :]
             at += VIS
     qkv, early = qkv_ref[...], grads_ref[...] + grads_other_ref[...]
+    second = second_ref[...] + second_other_ref[...]
     empty = jnp.zeros((1, 2 * LANES - heads * HEAD_DIM), wide_type)
     spread = []
     for part in (0, 2):
@@ -844,7 +866,7 @@
     put_rows(
         (
             jnp.concatenate(spread, axis=1), early[1:2], row_sum(enc_ref[...].astype(wide_type)), mask_ref[...],
-            own[0] + other[0], own[1] + other[1], second_ref[0:1, :], second_ref[1:2, :], second_ref[2:3, :],
+            own[0] + other[0], own[1] + other[1], second[0:1], second[1:2], second[2:3],
             early[0:1],
         ),
         rows_ref,
@@ -936,7 +958,7 @@
     late_columns = qkv_columns + head_columns
     turned = (1, 0) + bits[2:]
     back_exchange = Exchange(count, bits, 0, moved=VIS)
-    far = (0, 2, 1) + bits[3:]
+    far = bits
     up_exchange = Exchange(count, far, units // LANES * pads[0])
     down_exchange = Exchange(count, turned, units // LANES * pads[0])
     tiles = late_columns // LANES
@@ -1144,26 +1166,30 @@
         cost=20.0,
     )
     next(out_steps)
+    (normed_low,) = run(norm_kernel, [low(rows, width)], (patch_rows,), cost=0.6)
     next(second_steps)
     second_sum, second_other = finish(second_steps)
-    (normed_low,) = run(norm_kernel, [low(rows, width)], (patch_rows,), cost=40.0)
-    run.share = 3.0
-    grads, attn_low, own_grad, second_grads = run(
-        lambda *refs: attention_back_kernel(heads, *refs),
-        [low(rows, qkv_columns), low(rows, width), wide(own_rows, width), wide(3, width)],
-        (
-            facts, second_sum, second_other, hidden, down_low, down_low_other, second_gain, out_near, qkv,
-            first_probs, last_probs,
-        ),
-        (SMEM,) + (VMEM,) * 10,
-        scratch=[pltpu.VMEM((rows, width), wide_type), pltpu.VMEM((rows, heads * BLOCK), low_type)],
-        cost=5.5,
+
+    def attention_back(own, total, down_part, cost):
+        return run(
+            lambda *refs: attention_back_kernel(heads, own, *refs),
+            [low(half, qkv_columns), low(half, width), wide(half, width), wide(3, width)],
+            (facts, total, hidden, down_part, second_gain, out_near, qkv, first_probs, last_probs),
+            (SMEM,) + (VMEM,) * 8,
+            scratch=[pltpu.VMEM((half, heads * BLOCK), low_type)],
+            cost=cost,
+        )
+
+    grads, attn_low, hidden_grad, second_grads = attention_back(True, second_sum, down_low, COVER)
+    run.share = 2.0
+    grads_other, attn_low_other, hidden_grad_other, second_grads_other = attention_back(
+        False, second_other, down_low_other, 2.0
     )
     in_keep, in_sent = run(
         input_part_kernel,
         [low(half + EXTRA, width)] * 2,
-        (facts, normed_low, grads, qkv_weight_t),
-        (SMEM,) + (VMEM,) * 3,
+        (facts, normed_low, grads, grads_other, qkv_weight_t),
+        (SMEM,) + (VMEM,) * 4,
         scratch=[pltpu.VMEM((rows, width), wide_type), pltpu.VMEM((2, width), wide_type)],
         cost=2.0,
     )
@@ -1174,8 +1200,8 @@
         [low(late_exchange.rows(0), LANES)] * 2
         + [low(turned_exchange.rows(0), LANES)] * 2
         + [wide(1, qkv_columns)],
-        (facts, act_one, grads, attn_low, first_attended, last_attended),
-        (SMEM,) + (VMEM,) * 5,
+        (facts, act_one, grads, grads_other, attn_low, attn_low_other, first_attended, last_attended),
+        (SMEM,) + (VMEM,) * 7,
         scratch=[pltpu.VMEM((width, late_columns), wide_type)],
         cost=40.0,
     )
@@ -1219,9 +1245,9 @@
         [low(last_exchange.rows(0), LANES)] * 2,
         (
             facts, encoded, proj_grad, enc_grad, pos_grad_own, mask_grad, bias_grads, bias_grads_other, second_grads,
-            qkv_bias_grad, in_keep, in_other,
+            second_grads_other, qkv_bias_grad, in_keep, in_other,
         ),
-        (SMEM,) + (VMEM,) * 11,
+        (SMEM,) + (VMEM,) * 12,
         scratch=[pltpu.VMEM((VECTOR_ROWS, LANES), wide_type)],
         cost=0.6,
     )
@@ -1235,8 +1261,8 @@
     (input_grad,) = run(
         input_grad_kernel,
         [low(own_rows, width)],
-        (facts, patch_rows, in_keep, in_other, own_grad, first_gain),
-        (SMEM,) + (VMEM,) * 5,
+        (facts, patch_rows, in_keep, in_other, hidden_grad, hidden_grad_other, first_gain),
+        (SMEM,) + (VMEM,) * 6,
         final=True,
         cost=0.8,
     )
@@ -1256,17 +1282,17 @@
         ],
         [(bits[1], joint_sizes[0]), (turned[1], joint_sizes[1])],
     )
+    (up_keep,), (up_came,) = steps(
+        (up_keep,),
+        ((up_came, early_sizes[0]),),
+        [(up_exchange, 2, [(up_exchange, 0, (1, 0))], (0, 0))],
+        [(far[2], [up_exchange.rows(2)])],
+    )
     (down_keep,), (down_came,) = steps(
         (down_keep,),
         ((down_came, early_sizes[1]),),
         [(down_exchange, 2, [(down_exchange, 0, (1, 0))], (0, 0))],
         [(turned[2], [down_exchange.rows(2)])],
-    )
-    (up_keep,), (up_came,) = steps(
-        (up_keep,),
-        ((up_came, early_sizes[0]),),
-        [(up_exchange, 2, [(up_exchange, 0, (1, 0))], (0, 0))],
-        [(far[2], [up_exchange.rows(2)])],
     )
     early_came = (up_came, down_came)
     early_sizes = [[exchange.rows(2)] for exchange in early]

time: 102 us -> 102 us (level)
  starting transfers between devices: 31 us -> 37.5 us
  waiting for transfers between devices: 33.2 us -> 28.5 us
  Pallas kernels: 36.3 us -> 34.4 us
    ppermute x38, starting transfers between devices: 31 us -> 37.5 us  [swap(): return lax.ppermute(value, axis, [(i, i ^ bit) for i in range(count)])]
    ppermute x38, waiting for transfers between devices: 33.2 us -> 28.5 us  [swap(): return lax.ppermute(value, axis, [(i, i ^ bit) for i in range(count)])]
    pallas_call x34 -> x35, Pallas kernels: 36.3 us -> 34.4 us  [__call__(): pl.pallas_call(body, out_shape=tuple(shapes) + tuple((pltpu.VMEM(array.sh...]
  transfers between devices with their start and end apart: 38 -> 38, of which waited for: 15 -> 17; matrix products, arithmetic and copies ran while one was open for 0% -> 0% of each run, Pallas kernels for 33% -> 31%
where the time goes in v6:
time: 102 us
  starting transfers between devices  37.5 us (37%)
  Pallas kernels  34.4 us (34%)
  waiting for transfers between devices  28.5 us (28%)
  between operations  1.17 us (1%)
    ppermute x38, starting transfers between devices, swap(): return lax.ppermute(value, axis, [(i, i ^ bit) for i in range(count)])  37.5 us
    pallas_call x35, Pallas kernels, __call__(): pl.pallas_call(body, out_shape=tuple(shapes) + tuple((pltpu.VMEM(array.sh...  34.4 us
    ppermute x38, waiting for transfers between devices, swap(): return lax.ppermute(value, axis, [(i, i ^ bit) for i in range(count)])  28.5 us
  transfers between devices with their start and end apart: 38, of which 17 were waited for; matrix products, arithmetic and copies ran while one was open for 0% of the time, Pallas kernels for 31%

profile of v6, /device:TPU:0, one launch (start us, length us, event | category | flops | bytes accessed | tf_op | source)
XLA Modules:
  0.0 101.7 jit_solution(6645746356826362969)
XLA Ops:
  1.2 2.6 %collective-permute-start.4 = (bf16[768,128]{1,0:T(8,128)(2,1)}, bf16[768,128]{1,0:T(8,128)(2,1)S(1)}, u32[]{:S(2)}, u32[]{:S(2)}) collective-permute-start(bf16[768,128]{1,0:T(8,128)(2,1)} %refs_6_.4), channel_id=1, source_target_pairs={{0,2},{1,3},{2,0},{3,1},{4,6},{5,7},{6,4},{7,5},{8,10},{9,11},{10,... | collective-permute-start | bytes 589832 | tf_op jit(solution)/shard_map/ppermute | solution.py:923
  4.3 3.0 %shard_map.393 = (bf16[256,128]{1,0:T(8,128)(2,1)S(1)}, bf16[256,128]{1,0:T(8,128)(2,1)S(1)}, s32[42]{0:T(128)S(4)}, s32[8,64]{1,0:T(8,128)S(1)}, bf16[512,768]{...) custom-call(s32[2]{0:T(128)S(1)} %pad_add_fusion.refs_0_, ...), custom_call_target="tpu_custom_call" | custom-call | flops 3000000000 | tf_op jit(solution)/shard_map/pallas_call | solution.py:173
  7.3 1.8 %collective-permute-start.2 = (bf16[256,128]{1,0:T(8,128)(2,1)S(1)}, bf16[256,128]{1,0:T(8,128)(2,1)S(1)}, u32[]{:S(2)}, u32[]{:S(2)}) collective-permute-start(bf16[256,128]{1,0:T(8,128)(2,1)S(1)} %get-tuple-element.141), channel_id=1, source_target_pairs={{0,4},{4,0},{8,12},{12,8},{16,20},{20,16},{24,28},{28,24},{1,5},{5... | collective-permute-start | bytes 196616 | tf_op jit(solution)/shard_map/ppermute | solution.py:923
  11.6 1.9 %collective-permute-start.5 = (bf16[256,128]{1,0:T(8,128)(2,1)S(1)}, bf16[256,128]{1,0:T(8,128)(2,1)S(1)}, u32[]{:S(2)}, u32[]{:S(2)}) collective-permute-start(bf16[256,128]{1,0:T(8,128)(2,1)S(1)} %get-tuple-element.148), channel_id=1, source_target_pairs={{0,8},{4,12},{8,0},{12,4},{16,24},{20,28},{24,16},{28,20},{1,9},{5... | collective-permute-start | bytes 196616 | tf_op jit(solution)/shard_map/ppermute | solution.py:923
  13.5 2.4 %shard_map.396 = (bf16[384,128]{1,0:T(8,128)(2,1)S(1)}, bf16[256,768]{1,0:T(8,128)(2,1)S(1)}, bf16[256,192]{1,0:T(8,128)(2,1)S(1)}, bf16[768]{0:T(1024)(128)(2,1...) custom-call(s32[42]{0:T(128)S(4)} %get-tuple-element.130.refs_0_, ...), custom_call_target="tpu_custom_call" | custom-call | flops 2800000000 | tf_op jit(solution)/shard_map/pallas_call | solution.py:173
  17.5 2.7 %collective-permute-start.14 = (bf16[256,128]{1,0:T(8,128)(2,1)S(1)}, bf16[256,128]{1,0:T(8,128)(2,1)S(1)}, u32[]{:S(2)}, u32[]{:S(2)}) collective-permute-start(bf16[256,128]{1,0:T(8,128)(2,1)S(1)} %get-tuple-element.157), channel_id=1, source_target_pairs={{0,16},{4,20},{8,24},{12,28},{16,0},{20,4},{24,8},{28,12},{1,17},{... | collective-permute-start | bytes 196616 | tf_op jit(solution)/shard_map/ppermute | solution.py:923
  22.6 1.7 %collective-permute-done.14.refs_2_ = bf16[256,128]{1,0:T(8,128)(2,1)S(1)} collective-permute-done((bf16[256,128]{1,0:T(8,128)(2,1)S(1)}, bf16[256,128]{1,0:T(8,128)(2,1)S(1)}, u32[]{:S(2)}, u32[]{:S(2)}) %collective-permute-start.14) | collective-permute-done | bytes 65568 | tf_op jit(solution)/shard_map/ppermute | solution.py:923
  27.3 2.6 %collective-permute-done.16.refs_7_ = bf16[512,128]{1,0:T(8,128)(2,1)S(1)} collective-permute-done((bf16[512,128]{1,0:T(8,128)(2,1)S(1)}, bf16[512,128]{1,0:T(8,128)(2,1)S(1)}, u32[]{:S(2)}, u32[]{:S(2)}) %collective-permute-start.16) | collective-permute-done | bytes 131104 | tf_op jit(solution)/shard_map/ppermute | solution.py:923
  29.9 2.7 %shard_map.401 = (f32[512,768]{1,0:T(8,128)S(1)}, bf16[512,768]{1,0:T(8,128)(2,1)S(1)}, bf16[512,768]{1,0:T(8,128)(2,1)S(1)}, f32[512,768]{1,0:T(8,128)S(1)}) custom-call(s32[42]{0:T(128)S(4)} %get-tuple-element.130.refs_0_, bf16[512,768]{1,0:T(8,128)(2,1)S(1)} %get-tuple-element.132.refs_0_.refs_1_, bf16[768]{0:T(1024)(128)(2,1)S(1)} %get-tuple-element.143.refs_2_, ...), custom_call_target="tpu_custom_call" | custom-call | flops 2600000000 | tf_op jit(solution)/shard_map/pallas_call | solution.py:173
  36.2 2.9 %shard_map.405 = (bf16[2304,128]{1,0:T(8,128)(2,1)S(1)}, bf16[2304,128]{1,0:T(8,128)(2,1)}, bf16[2304,128]{1,0:T(8,128)(2,1)S(1)}, bf16[2304,128]{1,0:T(8,128)(2,1)}) custom-call(s32[42]{0:T(128)S(4)} %get-tuple-element.130.refs_0_, bf16[256,768]{1,0:T(8,128)(2,1)S(1)} %get-tuple-element.165.refs_1_.refs_3_, ...), custom_call_target="tpu_custom_call" | custom-call | flops 2200000000 | tf_op jit(solution)/shard_map/pallas_call | solution.py:173
  42.5 2.3 %shard_map.407 = (f32[256,128]{1,0:T(8,128)S(1)}, f32[1,128]{1,0:T(1,128)S(1)}, f32[3,256,128]{2,1,0:T(8,128)S(1)}) custom-call(s32[42]{0:T(128)S(4)} %get-tuple-element.130.refs_0_, s32[8,64]{1,0:T(8,128)S(1)} %get-tuple-element.131.refs_1_, bf16[8,256,128]{2,1,0:T(8,128)(2,1)} %refs_2_.7, bf16[2,256,256]{2,1,0:T(8,128)(2,1)} %constant.17.clone.refs_3_, ...), custom_call_target="tpu_custom_call" | custom-call | flops 20000000000 | tf_op jit(solution)/shard_map/pallas_call | solution.py:173
  47.4 2.3 %shard_map.411 = (bf16[256,576]{1,0:T(8,128)(2,1)S(1)}, bf16[256,768]{1,0:T(8,128)(2,1)S(1)}, f32[256,768]{1,0:T(8,128)S(1)}, f32[3,768]{1,0:T(4,128)S(1)}) custom-call(s32[42]{0:T(128)S(4)} %get-tuple-element.130.refs_0_, bf16[256,768]{1,0:T(8,128)(2,1)S(1)} %shard_map.410.refs_1_.refs_9_, f32[512,768]{1,0:T(8,128)S(1)} %get-tuple-element.161.refs_9_.refs_2_.refs_1_, ...), custom_call_target="tpu_custom_call" | custom-call | flops 40000000000 | tf_op jit(solution)/shard_map/pallas_call | solution.py:173
  49.7 2.1 %shard_map.412 = (bf16[256,576]{1,0:T(8,128)(2,1)S(1)}, bf16[256,768]{1,0:T(8,128)(2,1)S(1)}, f32[256,768]{1,0:T(8,128)S(1)}, f32[3,768]{1,0:T(4,128)S(1)}) custom-call(s32[42]{0:T(128)S(4)} %get-tuple-element.130.refs_0_, bf16[256,768]{1,0:T(8,128)(2,1)S(1)} %collective-permute-done.21.refs_1_, f32[512,768]{1,0:T(8,128)S(1)} %get-tuple-element.161.refs_9_.refs_2_.refs_1_, ...), custom_call_target="tpu_custom_call" | custom-call | flops 4000000000 | tf_op jit(solution)/shard_map/pallas_call | solution.py:173
  55.0 2.1 %collective-permute-start.28 = (bf16[1152,128]{1,0:T(8,128)(2,1)S(1)}, bf16[1152,128]{1,0:T(8,128)(2,1)S(1)}, u32[]{:S(2)}, u32[]{:S(2)}) collective-permute-start(bf16[1152,128]{1,0:T(8,128)(2,1)S(1)} %get-tuple-element.203), channel_id=1, source_target_pairs={{0,4},{4,0},{8,12},{12,8},{16,20},{20,16},{24,28},{28,24},{1,5},{5... | collective-permute-start | bytes 884744 | tf_op jit(solution)/shard_map/ppermute | solution.py:923
  57.4 1.8 %collective-permute-start.27 = (bf16[144,768]{1,0:T(8,128)(2,1)S(1)}, bf16[144,768]{1,0:T(8,128)(2,1)S(1)}, u32[]{:S(2)}, u32[]{:S(2)}) collective-permute-start(bf16[144,768]{1,0:T(8,128)(2,1)S(1)} %get-tuple-element.200), channel_id=1, source_target_pairs={{0,2},{1,3},{2,0},{3,1},{4,6},{5,7},{6,4},{7,5},{8,10},{9,11},{10,... | collective-permute-start | bytes 663560 | tf_op jit(solution)/shard_map/ppermute | solution.py:923
  61.8 2.6 %collective-permute-done.27.refs_12_.refs_3_ = bf16[144,768]{1,0:T(8,128)(2,1)S(1)} collective-permute-done((bf16[144,768]{1,0:T(8,128)(2,1)S(1)}, bf16[144,768]{1,0:T(8,128)(2,1)S(1)}, u32[]{:S(2)}, u32[]{:S(2)}) %collective-permute-start.27) | collective-permute-done | bytes 221216 | tf_op jit(solution)/shard_map/ppermute | solution.py:923
  67.9 1.7 %collective-permute-start.33 = (bf16[1152,128]{1,0:T(8,128)(2,1)S(1)}, bf16[1152,128]{1,0:T(8,128)(2,1)S(1)}, u32[]{:S(2)}, u32[]{:S(2)}) collective-permute-start(bf16[1152,128]{1,0:T(8,128)(2,1)S(1)} %get-tuple-element.211), channel_id=1, source_target_pairs={{0,4},{4,0},{8,12},{12,8},{16,20},{20,16},{24,28},{28,24},{1,5},{5... | collective-permute-start | bytes 884744 | tf_op jit(solution)/shard_map/ppermute | solution.py:923
  69.6 2.7 %collective-permute-done.29.refs_5_ = bf16[816,128]{1,0:T(8,128)(2,1)S(1)} collective-permute-done((bf16[816,128]{1,0:T(8,128)(2,1)S(1)}, bf16[816,128]{1,0:T(8,128)(2,1)S(1)}, u32[]{:S(2)}, u32[]{:S(2)}) %collective-permute-start.29) | collective-permute-done | bytes 208928 | tf_op jit(solution)/shard_map/ppermute | solution.py:923
  73.0 1.7 %collective-permute-start.31 = (bf16[1136,128]{1,0:T(8,128)(2,1)S(1)}, bf16[1136,128]{1,0:T(8,128)(2,1)S(1)}, u32[]{:S(2)}, u32[]{:S(2)}) collective-permute-start(bf16[1136,128]{1,0:T(8,128)(2,1)S(1)} %get-tuple-element.209), channel_id=1, source_target_pairs={{0,8},{4,12},{8,0},{12,4},{16,24},{20,28},{24,16},{28,20},{1,9},{5... | collective-permute-start | bytes 872456 | tf_op jit(solution)/shard_map/ppermute | solution.py:923
  78.3 2.3 %collective-permute-start.37 = (bf16[576,128]{1,0:T(8,128)(2,1)S(1)}, bf16[576,128]{1,0:T(8,128)(2,1)S(1)}, u32[]{:S(2)}, u32[]{:S(2)}) collective-permute-start(bf16[576,128]{1,0:T(8,128)(2,1)S(1)} %get-tuple-element.232), channel_id=1, source_target_pairs={{0,16},{4,20},{8,24},{12,28},{16,0},{20,4},{24,8},{28,12},{1,17},{... | collective-permute-start | bytes 442376 | tf_op jit(solution)/shard_map/ppermute | solution.py:923
  81.5 5.1 %collective-permute-start.35 = (bf16[1008,128]{1,0:T(8,128)(2,1)S(1)}, bf16[1008,128]{1,0:T(8,128)(2,1)S(1)}, u32[]{:S(2)}, u32[]{:S(2)}) collective-permute-start(bf16[1008,128]{1,0:T(8,128)(2,1)S(1)} %get-tuple-element.217), channel_id=1, source_target_pairs={{0,16},{4,20},{8,24},{12,28},{16,0},{20,4},{24,8},{28,12},{1,17},{... | collective-permute-start | bytes 774152 | tf_op jit(solution)/shard_map/ppermute | solution.py:923
  87.7 5.6 %collective-permute-done.36.refs_2_ = bf16[576,128]{1,0:T(8,128)(2,1)S(1)} collective-permute-done((bf16[576,128]{1,0:T(8,128)(2,1)S(1)}, bf16[576,128]{1,0:T(8,128)(2,1)S(1)}, u32[]{:S(2)}, u32[]{:S(2)}) %collective-permute-start.36) | collective-permute-done | bytes 147488 | tf_op jit(solution)/shard_map/ppermute | solution.py:923
  93.3 3.2 %collective-permute-done.37.refs_3_ = bf16[576,128]{1,0:T(8,128)(2,1)S(1)} collective-permute-done((bf16[576,128]{1,0:T(8,128)(2,1)S(1)}, bf16[576,128]{1,0:T(8,128)(2,1)S(1)}, u32[]{:S(2)}, u32[]{:S(2)}) %collective-permute-start.37) | collective-permute-done | bytes 147488 | tf_op jit(solution)/shard_map/ppermute | solution.py:923
  97.3 2.8 %collective-permute-done.35.refs_4_ = bf16[1008,128]{1,0:T(8,128)(2,1)S(1)} collective-permute-done((bf16[1008,128]{1,0:T(8,128)(2,1)S(1)}, bf16[1008,128]{1,0:T(8,128)(2,1)S(1)}, u32[]{:S(2)}, u32[]{:S(2)}) %collective-permute-start.35) | collective-permute-done | bytes 258080 | tf_op jit(solution)/shard_map/ppermute | solution.py:923
  (110 shorter events, 38.2 us)
Async XLA Ops:
  0.7 9.1 %collective-permute-start.1 = (bf16[768,128]{1,0:T(8,128)(2,1)}, bf16[768,128]{1,0:T(8,128)(2,1)S(1)}, u32[]{:S(2)}, u32[]{:S(2)}) collective-permute-start(bf16[768,128]{1,0:T(8,128)(2,1)} %refs_6_.4), channel_id=1, source_target_pairs={{0,1},{1,0},{2,3},{3,2},{4,5},{5,4},{6,7},{7,6},{8,9},{9,8},{10,11... | collective-permute-start | bytes 589832 | tf_op jit(solution)/shard_map/ppermute | solution.py:923
  1.2 8.6 %collective-permute-start.4 = (bf16[768,128]{1,0:T(8,128)(2,1)}, bf16[768,128]{1,0:T(8,128)(2,1)S(1)}, u32[]{:S(2)}, u32[]{:S(2)}) collective-permute-start(bf16[768,128]{1,0:T(8,128)(2,1)} %refs_6_.4), channel_id=1, source_target_pairs={{0,2},{1,3},{2,0},{3,1},{4,6},{5,7},{6,4},{7,5},{8,10},{9,11},{10,... | collective-permute-start | bytes 589832 | tf_op jit(solution)/shard_map/ppermute | solution.py:923
  3.8 6.0 %collective-permute-start = (bf16[192,768]{1,0:T(8,128)(2,1)}, bf16[192,768]{1,0:T(8,128)(2,1)S(1)}, u32[]{:S(2)}, u32[]{:S(2)}) collective-permute-start(bf16[192,768]{1,0:T(8,128)(2,1)} %refs_5_.7), channel_id=1, source_target_pairs={{0,1},{1,0},{2,3},{3,2},{4,5},{5,4},{6,7},{7,6},{8,9},{9,8},{10,11... | collective-permute-start | bytes 884744 | tf_op jit(solution)/shard_map/ppermute | solution.py:923
  3.9 13.6 %collective-permute-start.3 = (bf16[192,768]{1,0:T(8,128)(2,1)}, bf16[192,768]{1,0:T(8,128)(2,1)S(1)}, u32[]{:S(2)}, u32[]{:S(2)}) collective-permute-start(bf16[192,768]{1,0:T(8,128)(2,1)} %refs_5_.7), channel_id=1, source_target_pairs={{0,2},{1,3},{2,0},{3,1},{4,6},{5,7},{6,4},{7,5},{8,10},{9,11},{10,... | collective-permute-start | bytes 884744 | tf_op jit(solution)/shard_map/ppermute | solution.py:923
  9.7 12.6 %collective-permute-start.7 = (bf16[768,128]{1,0:T(8,128)(2,1)S(1)}, bf16[768,128]{1,0:T(8,128)(2,1)S(1)}, u32[]{:S(2)}, u32[]{:S(2)}) collective-permute-start(bf16[768,128]{1,0:T(8,128)(2,1)S(1)} %collective-permute-done.4.refs_10_.refs_7_), channel_id=1, source_target_pairs={{0,1},{1,0},{2,3},{3,2},{4,5},{5,4},{6,7},{7,6},{8,9},{9,8},{10,11... | collective-permute-start | bytes 589832 | tf_op jit(solution)/shard_map/ppermute | solution.py:923
  11.6 5.9 %collective-permute-start.5 = (bf16[256,128]{1,0:T(8,128)(2,1)S(1)}, bf16[256,128]{1,0:T(8,128)(2,1)S(1)}, u32[]{:S(2)}, u32[]{:S(2)}) collective-permute-start(bf16[256,128]{1,0:T(8,128)(2,1)S(1)} %get-tuple-element.148), channel_id=1, source_target_pairs={{0,8},{4,12},{8,0},{12,4},{16,24},{20,28},{24,16},{28,20},{1,9},{5... | collective-permute-start | bytes 196616 | tf_op jit(solution)/shard_map/ppermute | solution.py:923
  15.9 9.6 %collective-permute-start.9 = (bf16[384,128]{1,0:T(8,128)(2,1)S(1)}, bf16[384,128]{1,0:T(8,128)(2,1)S(1)}, u32[]{:S(2)}, u32[]{:S(2)}) collective-permute-start(bf16[384,128]{1,0:T(8,128)(2,1)S(1)} %get-tuple-element.149.refs_3_.refs_8_), channel_id=1, source_target_pairs={{0,2},{1,3},{2,0},{3,1},{4,6},{5,7},{6,4},{7,5},{8,10},{9,11},{10,... | collective-permute-start | bytes 294920 | tf_op jit(solution)/shard_map/ppermute | solution.py:923
  17.5 6.7 %collective-permute-start.14 = (bf16[256,128]{1,0:T(8,128)(2,1)S(1)}, bf16[256,128]{1,0:T(8,128)(2,1)S(1)}, u32[]{:S(2)}, u32[]{:S(2)}) collective-permute-start(bf16[256,128]{1,0:T(8,128)(2,1)S(1)} %get-tuple-element.157), channel_id=1, source_target_pairs={{0,16},{4,20},{8,24},{12,28},{16,0},{20,4},{24,8},{28,12},{1,17},{... | collective-permute-start | bytes 196616 | tf_op jit(solution)/shard_map/ppermute | solution.py:923
  26.8 5.8 %collective-permute-start.15 = (bf16[512,128]{1,0:T(8,128)(2,1)S(1)}, bf16[512,128]{1,0:T(8,128)(2,1)S(1)}, u32[]{:S(2)}, u32[]{:S(2)}) collective-permute-start(bf16[512,128]{1,0:T(8,128)(2,1)S(1)} %shard_map.400.refs_16_.refs_5_.refs_7_.refs_3_), channel_id=1, source_target_pairs={{0,1},{1,0},{2,3},{3,2},{4,5},{5,4},{6,7},{7,6},{8,9},{9,8},{10,11... | collective-permute-start | bytes 393224 | tf_op jit(solution)/shard_map/ppermute | solution.py:923
  35.8 11.5 %collective-permute-start.19 = (bf16[256,768]{1,0:T(8,128)(2,1)S(1)}, bf16[256,768]{1,0:T(8,128)(2,1)S(1)}, u32[]{:S(2)}, u32[]{:S(2)}) collective-permute-start(bf16[256,768]{1,0:T(8,128)(2,1)S(1)} %shard_map.404.refs_7_.refs_0_), channel_id=1, source_target_pairs={{0,2},{1,3},{2,0},{3,1},{4,6},{5,7},{6,4},{7,5},{8,10},{9,11},{10,... | collective-permute-start | bytes 1179656 | tf_op jit(solution)/shard_map/ppermute | solution.py:923
  40.0 17.0 %collective-permute-start.24 = (bf16[2304,128]{1,0:T(8,128)(2,1)}, bf16[2304,128]{1,0:T(8,128)(2,1)}, u32[]{:S(2)}, u32[]{:S(2)}) collective-permute-start(bf16[2304,128]{1,0:T(8,128)(2,1)} %get-tuple-element.185), channel_id=1, source_target_pairs={{0,4},{4,0},{8,12},{12,8},{16,20},{20,16},{24,28},{28,24},{1,5},{5... | collective-permute-start | bytes 1769480 | tf_op jit(solution)/shard_map/ppermute | solution.py:923
  41.5 15.7 %collective-permute-start.25 = (bf16[2304,128]{1,0:T(8,128)(2,1)}, bf16[2304,128]{1,0:T(8,128)(2,1)}, u32[]{:S(2)}, u32[]{:S(2)}) collective-permute-start(bf16[2304,128]{1,0:T(8,128)(2,1)} %get-tuple-element.186), channel_id=1, source_target_pairs={{0,8},{4,12},{8,0},{12,4},{16,24},{20,28},{24,16},{28,20},{1,9},{5... | collective-permute-start | bytes 1769480 | tf_op jit(solution)/shard_map/ppermute | solution.py:923
  44.9 14.2 %collective-permute-start.22 = (bf16[256,768]{1,0:T(8,128)(2,1)S(1)}, bf16[256,768]{1,0:T(8,128)(2,1)S(1)}, u32[]{:S(2)}, u32[]{:S(2)}) collective-permute-start(bf16[256,768]{1,0:T(8,128)(2,1)S(1)} %shard_map.408.refs_1_.refs_0_), channel_id=1, source_target_pairs={{0,2},{1,3},{2,0},{3,1},{4,6},{5,7},{6,4},{7,5},{8,10},{9,11},{10,... | collective-permute-start | bytes 1179656 | tf_op jit(solution)/shard_map/ppermute | solution.py:923
  55.0 14.6 %collective-permute-start.28 = (bf16[1152,128]{1,0:T(8,128)(2,1)S(1)}, bf16[1152,128]{1,0:T(8,128)(2,1)S(1)}, u32[]{:S(2)}, u32[]{:S(2)}) collective-permute-start(bf16[1152,128]{1,0:T(8,128)(2,1)S(1)} %get-tuple-element.203), channel_id=1, source_target_pairs={{0,4},{4,0},{8,12},{12,8},{16,20},{20,16},{24,28},{28,24},{1,5},{5... | collective-permute-start | bytes 884744 | tf_op jit(solution)/shard_map/ppermute | solution.py:923
  57.0 12.5 %collective-permute-start.30 = (bf16[1152,128]{1,0:T(8,128)(2,1)S(1)}, bf16[1152,128]{1,0:T(8,128)(2,1)S(1)}, u32[]{:S(2)}, u32[]{:S(2)}) collective-permute-start(bf16[1152,128]{1,0:T(8,128)(2,1)S(1)} %get-tuple-element.205), channel_id=1, source_target_pairs={{0,8},{4,12},{8,0},{12,4},{16,24},{20,28},{24,16},{28,20},{1,9},{5... | collective-permute-start | bytes 884744 | tf_op jit(solution)/shard_map/ppermute | solution.py:923
  57.4 7.0 %collective-permute-start.27 = (bf16[144,768]{1,0:T(8,128)(2,1)S(1)}, bf16[144,768]{1,0:T(8,128)(2,1)S(1)}, u32[]{:S(2)}, u32[]{:S(2)}) collective-permute-start(bf16[144,768]{1,0:T(8,128)(2,1)S(1)} %get-tuple-element.200), channel_id=1, source_target_pairs={{0,2},{1,3},{2,0},{3,1},{4,6},{5,7},{6,4},{7,5},{8,10},{9,11},{10,... | collective-permute-start | bytes 663560 | tf_op jit(solution)/shard_map/ppermute | solution.py:923
  64.5 7.8 %collective-permute-start.29 = (bf16[816,128]{1,0:T(8,128)(2,1)S(1)}, bf16[816,128]{1,0:T(8,128)(2,1)S(1)}, u32[]{:S(2)}, u32[]{:S(2)}) collective-permute-start(bf16[816,128]{1,0:T(8,128)(2,1)S(1)} %get-tuple-element.204), channel_id=1, source_target_pairs={{0,4},{4,0},{8,12},{12,8},{16,20},{20,16},{24,28},{28,24},{1,5},{5... | collective-permute-start | bytes 626696 | tf_op jit(solution)/shard_map/ppermute | solution.py:923
  65.7 10.0 %collective-permute-start.34 = (bf16[1152,128]{1,0:T(8,128)(2,1)S(1)}, bf16[1152,128]{1,0:T(8,128)(2,1)S(1)}, u32[]{:S(2)}, u32[]{:S(2)}) collective-permute-start(bf16[1152,128]{1,0:T(8,128)(2,1)S(1)} %get-tuple-element.212), channel_id=1, source_target_pairs={{0,8},{4,12},{8,0},{12,4},{16,24},{20,28},{24,16},{28,20},{1,9},{5... | collective-permute-start | bytes 884744 | tf_op jit(solution)/shard_map/ppermute | solution.py:923
  67.9 10.4 %collective-permute-start.33 = (bf16[1152,128]{1,0:T(8,128)(2,1)S(1)}, bf16[1152,128]{1,0:T(8,128)(2,1)S(1)}, u32[]{:S(2)}, u32[]{:S(2)}) collective-permute-start(bf16[1152,128]{1,0:T(8,128)(2,1)S(1)} %get-tuple-element.211), channel_id=1, source_target_pairs={{0,4},{4,0},{8,12},{12,8},{16,20},{20,16},{24,28},{28,24},{1,5},{5... | collective-permute-start | bytes 884744 | tf_op jit(solution)/shard_map/ppermute | solution.py:923
  72.5 8.2 %collective-permute-start.32 = (bf16[576,128]{1,0:T(8,128)(2,1)S(1)}, bf16[576,128]{1,0:T(8,128)(2,1)S(1)}, u32[]{:S(2)}, u32[]{:S(2)}) collective-permute-start(bf16[576,128]{1,0:T(8,128)(2,1)S(1)} %get-tuple-element.210), channel_id=1, source_target_pairs={{0,4},{4,0},{8,12},{12,8},{16,20},{20,16},{24,28},{28,24},{1,5},{5... | collective-permute-start | bytes 442376 | tf_op jit(solution)/shard_map/ppermute | solution.py:923
  73.0 8.4 %collective-permute-start.31 = (bf16[1136,128]{1,0:T(8,128)(2,1)S(1)}, bf16[1136,128]{1,0:T(8,128)(2,1)S(1)}, u32[]{:S(2)}, u32[]{:S(2)}) collective-permute-start(bf16[1136,128]{1,0:T(8,128)(2,1)S(1)} %get-tuple-element.209), channel_id=1, source_target_pairs={{0,8},{4,12},{8,0},{12,4},{16,24},{20,28},{24,16},{28,20},{1,9},{5... | collective-permute-start | bytes 872456 | tf_op jit(solution)/shard_map/ppermute | solution.py:923
  75.8 17.5 %collective-permute-start.36 = (bf16[576,128]{1,0:T(8,128)(2,1)S(1)}, bf16[576,128]{1,0:T(8,128)(2,1)S(1)}, u32[]{:S(2)}, u32[]{:S(2)}) collective-permute-start(bf16[576,128]{1,0:T(8,128)(2,1)S(1)} %get-tuple-element.231), channel_id=1, source_target_pairs={{0,16},{4,20},{8,24},{12,28},{16,0},{20,4},{24,8},{28,12},{1,17},{... | collective-permute-start | bytes 442376 | tf_op jit(solution)/shard_map/ppermute | solution.py:923
  78.3 18.1 %collective-permute-start.37 = (bf16[576,128]{1,0:T(8,128)(2,1)S(1)}, bf16[576,128]{1,0:T(8,128)(2,1)S(1)}, u32[]{:S(2)}, u32[]{:S(2)}) collective-permute-start(bf16[576,128]{1,0:T(8,128)(2,1)S(1)} %get-tuple-element.232), channel_id=1, source_target_pairs={{0,16},{4,20},{8,24},{12,28},{16,0},{20,4},{24,8},{28,12},{1,17},{... | collective-permute-start | bytes 442376 | tf_op jit(solution)/shard_map/ppermute | solution.py:923
  81.5 18.5 %collective-permute-start.35 = (bf16[1008,128]{1,0:T(8,128)(2,1)S(1)}, bf16[1008,128]{1,0:T(8,128)(2,1)S(1)}, u32[]{:S(2)}, u32[]{:S(2)}) collective-permute-start(bf16[1008,128]{1,0:T(8,128)(2,1)S(1)} %get-tuple-element.217), channel_id=1, source_target_pairs={{0,16},{4,20},{8,24},{12,28},{16,0},{20,4},{24,8},{28,12},{1,17},{... | collective-permute-start | bytes 774152 | tf_op jit(solution)/shard_map/ppermute | solution.py:923
  (25 other events, 124.2 us)

commit v7 on v6

--- a/solution.py
+++ b/solution.py
@@ -875,24 +875,32 @@
         ref[exchange.shared_at(0) :, :] = rows_ref[...].astype(low_type)
 
 
+def base_kernel(info, info_ref, seen_ref, mask_ref, layout_ref, base_ref):
+    cells = lax.broadcasted_iota(jnp.int32, (GRID, VIS), 0)
+    cell_column = lax.broadcasted_iota(jnp.int32, (GRID, 1), 0)
+    mask_row = wide_row(mask_ref)
+
+    def one_slot(slot):
+        size = info.cells(info_ref, slot)
+        seen = (seen_ref[pl.ds(slot, 1), :] == cells).astype(wide_type)
+        fill = (cell_column < size).astype(wide_type) - jnp.sum(seen, axis=1, keepdims=True)
+        base_ref[slot] = fill * mask_row + layout_ref[side_of(size)]
+
+    over_slots(info.count, one_slot)
+
+
 def late_out_kernel(
-    info, exchange, turned_exchange, pad, middle, sizes, info_ref, seen_ref, keep_ref, turned_ref, came_ref, mask_ref,
-    layout_ref, grids_ref, out_ref, qkv_ref, proj_ref, pos_ref, *refs
+    info, exchange, turned_exchange, pad, middle, sizes, info_ref, seen_ref, keep_ref, turned_ref, came_ref, base_ref,
+    grids_ref, out_ref, qkv_ref, proj_ref, pos_ref, *refs
 ):
     *vector_refs, wide_ref, rows_ref = refs
     other_ref, turned_other_ref = views(came_ref, sizes)
     cells = lax.broadcasted_iota(jnp.int32, (GRID, VIS), 0)
-    cell_column = lax.broadcasted_iota(jnp.int32, (GRID, 1), 0)
-    mask_row = wide_row(mask_ref)
     for relative, ref, start in exchange.arrived(keep_ref, other_ref):
         slot = info_ref[0] ^ relative
         seen = seen_ref[pl.ds(slot, 1), :] == cells
-        size = info.cells(info_ref, slot)
-        fill = (cell_column < size).astype(wide_type) - jnp.sum(
-            seen.astype(wide_type), axis=1, keepdims=True
-        )
         placed = dot(seen.astype(low_type), ref[start : start + VIS, :])
-        grids_ref[slot] = (placed + fill * mask_row + layout_ref[side_of(size)]).astype(low_type)
+        grids_ref[slot] = (placed + base_ref[slot]).astype(low_type)
     share = proj_ref.shape[0]
     tiles = wide_ref.shape[1] // LANES
     for tile in range(tiles):
@@ -1269,6 +1277,13 @@
 
     early = (up_exchange, down_exchange)
     late = (joint_exchange, turned_exchange)
+    (base,) = run(
+        lambda *refs: base_kernel(info, *refs),
+        [wide(count, GRID, columns)],
+        (facts, seen, mask_token, layouts),
+        (SMEM,) + (VMEM,) * 3,
+        cost=0.8,
+    )
     joint_sizes = [[exchange.rows(1)] for exchange in late]
     (late_keep, turned_keep), late_came = steps(
         (late_keep, last_keep, turned_keep),
@@ -1339,8 +1354,8 @@
             wide(pos_share, columns),
         ]
         + [wide(size) for size in (head_columns, head_columns, units, columns, columns) + (width,) * 6],
-        (facts, seen, late_keep, turned_keep, late_came, mask_token, layouts),
-        (SMEM,) + (VMEM,) * 6,
+        (facts, seen, late_keep, turned_keep, late_came, base),
+        (SMEM,) + (VMEM,) * 5,
         scratch=[pltpu.VMEM((share, late_columns), wide_type), pltpu.VMEM((VECTOR_ROWS, LANES), wide_type)],
         final=True,
         cost=2.5,

time: 102 us -> 101 us (level)
  starting transfers between devices: 37.5 us -> 34.5 us
  waiting for transfers between devices: 28.5 us -> 30.1 us
    ppermute x38, starting transfers between devices: 37.5 us -> 34.5 us  [swap(): return lax.ppermute(value, axis, [(i, i ^ bit) for i in range(count)])]
    ppermute x38, waiting for transfers between devices: 28.5 us -> 30.1 us  [swap(): return lax.ppermute(value, axis, [(i, i ^ bit) for i in range(count)])]
    pallas_call x35 -> x36, Pallas kernels: 34.4 us -> 34.5 us  [__call__(): pl.pallas_call(body, out_shape=tuple(shapes) + tuple((pltpu.VMEM(array.sh...]
  transfers between devices with their start and end apart: 38 -> 38, of which waited for: 17 -> 15; matrix products, arithmetic and copies ran while one was open for 0% -> 0% of each run, Pallas kernels for 31% -> 32%
where the time goes in v7:
time: 101 us; the launch traced here: 100 us
  starting transfers between devices  34.5 us (34%)
  Pallas kernels  34.5 us (34%)
  waiting for transfers between devices  30.1 us (30%)
  between operations  1.2 us (1%)
    ppermute x38, starting transfers between devices, swap(): return lax.ppermute(value, axis, [(i, i ^ bit) for i in range(count)])  34.5 us
    pallas_call x36, Pallas kernels, __call__(): pl.pallas_call(body, out_shape=tuple(shapes) + tuple((pltpu.VMEM(array.sh...  34.5 us
    ppermute x38, waiting for transfers between devices, swap(): return lax.ppermute(value, axis, [(i, i ^ bit) for i in range(count)])  30.1 us
  transfers between devices with their start and end apart: 38, of which 15 were waited for; matrix products, arithmetic and copies ran while one was open for 0% of the time, Pallas kernels for 32%

profile of v7, /device:TPU:0, one launch (start us, length us, event | category | flops | bytes accessed | tf_op | source)
XLA Modules:
  0.0 100.3 jit_solution(13216226849851400229)
XLA Ops:
  1.2 2.6 %collective-permute-start.4 = (bf16[768,128]{1,0:T(8,128)(2,1)}, bf16[768,128]{1,0:T(8,128)(2,1)S(1)}, u32[]{:S(2)}, u32[]{:S(2)}) collective-permute-start(bf16[768,128]{1,0:T(8,128)(2,1)} %refs_6_.4), channel_id=1, source_target_pairs={{0,2},{1,3},{2,0},{3,1},{4,6},{5,7},{6,4},{7,5},{8,10},{9,11},{10,... | collective-permute-start | bytes 589832 | tf_op jit(solution)/shard_map/ppermute | solution.py:931
  4.3 3.0 %shard_map.393 = (bf16[256,128]{1,0:T(8,128)(2,1)S(1)}, bf16[256,128]{1,0:T(8,128)(2,1)S(1)}, s32[42]{0:T(128)S(4)}, s32[8,64]{1,0:T(8,128)S(1)}, bf16[512,768]{...) custom-call(s32[2]{0:T(128)S(1)} %pad_add_fusion.refs_0_, ...), custom_call_target="tpu_custom_call" | custom-call | flops 3000000000 | tf_op jit(solution)/shard_map/pallas_call | solution.py:173
  7.3 1.8 %collective-permute-start.2 = (bf16[256,128]{1,0:T(8,128)(2,1)S(1)}, bf16[256,128]{1,0:T(8,128)(2,1)S(1)}, u32[]{:S(2)}, u32[]{:S(2)}) collective-permute-start(bf16[256,128]{1,0:T(8,128)(2,1)S(1)} %get-tuple-element.141), channel_id=1, source_target_pairs={{0,4},{4,0},{8,12},{12,8},{16,20},{20,16},{24,28},{28,24},{1,5},{5... | collective-permute-start | bytes 196616 | tf_op jit(solution)/shard_map/ppermute | solution.py:931
  11.6 1.9 %collective-permute-start.5 = (bf16[256,128]{1,0:T(8,128)(2,1)S(1)}, bf16[256,128]{1,0:T(8,128)(2,1)S(1)}, u32[]{:S(2)}, u32[]{:S(2)}) collective-permute-start(bf16[256,128]{1,0:T(8,128)(2,1)S(1)} %get-tuple-element.148), channel_id=1, source_target_pairs={{0,8},{4,12},{8,0},{12,4},{16,24},{20,28},{24,16},{28,20},{1,9},{5... | collective-permute-start | bytes 196616 | tf_op jit(solution)/shard_map/ppermute | solution.py:931
  13.5 2.4 %shard_map.396 = (bf16[384,128]{1,0:T(8,128)(2,1)S(1)}, bf16[256,768]{1,0:T(8,128)(2,1)S(1)}, bf16[256,192]{1,0:T(8,128)(2,1)S(1)}, bf16[768]{0:T(1024)(128)(2,1...) custom-call(s32[42]{0:T(128)S(4)} %get-tuple-element.130.refs_0_, ...), custom_call_target="tpu_custom_call" | custom-call | flops 2800000000 | tf_op jit(solution)/shard_map/pallas_call | solution.py:173
  17.5 2.7 %collective-permute-start.14 = (bf16[256,128]{1,0:T(8,128)(2,1)S(1)}, bf16[256,128]{1,0:T(8,128)(2,1)S(1)}, u32[]{:S(2)}, u32[]{:S(2)}) collective-permute-start(bf16[256,128]{1,0:T(8,128)(2,1)S(1)} %get-tuple-element.157), channel_id=1, source_target_pairs={{0,16},{4,20},{8,24},{12,28},{16,0},{20,4},{24,8},{28,12},{1,17},{... | collective-permute-start | bytes 196616 | tf_op jit(solution)/shard_map/ppermute | solution.py:931
  22.6 1.7 %collective-permute-done.14.refs_2_ = bf16[256,128]{1,0:T(8,128)(2,1)S(1)} collective-permute-done((bf16[256,128]{1,0:T(8,128)(2,1)S(1)}, bf16[256,128]{1,0:T(8,128)(2,1)S(1)}, u32[]{:S(2)}, u32[]{:S(2)}) %collective-permute-start.14) | collective-permute-done | bytes 65568 | tf_op jit(solution)/shard_map/ppermute | solution.py:931
  27.3 2.6 %collective-permute-done.16.refs_7_ = bf16[512,128]{1,0:T(8,128)(2,1)S(1)} collective-permute-done((bf16[512,128]{1,0:T(8,128)(2,1)S(1)}, bf16[512,128]{1,0:T(8,128)(2,1)S(1)}, u32[]{:S(2)}, u32[]{:S(2)}) %collective-permute-start.16) | collective-permute-done | bytes 131104 | tf_op jit(solution)/shard_map/ppermute | solution.py:931
  29.9 2.7 %shard_map.401 = (f32[512,768]{1,0:T(8,128)S(1)}, bf16[512,768]{1,0:T(8,128)(2,1)S(1)}, bf16[512,768]{1,0:T(8,128)(2,1)S(1)}, f32[512,768]{1,0:T(8,128)S(1)}) custom-call(s32[42]{0:T(128)S(4)} %get-tuple-element.130.refs_0_, bf16[512,768]{1,0:T(8,128)(2,1)S(1)} %get-tuple-element.132.refs_0_.refs_1_, bf16[768]{0:T(1024)(128)(2,1)S(1)} %get-tuple-element.143.refs_2_, ...), custom_call_target="tpu_custom_call" | custom-call | flops 2600000000 | tf_op jit(solution)/shard_map/pallas_call | solution.py:173
  36.2 2.9 %shard_map.405 = (bf16[2304,128]{1,0:T(8,128)(2,1)S(1)}, bf16[2304,128]{1,0:T(8,128)(2,1)}, bf16[2304,128]{1,0:T(8,128)(2,1)S(1)}, bf16[2304,128]{1,0:T(8,128)(2,1)}) custom-call(s32[42]{0:T(128)S(4)} %get-tuple-element.130.refs_0_, bf16[256,768]{1,0:T(8,128)(2,1)S(1)} %get-tuple-element.165.refs_1_.refs_3_, ...), custom_call_target="tpu_custom_call" | custom-call | flops 2200000000 | tf_op jit(solution)/shard_map/pallas_call | solution.py:173
  42.5 2.3 %shard_map.407 = (f32[256,128]{1,0:T(8,128)S(1)}, f32[1,128]{1,0:T(1,128)S(1)}, f32[3,256,128]{2,1,0:T(8,128)S(1)}) custom-call(s32[42]{0:T(128)S(4)} %get-tuple-element.130.refs_0_, s32[8,64]{1,0:T(8,128)S(1)} %get-tuple-element.131.refs_1_, bf16[8,256,128]{2,1,0:T(8,128)(2,1)} %refs_2_.8, bf16[2,256,256]{2,1,0:T(8,128)(2,1)} %constant.17.clone.refs_3_, ...), custom_call_target="tpu_custom_call" | custom-call | flops 20000000000 | tf_op jit(solution)/shard_map/pallas_call | solution.py:173
  47.4 2.3 %shard_map.411 = (bf16[256,576]{1,0:T(8,128)(2,1)S(1)}, bf16[256,768]{1,0:T(8,128)(2,1)S(1)}, f32[256,768]{1,0:T(8,128)S(1)}, f32[3,768]{1,0:T(4,128)S(1)}) custom-call(s32[42]{0:T(128)S(4)} %get-tuple-element.130.refs_0_, bf16[256,768]{1,0:T(8,128)(2,1)S(1)} %shard_map.410.refs_1_.refs_9_, f32[512,768]{1,0:T(8,128)S(1)} %get-tuple-element.161.refs_9_.refs_2_.refs_1_, ...), custom_call_target="tpu_custom_call" | custom-call | flops 40000000000 | tf_op jit(solution)/shard_map/pallas_call | solution.py:173
  49.7 2.1 %shard_map.412 = (bf16[256,576]{1,0:T(8,128)(2,1)S(1)}, bf16[256,768]{1,0:T(8,128)(2,1)S(1)}, f32[256,768]{1,0:T(8,128)S(1)}, f32[3,768]{1,0:T(4,128)S(1)}) custom-call(s32[42]{0:T(128)S(4)} %get-tuple-element.130.refs_0_, bf16[256,768]{1,0:T(8,128)(2,1)S(1)} %collective-permute-done.21.refs_1_, f32[512,768]{1,0:T(8,128)S(1)} %get-tuple-element.161.refs_9_.refs_2_.refs_1_, ...), custom_call_target="tpu_custom_call" | custom-call | flops 4000000000 | tf_op jit(solution)/shard_map/pallas_call | solution.py:173
  55.0 2.1 %collective-permute-start.28 = (bf16[1152,128]{1,0:T(8,128)(2,1)S(1)}, bf16[1152,128]{1,0:T(8,128)(2,1)S(1)}, u32[]{:S(2)}, u32[]{:S(2)}) collective-permute-start(bf16[1152,128]{1,0:T(8,128)(2,1)S(1)} %get-tuple-element.203), channel_id=1, source_target_pairs={{0,4},{4,0},{8,12},{12,8},{16,20},{20,16},{24,28},{28,24},{1,5},{5... | collective-permute-start | bytes 884744 | tf_op jit(solution)/shard_map/ppermute | solution.py:931
  57.4 1.8 %collective-permute-start.27 = (bf16[144,768]{1,0:T(8,128)(2,1)S(1)}, bf16[144,768]{1,0:T(8,128)(2,1)S(1)}, u32[]{:S(2)}, u32[]{:S(2)}) collective-permute-start(bf16[144,768]{1,0:T(8,128)(2,1)S(1)} %get-tuple-element.200), channel_id=1, source_target_pairs={{0,2},{1,3},{2,0},{3,1},{4,6},{5,7},{6,4},{7,5},{8,10},{9,11},{10,... | collective-permute-start | bytes 663560 | tf_op jit(solution)/shard_map/ppermute | solution.py:931
  62.3 2.1 %collective-permute-done.27.refs_12_.refs_3_ = bf16[144,768]{1,0:T(8,128)(2,1)S(1)} collective-permute-done((bf16[144,768]{1,0:T(8,128)(2,1)S(1)}, bf16[144,768]{1,0:T(8,128)(2,1)S(1)}, u32[]{:S(2)}, u32[]{:S(2)}) %collective-permute-start.27) | collective-permute-done | bytes 221216 | tf_op jit(solution)/shard_map/ppermute | solution.py:931
  68.3 4.4 %collective-permute-done.29.refs_5_ = bf16[816,128]{1,0:T(8,128)(2,1)S(1)} collective-permute-done((bf16[816,128]{1,0:T(8,128)(2,1)S(1)}, bf16[816,128]{1,0:T(8,128)(2,1)S(1)}, u32[]{:S(2)}, u32[]{:S(2)}) %collective-permute-start.29) | collective-permute-done | bytes 208928 | tf_op jit(solution)/shard_map/ppermute | solution.py:931
  74.8 2.2 %collective-permute-start.36 = (bf16[576,128]{1,0:T(8,128)(2,1)S(1)}, bf16[576,128]{1,0:T(8,128)(2,1)S(1)}, u32[]{:S(2)}, u32[]{:S(2)}) collective-permute-start(bf16[576,128]{1,0:T(8,128)(2,1)S(1)} %get-tuple-element.231), channel_id=1, source_target_pairs={{0,16},{4,20},{8,24},{12,28},{16,0},{20,4},{24,8},{28,12},{1,17},{... | collective-permute-start | bytes 442376 | tf_op jit(solution)/shard_map/ppermute | solution.py:931
  78.3 2.3 %collective-permute-start.37 = (bf16[576,128]{1,0:T(8,128)(2,1)S(1)}, bf16[576,128]{1,0:T(8,128)(2,1)S(1)}, u32[]{:S(2)}, u32[]{:S(2)}) collective-permute-start(bf16[576,128]{1,0:T(8,128)(2,1)S(1)} %get-tuple-element.232), channel_id=1, source_target_pairs={{0,16},{4,20},{8,24},{12,28},{16,0},{20,4},{24,8},{28,12},{1,17},{... | collective-permute-start | bytes 442376 | tf_op jit(solution)/shard_map/ppermute | solution.py:931
  80.7 2.9 %collective-permute-done.31.refs_3_ = bf16[1136,128]{1,0:T(8,128)(2,1)S(1)} collective-permute-done((bf16[1136,128]{1,0:T(8,128)(2,1)S(1)}, bf16[1136,128]{1,0:T(8,128)(2,1)S(1)}, u32[]{:S(2)}, u32[]{:S(2)}) %collective-permute-start.31) | collective-permute-done | bytes 290848 | tf_op jit(solution)/shard_map/ppermute | solution.py:931
  83.7 2.1 %collective-permute-start.35 = (bf16[1008,128]{1,0:T(8,128)(2,1)S(1)}, bf16[1008,128]{1,0:T(8,128)(2,1)S(1)}, u32[]{:S(2)}, u32[]{:S(2)}) collective-permute-start(bf16[1008,128]{1,0:T(8,128)(2,1)S(1)} %get-tuple-element.218), channel_id=1, source_target_pairs={{0,16},{4,20},{8,24},{12,28},{16,0},{20,4},{24,8},{28,12},{1,17},{... | collective-permute-start | bytes 774152 | tf_op jit(solution)/shard_map/ppermute | solution.py:931
  86.8 5.6 %collective-permute-done.36.refs_2_ = bf16[576,128]{1,0:T(8,128)(2,1)S(1)} collective-permute-done((bf16[576,128]{1,0:T(8,128)(2,1)S(1)}, bf16[576,128]{1,0:T(8,128)(2,1)S(1)}, u32[]{:S(2)}, u32[]{:S(2)}) %collective-permute-start.36) | collective-permute-done | bytes 147488 | tf_op jit(solution)/shard_map/ppermute | solution.py:931
  92.5 3.2 %collective-permute-done.37.refs_3_ = bf16[576,128]{1,0:T(8,128)(2,1)S(1)} collective-permute-done((bf16[576,128]{1,0:T(8,128)(2,1)S(1)}, bf16[576,128]{1,0:T(8,128)(2,1)S(1)}, u32[]{:S(2)}, u32[]{:S(2)}) %collective-permute-start.37) | collective-permute-done | bytes 147488 | tf_op jit(solution)/shard_map/ppermute | solution.py:931
  96.5 2.5 %collective-permute-done.35.refs_4_ = bf16[1008,128]{1,0:T(8,128)(2,1)S(1)} collective-permute-done((bf16[1008,128]{1,0:T(8,128)(2,1)S(1)}, bf16[1008,128]{1,0:T(8,128)(2,1)S(1)}, u32[]{:S(2)}, u32[]{:S(2)}) %collective-permute-start.35) | collective-permute-done | bytes 258080 | tf_op jit(solution)/shard_map/ppermute | solution.py:931
  (111 shorter events, 37.1 us)
Async XLA Ops:
  0.7 9.1 %collective-permute-start.1 = (bf16[768,128]{1,0:T(8,128)(2,1)}, bf16[768,128]{1,0:T(8,128)(2,1)S(1)}, u32[]{:S(2)}, u32[]{:S(2)}) collective-permute-start(bf16[768,128]{1,0:T(8,128)(2,1)} %refs_6_.4), channel_id=1, source_target_pairs={{0,1},{1,0},{2,3},{3,2},{4,5},{5,4},{6,7},{7,6},{8,9},{9,8},{10,11... | collective-permute-start | bytes 589832 | tf_op jit(solution)/shard_map/ppermute | solution.py:931
  1.2 8.6 %collective-permute-start.4 = (bf16[768,128]{1,0:T(8,128)(2,1)}, bf16[768,128]{1,0:T(8,128)(2,1)S(1)}, u32[]{:S(2)}, u32[]{:S(2)}) collective-permute-start(bf16[768,128]{1,0:T(8,128)(2,1)} %refs_6_.4), channel_id=1, source_target_pairs={{0,2},{1,3},{2,0},{3,1},{4,6},{5,7},{6,4},{7,5},{8,10},{9,11},{10,... | collective-permute-start | bytes 589832 | tf_op jit(solution)/shard_map/ppermute | solution.py:931
  3.8 6.0 %collective-permute-start = (bf16[192,768]{1,0:T(8,128)(2,1)}, bf16[192,768]{1,0:T(8,128)(2,1)S(1)}, u32[]{:S(2)}, u32[]{:S(2)}) collective-permute-start(bf16[192,768]{1,0:T(8,128)(2,1)} %refs_5_.6), channel_id=1, source_target_pairs={{0,1},{1,0},{2,3},{3,2},{4,5},{5,4},{6,7},{7,6},{8,9},{9,8},{10,11... | collective-permute-start | bytes 884744 | tf_op jit(solution)/shard_map/ppermute | solution.py:931
  3.9 13.6 %collective-permute-start.3 = (bf16[192,768]{1,0:T(8,128)(2,1)}, bf16[192,768]{1,0:T(8,128)(2,1)S(1)}, u32[]{:S(2)}, u32[]{:S(2)}) collective-permute-start(bf16[192,768]{1,0:T(8,128)(2,1)} %refs_5_.6), channel_id=1, source_target_pairs={{0,2},{1,3},{2,0},{3,1},{4,6},{5,7},{6,4},{7,5},{8,10},{9,11},{10,... | collective-permute-start | bytes 884744 | tf_op jit(solution)/shard_map/ppermute | solution.py:931
  9.7 12.6 %collective-permute-start.7 = (bf16[768,128]{1,0:T(8,128)(2,1)S(1)}, bf16[768,128]{1,0:T(8,128)(2,1)S(1)}, u32[]{:S(2)}, u32[]{:S(2)}) collective-permute-start(bf16[768,128]{1,0:T(8,128)(2,1)S(1)} %collective-permute-done.4.refs_10_.refs_7_), channel_id=1, source_target_pairs={{0,1},{1,0},{2,3},{3,2},{4,5},{5,4},{6,7},{7,6},{8,9},{9,8},{10,11... | collective-permute-start | bytes 589832 | tf_op jit(solution)/shard_map/ppermute | solution.py:931
  11.6 5.9 %collective-permute-start.5 = (bf16[256,128]{1,0:T(8,128)(2,1)S(1)}, bf16[256,128]{1,0:T(8,128)(2,1)S(1)}, u32[]{:S(2)}, u32[]{:S(2)}) collective-permute-start(bf16[256,128]{1,0:T(8,128)(2,1)S(1)} %get-tuple-element.148), channel_id=1, source_target_pairs={{0,8},{4,12},{8,0},{12,4},{16,24},{20,28},{24,16},{28,20},{1,9},{5... | collective-permute-start | bytes 196616 | tf_op jit(solution)/shard_map/ppermute | solution.py:931
  15.9 9.6 %collective-permute-start.9 = (bf16[384,128]{1,0:T(8,128)(2,1)S(1)}, bf16[384,128]{1,0:T(8,128)(2,1)S(1)}, u32[]{:S(2)}, u32[]{:S(2)}) collective-permute-start(bf16[384,128]{1,0:T(8,128)(2,1)S(1)} %get-tuple-element.149.refs_3_.refs_8_), channel_id=1, source_target_pairs={{0,2},{1,3},{2,0},{3,1},{4,6},{5,7},{6,4},{7,5},{8,10},{9,11},{10,... | collective-permute-start | bytes 294920 | tf_op jit(solution)/shard_map/ppermute | solution.py:931
  17.5 6.7 %collective-permute-start.14 = (bf16[256,128]{1,0:T(8,128)(2,1)S(1)}, bf16[256,128]{1,0:T(8,128)(2,1)S(1)}, u32[]{:S(2)}, u32[]{:S(2)}) collective-permute-start(bf16[256,128]{1,0:T(8,128)(2,1)S(1)} %get-tuple-element.157), channel_id=1, source_target_pairs={{0,16},{4,20},{8,24},{12,28},{16,0},{20,4},{24,8},{28,12},{1,17},{... | collective-permute-start | bytes 196616 | tf_op jit(solution)/shard_map/ppermute | solution.py:931
  26.8 5.8 %collective-permute-start.15 = (bf16[512,128]{1,0:T(8,128)(2,1)S(1)}, bf16[512,128]{1,0:T(8,128)(2,1)S(1)}, u32[]{:S(2)}, u32[]{:S(2)}) collective-permute-start(bf16[512,128]{1,0:T(8,128)(2,1)S(1)} %shard_map.400.refs_16_.refs_5_.refs_7_.refs_3_), channel_id=1, source_target_pairs={{0,1},{1,0},{2,3},{3,2},{4,5},{5,4},{6,7},{7,6},{8,9},{9,8},{10,11... | collective-permute-start | bytes 393224 | tf_op jit(solution)/shard_map/ppermute | solution.py:931
  35.8 11.5 %collective-permute-start.19 = (bf16[256,768]{1,0:T(8,128)(2,1)S(1)}, bf16[256,768]{1,0:T(8,128)(2,1)S(1)}, u32[]{:S(2)}, u32[]{:S(2)}) collective-permute-start(bf16[256,768]{1,0:T(8,128)(2,1)S(1)} %shard_map.404.refs_7_.refs_0_), channel_id=1, source_target_pairs={{0,2},{1,3},{2,0},{3,1},{4,6},{5,7},{6,4},{7,5},{8,10},{9,11},{10,... | collective-permute-start | bytes 1179656 | tf_op jit(solution)/shard_map/ppermute | solution.py:931
  40.0 17.0 %collective-permute-start.24 = (bf16[2304,128]{1,0:T(8,128)(2,1)}, bf16[2304,128]{1,0:T(8,128)(2,1)}, u32[]{:S(2)}, u32[]{:S(2)}) collective-permute-start(bf16[2304,128]{1,0:T(8,128)(2,1)} %get-tuple-element.185), channel_id=1, source_target_pairs={{0,4},{4,0},{8,12},{12,8},{16,20},{20,16},{24,28},{28,24},{1,5},{5... | collective-permute-start | bytes 1769480 | tf_op jit(solution)/shard_map/ppermute | solution.py:931
  41.5 15.7 %collective-permute-start.25 = (bf16[2304,128]{1,0:T(8,128)(2,1)}, bf16[2304,128]{1,0:T(8,128)(2,1)}, u32[]{:S(2)}, u32[]{:S(2)}) collective-permute-start(bf16[2304,128]{1,0:T(8,128)(2,1)} %get-tuple-element.186), channel_id=1, source_target_pairs={{0,8},{4,12},{8,0},{12,4},{16,24},{20,28},{24,16},{28,20},{1,9},{5... | collective-permute-start | bytes 1769480 | tf_op jit(solution)/shard_map/ppermute | solution.py:931
  44.9 14.2 %collective-permute-start.22 = (bf16[256,768]{1,0:T(8,128)(2,1)S(1)}, bf16[256,768]{1,0:T(8,128)(2,1)S(1)}, u32[]{:S(2)}, u32[]{:S(2)}) collective-permute-start(bf16[256,768]{1,0:T(8,128)(2,1)S(1)} %shard_map.408.refs_1_.refs_0_), channel_id=1, source_target_pairs={{0,2},{1,3},{2,0},{3,1},{4,6},{5,7},{6,4},{7,5},{8,10},{9,11},{10,... | collective-permute-start | bytes 1179656 | tf_op jit(solution)/shard_map/ppermute | solution.py:931
  55.0 13.3 %collective-permute-start.28 = (bf16[1152,128]{1,0:T(8,128)(2,1)S(1)}, bf16[1152,128]{1,0:T(8,128)(2,1)S(1)}, u32[]{:S(2)}, u32[]{:S(2)}) collective-permute-start(bf16[1152,128]{1,0:T(8,128)(2,1)S(1)} %get-tuple-element.203), channel_id=1, source_target_pairs={{0,4},{4,0},{8,12},{12,8},{16,20},{20,16},{24,28},{28,24},{1,5},{5... | collective-permute-start | bytes 884744 | tf_op jit(solution)/shard_map/ppermute | solution.py:931
  57.0 11.2 %collective-permute-start.30 = (bf16[1152,128]{1,0:T(8,128)(2,1)S(1)}, bf16[1152,128]{1,0:T(8,128)(2,1)S(1)}, u32[]{:S(2)}, u32[]{:S(2)}) collective-permute-start(bf16[1152,128]{1,0:T(8,128)(2,1)S(1)} %get-tuple-element.205), channel_id=1, source_target_pairs={{0,8},{4,12},{8,0},{12,4},{16,24},{20,28},{24,16},{28,20},{1,9},{5... | collective-permute-start | bytes 884744 | tf_op jit(solution)/shard_map/ppermute | solution.py:931
  57.4 7.0 %collective-permute-start.27 = (bf16[144,768]{1,0:T(8,128)(2,1)S(1)}, bf16[144,768]{1,0:T(8,128)(2,1)S(1)}, u32[]{:S(2)}, u32[]{:S(2)}) collective-permute-start(bf16[144,768]{1,0:T(8,128)(2,1)S(1)} %get-tuple-element.200), channel_id=1, source_target_pairs={{0,2},{1,3},{2,0},{3,1},{4,6},{5,7},{6,4},{7,5},{8,10},{9,11},{10,... | collective-permute-start | bytes 663560 | tf_op jit(solution)/shard_map/ppermute | solution.py:931
  60.6 14.1 %collective-permute-start.34 = (bf16[1152,128]{1,0:T(8,128)(2,1)S(1)}, bf16[1152,128]{1,0:T(8,128)(2,1)S(1)}, u32[]{:S(2)}, u32[]{:S(2)}) collective-permute-start(bf16[1152,128]{1,0:T(8,128)(2,1)S(1)} %get-tuple-element.213), channel_id=1, source_target_pairs={{0,8},{4,12},{8,0},{12,4},{16,24},{20,28},{24,16},{28,20},{1,9},{5... | collective-permute-start | bytes 884744 | tf_op jit(solution)/shard_map/ppermute | solution.py:931
  64.5 8.2 %collective-permute-start.29 = (bf16[816,128]{1,0:T(8,128)(2,1)S(1)}, bf16[816,128]{1,0:T(8,128)(2,1)S(1)}, u32[]{:S(2)}, u32[]{:S(2)}) collective-permute-start(bf16[816,128]{1,0:T(8,128)(2,1)S(1)} %get-tuple-element.204), channel_id=1, source_target_pairs={{0,4},{4,0},{8,12},{12,8},{16,20},{20,16},{24,28},{28,24},{1,5},{5... | collective-permute-start | bytes 626696 | tf_op jit(solution)/shard_map/ppermute | solution.py:931
  66.9 11.3 %collective-permute-start.33 = (bf16[1152,128]{1,0:T(8,128)(2,1)S(1)}, bf16[1152,128]{1,0:T(8,128)(2,1)S(1)}, u32[]{:S(2)}, u32[]{:S(2)}) collective-permute-start(bf16[1152,128]{1,0:T(8,128)(2,1)S(1)} %get-tuple-element.212), channel_id=1, source_target_pairs={{0,4},{4,0},{8,12},{12,8},{16,20},{20,16},{24,28},{28,24},{1,5},{5... | collective-permute-start | bytes 884744 | tf_op jit(solution)/shard_map/ppermute | solution.py:931
  72.9 7.8 %collective-permute-start.32 = (bf16[576,128]{1,0:T(8,128)(2,1)S(1)}, bf16[576,128]{1,0:T(8,128)(2,1)S(1)}, u32[]{:S(2)}, u32[]{:S(2)}) collective-permute-start(bf16[576,128]{1,0:T(8,128)(2,1)S(1)} %get-tuple-element.211), channel_id=1, source_target_pairs={{0,4},{4,0},{8,12},{12,8},{16,20},{20,16},{24,28},{28,24},{1,5},{5... | collective-permute-start | bytes 442376 | tf_op jit(solution)/shard_map/ppermute | solution.py:931
  74.0 9.6 %collective-permute-start.31 = (bf16[1136,128]{1,0:T(8,128)(2,1)S(1)}, bf16[1136,128]{1,0:T(8,128)(2,1)S(1)}, u32[]{:S(2)}, u32[]{:S(2)}) collective-permute-start(bf16[1136,128]{1,0:T(8,128)(2,1)S(1)} %get-tuple-element.210), channel_id=1, source_target_pairs={{0,8},{4,12},{8,0},{12,4},{16,24},{20,28},{24,16},{28,20},{1,9},{5... | collective-permute-start | bytes 872456 | tf_op jit(solution)/shard_map/ppermute | solution.py:931
  74.8 17.7 %collective-permute-start.36 = (bf16[576,128]{1,0:T(8,128)(2,1)S(1)}, bf16[576,128]{1,0:T(8,128)(2,1)S(1)}, u32[]{:S(2)}, u32[]{:S(2)}) collective-permute-start(bf16[576,128]{1,0:T(8,128)(2,1)S(1)} %get-tuple-element.231), channel_id=1, source_target_pairs={{0,16},{4,20},{8,24},{12,28},{16,0},{20,4},{24,8},{28,12},{1,17},{... | collective-permute-start | bytes 442376 | tf_op jit(solution)/shard_map/ppermute | solution.py:931
  78.3 17.3 %collective-permute-start.37 = (bf16[576,128]{1,0:T(8,128)(2,1)S(1)}, bf16[576,128]{1,0:T(8,128)(2,1)S(1)}, u32[]{:S(2)}, u32[]{:S(2)}) collective-permute-start(bf16[576,128]{1,0:T(8,128)(2,1)S(1)} %get-tuple-element.232), channel_id=1, source_target_pairs={{0,16},{4,20},{8,24},{12,28},{16,0},{20,4},{24,8},{28,12},{1,17},{... | collective-permute-start | bytes 442376 | tf_op jit(solution)/shard_map/ppermute | solution.py:931
  83.7 15.3 %collective-permute-start.35 = (bf16[1008,128]{1,0:T(8,128)(2,1)S(1)}, bf16[1008,128]{1,0:T(8,128)(2,1)S(1)}, u32[]{:S(2)}, u32[]{:S(2)}) collective-permute-start(bf16[1008,128]{1,0:T(8,128)(2,1)S(1)} %get-tuple-element.218), channel_id=1, source_target_pairs={{0,16},{4,20},{8,24},{12,28},{16,0},{20,4},{24,8},{28,12},{1,17},{... | collective-permute-start | bytes 774152 | tf_op jit(solution)/shard_map/ppermute | solution.py:931
  (25 other events, 119.3 us)

commit v8 on v7

--- a/solution.py
+++ b/solution.py
@@ -875,7 +875,7 @@
         ref[exchange.shared_at(0) :, :] = rows_ref[...].astype(low_type)
 
 
-def base_kernel(info, info_ref, seen_ref, mask_ref, layout_ref, base_ref):
+def base_kernel(info, info_ref, seen_ref, mask_ref, layout_ref, base_ref, chosen_ref):
     cells = lax.broadcasted_iota(jnp.int32, (GRID, VIS), 0)
     cell_column = lax.broadcasted_iota(jnp.int32, (GRID, 1), 0)
     mask_row = wide_row(mask_ref)
@@ -885,21 +885,20 @@
         seen = (seen_ref[pl.ds(slot, 1), :] == cells).astype(wide_type)
         fill = (cell_column < size).astype(wide_type) - jnp.sum(seen, axis=1, keepdims=True)
         base_ref[slot] = fill * mask_row + layout_ref[side_of(size)]
+        chosen_ref[slot] = seen.astype(low_type)
 
     over_slots(info.count, one_slot)
 
 
 def late_out_kernel(
-    info, exchange, turned_exchange, pad, middle, sizes, info_ref, seen_ref, keep_ref, turned_ref, came_ref, base_ref,
+    info, exchange, turned_exchange, pad, middle, sizes, info_ref, chosen_ref, keep_ref, turned_ref, came_ref, base_ref,
     grids_ref, out_ref, qkv_ref, proj_ref, pos_ref, *refs
 ):
     *vector_refs, wide_ref, rows_ref = refs
     other_ref, turned_other_ref = views(came_ref, sizes)
-    cells = lax.broadcasted_iota(jnp.int32, (GRID, VIS), 0)
     for relative, ref, start in exchange.arrived(keep_ref, other_ref):
         slot = info_ref[0] ^ relative
-        seen = seen_ref[pl.ds(slot, 1), :] == cells
-        placed = dot(seen.astype(low_type), ref[start : start + VIS, :])
+        placed = dot(chosen_ref[slot], ref[start : start + VIS, :])
         grids_ref[slot] = (placed + base_ref[slot]).astype(low_type)
     share = proj_ref.shape[0]
     tiles = wide_ref.shape[1] // LANES
@@ -1277,9 +1276,9 @@
 
     early = (up_exchange, down_exchange)
     late = (joint_exchange, turned_exchange)
-    (base,) = run(
+    base, chosen = run(
         lambda *refs: base_kernel(info, *refs),
-        [wide(count, GRID, columns)],
+        [wide(count, GRID, columns), low(count, GRID, VIS)],
         (facts, seen, mask_token, layouts),
         (SMEM,) + (VMEM,) * 3,
         cost=0.8,
@@ -1354,7 +1353,7 @@
             wide(pos_share, columns),
         ]
         + [wide(size) for size in (head_columns, head_columns, units, columns, columns) + (width,) * 6],
-        (facts, seen, late_keep, turned_keep, late_came, base),
+        (facts, chosen, late_keep, turned_keep, late_came, base),
         (SMEM,) + (VMEM,) * 5,
         scratch=[pltpu.VMEM((share, late_columns), wide_type), pltpu.VMEM((VECTOR_ROWS, LANES), wide_type)],
         final=True,

time: 101 us -> 101 us (level)
  transfers between devices with their start and end apart: 38 -> 38, of which waited for: 15 -> 14; matrix products, arithmetic and copies ran while one was open for 0% -> 0% of each run, Pallas kernels for 32% -> 32%
where the time goes in v8:
time: 101 us; the launch traced here: 100 us
  Pallas kernels  34.5 us (34%)
  starting transfers between devices  34.4 us (34%)
  waiting for transfers between devices  30.1 us (30%)
  between operations  1.21 us (1%)
    pallas_call x36, Pallas kernels, __call__(): pl.pallas_call(body, out_shape=tuple(shapes) + tuple((pltpu.VMEM(array.sh...  34.5 us
    ppermute x38, starting transfers between devices, swap(): return lax.ppermute(value, axis, [(i, i ^ bit) for i in range(count)])  34.4 us
    ppermute x38, waiting for transfers between devices, swap(): return lax.ppermute(value, axis, [(i, i ^ bit) for i in range(count)])  30.1 us
  transfers between devices with their start and end apart: 38, of which 14 were waited for; matrix products, arithmetic and copies ran while one was open for 0% of the time, Pallas kernels for 32%

profile of v8, /device:TPU:0, one launch (start us, length us, event | category | flops | bytes accessed | tf_op | source)
XLA Modules:
  0.0 100.3 jit_solution(5999190169686881478)
XLA Ops:
  1.2 2.6 %collective-permute-start.4 = (bf16[768,128]{1,0:T(8,128)(2,1)}, bf16[768,128]{1,0:T(8,128)(2,1)S(1)}, u32[]{:S(2)}, u32[]{:S(2)}) collective-permute-start(bf16[768,128]{1,0:T(8,128)(2,1)} %refs_6_.4), channel_id=1, source_target_pairs={{0,2},{1,3},{2,0},{3,1},{4,6},{5,7},{6,4},{7,5},{8,10},{9,11},{10,... | collective-permute-start | bytes 589832 | tf_op jit(solution)/shard_map/ppermute | solution.py:930
  4.3 3.0 %shard_map.393 = (bf16[256,128]{1,0:T(8,128)(2,1)S(1)}, bf16[256,128]{1,0:T(8,128)(2,1)S(1)}, s32[42]{0:T(128)S(4)}, s32[8,64]{1,0:T(8,128)S(1)}, bf16[512,768]{...) custom-call(s32[2]{0:T(128)S(1)} %pad_add_fusion.refs_0_, ...), custom_call_target="tpu_custom_call" | custom-call | flops 3000000000 | tf_op jit(solution)/shard_map/pallas_call | solution.py:173
  7.3 1.8 %collective-permute-start.2 = (bf16[256,128]{1,0:T(8,128)(2,1)S(1)}, bf16[256,128]{1,0:T(8,128)(2,1)S(1)}, u32[]{:S(2)}, u32[]{:S(2)}) collective-permute-start(bf16[256,128]{1,0:T(8,128)(2,1)S(1)} %get-tuple-element.142), channel_id=1, source_target_pairs={{0,4},{4,0},{8,12},{12,8},{16,20},{20,16},{24,28},{28,24},{1,5},{5... | collective-permute-start | bytes 196616 | tf_op jit(solution)/shard_map/ppermute | solution.py:930
  11.6 1.9 %collective-permute-start.5 = (bf16[256,128]{1,0:T(8,128)(2,1)S(1)}, bf16[256,128]{1,0:T(8,128)(2,1)S(1)}, u32[]{:S(2)}, u32[]{:S(2)}) collective-permute-start(bf16[256,128]{1,0:T(8,128)(2,1)S(1)} %get-tuple-element.150), channel_id=1, source_target_pairs={{0,8},{4,12},{8,0},{12,4},{16,24},{20,28},{24,16},{28,20},{1,9},{5... | collective-permute-start | bytes 196616 | tf_op jit(solution)/shard_map/ppermute | solution.py:930
  13.5 2.4 %shard_map.396 = (bf16[384,128]{1,0:T(8,128)(2,1)S(1)}, bf16[256,768]{1,0:T(8,128)(2,1)S(1)}, bf16[256,192]{1,0:T(8,128)(2,1)S(1)}, bf16[768]{0:T(1024)(128)(2,1...) custom-call(s32[42]{0:T(128)S(4)} %get-tuple-element.132.refs_0_, ...), custom_call_target="tpu_custom_call" | custom-call | flops 2800000000 | tf_op jit(solution)/shard_map/pallas_call | solution.py:173
  17.5 2.7 %collective-permute-start.14 = (bf16[256,128]{1,0:T(8,128)(2,1)S(1)}, bf16[256,128]{1,0:T(8,128)(2,1)S(1)}, u32[]{:S(2)}, u32[]{:S(2)}) collective-permute-start(bf16[256,128]{1,0:T(8,128)(2,1)S(1)} %get-tuple-element.159), channel_id=1, source_target_pairs={{0,16},{4,20},{8,24},{12,28},{16,0},{20,4},{24,8},{28,12},{1,17},{... | collective-permute-start | bytes 196616 | tf_op jit(solution)/shard_map/ppermute | solution.py:930
  22.6 1.7 %collective-permute-done.14.refs_2_ = bf16[256,128]{1,0:T(8,128)(2,1)S(1)} collective-permute-done((bf16[256,128]{1,0:T(8,128)(2,1)S(1)}, bf16[256,128]{1,0:T(8,128)(2,1)S(1)}, u32[]{:S(2)}, u32[]{:S(2)}) %collective-permute-start.14) | collective-permute-done | bytes 65568 | tf_op jit(solution)/shard_map/ppermute | solution.py:930
  27.3 2.6 %collective-permute-done.16.refs_7_ = bf16[512,128]{1,0:T(8,128)(2,1)S(1)} collective-permute-done((bf16[512,128]{1,0:T(8,128)(2,1)S(1)}, bf16[512,128]{1,0:T(8,128)(2,1)S(1)}, u32[]{:S(2)}, u32[]{:S(2)}) %collective-permute-start.16) | collective-permute-done | bytes 131104 | tf_op jit(solution)/shard_map/ppermute | solution.py:930
  29.9 2.7 %shard_map.401 = (f32[512,768]{1,0:T(8,128)S(1)}, bf16[512,768]{1,0:T(8,128)(2,1)S(1)}, bf16[512,768]{1,0:T(8,128)(2,1)S(1)}, f32[512,768]{1,0:T(8,128)S(1)}) custom-call(s32[42]{0:T(128)S(4)} %get-tuple-element.132.refs_0_, bf16[512,768]{1,0:T(8,128)(2,1)S(1)} %get-tuple-element.134.refs_0_.refs_1_, bf16[768]{0:T(1024)(128)(2,1)S(1)} %get-tuple-element.145.refs_2_, ...), custom_call_target="tpu_custom_call" | custom-call | flops 2600000000 | tf_op jit(solution)/shard_map/pallas_call | solution.py:173
  36.2 2.9 %shard_map.405 = (bf16[2304,128]{1,0:T(8,128)(2,1)S(1)}, bf16[2304,128]{1,0:T(8,128)(2,1)}, bf16[2304,128]{1,0:T(8,128)(2,1)S(1)}, bf16[2304,128]{1,0:T(8,128)(2,1)}) custom-call(s32[42]{0:T(128)S(4)} %get-tuple-element.132.refs_0_, bf16[256,768]{1,0:T(8,128)(2,1)S(1)} %get-tuple-element.166.refs_1_.refs_3_, ...), custom_call_target="tpu_custom_call" | custom-call | flops 2200000000 | tf_op jit(solution)/shard_map/pallas_call | solution.py:173
  42.5 2.3 %shard_map.407 = (f32[256,128]{1,0:T(8,128)S(1)}, f32[1,128]{1,0:T(1,128)S(1)}, f32[3,256,128]{2,1,0:T(8,128)S(1)}) custom-call(s32[42]{0:T(128)S(4)} %get-tuple-element.132.refs_0_, s32[8,64]{1,0:T(8,128)S(1)} %get-tuple-element.133.refs_1_, bf16[8,256,128]{2,1,0:T(8,128)(2,1)} %refs_2_.8, bf16[2,256,256]{2,1,0:T(8,128)(2,1)} %constant.17.clone.refs_3_, ...), custom_call_target="tpu_custom_call" | custom-call | flops 20000000000 | tf_op jit(solution)/shard_map/pallas_call | solution.py:173
  47.4 2.3 %shard_map.411 = (bf16[256,576]{1,0:T(8,128)(2,1)S(1)}, bf16[256,768]{1,0:T(8,128)(2,1)S(1)}, f32[256,768]{1,0:T(8,128)S(1)}, f32[3,768]{1,0:T(4,128)S(1)}) custom-call(s32[42]{0:T(128)S(4)} %get-tuple-element.132.refs_0_, bf16[256,768]{1,0:T(8,128)(2,1)S(1)} %shard_map.410.refs_1_.refs_9_, f32[512,768]{1,0:T(8,128)S(1)} %get-tuple-element.164.refs_9_.refs_2_.refs_1_, ...), custom_call_target="tpu_custom_call" | custom-call | flops 40000000000 | tf_op jit(solution)/shard_map/pallas_call | solution.py:173
  49.7 2.1 %shard_map.412 = (bf16[256,576]{1,0:T(8,128)(2,1)S(1)}, bf16[256,768]{1,0:T(8,128)(2,1)S(1)}, f32[256,768]{1,0:T(8,128)S(1)}, f32[3,768]{1,0:T(4,128)S(1)}) custom-call(s32[42]{0:T(128)S(4)} %get-tuple-element.132.refs_0_, bf16[256,768]{1,0:T(8,128)(2,1)S(1)} %collective-permute-done.23.refs_1_, f32[512,768]{1,0:T(8,128)S(1)} %get-tuple-element.164.refs_9_.refs_2_.refs_1_, ...), custom_call_target="tpu_custom_call" | custom-call | flops 4000000000 | tf_op jit(solution)/shard_map/pallas_call | solution.py:173
  55.0 2.1 %collective-permute-start.28 = (bf16[1152,128]{1,0:T(8,128)(2,1)S(1)}, bf16[1152,128]{1,0:T(8,128)(2,1)S(1)}, u32[]{:S(2)}, u32[]{:S(2)}) collective-permute-start(bf16[1152,128]{1,0:T(8,128)(2,1)S(1)} %get-tuple-element.208), channel_id=1, source_target_pairs={{0,4},{4,0},{8,12},{12,8},{16,20},{20,16},{24,28},{28,24},{1,5},{5... | collective-permute-start | bytes 884744 | tf_op jit(solution)/shard_map/ppermute | solution.py:930
  59.7 1.8 %collective-permute-start.34 = (bf16[1152,128]{1,0:T(8,128)(2,1)S(1)}, bf16[1152,128]{1,0:T(8,128)(2,1)S(1)}, u32[]{:S(2)}, u32[]{:S(2)}) collective-permute-start(bf16[1152,128]{1,0:T(8,128)(2,1)S(1)} %get-tuple-element.217), channel_id=1, source_target_pairs={{0,8},{4,12},{8,0},{12,4},{16,24},{20,28},{24,16},{28,20},{1,9},{5... | collective-permute-start | bytes 884744 | tf_op jit(solution)/shard_map/ppermute | solution.py:930
  62.3 2.1 %collective-permute-done.27.refs_12_.refs_3_ = bf16[144,768]{1,0:T(8,128)(2,1)S(1)} collective-permute-done((bf16[144,768]{1,0:T(8,128)(2,1)S(1)}, bf16[144,768]{1,0:T(8,128)(2,1)S(1)}, u32[]{:S(2)}, u32[]{:S(2)}) %collective-permute-start.27) | collective-permute-done | bytes 221216 | tf_op jit(solution)/shard_map/ppermute | solution.py:930
  68.3 4.4 %collective-permute-done.29.refs_5_ = bf16[816,128]{1,0:T(8,128)(2,1)S(1)} collective-permute-done((bf16[816,128]{1,0:T(8,128)(2,1)S(1)}, bf16[816,128]{1,0:T(8,128)(2,1)S(1)}, u32[]{:S(2)}, u32[]{:S(2)}) %collective-permute-start.29) | collective-permute-done | bytes 208928 | tf_op jit(solution)/shard_map/ppermute | solution.py:930
  74.8 2.5 %collective-permute-start.36 = (bf16[576,128]{1,0:T(8,128)(2,1)S(1)}, bf16[576,128]{1,0:T(8,128)(2,1)S(1)}, u32[]{:S(2)}, u32[]{:S(2)}) collective-permute-start(bf16[576,128]{1,0:T(8,128)(2,1)S(1)} %get-tuple-element.235), channel_id=1, source_target_pairs={{0,16},{4,20},{8,24},{12,28},{16,0},{20,4},{24,8},{28,12},{1,17},{... | collective-permute-start | bytes 442376 | tf_op jit(solution)/shard_map/ppermute | solution.py:930
  78.5 1.9 %collective-permute-start.37 = (bf16[576,128]{1,0:T(8,128)(2,1)S(1)}, bf16[576,128]{1,0:T(8,128)(2,1)S(1)}, u32[]{:S(2)}, u32[]{:S(2)}) collective-permute-start(bf16[576,128]{1,0:T(8,128)(2,1)S(1)} %get-tuple-element.236), channel_id=1, source_target_pairs={{0,16},{4,20},{8,24},{12,28},{16,0},{20,4},{24,8},{28,12},{1,17},{... | collective-permute-start | bytes 442376 | tf_op jit(solution)/shard_map/ppermute | solution.py:930
  80.4 3.2 %collective-permute-done.31.refs_3_ = bf16[1136,128]{1,0:T(8,128)(2,1)S(1)} collective-permute-done((bf16[1136,128]{1,0:T(8,128)(2,1)S(1)}, bf16[1136,128]{1,0:T(8,128)(2,1)S(1)}, u32[]{:S(2)}, u32[]{:S(2)}) %collective-permute-start.31) | collective-permute-done | bytes 290848 | tf_op jit(solution)/shard_map/ppermute | solution.py:930
  83.6 2.1 %collective-permute-start.35 = (bf16[1008,128]{1,0:T(8,128)(2,1)S(1)}, bf16[1008,128]{1,0:T(8,128)(2,1)S(1)}, u32[]{:S(2)}, u32[]{:S(2)}) collective-permute-start(bf16[1008,128]{1,0:T(8,128)(2,1)S(1)} %get-tuple-element.222), channel_id=1, source_target_pairs={{0,16},{4,20},{8,24},{12,28},{16,0},{20,4},{24,8},{28,12},{1,17},{... | collective-permute-start | bytes 774152 | tf_op jit(solution)/shard_map/ppermute | solution.py:930
  86.8 5.6 %collective-permute-done.36.refs_2_ = bf16[576,128]{1,0:T(8,128)(2,1)S(1)} collective-permute-done((bf16[576,128]{1,0:T(8,128)(2,1)S(1)}, bf16[576,128]{1,0:T(8,128)(2,1)S(1)}, u32[]{:S(2)}, u32[]{:S(2)}) %collective-permute-start.36) | collective-permute-done | bytes 147488 | tf_op jit(solution)/shard_map/ppermute | solution.py:930
  92.4 3.2 %collective-permute-done.37.refs_3_ = bf16[576,128]{1,0:T(8,128)(2,1)S(1)} collective-permute-done((bf16[576,128]{1,0:T(8,128)(2,1)S(1)}, bf16[576,128]{1,0:T(8,128)(2,1)S(1)}, u32[]{:S(2)}, u32[]{:S(2)}) %collective-permute-start.37) | collective-permute-done | bytes 147488 | tf_op jit(solution)/shard_map/ppermute | solution.py:930
  96.4 2.5 %collective-permute-done.35.refs_4_ = bf16[1008,128]{1,0:T(8,128)(2,1)S(1)} collective-permute-done((bf16[1008,128]{1,0:T(8,128)(2,1)S(1)}, bf16[1008,128]{1,0:T(8,128)(2,1)S(1)}, u32[]{:S(2)}, u32[]{:S(2)}) %collective-permute-start.35) | collective-permute-done | bytes 258080 | tf_op jit(solution)/shard_map/ppermute | solution.py:930
  (111 shorter events, 37.0 us)
Async XLA Ops:
  0.7 9.1 %collective-permute-start.1 = (bf16[768,128]{1,0:T(8,128)(2,1)}, bf16[768,128]{1,0:T(8,128)(2,1)S(1)}, u32[]{:S(2)}, u32[]{:S(2)}) collective-permute-start(bf16[768,128]{1,0:T(8,128)(2,1)} %refs_6_.4), channel_id=1, source_target_pairs={{0,1},{1,0},{2,3},{3,2},{4,5},{5,4},{6,7},{7,6},{8,9},{9,8},{10,11... | collective-permute-start | bytes 589832 | tf_op jit(solution)/shard_map/ppermute | solution.py:930
  1.2 8.6 %collective-permute-start.4 = (bf16[768,128]{1,0:T(8,128)(2,1)}, bf16[768,128]{1,0:T(8,128)(2,1)S(1)}, u32[]{:S(2)}, u32[]{:S(2)}) collective-permute-start(bf16[768,128]{1,0:T(8,128)(2,1)} %refs_6_.4), channel_id=1, source_target_pairs={{0,2},{1,3},{2,0},{3,1},{4,6},{5,7},{6,4},{7,5},{8,10},{9,11},{10,... | collective-permute-start | bytes 589832 | tf_op jit(solution)/shard_map/ppermute | solution.py:930
  3.8 6.0 %collective-permute-start = (bf16[192,768]{1,0:T(8,128)(2,1)}, bf16[192,768]{1,0:T(8,128)(2,1)S(1)}, u32[]{:S(2)}, u32[]{:S(2)}) collective-permute-start(bf16[192,768]{1,0:T(8,128)(2,1)} %refs_5_.6), channel_id=1, source_target_pairs={{0,1},{1,0},{2,3},{3,2},{4,5},{5,4},{6,7},{7,6},{8,9},{9,8},{10,11... | collective-permute-start | bytes 884744 | tf_op jit(solution)/shard_map/ppermute | solution.py:930
  3.9 13.6 %collective-permute-start.3 = (bf16[192,768]{1,0:T(8,128)(2,1)}, bf16[192,768]{1,0:T(8,128)(2,1)S(1)}, u32[]{:S(2)}, u32[]{:S(2)}) collective-permute-start(bf16[192,768]{1,0:T(8,128)(2,1)} %refs_5_.6), channel_id=1, source_target_pairs={{0,2},{1,3},{2,0},{3,1},{4,6},{5,7},{6,4},{7,5},{8,10},{9,11},{10,... | collective-permute-start | bytes 884744 | tf_op jit(solution)/shard_map/ppermute | solution.py:930
  9.7 12.6 %collective-permute-start.7 = (bf16[768,128]{1,0:T(8,128)(2,1)S(1)}, bf16[768,128]{1,0:T(8,128)(2,1)S(1)}, u32[]{:S(2)}, u32[]{:S(2)}) collective-permute-start(bf16[768,128]{1,0:T(8,128)(2,1)S(1)} %collective-permute-done.4.refs_10_.refs_7_), channel_id=1, source_target_pairs={{0,1},{1,0},{2,3},{3,2},{4,5},{5,4},{6,7},{7,6},{8,9},{9,8},{10,11... | collective-permute-start | bytes 589832 | tf_op jit(solution)/shard_map/ppermute | solution.py:930
  11.6 5.9 %collective-permute-start.5 = (bf16[256,128]{1,0:T(8,128)(2,1)S(1)}, bf16[256,128]{1,0:T(8,128)(2,1)S(1)}, u32[]{:S(2)}, u32[]{:S(2)}) collective-permute-start(bf16[256,128]{1,0:T(8,128)(2,1)S(1)} %get-tuple-element.150), channel_id=1, source_target_pairs={{0,8},{4,12},{8,0},{12,4},{16,24},{20,28},{24,16},{28,20},{1,9},{5... | collective-permute-start | bytes 196616 | tf_op jit(solution)/shard_map/ppermute | solution.py:930
  15.9 9.6 %collective-permute-start.9 = (bf16[384,128]{1,0:T(8,128)(2,1)S(1)}, bf16[384,128]{1,0:T(8,128)(2,1)S(1)}, u32[]{:S(2)}, u32[]{:S(2)}) collective-permute-start(bf16[384,128]{1,0:T(8,128)(2,1)S(1)} %get-tuple-element.151.refs_3_.refs_8_), channel_id=1, source_target_pairs={{0,2},{1,3},{2,0},{3,1},{4,6},{5,7},{6,4},{7,5},{8,10},{9,11},{10,... | collective-permute-start | bytes 294920 | tf_op jit(solution)/shard_map/ppermute | solution.py:930
  17.5 6.7 %collective-permute-start.14 = (bf16[256,128]{1,0:T(8,128)(2,1)S(1)}, bf16[256,128]{1,0:T(8,128)(2,1)S(1)}, u32[]{:S(2)}, u32[]{:S(2)}) collective-permute-start(bf16[256,128]{1,0:T(8,128)(2,1)S(1)} %get-tuple-element.159), channel_id=1, source_target_pairs={{0,16},{4,20},{8,24},{12,28},{16,0},{20,4},{24,8},{28,12},{1,17},{... | collective-permute-start | bytes 196616 | tf_op jit(solution)/shard_map/ppermute | solution.py:930
  26.8 5.8 %collective-permute-start.15 = (bf16[512,128]{1,0:T(8,128)(2,1)S(1)}, bf16[512,128]{1,0:T(8,128)(2,1)S(1)}, u32[]{:S(2)}, u32[]{:S(2)}) collective-permute-start(bf16[512,128]{1,0:T(8,128)(2,1)S(1)} %shard_map.400.refs_16_.refs_5_.refs_7_.refs_3_), channel_id=1, source_target_pairs={{0,1},{1,0},{2,3},{3,2},{4,5},{5,4},{6,7},{7,6},{8,9},{9,8},{10,11... | collective-permute-start | bytes 393224 | tf_op jit(solution)/shard_map/ppermute | solution.py:930
  35.8 11.5 %collective-permute-start.22 = (bf16[256,768]{1,0:T(8,128)(2,1)S(1)}, bf16[256,768]{1,0:T(8,128)(2,1)S(1)}, u32[]{:S(2)}, u32[]{:S(2)}) collective-permute-start(bf16[256,768]{1,0:T(8,128)(2,1)S(1)} %shard_map.404.refs_7_.refs_0_), channel_id=1, source_target_pairs={{0,2},{1,3},{2,0},{3,1},{4,6},{5,7},{6,4},{7,5},{8,10},{9,11},{10,... | collective-permute-start | bytes 1179656 | tf_op jit(solution)/shard_map/ppermute | solution.py:930
  40.0 17.1 %collective-permute-start.19 = (bf16[2304,128]{1,0:T(8,128)(2,1)}, bf16[2304,128]{1,0:T(8,128)(2,1)}, u32[]{:S(2)}, u32[]{:S(2)}) collective-permute-start(bf16[2304,128]{1,0:T(8,128)(2,1)} %get-tuple-element.175), channel_id=1, source_target_pairs={{0,8},{4,12},{8,0},{12,4},{16,24},{20,28},{24,16},{28,20},{1,9},{5... | collective-permute-start | bytes 1769480 | tf_op jit(solution)/shard_map/ppermute | solution.py:930
  41.0 16.0 %collective-permute-start.25 = (bf16[2304,128]{1,0:T(8,128)(2,1)}, bf16[2304,128]{1,0:T(8,128)(2,1)}, u32[]{:S(2)}, u32[]{:S(2)}) collective-permute-start(bf16[2304,128]{1,0:T(8,128)(2,1)} %get-tuple-element.184), channel_id=1, source_target_pairs={{0,4},{4,0},{8,12},{12,8},{16,20},{20,16},{24,28},{28,24},{1,5},{5... | collective-permute-start | bytes 1769480 | tf_op jit(solution)/shard_map/ppermute | solution.py:930
  44.9 13.3 %collective-permute-start.21 = (bf16[256,768]{1,0:T(8,128)(2,1)S(1)}, bf16[256,768]{1,0:T(8,128)(2,1)S(1)}, u32[]{:S(2)}, u32[]{:S(2)}) collective-permute-start(bf16[256,768]{1,0:T(8,128)(2,1)S(1)} %shard_map.408.refs_1_.refs_0_), channel_id=1, source_target_pairs={{0,2},{1,3},{2,0},{3,1},{4,6},{5,7},{6,4},{7,5},{8,10},{9,11},{10,... | collective-permute-start | bytes 1179656 | tf_op jit(solution)/shard_map/ppermute | solution.py:930
  55.0 13.3 %collective-permute-start.28 = (bf16[1152,128]{1,0:T(8,128)(2,1)S(1)}, bf16[1152,128]{1,0:T(8,128)(2,1)S(1)}, u32[]{:S(2)}, u32[]{:S(2)}) collective-permute-start(bf16[1152,128]{1,0:T(8,128)(2,1)S(1)} %get-tuple-element.208), channel_id=1, source_target_pairs={{0,4},{4,0},{8,12},{12,8},{16,20},{20,16},{24,28},{28,24},{1,5},{5... | collective-permute-start | bytes 884744 | tf_op jit(solution)/shard_map/ppermute | solution.py:930
  57.0 11.3 %collective-permute-start.30 = (bf16[1152,128]{1,0:T(8,128)(2,1)S(1)}, bf16[1152,128]{1,0:T(8,128)(2,1)S(1)}, u32[]{:S(2)}, u32[]{:S(2)}) collective-permute-start(bf16[1152,128]{1,0:T(8,128)(2,1)S(1)} %get-tuple-element.210), channel_id=1, source_target_pairs={{0,8},{4,12},{8,0},{12,4},{16,24},{20,28},{24,16},{28,20},{1,9},{5... | collective-permute-start | bytes 884744 | tf_op jit(solution)/shard_map/ppermute | solution.py:930
  57.2 7.1 %collective-permute-start.27 = (bf16[144,768]{1,0:T(8,128)(2,1)S(1)}, bf16[144,768]{1,0:T(8,128)(2,1)S(1)}, u32[]{:S(2)}, u32[]{:S(2)}) collective-permute-start(bf16[144,768]{1,0:T(8,128)(2,1)S(1)} %get-tuple-element.203), channel_id=1, source_target_pairs={{0,2},{1,3},{2,0},{3,1},{4,6},{5,7},{6,4},{7,5},{8,10},{9,11},{10,... | collective-permute-start | bytes 663560 | tf_op jit(solution)/shard_map/ppermute | solution.py:930
  59.7 15.0 %collective-permute-start.34 = (bf16[1152,128]{1,0:T(8,128)(2,1)S(1)}, bf16[1152,128]{1,0:T(8,128)(2,1)S(1)}, u32[]{:S(2)}, u32[]{:S(2)}) collective-permute-start(bf16[1152,128]{1,0:T(8,128)(2,1)S(1)} %get-tuple-element.217), channel_id=1, source_target_pairs={{0,8},{4,12},{8,0},{12,4},{16,24},{20,28},{24,16},{28,20},{1,9},{5... | collective-permute-start | bytes 884744 | tf_op jit(solution)/shard_map/ppermute | solution.py:930
  64.5 8.2 %collective-permute-start.29 = (bf16[816,128]{1,0:T(8,128)(2,1)S(1)}, bf16[816,128]{1,0:T(8,128)(2,1)S(1)}, u32[]{:S(2)}, u32[]{:S(2)}) collective-permute-start(bf16[816,128]{1,0:T(8,128)(2,1)S(1)} %get-tuple-element.209), channel_id=1, source_target_pairs={{0,4},{4,0},{8,12},{12,8},{16,20},{20,16},{24,28},{28,24},{1,5},{5... | collective-permute-start | bytes 626696 | tf_op jit(solution)/shard_map/ppermute | solution.py:930
  66.9 11.5 %collective-permute-start.33 = (bf16[1152,128]{1,0:T(8,128)(2,1)S(1)}, bf16[1152,128]{1,0:T(8,128)(2,1)S(1)}, u32[]{:S(2)}, u32[]{:S(2)}) collective-permute-start(bf16[1152,128]{1,0:T(8,128)(2,1)S(1)} %get-tuple-element.216), channel_id=1, source_target_pairs={{0,4},{4,0},{8,12},{12,8},{16,20},{20,16},{24,28},{28,24},{1,5},{5... | collective-permute-start | bytes 884744 | tf_op jit(solution)/shard_map/ppermute | solution.py:930
  72.9 7.5 %collective-permute-start.32 = (bf16[576,128]{1,0:T(8,128)(2,1)S(1)}, bf16[576,128]{1,0:T(8,128)(2,1)S(1)}, u32[]{:S(2)}, u32[]{:S(2)}) collective-permute-start(bf16[576,128]{1,0:T(8,128)(2,1)S(1)} %get-tuple-element.215), channel_id=1, source_target_pairs={{0,4},{4,0},{8,12},{12,8},{16,20},{20,16},{24,28},{28,24},{1,5},{5... | collective-permute-start | bytes 442376 | tf_op jit(solution)/shard_map/ppermute | solution.py:930
  74.0 9.6 %collective-permute-start.31 = (bf16[1136,128]{1,0:T(8,128)(2,1)S(1)}, bf16[1136,128]{1,0:T(8,128)(2,1)S(1)}, u32[]{:S(2)}, u32[]{:S(2)}) collective-permute-start(bf16[1136,128]{1,0:T(8,128)(2,1)S(1)} %get-tuple-element.214), channel_id=1, source_target_pairs={{0,8},{4,12},{8,0},{12,4},{16,24},{20,28},{24,16},{28,20},{1,9},{5... | collective-permute-start | bytes 872456 | tf_op jit(solution)/shard_map/ppermute | solution.py:930
  74.8 17.6 %collective-permute-start.36 = (bf16[576,128]{1,0:T(8,128)(2,1)S(1)}, bf16[576,128]{1,0:T(8,128)(2,1)S(1)}, u32[]{:S(2)}, u32[]{:S(2)}) collective-permute-start(bf16[576,128]{1,0:T(8,128)(2,1)S(1)} %get-tuple-element.235), channel_id=1, source_target_pairs={{0,16},{4,20},{8,24},{12,28},{16,0},{20,4},{24,8},{28,12},{1,17},{... | collective-permute-start | bytes 442376 | tf_op jit(solution)/shard_map/ppermute | solution.py:930
  78.5 17.1 %collective-permute-start.37 = (bf16[576,128]{1,0:T(8,128)(2,1)S(1)}, bf16[576,128]{1,0:T(8,128)(2,1)S(1)}, u32[]{:S(2)}, u32[]{:S(2)}) collective-permute-start(bf16[576,128]{1,0:T(8,128)(2,1)S(1)} %get-tuple-element.236), channel_id=1, source_target_pairs={{0,16},{4,20},{8,24},{12,28},{16,0},{20,4},{24,8},{28,12},{1,17},{... | collective-permute-start | bytes 442376 | tf_op jit(solution)/shard_map/ppermute | solution.py:930
  83.6 15.3 %collective-permute-start.35 = (bf16[1008,128]{1,0:T(8,128)(2,1)S(1)}, bf16[1008,128]{1,0:T(8,128)(2,1)S(1)}, u32[]{:S(2)}, u32[]{:S(2)}) collective-permute-start(bf16[1008,128]{1,0:T(8,128)(2,1)S(1)} %get-tuple-element.222), channel_id=1, source_target_pairs={{0,16},{4,20},{8,24},{12,28},{16,0},{20,4},{24,8},{28,12},{1,17},{... | collective-permute-start | bytes 774152 | tf_op jit(solution)/shard_map/ppermute | solution.py:930
  (25 other events, 122.1 us)
